TPU v7x, 256 devices: a whole 4x4x8 slice. The times are simulated.
256 devices in a mesh: seq: 16 (over x, y_lo, core), head: 16 (over z, y_hi).
Axes of the slice: x: 4, y: 4 (y_hi: 2, y_lo: 2; y = y_hi * 2 + y_lo), z: 8, core: 2. Of those that a mesh axis runs over, the one named last changes fastest.
Arguments:
- attn_out: bfloat16 [4096, 8192], P('seq', 'head'), may hold values from -6 to 6
- out_weight: bfloat16 [8192, 7168], P('head'), may hold values from -0.0625 to 0.0625
- residual: bfloat16 [4096, 7168], P(('seq', 'head')), may hold values from -6 to 6
- norm_gain: bfloat16 [7168], replicated, may hold values from 0.25 to 1.75
- latent_weight: bfloat16 [7168, 1536], P(None, 'head'), may hold values from -0.0625 to 0.0625
- index_proj: bfloat16 [7168, 64], P(None, 'head'), may hold values from -0.25 to 0.25
- latent_gain: bfloat16 [1536], replicated, may hold values from 0.25 to 1.75
- index_weight: bfloat16 [1536, 8192], P(None, 'head'), may hold values from -0.15625 to 0.15625
- index_keys: bfloat16 [16384, 128], P('seq'), may hold values from -6 to 6
- positions: int32 [4096], replicated, may hold values from 0 to 16383
- cache_len: int32 [16], P('seq'), may hold values from 256 to 1024, as said below
Outputs:
- hidden: bfloat16 [4096, 7168], P(('seq', 'head'))
- latent: bfloat16 [4096, 1536], P('seq', 'head')
- index_scores: float32 [4096, 16384], P('head', 'seq')
Inputs may be any that keep to these rules, and one draw needn't show every extreme that they name: Cache block b holds keys in its first cache_len[b] slots; some block is full in every draw.
All inputs are finite; a program needn't handle non-finite values.
Results may differ from a plain program's by a relative error of at most 0.035.
Values may be sent and summed in bfloat16 or wider, within the bound.
No kernel may reach another device: no remote copies, remote signals or barrier semaphores. Data moves between devices by JAX's collectives and lax.ppermute only.
A program may use at most 128 MiB of HBM per device.

v0:
```python
import math

import jax
import jax.numpy as jnp
from jax import lax
from jax.sharding import PartitionSpec as P

IHEADS = 64
IDIM = 128


EPSILON = 1e-06


def rms_round(values, gain):
    widened = values.astype(jnp.float32)
    inverse = lax.rsqrt(jnp.mean(widened * widened, axis=-1, keepdims=True) + EPSILON)
    return (widened * inverse * gain.astype(jnp.float32)).astype(jnp.bfloat16)


def score_group(query_rows, weight_rows, keys_block):
    count = query_rows.shape[0]
    head_count = weight_rows.shape[1]
    group = math.gcd(head_count, 8)
    scale = IDIM ** (-0.5)

    def add_group(step, total):
        q_part = query_rows.reshape(count, group, IDIM)
        w_part = weight_rows.astype(jnp.float32)
        logits = (
            jnp.einsum("njd,sd->njs", q_part, keys_block, preferred_element_type=jnp.float32)
            * scale
        )
        return total + jnp.einsum(
            "njs,nj->ns", jnp.maximum(logits, 0.0), w_part, precision=lax.Precision.HIGHEST
        )

    return lax.fori_loop(
        0, head_count // group, add_group, jnp.zeros((count, keys_block.shape[0]), jnp.float32)
    )


def score_rows(query_rows, weight_rows, keys_block):
    count = query_rows.shape[0]
    block_size = math.gcd(count, 512)
    q_blocks = query_rows.reshape(count // block_size, block_size, query_rows.shape[1])
    w_blocks = weight_rows.reshape(count // block_size, block_size, weight_rows.shape[1])

    def one_block(pair):
        return score_group(pair[0], pair[1], keys_block)

    return lax.map(one_block, (q_blocks, w_blocks)).reshape(count, keys_block.shape[0])


def shards(
    attn_out,
    out_weight,
    residual,
    norm_gain,
    latent_weight,
    index_proj,
    latent_gain,
    index_weight,
    index_keys,
    positions,
    cache_len,
):
    latent_local = latent_weight.shape[1]
    both_weights = jnp.concatenate([latent_weight, index_proj], axis=1)
    summed = lax.psum_scatter(
        jnp.dot(attn_out, out_weight, preferred_element_type=jnp.float32).astype(jnp.bfloat16),
        "head",
        scatter_dimension=0,
        tiled=True,
    ).astype(jnp.float32)
    hidden = (summed + residual.astype(jnp.float32)).astype(jnp.bfloat16)
    normed = rms_round(hidden, norm_gain)
    lifted = jnp.dot(
        lax.all_gather(normed, "head", axis=0, tiled=True),
        both_weights,
        preferred_element_type=jnp.float32,
    )
    latent_part = lifted[:, :latent_local].astype(jnp.bfloat16)
    head_weights = (lifted[:, latent_local:] * IHEADS ** (-0.5)).astype(jnp.bfloat16)
    latent_full = lax.all_gather(latent_part, "head", axis=1, tiled=True)
    latent_normed = rms_round(latent_full, latent_gain)
    latent_out = lax.dynamic_slice_in_dim(
        latent_normed, lax.axis_index("head") * latent_local, latent_local, 1
    )
    queries = jnp.dot(latent_normed, index_weight, preferred_element_type=jnp.float32).astype(
        jnp.bfloat16
    )
    all_queries, all_weights = (
        lax.all_gather(queries, "seq", axis=0, tiled=True),
        lax.all_gather(head_weights, "seq", axis=0, tiled=True),
    )
    result_rows = all_queries.shape[0] // lax.axis_size("head")
    scores = lax.psum_scatter(
        score_rows(all_queries, all_weights, index_keys).astype(jnp.bfloat16),
        "head",
        scatter_dimension=0,
        tiled=True,
    ).astype(jnp.float32)
    key_count = index_keys.shape[0]
    slot_local = jnp.arange(key_count, dtype=jnp.int32)
    slot_global = lax.axis_index("seq") * key_count + slot_local
    filled = slot_local < cache_len[0]
    own_positions = lax.dynamic_slice_in_dim(
        positions, lax.axis_index("head") * result_rows, result_rows, 0
    )
    visible = filled[None, :] & (slot_global[None, :] <= own_positions[:, None])
    index_scores = jnp.where(visible, scores, jnp.float32(0.0))
    return (hidden, latent_out, index_scores)


def solution(mesh):
    in_specs = (
        P("seq", "head"),
        P("head", None),
        P(("seq", "head"), None),
        P(),
        P(None, "head"),
        P(None, "head"),
        P(),
        P(None, "head"),
        P("seq", None),
        P(),
        P("seq"),
    )
    out_specs = (P(("seq", "head"), None), P("seq", "head"), P("head", "seq"))
    return jax.shard_map(shards, mesh=mesh, in_specs=in_specs, out_specs=out_specs, check_vma=False)
```

profile of v0, /device:TPU:1, one launch (start us, length us, event | category | flops | bytes accessed | tf_op | source)
XLA Modules:
  0.0 776.2 jit_solution(2908090917390887999)
XLA Ops:
  7.2 7.2 convolution_convert_fusion
  15.1 211.1 %reduce-scatter.3.cloned.1.call-done = bf16[16,7168]{1,0:T(8,128)(2,1)} async-done(((bf16[256,7168]{1,0:T(8,128)(2,1)}), bf16[16,7168]{1,0:T(8,128)(2,1)}) %reduce-scatter.3.cloned.1.call-update) | async-done | bytes 229392 | tf_op jit(solution)/shard_map/reduce_scatter | solution.py:70
  228.2 96.7 %all-gather.3.cloned.1.call-done = bf16[256,7168]{1,0:T(8,128)(2,1)} async-done(((bf16[16,7168]{1,0:T(8,128)(2,1)}), bf16[256,7168]{1,0:T(8,128)(2,1)}) %all-gather.3.cloned.1.call-update) | async-done | bytes 3670032 | tf_op jit(solution)/shard_map/all_gather | solution.py:79
  324.9 3.3 fusion.13
  328.3 35.1 %all_gather.13 = bf16[256,1536]{0,1:T(8,128)(2,1)S(1)} all-gather(bf16[256,96]{0,1:T(8,128)(2,1)S(1)} %slice.15), channel_id=1, replica_groups=mesh['seq'=16,'head'=16] {'head'}, dimensions={1}, use_global_device_ids=true | all-gather | bytes 835584 | tf_op jit(solution)/shard_map/all_gather | solution.py:85
  366.1 31.1 %all_gather.15 = bf16[4096,4]{0,1:T(4,128)(2,1)S(1)} all-gather(bf16[256,4]{0,1:T(4,128)(2,1)S(1)} %fusion.20), channel_id=1, replica_groups=mesh['seq'=16,'head'=16] {'seq'}, dimensions={0}, use_global_device_ids=true | all-gather | bytes 34816 | tf_op jit(solution)/shard_map/all_gather | solution.py:95
  397.2 17.5 %all-gather.5.cloned.1.call-done = bf16[4096,512]{1,0:T(8,128)(2,1)} async-done(((bf16[256,512]{1,0:T(8,128)(2,1)}), bf16[4096,512]{1,0:T(8,128)(2,1)}) %all-gather.5.cloned.1.call-update) | async-done | bytes 4194320 | tf_op jit(solution)/shard_map/all_gather | solution.py:94
  414.7 134.0 %while.10 = (s32[]{:T(128)}, bf16[8,512,1024]{2,1,0:T(8,128)(2,1)}, bf16[8,512,512]{2,1,0:T(8,128)(2,1)}, bf16[1024,128]{1,0:T(8,128)(2,1)S(1)}, bf16[8,512,4]{1,2,0:T(4,128)(2,1)S(1)}, /*index=5*/s32[]{:T(128)}) while((s32[]{:T(128)}, bf16[8,512,1024]{2,1,0:T(8,128)(2,1)}, bf16[8,512,512]{2,1,0:T(8,128)(2,1)}, ...), condition=%wide.region_4.5_spmd, body=%wide.region_3.4_spmd.sunk | while | flops 566231040 | bytes 22827096 | solution.py:52
  417.4 12.7 %fusion.39 = bf16[512,1,1024]{2,1,0:T(2,128)(2,1)S(1)} fusion(bf16[512,4,1]{1,2,0:T(2,128)(2,1)S(1)} %copy.33, f32[512,4,1024]{2,0,1:T(8,128)S(1)} %fusion.38), kind=kOutput, calls=%fused_computation.2.clone.1 | convolution fusion | flops 29360128 | bytes 9441280 | tf_op jit(solution)/shard_map/while/body/eval_jaxpr/while/body/eval_jaxpr/njs,nj->ns/dot_general | solution.py:34
  434.1 12.7 %fusion.39 = bf16[512,1,1024]{2,1,0:T(2,128)(2,1)S(1)} fusion(bf16[512,4,1]{1,2,0:T(2,128)(2,1)S(1)} %copy.33, f32[512,4,1024]{2,0,1:T(8,128)S(1)} %fusion.38), kind=kOutput, calls=%fused_computation.2.clone.1 | convolution fusion | flops 29360128 | bytes 9441280 | tf_op jit(solution)/shard_map/while/body/eval_jaxpr/while/body/eval_jaxpr/njs,nj->ns/dot_general | solution.py:34
  446.8 1.4 bitcast_dynamic-update-slice_fusion.2
  450.9 12.7 %fusion.39 = bf16[512,1,1024]{2,1,0:T(2,128)(2,1)S(1)} fusion(bf16[512,4,1]{1,2,0:T(2,128)(2,1)S(1)} %copy.33, f32[512,4,1024]{2,0,1:T(8,128)S(1)} %fusion.38), kind=kOutput, calls=%fused_computation.2.clone.1 | convolution fusion | flops 29360128 | bytes 9441280 | tf_op jit(solution)/shard_map/while/body/eval_jaxpr/while/body/eval_jaxpr/njs,nj->ns/dot_general | solution.py:34
  463.6 1.4 bitcast_dynamic-update-slice_fusion.2
  467.6 12.7 %fusion.39 = bf16[512,1,1024]{2,1,0:T(2,128)(2,1)S(1)} fusion(bf16[512,4,1]{1,2,0:T(2,128)(2,1)S(1)} %copy.33, f32[512,4,1024]{2,0,1:T(8,128)S(1)} %fusion.38), kind=kOutput, calls=%fused_computation.2.clone.1 | convolution fusion | flops 29360128 | bytes 9441280 | tf_op jit(solution)/shard_map/while/body/eval_jaxpr/while/body/eval_jaxpr/njs,nj->ns/dot_general | solution.py:34
  484.4 12.7 %fusion.39 = bf16[512,1,1024]{2,1,0:T(2,128)(2,1)S(1)} fusion(bf16[512,4,1]{1,2,0:T(2,128)(2,1)S(1)} %copy.33, f32[512,4,1024]{2,0,1:T(8,128)S(1)} %fusion.38), kind=kOutput, calls=%fused_computation.2.clone.1 | convolution fusion | flops 29360128 | bytes 9441280 | tf_op jit(solution)/shard_map/while/body/eval_jaxpr/while/body/eval_jaxpr/njs,nj->ns/dot_general | solution.py:34
  501.1 12.7 %fusion.39 = bf16[512,1,1024]{2,1,0:T(2,128)(2,1)S(1)} fusion(bf16[512,4,1]{1,2,0:T(2,128)(2,1)S(1)} %copy.33, f32[512,4,1024]{2,0,1:T(8,128)S(1)} %fusion.38), kind=kOutput, calls=%fused_computation.2.clone.1 | convolution fusion | flops 29360128 | bytes 9441280 | tf_op jit(solution)/shard_map/while/body/eval_jaxpr/while/body/eval_jaxpr/njs,nj->ns/dot_general | solution.py:34
  513.8 1.4 bitcast_dynamic-update-slice_fusion.2
  517.9 12.7 %fusion.39 = bf16[512,1,1024]{2,1,0:T(2,128)(2,1)S(1)} fusion(bf16[512,4,1]{1,2,0:T(2,128)(2,1)S(1)} %copy.33, f32[512,4,1024]{2,0,1:T(8,128)S(1)} %fusion.38), kind=kOutput, calls=%fused_computation.2.clone.1 | convolution fusion | flops 29360128 | bytes 9441280 | tf_op jit(solution)/shard_map/while/body/eval_jaxpr/while/body/eval_jaxpr/njs,nj->ns/dot_general | solution.py:34
  530.5 1.4 bitcast_dynamic-update-slice_fusion.2
  534.6 12.7 %fusion.39 = bf16[512,1,1024]{2,1,0:T(2,128)(2,1)S(1)} fusion(bf16[512,4,1]{1,2,0:T(2,128)(2,1)S(1)} %copy.33, f32[512,4,1024]{2,0,1:T(8,128)S(1)} %fusion.38), kind=kOutput, calls=%fused_computation.2.clone.1 | convolution fusion | flops 29360128 | bytes 9441280 | tf_op jit(solution)/shard_map/while/body/eval_jaxpr/while/body/eval_jaxpr/njs,nj->ns/dot_general | solution.py:34
  547.3 1.4 bitcast_dynamic-update-slice_fusion.2
  550.1 1.4 constant_dynamic-slice_fusion.1
  551.6 215.8 %reduce-scatter.5.cloned.1.call-done = bf16[256,1024]{1,0:T(8,128)(2,1)} async-done(((bf16[4096,1024]{1,0:T(8,128)(2,1)}), bf16[256,1024]{1,0:T(8,128)(2,1)}) %reduce-scatter.5.cloned.1.call-update) | async-done | bytes 524304 | tf_op jit(solution)/shard_map/reduce_scatter | solution.py:98
  767.4 2.3 convert_select_fusion
  (82 shorter events, 31.7 us)
Async XLA Ops:
  7.2 357.6 %copy-start = (bf16[1536,512]{1,0:T(8,128)(2,1)S(1)}, bf16[1536,512]{1,0:T(8,128)(2,1)}, u32[]{:S(2)}) copy-start(bf16[1536,512]{1,0:T(8,128)(2,1)} %param.20) | copy-start | bytes 4718596
  7.2 219.0 %reduce-scatter.3.cloned.1.call-start = ((), (), s32[]{:S(2)}) async-start(), calls=%async_computation.2 | async-start | bytes 3899392 | tf_op jit(solution)/shard_map/reduce_scatter | solution.py:70
  14.4 0.7 copy-start.5
  14.4 211.8 %copy-start.4 = (bf16[16,7168]{1,0:T(8,128)(2,1)S(1)}, bf16[16,7168]{1,0:T(8,128)(2,1)}, u32[]{:S(2)}) copy-start(bf16[16,7168]{1,0:T(8,128)(2,1)} %param.15) | copy-start | bytes 688132
  14.4 213.8 %copy-start.6 = (bf16[1536]{0:T(1024)(128)(2,1)S(1)}, bf16[1536]{0:T(1024)(128)(2,1)}, u32[]{:S(2)}) copy-start(bf16[1536]{0:T(1024)(128)(2,1)} %param.19) | copy-start | bytes 9220
  14.4 310.6 %copy-start.7 = (bf16[7168,96]{0,1:T(8,128)(2,1)S(1)}, bf16[7168,96]{0,1:T(8,128)(2,1)}, u32[]{:S(2)}) copy-start(bf16[7168,96]{0,1:T(8,128)(2,1)} %param.17) | copy-start | bytes 4128772
  14.4 310.5 %all-gather.3.cloned.1.call-start = ((), (), s32[]{:S(2)}) async-start(), calls=%async_computation.3 | async-start | bytes 3899392 | tf_op jit(solution)/shard_map/all_gather | solution.py:79
  227.3 136.0 %copy-start.3 = (bf16[16,7168]{1,0:T(8,128)(2,1)}, bf16[16,7168]{1,0:T(8,128)(2,1)S(1)}, u32[]{:S(2)}) copy-start(bf16[16,7168]{1,0:T(8,128)(2,1)S(1)} %get-tuple-element.62) | copy-start | bytes 688132
  228.2 186.5 %all-gather.5.cloned.1.call-start = ((), (), s32[]{:S(2)}) async-start(), calls=%async_computation.4 | async-start | bytes 4456448 | tf_op jit(solution)/shard_map/all_gather | solution.py:94
  328.2 86.5 %copy-start.1 = (bf16[1024,128]{1,0:T(8,128)(2,1)S(1)}, bf16[1024,128]{1,0:T(8,128)(2,1)}, u32[]{:S(2)}) copy-start(bf16[1024,128]{1,0:T(8,128)(2,1)} %param.21) | copy-start | bytes 786436
  363.9 0.9 copy-start.2
  366.1 401.3 %reduce-scatter.5.cloned.1.call-start = ((), (), s32[]{:S(2)}) async-start(), calls=%async_computation.5 | async-start | bytes 8912896 | tf_op jit(solution)/shard_map/reduce_scatter | solution.py:98
Sparse Core Ops, SparseCore 0:
  14.5 211.5 reduce-scatter.2
  229.7 95.2 all-gather.2
  366.2 48.4 all-gather.4
  548.8 218.4 reduce-scatter.4
where the time goes:
time: 780 us; the launch traced here: 776 us
  waiting for transfers between devices  541 us (69%)
  matrix products  123 us (16%)
  blocking collectives  66.1 us (8%)
  local copies, waits for them, and re-layouts  26 us (3%)
  between operations  14.5 us (2%)
    reduce_scatter x1, waiting for transfers between devices, shards(): lax.psum_scatter(score_rows(all_queries, all_weights, index_keys).astype(...  216 us
    reduce_scatter x1, waiting for transfers between devices, shards(): lax.psum_scatter(jnp.dot(attn_out, out_weight, preferred_element_type=jnp...  211 us
    dot_general x8, matrix products, add_group(): jnp.einsum('njs,nj->ns', jnp.maximum(logits, 0.0), w_part, precision=lax....  101 us
    all_gather x1, waiting for transfers between devices, shards(): lax.all_gather(normed, 'head', axis=0, tiled=True)  96.7 us
    all_gather x1, blocking collectives, shards(): latent_full = lax.all_gather(latent_part, 'head', axis=1, tiled=True)  35.1 us
    all_gather x1, blocking collectives, shards(): lax.all_gather(head_weights, 'seq', axis=0, tiled=True)  31.1 us
    all_gather x1, waiting for transfers between devices, shards(): lax.all_gather(queries, 'seq', axis=0, tiled=True)  17.5 us
  transfers between devices with their start and end apart: 4, of which 4 were waited for; matrix products, arithmetic and copies ran while one was open for 0% of the time, Pallas kernels for 0%

commit v1 on v0

v1 whole, which is shorter than its diff:
```python
import functools

import jax
import jax.numpy as jnp
from jax import lax
from jax.experimental import pallas as pl
from jax.experimental.pallas import tpu as pltpu
from jax.sharding import Mesh
from jax.sharding import PartitionSpec as P

D = 7168
QL = 1536
IHEADS = 64
IDIM = 128
N_SEQ = 16
N_HEAD = 16
NZ = 8
DZ = D // NZ
EPSILON = 1e-06
SEQ = ("x", "yl", "c")
HEAD = ("z", "yh")
WIDE = 512 + 128


def rms_round(values, gain):
    widened = values.astype(jnp.float32)
    inverse = lax.rsqrt(jnp.mean(widened * widened, axis=-1, keepdims=True) + EPSILON)
    return (widened * inverse * gain.astype(jnp.float32)).astype(jnp.bfloat16)


def swap(values, axis):
    return lax.ppermute(values, axis, [(0, 1), (1, 0)])


def in_order(mine, other, index, axis):
    first = jnp.where(index == 0, mine, other)
    second = jnp.where(index == 0, other, mine)
    return jnp.stack([first, second], axis=axis)


def project_kernel(a_ref, b_ref, o_ref):
    o_ref[0] = jnp.dot(a_ref[...], b_ref[...], preferred_element_type=jnp.float32).astype(o_ref.dtype)


def project(attn_out, out_weight):
    rows, depth = attn_out.shape
    return pl.pallas_call(
        project_kernel,
        grid=(NZ,),
        in_specs=[
            pl.BlockSpec((rows, depth), lambda i: (0, 0)),
            pl.BlockSpec((depth, DZ), lambda i: (0, i)),
        ],
        out_specs=pl.BlockSpec((1, rows, DZ), lambda i: (i, 0, 0)),
        out_shape=jax.ShapeDtypeStruct((NZ, rows, DZ), jnp.bfloat16),
        compiler_params=pltpu.CompilerParams(vmem_limit_bytes=32 * 1024 * 1024),
    )(attn_out, out_weight)


def query_kernel(latent_ref, weight_ref, heads_ref, pick_ref, o_ref):
    o_ref[:, :512] = jnp.dot(
        latent_ref[...], weight_ref[...], preferred_element_type=jnp.float32
    ).astype(jnp.bfloat16)
    o_ref[:, 512:] = jnp.dot(
        heads_ref[...], pick_ref[...], preferred_element_type=jnp.float32
    ).astype(jnp.bfloat16)


def make_queries(latent, weight, heads, pick):
    rows = latent.shape[0]
    return pl.pallas_call(
        query_kernel,
        out_shape=jax.ShapeDtypeStruct((rows, WIDE), jnp.bfloat16),
        compiler_params=pltpu.CompilerParams(vmem_limit_bytes=32 * 1024 * 1024),
    )(latent, weight, heads, pick)


def score_kernel(limits_ref, q_ref, k_ref, pos_ref, o_ref):
    step = pl.program_id(0)
    scale = IDIM ** (-0.5)
    rows, slots = o_ref.shape
    tile_rows, tile_slots = 64, 256

    @pl.when(step == 0)
    def _():
        o_ref[...] = jnp.zeros_like(o_ref)

    for at in range(0, rows, tile_rows):
        weights = [
            jnp.broadcast_to(
                q_ref[0, at : at + tile_rows, 512 : 640].astype(jnp.float32)[:, j : j + 1] * scale,
                (tile_rows, tile_slots),
            )
            for j in range(4)
        ]
        for slot in range(0, slots, tile_slots):
            total = o_ref[at : at + tile_rows, slot : slot + tile_slots]
            for j in range(4):
                logits = jnp.dot(
                    q_ref[0, at : at + tile_rows, j * IDIM : (j + 1) * IDIM],
                    k_ref[:, slot : slot + tile_slots],
                    preferred_element_type=jnp.float32,
                )
                total = total + jnp.maximum(logits, 0.0) * weights[j]
            o_ref[at : at + tile_rows, slot : slot + tile_slots] = total

    @pl.when(step == pl.num_programs(0) - 1)
    def _():
        local = lax.broadcasted_iota(jnp.int32, (tile_rows, slots), 1)
        for at in range(0, rows, tile_rows):
            reach = jnp.minimum(limits_ref[0], pos_ref[at : at + tile_rows, :] - limits_ref[1] + 1)
            o_ref[at : at + tile_rows, :] = jnp.where(
                local < reach, o_ref[at : at + tile_rows, :], 0.0
            )


def make_scores(limits, queries, keys_t, own_positions):
    chunks, rows, _ = queries.shape
    slots = keys_t.shape[1]
    return pl.pallas_call(
        score_kernel,
        grid=(chunks,),
        in_specs=[
            pl.BlockSpec(memory_space=pltpu.SMEM),
            pl.BlockSpec((1, rows, WIDE), lambda i: (i, 0, 0)),
            pl.BlockSpec((IDIM, slots), lambda i: (0, 0)),
            pl.BlockSpec((rows, 1), lambda i: (0, 0)),
        ],
        out_specs=pl.BlockSpec((rows, slots), lambda i: (0, 0)),
        out_shape=jax.ShapeDtypeStruct((rows, slots), jnp.float32),
        compiler_params=pltpu.CompilerParams(vmem_limit_bytes=32 * 1024 * 1024),
    )(limits, queries, keys_t, own_positions)


def down_weight_rows(latent_weight, index_proj, z, yl, yh, x, c):
    piece = c * 8 + x * 2 + yl
    share = DZ // N_SEQ

    def own_rows(weight):
        return lax.dynamic_slice_in_dim(weight.reshape(NZ, DZ, weight.shape[1]), piece * share, share, 1)

    own = jnp.concatenate([own_rows(latent_weight), own_rows(index_proj)], axis=2)
    mine = lax.all_to_all(own, "z", 0, 0)
    both = in_order(mine, swap(mine, "yh"), yh, 1)
    by_head = both.reshape(N_HEAD, share, own.shape[2]).transpose(1, 0, 2)
    local = latent_weight.shape[1]
    wide = jnp.concatenate(
        [by_head[:, :, :local].reshape(share, QL), by_head[:, :, local:].reshape(share, IHEADS)], axis=1
    )
    half = lax.all_to_all(jnp.broadcast_to(wide[None], (8,) + wide.shape), ("x", "yl"), 0, 0)
    half = half.reshape(8 * share, wide.shape[1])
    return in_order(half, swap(half, "c"), c, 0).reshape(DZ, wide.shape[1])


def shards(
    attn_out,
    out_weight,
    residual,
    norm_gain,
    latent_weight,
    index_proj,
    latent_gain,
    index_weight,
    index_keys,
    positions,
    cache_len,
):
    x, yl, c = (lax.axis_index(a) for a in SEQ)
    z, yh = (lax.axis_index(a) for a in HEAD)
    seq = (x * 2 + yl) * 2 + c
    head = z * 2 + yh
    rows = attn_out.shape[0]
    own = rows // N_HEAD

    partial = project(attn_out, out_weight)
    summed = lax.psum_scatter(partial, "z", scatter_dimension=0, tiled=False)

    down = down_weight_rows(latent_weight, index_proj, z, yl, yh, x, c)
    residual_cols = lax.all_to_all(residual.reshape(own, NZ, DZ).transpose(1, 0, 2), "z", 0, 0)

    halves = summed.reshape(NZ, 2, own, DZ)
    kept = lax.dynamic_index_in_dim(halves, yh, 1, keepdims=False)
    given = lax.dynamic_index_in_dim(halves, 1 - yh, 1, keepdims=False)
    got = swap(given, "yh")
    hidden = (
        kept.astype(jnp.float32) + got.astype(jnp.float32) + residual_cols.astype(jnp.float32)
    ).astype(jnp.bfloat16)
    wide_hidden = hidden.reshape(NZ * own, DZ).astype(jnp.float32)
    gain = lax.dynamic_slice_in_dim(norm_gain, z * DZ, DZ).astype(jnp.float32)
    squares = jnp.sum(wide_hidden * wide_hidden, axis=1, keepdims=True)
    high = lax.reduce_precision(squares, 8, 7)
    lifted = jnp.dot(
        (wide_hidden * gain).astype(jnp.bfloat16), down, preferred_element_type=jnp.float32
    )
    lifted = jnp.concatenate(
        [
            lifted.astype(jnp.bfloat16),
            high.astype(jnp.bfloat16),
            (squares - high).astype(jnp.bfloat16),
            jnp.zeros((NZ * own, 62), jnp.bfloat16),
        ],
        axis=1,
    )
    parts = lax.all_to_all(lifted.reshape(NZ, own, lifted.shape[1]), "z", 0, 0)
    total = jnp.sum(parts.astype(jnp.float32), axis=0)
    mean = (total[:, 1600:1601] + total[:, 1601:1602]) / D
    inverse = lax.rsqrt(mean + EPSILON)
    latent_raw = (total[:, :QL] * inverse).astype(jnp.bfloat16)
    head_weights = (total[:, QL:1600] * inverse * IHEADS ** (-0.5)).astype(jnp.bfloat16)
    latent = rms_round(latent_raw, latent_gain)
    packed = jnp.concatenate([latent, head_weights, jnp.zeros((own, 64), jnp.bfloat16)], axis=1)
    pair = in_order(packed, swap(packed, "yh"), yh, 0)
    everyone = lax.all_gather(pair, "z", axis=0, tiled=False).reshape(rows, packed.shape[1])
    latent_full = everyone[:, :QL]
    latent_out = lax.dynamic_slice_in_dim(latent_full, head * 96, 96, 1)
    pick = (
        lax.broadcasted_iota(jnp.int32, (128, 128), 0)
        == lax.broadcasted_iota(jnp.int32, (128, 128), 1) + head * 4
    ) & (lax.broadcasted_iota(jnp.int32, (128, 128), 1) < 4)
    queries = make_queries(latent_full, index_weight, everyone[:, QL:], pick.astype(jnp.bfloat16))
    turned = lax.ppermute(
        queries, SEQ + HEAD, [(s * N_HEAD + h, h * N_HEAD + s) for s in range(N_SEQ) for h in range(N_HEAD)]
    )
    hidden, turned = lax.optimization_barrier((hidden, turned))
    hidden_rows = lax.all_to_all(hidden, "z", 0, 0).transpose(1, 0, 2).reshape(own, D)
    all_queries = lax.all_gather(turned, SEQ, axis=0, tiled=False)
    own_positions = lax.dynamic_slice_in_dim(positions, head * rows, rows).reshape(rows, 1)
    limits = jnp.stack([cache_len[0], seq * index_keys.shape[0]]).astype(jnp.int32)
    scores = make_scores(limits, all_queries, index_keys.T, own_positions)
    return (hidden_rows, latent_out, scores)


def solution(mesh):
    fine = Mesh(mesh.devices.reshape(4, 2, 2, 8, 2), SEQ + HEAD)
    in_specs = (
        P(SEQ, HEAD),
        P(HEAD, None),
        P(SEQ + HEAD, None),
        P(),
        P(None, HEAD),
        P(None, HEAD),
        P(),
        P(None, HEAD),
        P(SEQ, None),
        P(),
        P(SEQ),
    )
    out_specs = (P(SEQ + HEAD, None), P(SEQ, HEAD), P(HEAD, SEQ))
    return jax.shard_map(shards, mesh=fine, in_specs=in_specs, out_specs=out_specs, check_vma=False)
```

time: 780 us -> 253 us (0.32)
  waiting for transfers between devices: 541 us -> 62.1 us
  matrix products: 123 us -> 1.27 us
  starting transfers between devices: 0.16 us -> 62.7 us
  Pallas kernels: 0 us -> 18.3 us
    reduce_scatter x2 -> x1, waiting for transfers between devices: 427 us -> 0.01 us  [shards(): summed = lax.psum_scatter(partial, 'z', scatter_dimension=0, tiled=False)]
    dot_general x19 -> x1, matrix products: 123 us -> 1.27 us  [shards(): jnp.dot((wide_hidden * gain).astype(jnp.bfloat16), down, preferred_elemen...]
    all_gather x2 -> x1, waiting for transfers between devices: 114 us -> 25 us  [shards(): all_queries = lax.all_gather(turned, SEQ, axis=0, tiled=False)]
    all_gather x2 -> x1, blocking collectives: 66.1 us -> 20.9 us  [shards(): lax.all_gather(pair, 'z', axis=0, tiled=False)]
    all_to_all x0 -> x2, blocking collectives: none -> 41.1 us  [the longest x1 22.8 us: down_weight_rows(): lax.all_to_all(jnp.broadcast_to(wide[None], (8,) + wide.shape), ('x', 'yl...]
    all_to_all x0 -> x3, starting transfers between devices: none -> 33.4 us  [the longest x1 23.8 us: shards(): lax.all_to_all(hidden, 'z', 0, 0).transpose(1, 0, 2).reshape(own, D)]
    ppermute x0 -> x5, starting transfers between devices: none -> 29.2 us  [the longest x1 17.5 us: shards(): lax.ppermute(queries, SEQ + HEAD, [(s * N_HEAD + h, h * N_HEAD + s) for s...]
    all_to_all x0 -> x3, waiting for transfers between devices: none -> 25.6 us  [the longest x1 13.9 us: shards(): parts = lax.all_to_all(lifted.reshape(NZ, own, lifted.shape[1]), 'z', 0, 0)]
  transfers between devices with their start and end apart: 4 -> 10, of which waited for: 4 -> 8; matrix products, arithmetic and copies ran while one was open for 0% -> 6% of each run, Pallas kernels for 0% -> 0%
where the time goes in v1:
time: 253 us; the launch traced here: 252 us
  starting transfers between devices  62.7 us (25%)
  waiting for transfers between devices  62.1 us (25%)
  blocking collectives  61.9 us (24%)
  local copies, waits for them, and re-layouts  21.8 us (9%)
  Pallas kernels  18.3 us (7%)
  between operations  15 us (6%)
  other arithmetic  8.62 us (3%)
    all_gather x1, waiting for transfers between devices, shards(): all_queries = lax.all_gather(turned, SEQ, axis=0, tiled=False)  25 us
    all_to_all x1, starting transfers between devices, shards(): lax.all_to_all(hidden, 'z', 0, 0).transpose(1, 0, 2).reshape(own, D)  23.8 us
    all_to_all x1, blocking collectives, down_weight_rows(): lax.all_to_all(jnp.broadcast_to(wide[None], (8,) + wide.shape), ('x', 'yl...  22.8 us
    all_gather x1, blocking collectives, shards(): lax.all_gather(pair, 'z', axis=0, tiled=False)  20.9 us
    all_to_all x1, blocking collectives, down_weight_rows(): mine = lax.all_to_all(own, 'z', 0, 0)  18.3 us
    ppermute x1, starting transfers between devices, shards(): lax.ppermute(queries, SEQ + HEAD, [(s * N_HEAD + h, h * N_HEAD + s) for s...  17.5 us
    unnamed x26, local copies, waits for them, and re-layouts  14.4 us
    all_to_all x1, waiting for transfers between devices, shards(): parts = lax.all_to_all(lifted.reshape(NZ, own, lifted.shape[1]), 'z', 0, 0)  13.9 us
  transfers between devices with their start and end apart: 10, of which 8 were waited for; matrix products, arithmetic and copies ran while one was open for 6% of the time, Pallas kernels for 0%

profile of v1, /device:TPU:1, one launch (start us, length us, event | category | flops | bytes accessed | tf_op | source)
XLA Modules:
  0.0 251.7 jit_solution(17918537027488122638)
XLA Ops:
  7.2 3.1 %copy-done.1 = bf16[512,7168]{1,0:T(8,128)(2,1)S(1)} copy-done((bf16[512,7168]{1,0:T(8,128)(2,1)S(1)}, bf16[512,7168]{1,0:T(8,128)(2,1)}, u32[]{:S(2)}) %copy-start.1) | copy-done | bytes 7340056
  11.3 4.3 %shard_map.130 = bf16[8,256,896]{2,1,0:T(8,128)(2,1)S(1)} custom-call(bf16[256,512]{1,0:T(8,128)(2,1)S(1)} %copy-done.4, bf16[512,7168]{1,0:T(8,128)(2,1)S(1)} %copy-done.1), custom_call_target="tpu_custom_call" | custom-call | tf_op jit(solution)/shard_map/pallas_call | solution.py:47
  23.0 18.3 %all_to_all.25 = bf16[8,56,100]{2,1,0:T(8,128)(2,1)S(1)} all-to-all(bf16[8,56,100]{2,1,0:T(8,128)(2,1)S(1)} %pad_maximum_fusion.3), channel_id=1, replica_groups=mesh['x'=4,'yl'=2,'c'=2,'z'=8,'yh'=2] {'z'}, dimensions={0} | all-to-all | bytes 179200 | tf_op jit(solution)/shard_map/all_to_all | solution.py:143
  41.2 2.9 %collective-permute-start.1 = (bf16[8,56,100]{2,1,0:T(8,128)(2,1)S(1)}, bf16[8,56,100]{2,1,0:T(8,128)(2,1)S(1)}, u32[]{:S(2)}, u32[]{:S(2)}) collective-permute-start(bf16[8,56,100]{2,1,0:T(8,128)(2,1)S(1)} %all_to_all.25), channel_id=1, source_target_pairs={{0,1},{1,0},{2,3},{3,2},{4,5},{5,4},{6,7},{7,6},{8,9},{9,8},{10,11... | collective-permute-start | bytes 268808 | tf_op jit(solution)/shard_map/ppermute | solution.py:32
  44.1 2.2 collective-permute-done.1
  47.3 22.8 %all_to_all.26 = bf16[8,56,1600]{2,1,0:T(8,128)(2,1)S(1)} all-to-all(bf16[8,56,1600]{2,1,0:T(8,128)(2,1)S(1)} %broadcast_in_dim.6), channel_id=1, replica_groups=mesh['x'=4,'yl'=2,'c'=2,'z'=8,'yh'=2] {'x','yl'}, dimensions={0} | all-to-all | bytes 2867200 | tf_op jit(solution)/shard_map/all_to_all | solution.py:150
  70.1 3.9 %collective-permute-start.2 = (bf16[448,1600]{1,0:T(8,128)(2,1)S(1)}, bf16[448,1600]{1,0:T(8,128)(2,1)S(1)}, u32[]{:S(2)}, u32[]{:S(2)}) collective-permute-start(bf16[448,1600]{1,0:T(8,128)(2,1)S(1)} %bitcast.57), channel_id=1, source_target_pairs={{0,16},{16,0},{1,17},{17,1},{2,18},{18,2},{3,19},{19,3},{4,20},{20... | collective-permute-start | bytes 4300808 | tf_op jit(solution)/shard_map/ppermute | solution.py:32
  74.7 3.4 %all-to-all-start = ((bf16[8,16,896]{2,1,0:T(8,128)(2,1)}), bf16[8,16,896]{2,1,0:T(8,128)(2,1)S(1)}, u32[]{:S(2)}, u32[]{:S(2)}) async-start(bf16[8,16,896]{2,1,0:T(8,128)(2,1)} %bitcast.52), calls=%async_computation.1 | async-start | bytes 458752 | tf_op jit(solution)/shard_map/all_to_all | solution.py:179
  78.9 2.0 select_bitcast_fusion.1
  82.6 2.4 collective-permute-start
  85.0 2.1 pad_maximum_fusion
  87.1 2.6 %all-to-all-done = bf16[8,16,896]{2,1,0:T(8,128)(2,1)S(1)} async-done(((bf16[8,16,896]{2,1,0:T(8,128)(2,1)}), bf16[8,16,896]{2,1,0:T(8,128)(2,1)S(1)}, u32[]{:S(2)}, u32[]{:S(2)}) %all-to-all-start) | async-done | bytes 229408 | tf_op jit(solution)/shard_map/all_to_all | solution.py:179
  97.0 6.2 %all-to-all-start.3 = ((bf16[8,16,1664]{2,1,0:T(8,128)(2,1)}), bf16[8,16,1664]{2,1,0:T(8,128)(2,1)S(1)}, u32[]{:S(2)}, u32[]{:S(2)}) async-start(bf16[8,16,1664]{2,1,0:T(8,128)(2,1)} %concatenate.18), calls=%async_computation.4 | async-start | bytes 851968 | tf_op jit(solution)/shard_map/all_to_all | solution.py:204
  103.3 13.9 %all-to-all-done.3 = bf16[8,16,1664]{2,1,0:T(8,128)(2,1)S(1)} async-done(((bf16[8,16,1664]{2,1,0:T(8,128)(2,1)}), bf16[8,16,1664]{2,1,0:T(8,128)(2,1)S(1)}, u32[]{:S(2)}, u32[]{:S(2)}) %all-to-all-start.3) | async-done | bytes 426016 | tf_op jit(solution)/shard_map/all_to_all | solution.py:204
  118.0 2.4 collective-permute-start.3
  120.4 2.1 collective-permute-done.3
  122.5 20.9 %all-gather = bf16[16,16,1664]{2,1,0:T(8,128)(2,1)S(1)} all-gather(bf16[2,16,1664]{2,1,0:T(8,128)(2,1)S(1)} %pad_maximum_fusion.4), channel_id=2, replica_groups=mesh['x'=4,'yl'=2,'c'=2,'z'=8,'yh'=2] {'z'}, dimensions={0}, use_global_device_ids=true | all-gather | bytes 958464 | tf_op jit(solution)/shard_map/all_gather | solution.py:213
  144.1 17.5 %collective-permute-start.4 = (bf16[256,640]{1,0:T(8,128)(2,1)S(1)}, bf16[256,640]{1,0:T(8,128)(2,1)S(1)}, u32[]{:S(2)}, u32[]{:S(2)}) collective-permute-start(bf16[256,640]{1,0:T(8,128)(2,1)S(1)} %shard_map.131), channel_id=1, source_target_pairs={{0,0},{1,16},{2,32},{3,48},{4,64},{5,80},{6,96},{7,112},{8,128},{9... | collective-permute-start | bytes 983048 | tf_op jit(solution)/shard_map/ppermute | solution.py:221
  161.6 5.3 %collective-permute-done.4 = bf16[256,640]{1,0:T(8,128)(2,1)S(1)} collective-permute-done((bf16[256,640]{1,0:T(8,128)(2,1)S(1)}, bf16[256,640]{1,0:T(8,128)(2,1)S(1)}, u32[]{:S(2)}, u32[]{:S(2)}) %collective-permute-start.4) | collective-permute-done | bytes 327712 | tf_op jit(solution)/shard_map/ppermute | solution.py:221
  167.7 23.8 %all-to-all-start.4 = ((bf16[8,16,896]{2,1,0:T(8,128)(2,1)}), bf16[8,16,896]{2,1,0:T(8,128)(2,1)S(1)}, u32[]{:S(2)}, u32[]{:S(2)}) async-start(bf16[8,16,896]{2,1,0:T(8,128)(2,1)} %get-tuple-element.5), calls=%async_computation.5 | async-start | bytes 458752 | tf_op jit(solution)/shard_map/all_to_all | solution.py:225
  194.1 9.1 %all-to-all-done.4 = bf16[8,16,896]{2,1,0:T(8,128)(2,1)S(1)} async-done(((bf16[8,16,896]{2,1,0:T(8,128)(2,1)}), bf16[8,16,896]{2,1,0:T(8,128)(2,1)S(1)}, u32[]{:S(2)}, u32[]{:S(2)}) %all-to-all-start.4) | async-done | bytes 229408 | tf_op jit(solution)/shard_map/all_to_all | solution.py:225
  203.9 25.0 %all-gather.4.cloned.1.call-done = bf16[4096,640]{1,0:T(8,128)(2,1)} async-done(((bf16[256,640]{1,0:T(8,128)(2,1)}), bf16[4096,640]{1,0:T(8,128)(2,1)}) %all-gather.4.cloned.1.call-update) | async-done | bytes 5242896 | tf_op jit(solution)/shard_map/all_gather | solution.py:226
  229.0 2.5 copy-done.2
  231.5 13.4 %shard_map.132 = f32[256,1024]{1,0:T(8,128)} custom-call(s32[2]{0:T(128)S(1)} %pad_add_fusion.limits_ref, bf16[16,256,640]{2,1,0:T(8,128)(2,1)S(1)} %bitcast.54, bf16[128,1024]{1,0:T(8,128)(2,1)S(1)} %bitcast.55, s32[256,1]{1,0:T(8,128)S(1)} %copy.88.pos_ref), custom_call_target="tpu_custom_call" | custom-call | tf_op jit(solution)/shard_map/pallas_call | solution.py:120
  (77 shorter events, 24.4 us)
Async XLA Ops:
  7.2 73.8 %reduce-scatter.2.cloned.1.call-start = ((), (), s32[]{:S(2)}) async-start(), calls=%async_computation.6 | async-start | bytes 4128768 | tf_op jit(solution)/shard_map/reduce_scatter | solution.py:176
  7.2 3.1 %copy-start.1 = (bf16[512,7168]{1,0:T(8,128)(2,1)S(1)}, bf16[512,7168]{1,0:T(8,128)(2,1)}, u32[]{:S(2)}) copy-start(bf16[512,7168]{1,0:T(8,128)(2,1)} %b_ref.1) | copy-start | bytes 22020100
  10.3 0.9 copy-start.4
  15.6 1.8 copy-start
  17.3 0.8 copy-start.9
  17.4 2.6 %copy-start.5 = (bf16[7168,96]{0,1:T(8,128)(2,1)S(1)}, bf16[7168,96]{0,1:T(8,128)(2,1)}, u32[]{:S(2)}) copy-start(bf16[7168,96]{0,1:T(8,128)(2,1)} %param.15) | copy-start | bytes 4128772
  41.2 5.1 %collective-permute-start.1 = (bf16[8,56,100]{2,1,0:T(8,128)(2,1)S(1)}, bf16[8,56,100]{2,1,0:T(8,128)(2,1)S(1)}, u32[]{:S(2)}, u32[]{:S(2)}) collective-permute-start(bf16[8,56,100]{2,1,0:T(8,128)(2,1)S(1)} %all_to_all.25), channel_id=1, source_target_pairs={{0,1},{1,0},{2,3},{3,2},{4,5},{5,4},{6,7},{7,6},{8,9},{9,8},{10,11... | collective-permute-start | bytes 268808 | tf_op jit(solution)/shard_map/ppermute | solution.py:32
  47.3 26.7 %copy-start.8 = (bf16[16,7168]{1,0:T(8,128)(2,1)S(1)}, bf16[16,7168]{1,0:T(8,128)(2,1)}, u32[]{:S(2)}) copy-start(bf16[16,7168]{1,0:T(8,128)(2,1)} %param.13) | copy-start | bytes 688132
  70.1 8.8 %collective-permute-start.2 = (bf16[448,1600]{1,0:T(8,128)(2,1)S(1)}, bf16[448,1600]{1,0:T(8,128)(2,1)S(1)}, u32[]{:S(2)}, u32[]{:S(2)}) collective-permute-start(bf16[448,1600]{1,0:T(8,128)(2,1)S(1)} %bitcast.57), channel_id=1, source_target_pairs={{0,16},{16,0},{1,17},{17,1},{2,18},{18,2},{3,19},{19,3},{4,20},{20... | collective-permute-start | bytes 4300808 | tf_op jit(solution)/shard_map/ppermute | solution.py:32
  74.7 15.0 %all-to-all-start = ((bf16[8,16,896]{2,1,0:T(8,128)(2,1)}), bf16[8,16,896]{2,1,0:T(8,128)(2,1)S(1)}, u32[]{:S(2)}, u32[]{:S(2)}) async-start(bf16[8,16,896]{2,1,0:T(8,128)(2,1)} %bitcast.52), calls=%async_computation.1 | async-start | bytes 458752 | tf_op jit(solution)/shard_map/all_to_all | solution.py:179
  82.6 8.9 %collective-permute-start = (bf16[8,16,896]{2,1,0:T(8,128)(2,1)}, bf16[8,16,896]{2,1,0:T(8,128)(2,1)S(1)}, u32[]{:S(2)}, u32[]{:S(2)}) collective-permute-start(bf16[8,16,896]{2,1,0:T(8,128)(2,1)} %dynamic-slice_bitcast_fusion), channel_id=1, source_target_pairs={{0,1},{1,0},{2,3},{3,2},{4,5},{5,4},{6,7},{7,6},{8,9},{9,8},{10,11... | collective-permute-start | bytes 688136 | tf_op jit(solution)/shard_map/ppermute | solution.py:32
  95.5 7.7 %copy-start.10 = (bf16[1536]{0:T(1024)(128)(2,1)S(1)}, bf16[1536]{0:T(1024)(128)(2,1)}, u32[]{:S(2)}) copy-start(bf16[1536]{0:T(1024)(128)(2,1)} %param.17) | copy-start | bytes 9220
  97.0 20.3 %all-to-all-start.3 = ((bf16[8,16,1664]{2,1,0:T(8,128)(2,1)}), bf16[8,16,1664]{2,1,0:T(8,128)(2,1)S(1)}, u32[]{:S(2)}, u32[]{:S(2)}) async-start(bf16[8,16,1664]{2,1,0:T(8,128)(2,1)} %concatenate.18), calls=%async_computation.4 | async-start | bytes 851968 | tf_op jit(solution)/shard_map/all_to_all | solution.py:204
  103.2 125.8 %all-gather.4.cloned.1.call-start = ((), (), s32[]{:S(2)}) async-start(), calls=%async_computation.7 | async-start | bytes 5570560 | tf_op jit(solution)/shard_map/all_gather | solution.py:226
  117.3 26.2 %copy-start.3 = (bf16[1536,512]{1,0:T(8,128)(2,1)S(1)}, bf16[1536,512]{1,0:T(8,128)(2,1)}, u32[]{:S(2)}) copy-start(bf16[1536,512]{1,0:T(8,128)(2,1)} %weight_ref.1) | copy-start | bytes 4718596
  118.0 4.5 %collective-permute-start.3 = (bf16[16,1664]{1,0:T(8,128)(2,1)S(1)}, bf16[16,1664]{1,0:T(8,128)(2,1)S(1)}, u32[]{:S(2)}, u32[]{:S(2)}) collective-permute-start(bf16[16,1664]{1,0:T(8,128)(2,1)S(1)} %concatenate.19), channel_id=1, source_target_pairs={{0,1},{1,0},{2,3},{3,2},{4,5},{5,4},{6,7},{7,6},{8,9},{9,8},{10,11... | collective-permute-start | bytes 159752 | tf_op jit(solution)/shard_map/ppermute | solution.py:32
  143.5 48.7 %copy-start.7 = (bf16[1024,128]{1,0:T(8,128)(2,1)S(1)}, bf16[1024,128]{1,0:T(8,128)(2,1)}, u32[]{:S(2)}) copy-start(bf16[1024,128]{1,0:T(8,128)(2,1)} %param.19) | copy-start | bytes 786436
  144.1 22.8 %collective-permute-start.4 = (bf16[256,640]{1,0:T(8,128)(2,1)S(1)}, bf16[256,640]{1,0:T(8,128)(2,1)S(1)}, u32[]{:S(2)}, u32[]{:S(2)}) collective-permute-start(bf16[256,640]{1,0:T(8,128)(2,1)S(1)} %shard_map.131), channel_id=1, source_target_pairs={{0,0},{1,16},{2,32},{3,48},{4,64},{5,80},{6,96},{7,112},{8,128},{9... | collective-permute-start | bytes 983048 | tf_op jit(solution)/shard_map/ppermute | solution.py:221
  166.9 0.7 copy-start.6
  167.7 35.5 %all-to-all-start.4 = ((bf16[8,16,896]{2,1,0:T(8,128)(2,1)}), bf16[8,16,896]{2,1,0:T(8,128)(2,1)S(1)}, u32[]{:S(2)}, u32[]{:S(2)}) async-start(bf16[8,16,896]{2,1,0:T(8,128)(2,1)} %get-tuple-element.5), calls=%async_computation.5 | async-start | bytes 458752 | tf_op jit(solution)/shard_map/all_to_all | solution.py:225
  229.0 2.5 copy-start.2
Sparse Core Ops, SparseCore 0:
  17.5 56.1 reduce-scatter.1
  167.8 61.1 all-gather.3

commit v2 on v1

v2 whole, which is shorter than its diff:
```python
import functools

import jax
import jax.numpy as jnp
from jax import lax
from jax.experimental import pallas as pl
from jax.experimental.pallas import tpu as pltpu
from jax.sharding import Mesh
from jax.sharding import PartitionSpec as P

D = 7168
QL = 1536
IHEADS = 64
IDIM = 128
N_SEQ = 16
N_HEAD = 16
NZ = 8
DZ = D // NZ
EPSILON = 1e-06
SEQ = ("x", "yl", "c")
HEAD = ("z", "yh")
HALF = 128
SLOTS = 1024
WIDE = 1024 + 128


def rms_round(values, gain):
    widened = values.astype(jnp.float32)
    inverse = lax.rsqrt(jnp.mean(widened * widened, axis=-1, keepdims=True) + EPSILON)
    return (widened * inverse * gain.astype(jnp.float32)).astype(jnp.bfloat16)


def swap(values, axis):
    return lax.ppermute(values, axis, [(0, 1), (1, 0)])


def shift(values, axis, size, by):
    return lax.ppermute(values, axis, [(i, (i + by) % size) for i in range(size)])


def kernel_params():
    return pltpu.CompilerParams(vmem_limit_bytes=48 * 1024 * 1024)


def project_kernel(a_ref, b_ref, o_ref):
    product = jnp.dot(a_ref[...], b_ref[...], preferred_element_type=jnp.float32).astype(o_ref.dtype)
    for group in range(NZ):
        for half in range(2):
            o_ref[0, half, group * 16 : (group + 1) * 16, :] = product[
                group * 32 + half * 16 : group * 32 + (half + 1) * 16, :
            ]


def project(attn_out, out_weight):
    rows, depth = attn_out.shape
    return pl.pallas_call(
        project_kernel,
        grid=(NZ,),
        in_specs=[
            pl.BlockSpec((rows, depth), lambda i: (0, 0)),
            pl.BlockSpec((depth, DZ), lambda i: (0, i)),
        ],
        out_specs=pl.BlockSpec((1, 2, HALF, DZ), lambda i: (i, 0, 0, 0)),
        out_shape=jax.ShapeDtypeStruct((NZ, 2, HALF, DZ), jnp.bfloat16),
        compiler_params=pltpu.CompilerParams(vmem_limit_bytes=60 * 1024 * 1024),
    )(attn_out, out_weight)


def lift_kernel(core_ref, kept_ref, got_ref, res_ref, gain_ref, mine_ref, other_ref, hidden_ref, o_ref):
    hidden = (
        kept_ref[...].astype(jnp.float32)
        + got_ref[...].astype(jnp.float32)
        + res_ref[...].astype(jnp.float32)
    ).astype(jnp.bfloat16)
    hidden_ref[...] = hidden
    wide = hidden.astype(jnp.float32)
    squares = jnp.sum(wide * wide, axis=1, keepdims=True)
    high = squares.astype(jnp.bfloat16).astype(jnp.float32)
    scaled = wide * gain_ref[...].astype(jnp.float32)
    first, second = scaled[:, : DZ // 2], scaled[:, DZ // 2 :]
    is_first = core_ref[0] == 0
    mine = jnp.where(is_first, first, second).astype(jnp.bfloat16)
    other = jnp.where(is_first, second, first).astype(jnp.bfloat16)
    lifted = jnp.dot(mine, mine_ref[...], preferred_element_type=jnp.float32) + jnp.dot(
        other, other_ref[...], preferred_element_type=jnp.float32
    )
    lane = lax.broadcasted_iota(jnp.int32, (HALF, 128), 1)
    tail = jnp.where(lane == IHEADS, high, jnp.where(lane == IHEADS + 1, squares - high, 0.0))
    o_ref[:, :QL] = lifted[:, :QL].astype(jnp.bfloat16)
    o_ref[:, QL:] = jnp.where(lane < IHEADS, lifted[:, QL:], tail).astype(jnp.bfloat16)


def lift(core, kept, got, residual, gain, mine, other):
    whole = pl.BlockSpec(memory_space=pltpu.VMEM)
    return pl.pallas_call(
        lift_kernel,
        in_specs=[pl.BlockSpec(memory_space=pltpu.SMEM)] + [whole] * 6,
        out_specs=[whole, whole],
        out_shape=[
            jax.ShapeDtypeStruct((HALF, DZ), jnp.bfloat16),
            jax.ShapeDtypeStruct((HALF, QL + 128), jnp.bfloat16),
        ],
        compiler_params=kernel_params(),
    )(core, kept, got, residual, gain, mine, other)


def query_kernel(latent_ref, own_ref, other_ref, pick_ref, o_ref):
    latent = latent_ref[:, :QL]
    o_ref[:, :512] = jnp.dot(latent, own_ref[...], preferred_element_type=jnp.float32).astype(jnp.bfloat16)
    o_ref[:, 512:1024] = jnp.dot(latent, other_ref[...], preferred_element_type=jnp.float32).astype(
        jnp.bfloat16
    )
    o_ref[:, 1024:] = jnp.dot(
        latent_ref[:, QL:], pick_ref[...], preferred_element_type=jnp.float32
    ).astype(jnp.bfloat16)


def make_queries(latent, own, other, pick):
    whole = pl.BlockSpec(memory_space=pltpu.VMEM)
    return pl.pallas_call(
        query_kernel,
        in_specs=[whole] * 4,
        out_specs=whole,
        out_shape=jax.ShapeDtypeStruct((HALF, WIDE), jnp.bfloat16),
        compiler_params=kernel_params(),
    )(latent, own, other, pick)


def score_kernel(count, first, *refs):
    pieces, k_ref = refs[:count], refs[count]
    before, o_ref = (None if first else refs[count + 1]), refs[-1]
    scale = IDIM ** (-0.5)
    rows, slots = o_ref.shape
    tile_rows, tile_slots = 64, 256
    for at in range(0, rows, tile_rows):
        weights = [piece[at : at + tile_rows, 1024:].astype(jnp.float32) * scale for piece in pieces]
        for slot in range(0, slots, tile_slots):
            here = (slice(at, at + tile_rows), slice(slot, slot + tile_slots))
            total = jnp.zeros((tile_rows, tile_slots), jnp.float32) if first else before[here]
            for piece, weight in zip(pieces, weights):
                for j in range(8):
                    logits = jnp.dot(
                        piece[at : at + tile_rows, j * IDIM : (j + 1) * IDIM],
                        k_ref[:, slot : slot + tile_slots],
                        preferred_element_type=jnp.float32,
                    )
                    total = total + jnp.maximum(logits, 0.0) * weight[:, j : j + 1]
            o_ref[here] = total


def add_scores(pieces, keys_t, before):
    count, slots, block = len(pieces), keys_t.shape[1], 512
    tile = pl.BlockSpec((HALF, block), lambda i: (0, i))
    specs = [pl.BlockSpec((HALF, WIDE), lambda i: (0, 0))] * count
    specs += [pl.BlockSpec((IDIM, block), lambda i: (0, i))]
    args = list(pieces) + [keys_t]
    if before is not None:
        specs.append(tile)
        args.append(before)
    return pl.pallas_call(
        functools.partial(score_kernel, count, before is None),
        grid=(slots // block,),
        in_specs=specs,
        out_specs=tile,
        out_shape=jax.ShapeDtypeStruct((HALF, slots), jnp.float32),
        compiler_params=kernel_params(),
        cost_estimate=pl.CostEstimate(
            flops=2 * count * 8 * HALF * slots * IDIM * 2, bytes_accessed=2 * HALF * slots * 4, transcendentals=0
        ),
    )(*args)


def finish_kernel(numbers_ref, own_ref, got_ref, pos_ref, o_ref):
    local = lax.broadcasted_iota(jnp.int32, (16, SLOTS), 1)
    core, filled, base = numbers_ref[0], numbers_ref[1], numbers_ref[2]
    for group in range(NZ):
        own = own_ref[group * 16 : (group + 1) * 16, :]
        got = got_ref[group * 16 : (group + 1) * 16, :]
        for half in range(2):
            at = group * 32 + half * 16
            reach = jnp.minimum(filled, pos_ref[at : at + 16, :] - base + 1)
            rows = jnp.where(core == half, own, got)
            o_ref[at : at + 16, :] = jnp.where(local < reach, rows, 0.0)


def finish(numbers, own, got, own_positions):
    whole = pl.BlockSpec(memory_space=pltpu.VMEM)
    return pl.pallas_call(
        finish_kernel,
        in_specs=[pl.BlockSpec(memory_space=pltpu.SMEM), whole, whole, whole],
        out_specs=whole,
        out_shape=jax.ShapeDtypeStruct((2 * HALF, SLOTS), jnp.float32),
        compiler_params=kernel_params(),
    )(numbers, own, got, own_positions)


def down_weight_rows(latent_weight, index_proj, x, yl, c):
    piece = c * 8 + x * 2 + yl
    share = DZ // N_SEQ

    def own_rows(weight):
        return lax.dynamic_slice_in_dim(weight.reshape(NZ, DZ, weight.shape[1]), piece * share, share, 1)

    own = jnp.concatenate([own_rows(latent_weight), own_rows(index_proj)], axis=2)
    by_head = lax.all_to_all(jnp.repeat(own, 2, axis=0), HEAD, 0, 0).transpose(1, 0, 2)
    local = latent_weight.shape[1]
    wide = jnp.concatenate(
        [
            by_head[:, :, :local].reshape(share, QL),
            by_head[:, :, local:].reshape(share, IHEADS),
            jnp.zeros((share, 64), jnp.bfloat16),
        ],
        axis=1,
    )
    half = lax.all_to_all(jnp.broadcast_to(wide[None], (8,) + wide.shape), ("x", "yl"), 0, 0)
    half = half.reshape(8 * share, wide.shape[1])
    return half, swap(half, "c")


def turn(queries):
    moves = []
    for at in range(N_SEQ * N_HEAD):
        s, h = divmod(at, N_HEAD)
        pair, core = divmod(s, 2)
        level, high = divmod(h, 2)
        moves.append((at, ((pair ^ level) * 2 + high) * N_HEAD + pair * 2 + core))
    return lax.ppermute(queries, SEQ + HEAD, moves)


def shards(
    attn_out,
    out_weight,
    residual,
    norm_gain,
    latent_weight,
    index_proj,
    latent_gain,
    index_weight,
    index_keys,
    positions,
    cache_len,
):
    x, yl, c = (lax.axis_index(a) for a in SEQ)
    z, yh = (lax.axis_index(a) for a in HEAD)
    seq = (x * 2 + yl) * 2 + c
    head = z * 2 + yh
    rows = attn_out.shape[0]
    own = rows // N_HEAD
    local = latent_weight.shape[1]

    partial = project(attn_out, out_weight)
    summed = lax.psum_scatter(partial, "z", scatter_dimension=0, tiled=False)

    down_mine, down_other = down_weight_rows(latent_weight, index_proj, x, yl, c)
    residual_cols = lax.all_to_all(residual.reshape(own, NZ, DZ).transpose(1, 0, 2), "z", 0, 0)
    weight_other = swap(index_weight, "yh")
    keys_other = swap(index_keys, "c")
    keys_t = jnp.concatenate([index_keys, keys_other], axis=0).T

    kept = lax.dynamic_index_in_dim(summed, yh, 0, keepdims=False)
    got = swap(lax.dynamic_index_in_dim(summed, 1 - yh, 0, keepdims=False), "yh")
    gain = lax.dynamic_slice_in_dim(norm_gain, z * DZ, DZ).reshape(1, DZ)
    core = jnp.stack([c]).astype(jnp.int32)
    hidden, lifted = lift(
        core, kept, got, residual_cols.reshape(HALF, DZ), gain, down_mine, down_other
    )
    parts = lax.all_to_all(lifted.reshape(NZ, own, lifted.shape[1]), "z", 0, 0)
    total = jnp.sum(parts.astype(jnp.float32), axis=0)
    mean = (total[:, 1600:1601] + total[:, 1601:1602]) / D
    inverse = lax.rsqrt(mean + EPSILON)
    latent_raw = (total[:, :QL] * inverse).astype(jnp.bfloat16)
    head_weights = (total[:, QL:1600] * inverse * IHEADS ** (-0.5)).astype(jnp.bfloat16)
    latent = rms_round(latent_raw, latent_gain)
    packed = jnp.concatenate([latent, head_weights, jnp.zeros((own, 64), jnp.bfloat16)], axis=1)
    everyone = lax.all_to_all(jnp.broadcast_to(packed[None], (NZ,) + packed.shape), "z", 0, 0)
    everyone = everyone.reshape(HALF, packed.shape[1])

    lane = lax.broadcasted_iota(jnp.int32, (128, 128), 1)
    source = jnp.where(lane < 4, head * 4 + lane, (head ^ 1) * 4 + lane - 4)
    pick = (lax.broadcasted_iota(jnp.int32, (128, 128), 0) == source) & (lane < 8)
    queries = make_queries(everyone, index_weight, weight_other, pick.astype(jnp.bfloat16))
    queries, everyone, hidden = lax.optimization_barrier((queries, everyone, hidden))

    piece = turn(queries)
    hidden_rows = lax.all_to_all(hidden.reshape(NZ, own, DZ), "z", 0, 0).transpose(1, 0, 2).reshape(own, D)
    latent_mine = lax.dynamic_slice_in_dim(everyone, head * local, local, 1).reshape(NZ, own, local)
    latent_give = lax.dynamic_slice_in_dim(everyone, (head ^ 1) * local, local, 1)
    latent_got = swap(latent_give, "yh").reshape(NZ, own, local)
    latent_out = jnp.stack(
        [jnp.where(yh == 0, latent_mine, latent_got), jnp.where(yh == 0, latent_got, latent_mine)], axis=1
    ).reshape(rows, local)

    beside = swap(piece, "yl")
    right, left = shift(piece, "x", 4, 1), shift(piece, "x", 4, -1)
    scores = add_scores([piece], keys_t, None)
    beside_right, beside_left = shift(beside, "x", 4, 1), shift(beside, "x", 4, -1)
    across = shift(right, "x", 4, 1)
    scores = add_scores([beside, right, left], keys_t, scores)
    beside_across = shift(beside_left, "x", 4, -1)
    scores = add_scores([beside_right, beside_left], keys_t, scores)
    scores = add_scores([across, beside_across], keys_t, scores)
    got_scores = swap(scores[:, SLOTS:], "c")
    own_positions = lax.dynamic_slice_in_dim(positions, head * rows, rows).reshape(rows, 1)
    numbers = jnp.stack([c, cache_len[0], seq * SLOTS]).astype(jnp.int32)
    return (hidden_rows, latent_out, finish(numbers, scores[:, :SLOTS], got_scores, own_positions))


def solution(mesh):
    fine = Mesh(mesh.devices.reshape(4, 2, 2, 8, 2), SEQ + HEAD)
    in_specs = (
        P(SEQ, HEAD),
        P(HEAD, None),
        P(SEQ + HEAD, None),
        P(),
        P(None, HEAD),
        P(None, HEAD),
        P(),
        P(None, HEAD),
        P(SEQ, None),
        P(),
        P(SEQ),
    )
    out_specs = (P(SEQ + HEAD, None), P(SEQ, HEAD), P(HEAD, SEQ))
    return jax.shard_map(shards, mesh=fine, in_specs=in_specs, out_specs=out_specs, check_vma=False)
```

time: 253 us -> 221 us (0.87)
  blocking collectives: 61.9 us -> 44.7 us
  waiting for transfers between devices: 62.1 us -> 45.1 us
  starting transfers between devices: 62.7 us -> 74.1 us
  local copies, waits for them, and re-layouts: 21.8 us -> 12.9 us
  Pallas kernels: 18.3 us -> 27 us
  other arithmetic: 8.62 us -> 0.92 us
    all_gather x1 -> x0, waiting for transfers between devices: 25 us -> none  [shards(): all_queries = lax.all_gather(turned, SEQ, axis=0, tiled=False)]
    all_gather x1 -> x0, blocking collectives: 20.9 us -> none  [shards(): lax.all_gather(pair, 'z', axis=0, tiled=False)]
    ppermute x4 -> x7, starting transfers between devices: 11.7 us -> 30.7 us  [swap(): return lax.ppermute(values, axis, [(0, 1), (1, 0)])]
    all_to_all x1 -> x2, starting transfers between devices: 23.8 us -> 6.88 us  [the longest x1 3.46 us: shards(): lax.all_to_all(jnp.broadcast_to(packed[None], (NZ,) + packed.shape), 'z',...]
    ppermute x4 -> x7, waiting for transfers between devices: 6.1 us -> 18.4 us  [swap(): return lax.ppermute(values, axis, [(0, 1), (1, 0)])]
    ppermute x1 -> x7, starting transfers between devices: 17.5 us -> 28.8 us  [the longest x6 23.3 us: shift(): lax.ppermute(values, axis, [(i, (i + by) % size) for i in range(size)])]
    all_to_all x1 -> x2, waiting for transfers between devices: 9.1 us -> 0.01 us  [the longest x1 0.01 us: shards(): lax.all_to_all(jnp.broadcast_to(packed[None], (NZ,) + packed.shape), 'z',...]
    unnamed x26 -> x22, local copies, waits for them, and re-layouts: 14.4 us -> 5.71 us
  transfers between devices with their start and end apart: 10 -> 19, of which waited for: 8 -> 7; matrix products, arithmetic and copies ran while one was open for 6% -> 4% of each run, Pallas kernels for 0% -> 6%
where the time goes in v2:
time: 221 us; the launch traced here: 220 us
  starting transfers between devices  74.1 us (34%)
  waiting for transfers between devices  45.1 us (20%)
  blocking collectives  44.7 us (20%)
  Pallas kernels  27 us (12%)
  between operations  15 us (7%)
  local copies, waits for them, and re-layouts  12.9 us (6%)
    ppermute x7, starting transfers between devices, swap(): return lax.ppermute(values, axis, [(0, 1), (1, 0)])  30.7 us
    all_to_all x1, blocking collectives, down_weight_rows(): lax.all_to_all(jnp.repeat(own, 2, axis=0), HEAD, 0, 0).transpose(1, 0, 2)  24.1 us
    ppermute x6, starting transfers between devices, shift(): lax.ppermute(values, axis, [(i, (i + by) % size) for i in range(size)])  23.3 us
    all_to_all x1, blocking collectives, down_weight_rows(): lax.all_to_all(jnp.broadcast_to(wide[None], (8,) + wide.shape), ('x', 'yl...  20.6 us
    ppermute x7, waiting for transfers between devices, swap(): return lax.ppermute(values, axis, [(0, 1), (1, 0)])  18.4 us
    pallas_call x4, Pallas kernels, add_scores(): pl.pallas_call(functools.partial(score_kernel, count, before is None), gr...  12.7 us
    all_to_all x1, waiting for transfers between devices, shards(): parts = lax.all_to_all(lifted.reshape(NZ, own, lifted.shape[1]), 'z', 0, 0)  12.6 us
    pallas_call x1, Pallas kernels, project(): pl.pallas_call(project_kernel, grid=(NZ,), in_specs=[pl.BlockSpec((rows,...  8.69 us
  transfers between devices with their start and end apart: 19, of which 7 were waited for; matrix products, arithmetic and copies ran while one was open for 4% of the time, Pallas kernels for 6%

profile of v2, /device:TPU:1, one launch (start us, length us, event | category | flops | bytes accessed | tf_op | source)
XLA Modules:
  0.0 219.7 jit_solution(14744176698454662244)
XLA Ops:
  7.2 8.7 %shard_map.130 = bf16[8,2,128,896]{3,2,1,0:T(8,128)(2,1)} custom-call(bf16[256,512]{1,0:T(8,128)(2,1)} %a_ref.1, bf16[512,7168]{1,0:T(8,128)(2,1)} %b_ref.1), custom_call_target="tpu_custom_call" | custom-call | tf_op jit(solution)/shard_map/pallas_call | solution.py:56
  18.0 24.1 %all_to_all.30 = bf16[16,56,100]{2,1,0:T(8,128)(2,1)S(1)} all-to-all(bf16[16,56,100]{2,1,0:T(8,128)(2,1)S(1)} %bitcast.57), channel_id=1, replica_groups=mesh['x'=4,'yl'=2,'c'=2,'z'=8,'yh'=2] {'z','yh'}, dimensions={0} | all-to-all | bytes 358400 | tf_op jit(solution)/shard_map/all_to_all | solution.py:205
  43.0 20.6 %all_to_all.31 = bf16[8,56,1664]{2,1,0:T(8,128)(2,1)S(1)} all-to-all(bf16[8,56,1664]{2,1,0:T(8,128)(2,1)S(1)} %broadcast_in_dim.12), channel_id=1, replica_groups=mesh['x'=4,'yl'=2,'c'=2,'z'=8,'yh'=2] {'x','yl'}, dimensions={0} | all-to-all | bytes 2981888 | tf_op jit(solution)/shard_map/all_to_all | solution.py:215
  63.6 5.1 %collective-permute-start.1 = (bf16[448,1664]{1,0:T(8,128)(2,1)S(1)}, bf16[448,1664]{1,0:T(8,128)(2,1)S(1)}, u32[]{:S(2)}, u32[]{:S(2)}) collective-permute-start(bf16[448,1664]{1,0:T(8,128)(2,1)S(1)} %bitcast.45), channel_id=1, source_target_pairs={{0,16},{16,0},{1,17},{17,1},{2,18},{18,2},{3,19},{19,3},{4,20},{20... | collective-permute-start | bytes 4472840 | tf_op jit(solution)/shard_map/ppermute | solution.py:34
  69.5 3.4 %all-to-all-start = ((bf16[8,16,896]{2,1,0:T(8,128)(2,1)}), bf16[8,16,896]{2,1,0:T(8,128)(2,1)S(1)}, u32[]{:S(2)}, u32[]{:S(2)}) async-start(bf16[8,16,896]{2,1,0:T(8,128)(2,1)} %bitcast.42), calls=%async_computation.1 | async-start | bytes 458752 | tf_op jit(solution)/shard_map/all_to_all | solution.py:255
  75.8 2.7 %collective-permute-start = (bf16[128,896]{1,0:T(8,128)(2,1)}, bf16[128,896]{1,0:T(8,128)(2,1)}, u32[]{:S(2)}, u32[]{:S(2)}) collective-permute-start(bf16[128,896]{1,0:T(8,128)(2,1)} %get-tuple-element.26), channel_id=1, source_target_pairs={{0,1},{1,0},{2,3},{3,2},{4,5},{5,4},{6,7},{7,6},{8,9},{9,8},{10,11... | collective-permute-start | bytes 688136 | tf_op jit(solution)/shard_map/ppermute | solution.py:34
  79.3 5.2 %all-to-all-done = bf16[8,16,896]{2,1,0:T(8,128)(2,1)S(1)} async-done(((bf16[8,16,896]{2,1,0:T(8,128)(2,1)}), bf16[8,16,896]{2,1,0:T(8,128)(2,1)S(1)}, u32[]{:S(2)}, u32[]{:S(2)}) %all-to-all-start) | async-done | bytes 229408 | tf_op jit(solution)/shard_map/all_to_all | solution.py:255
  89.7 4.3 %all-to-all-start.3 = ((bf16[8,16,1664]{2,1,0:T(8,128)(2,1)}), bf16[8,16,1664]{2,1,0:T(8,128)(2,1)S(1)}, u32[]{:S(2)}, u32[]{:S(2)}) async-start(bf16[8,16,1664]{2,1,0:T(8,128)(2,1)} %bitcast.51), calls=%async_computation.4 | async-start | bytes 851968 | tf_op jit(solution)/shard_map/all_to_all | solution.py:267
  95.5 12.6 %all-to-all-done.3 = bf16[8,16,1664]{2,1,0:T(8,128)(2,1)S(1)} async-done(((bf16[8,16,1664]{2,1,0:T(8,128)(2,1)}), bf16[8,16,1664]{2,1,0:T(8,128)(2,1)S(1)}, u32[]{:S(2)}, u32[]{:S(2)}) %all-to-all-start.3) | async-done | bytes 426016 | tf_op jit(solution)/shard_map/all_to_all | solution.py:267
  109.6 3.5 %all-to-all-start.4 = ((bf16[8,16,1664]{2,1,0:T(8,128)(2,1)}), bf16[8,16,1664]{2,1,0:T(8,128)(2,1)S(1)}, u32[]{:S(2)}, u32[]{:S(2)}) async-start(bf16[8,16,1664]{2,1,0:T(8,128)(2,1)} %broadcast_in_dim.27), calls=%async_computation.5 | async-start | bytes 851968 | tf_op jit(solution)/shard_map/all_to_all | solution.py:275
  113.1 17.1 %collective-permute-done.2.other_ref = bf16[1536,512]{1,0:T(8,128)(2,1)} collective-permute-done((bf16[1536,512]{1,0:T(8,128)(2,1)S(1)}, bf16[1536,512]{1,0:T(8,128)(2,1)}, u32[]{:S(2)}, u32[]{:S(2)}) %collective-permute-start.2) | collective-permute-done | bytes 1572896 | tf_op jit(solution)/shard_map/ppermute | solution.py:34
  132.3 5.5 %collective-permute-start.4 = (bf16[128,1152]{1,0:T(8,128)(2,1)S(1)}, bf16[128,1152]{1,0:T(8,128)(2,1)S(1)}, u32[]{:S(2)}, u32[]{:S(2)}) collective-permute-start(bf16[128,1152]{1,0:T(8,128)(2,1)S(1)} %shard_map.132), channel_id=1, source_target_pairs={{0,0},{1,16},{2,32},{3,48},{4,64},{5,80},{6,96},{7,112},{8,128},{9... | collective-permute-start | bytes 884744 | tf_op jit(solution)/shard_map/ppermute | solution.py:227
  137.7 4.9 %collective-permute-done.4.refs_0_ = bf16[128,1152]{1,0:T(8,128)(2,1)S(1)} collective-permute-done((bf16[128,1152]{1,0:T(8,128)(2,1)S(1)}, bf16[128,1152]{1,0:T(8,128)(2,1)S(1)}, u32[]{:S(2)}, u32[]{:S(2)}) %collective-permute-start.4) | collective-permute-done | bytes 294944 | tf_op jit(solution)/shard_map/ppermute | solution.py:227
  142.6 16.1 %collective-permute-start.7 = (bf16[128,1152]{1,0:T(8,128)(2,1)S(1)}, bf16[128,1152]{1,0:T(8,128)(2,1)S(1)}, u32[]{:S(2)}, u32[]{:S(2)}) collective-permute-start(bf16[128,1152]{1,0:T(8,128)(2,1)S(1)} %collective-permute-done.4.refs_0_), channel_id=1, source_target_pairs={{0,32},{32,0},{1,33},{33,1},{2,34},{34,2},{3,35},{35,3},{4,36},{36... | collective-permute-start | bytes 884744 | tf_op jit(solution)/shard_map/ppermute | solution.py:34
  160.2 5.4 %collective-permute-start.5 = (bf16[128,1152]{1,0:T(8,128)(2,1)S(1)}, bf16[128,1152]{1,0:T(8,128)(2,1)S(1)}, u32[]{:S(2)}, u32[]{:S(2)}) collective-permute-start(bf16[128,1152]{1,0:T(8,128)(2,1)S(1)} %collective-permute-done.4.refs_0_), channel_id=1, source_target_pairs={{0,64},{64,128},{128,192},{192,0},{1,65},{65,129},{129,193},{193,1... | collective-permute-start | bytes 884744 | tf_op jit(solution)/shard_map/ppermute | solution.py:38
  165.7 5.9 %collective-permute-start.12 = (bf16[128,1152]{1,0:T(8,128)(2,1)S(1)}, bf16[128,1152]{1,0:T(8,128)(2,1)S(1)}, u32[]{:S(2)}, u32[]{:S(2)}) collective-permute-start(bf16[128,1152]{1,0:T(8,128)(2,1)S(1)} %collective-permute-done.4.refs_0_), channel_id=1, source_target_pairs={{0,192},{64,0},{128,64},{192,128},{1,193},{65,1},{129,65},{193,129... | collective-permute-start | bytes 884744 | tf_op jit(solution)/shard_map/ppermute | solution.py:38
  171.6 7.8 %collective-permute-start.8 = (bf16[128,1152]{1,0:T(8,128)(2,1)S(1)}, bf16[128,1152]{1,0:T(8,128)(2,1)S(1)}, u32[]{:S(2)}, u32[]{:S(2)}) collective-permute-start(bf16[128,1152]{1,0:T(8,128)(2,1)S(1)} %collective-permute-done.7.refs_0_), channel_id=1, source_target_pairs={{0,192},{64,0},{128,64},{192,128},{1,193},{65,1},{129,65},{193,129... | collective-permute-start | bytes 884744 | tf_op jit(solution)/shard_map/ppermute | solution.py:38
  179.5 3.4 %all-to-all-start.5 = ((bf16[8,16,896]{2,1,0:T(8,128)(2,1)}), bf16[8,16,896]{2,1,0:T(8,128)(2,1)S(1)}, u32[]{:S(2)}, u32[]{:S(2)}) async-start(bf16[8,16,896]{2,1,0:T(8,128)(2,1)} %bitcast.11), calls=%async_computation.6 | async-start | bytes 458752 | tf_op jit(solution)/shard_map/all_to_all | solution.py:285
  185.6 3.4 %collective-permute-start.9 = (bf16[128,1152]{1,0:T(8,128)(2,1)S(1)}, bf16[128,1152]{1,0:T(8,128)(2,1)S(1)}, u32[]{:S(2)}, u32[]{:S(2)}) collective-permute-start(bf16[128,1152]{1,0:T(8,128)(2,1)S(1)} %collective-permute-done.8.refs_1_), channel_id=1, source_target_pairs={{0,192},{64,0},{128,64},{192,128},{1,193},{65,1},{129,65},{193,129... | collective-permute-start | bytes 884744 | tf_op jit(solution)/shard_map/ppermute | solution.py:38
  189.0 4.4 %shard_map.134.refs_3_ = f32[128,2048]{1,0:T(8,128)S(1)} custom-call(bf16[128,1152]{1,0:T(8,128)(2,1)S(1)} %collective-permute-done.7.refs_0_, bf16[128,1152]{1,0:T(8,128)(2,1)S(1)} %collective-permute-done.5.refs_1_, bf16[128,1152]{1,0:T(8,128)(2,1)S(1)} %collective-permute-done.12.refs_2_, ...), custom_call_target="tpu_custom_call" | custom-call | flops 3221225472 | bytes 2097152 | tf_op jit(solution)/shard_map/pallas_call | solution.py:160
  193.4 3.2 %shard_map.135.refs_3_ = f32[128,2048]{1,0:T(8,128)S(1)} custom-call(bf16[128,1152]{1,0:T(8,128)(2,1)S(1)} %collective-permute-done.11.refs_0_, bf16[128,1152]{1,0:T(8,128)(2,1)S(1)} %collective-permute-done.8.refs_1_, bf16[128,2048]{1,0:T(8,128)(2,1)S(1)} %maximum_bitcast_fusion.refs_1_.refs_3_.refs_2_, f32[128,2048]{1,0:T(8,128)S(1)} %shard_map.134.refs_3_), custom_call_target="tpu_custom_call" | custom-call | flops 2147483648 | bytes 2097152 | tf_op jit(solution)/shard_map/pallas_call | solution.py:160
  196.6 2.9 %collective-permute-done.6.refs_0_ = bf16[128,1152]{1,0:T(8,128)(2,1)S(1)} collective-permute-done((bf16[128,1152]{1,0:T(8,128)(2,1)S(1)}, bf16[128,1152]{1,0:T(8,128)(2,1)S(1)}, u32[]{:S(2)}, u32[]{:S(2)}) %collective-permute-start.6) | collective-permute-done | bytes 294944 | tf_op jit(solution)/shard_map/ppermute | solution.py:38
  199.5 3.1 %shard_map.136 = f32[128,2048]{1,0:T(8,128)S(1)} custom-call(bf16[128,1152]{1,0:T(8,128)(2,1)S(1)} %collective-permute-done.6.refs_0_, bf16[128,1152]{1,0:T(8,128)(2,1)S(1)} %collective-permute-done.9.refs_1_, bf16[128,2048]{1,0:T(8,128)(2,1)S(1)} %maximum_bitcast_fusion.refs_1_.refs_3_.refs_2_, f32[128,2048]{1,0:T(8,128)S(1)} %shard_map.135.refs_3_), custom_call_target="tpu_custom_call" | custom-call | flops 2147483648 | bytes 2097152 | tf_op jit(solution)/shard_map/pallas_call | solution.py:160
  202.7 2.5 %collective-permute-start.13 = (f32[128,1024]{1,0:T(8,128)S(1)}, f32[128,1024]{1,0:T(8,128)S(1)}, u32[]{:S(2)}, u32[]{:S(2)}) collective-permute-start(f32[128,1024]{1,0:T(8,128)S(1)} %get-tuple-element.22), channel_id=1, source_target_pairs={{0,16},{16,0},{1,17},{17,1},{2,18},{18,2},{3,19},{19,3},{4,20},{20... | collective-permute-start | bytes 1572872 | tf_op jit(solution)/shard_map/ppermute | solution.py:34
  (86 shorter events, 29.0 us)
Async XLA Ops:
  7.2 66.9 %reduce-scatter.2.cloned.1.call-start = ((), (), s32[]{:S(2)}) async-start(), calls=%async_computation.7 | async-start | bytes 4128768 | tf_op jit(solution)/shard_map/reduce_scatter | solution.py:252
  43.0 25.8 %copy-start.6 = (bf16[16,7168]{1,0:T(8,128)(2,1)S(1)}, bf16[16,7168]{1,0:T(8,128)(2,1)}, u32[]{:S(2)}) copy-start(bf16[16,7168]{1,0:T(8,128)(2,1)} %param.13) | copy-start | bytes 688132
  63.6 20.9 %collective-permute-start.1 = (bf16[448,1664]{1,0:T(8,128)(2,1)S(1)}, bf16[448,1664]{1,0:T(8,128)(2,1)S(1)}, u32[]{:S(2)}, u32[]{:S(2)}) collective-permute-start(bf16[448,1664]{1,0:T(8,128)(2,1)S(1)} %bitcast.45), channel_id=1, source_target_pairs={{0,16},{16,0},{1,17},{17,1},{2,18},{18,2},{3,19},{19,3},{4,20},{20... | collective-permute-start | bytes 4472840 | tf_op jit(solution)/shard_map/ppermute | solution.py:34
  69.5 15.0 %all-to-all-start = ((bf16[8,16,896]{2,1,0:T(8,128)(2,1)}), bf16[8,16,896]{2,1,0:T(8,128)(2,1)S(1)}, u32[]{:S(2)}, u32[]{:S(2)}) async-start(bf16[8,16,896]{2,1,0:T(8,128)(2,1)} %bitcast.42), calls=%async_computation.1 | async-start | bytes 458752 | tf_op jit(solution)/shard_map/all_to_all | solution.py:255
  75.8 9.8 %collective-permute-start = (bf16[128,896]{1,0:T(8,128)(2,1)}, bf16[128,896]{1,0:T(8,128)(2,1)}, u32[]{:S(2)}, u32[]{:S(2)}) collective-permute-start(bf16[128,896]{1,0:T(8,128)(2,1)} %get-tuple-element.26), channel_id=1, source_target_pairs={{0,1},{1,0},{2,3},{3,2},{4,5},{5,4},{6,7},{7,6},{8,9},{9,8},{10,11... | collective-permute-start | bytes 688136 | tf_op jit(solution)/shard_map/ppermute | solution.py:34
  85.6 1.4 copy-start.2
  87.0 7.0 %copy-start = (bf16[1536,512]{1,0:T(8,128)(2,1)S(1)}, bf16[1536,512]{1,0:T(8,128)(2,1)}, u32[]{:S(2)}) copy-start(bf16[1536,512]{1,0:T(8,128)(2,1)} %own_ref.1) | copy-start | bytes 4718596
  87.0 8.4 %copy-start.8 = (bf16[1536]{0:T(1024)(128)(2,1)S(1)}, bf16[1536]{0:T(1024)(128)(2,1)}, u32[]{:S(2)}) copy-start(bf16[1536]{0:T(1024)(128)(2,1)} %param.17) | copy-start | bytes 9220
  89.7 18.4 %all-to-all-start.3 = ((bf16[8,16,1664]{2,1,0:T(8,128)(2,1)}), bf16[8,16,1664]{2,1,0:T(8,128)(2,1)S(1)}, u32[]{:S(2)}, u32[]{:S(2)}) async-start(bf16[8,16,1664]{2,1,0:T(8,128)(2,1)} %bitcast.51), calls=%async_computation.4 | async-start | bytes 851968 | tf_op jit(solution)/shard_map/all_to_all | solution.py:267
  94.0 36.2 %collective-permute-start.2 = (bf16[1536,512]{1,0:T(8,128)(2,1)S(1)}, bf16[1536,512]{1,0:T(8,128)(2,1)}, u32[]{:S(2)}, u32[]{:S(2)}) collective-permute-start(bf16[1536,512]{1,0:T(8,128)(2,1)S(1)} %copy-done), channel_id=1, source_target_pairs={{0,1},{1,0},{2,3},{3,2},{4,5},{5,4},{6,7},{7,6},{8,9},{9,8},{10,11... | collective-permute-start | bytes 4718600 | tf_op jit(solution)/shard_map/ppermute | solution.py:34
  109.6 20.7 %all-to-all-start.4 = ((bf16[8,16,1664]{2,1,0:T(8,128)(2,1)}), bf16[8,16,1664]{2,1,0:T(8,128)(2,1)S(1)}, u32[]{:S(2)}, u32[]{:S(2)}) async-start(bf16[8,16,1664]{2,1,0:T(8,128)(2,1)} %broadcast_in_dim.27), calls=%async_computation.5 | async-start | bytes 851968 | tf_op jit(solution)/shard_map/all_to_all | solution.py:275
  130.2 28.4 %copy-start.5 = (bf16[1024,128]{1,0:T(8,128)(2,1)S(1)}, bf16[1024,128]{1,0:T(8,128)(2,1)}, u32[]{:S(2)}) copy-start(bf16[1024,128]{1,0:T(8,128)(2,1)} %param.19) | copy-start | bytes 786436
  132.3 10.3 %collective-permute-start.4 = (bf16[128,1152]{1,0:T(8,128)(2,1)S(1)}, bf16[128,1152]{1,0:T(8,128)(2,1)S(1)}, u32[]{:S(2)}, u32[]{:S(2)}) collective-permute-start(bf16[128,1152]{1,0:T(8,128)(2,1)S(1)} %shard_map.132), channel_id=1, source_target_pairs={{0,0},{1,16},{2,32},{3,48},{4,64},{5,80},{6,96},{7,112},{8,128},{9... | collective-permute-start | bytes 884744 | tf_op jit(solution)/shard_map/ppermute | solution.py:227
  142.6 29.0 %collective-permute-start.7 = (bf16[128,1152]{1,0:T(8,128)(2,1)S(1)}, bf16[128,1152]{1,0:T(8,128)(2,1)S(1)}, u32[]{:S(2)}, u32[]{:S(2)}) collective-permute-start(bf16[128,1152]{1,0:T(8,128)(2,1)S(1)} %collective-permute-done.4.refs_0_), channel_id=1, source_target_pairs={{0,32},{32,0},{1,33},{33,1},{2,34},{34,2},{3,35},{35,3},{4,36},{36... | collective-permute-start | bytes 884744 | tf_op jit(solution)/shard_map/ppermute | solution.py:34
  158.8 20.6 %collective-permute-start.10 = (bf16[1024,128]{0,1:T(8,128)(2,1)S(1)}, bf16[1024,128]{0,1:T(8,128)(2,1)S(1)}, u32[]{:S(2)}, u32[]{:S(2)}) collective-permute-start(bf16[1024,128]{0,1:T(8,128)(2,1)S(1)} %copy.52), channel_id=1, source_target_pairs={{0,16},{16,0},{1,17},{17,1},{2,18},{18,2},{3,19},{19,3},{4,20},{20... | collective-permute-start | bytes 786440 | tf_op jit(solution)/shard_map/ppermute | solution.py:34
  160.2 24.7 %collective-permute-start.5 = (bf16[128,1152]{1,0:T(8,128)(2,1)S(1)}, bf16[128,1152]{1,0:T(8,128)(2,1)S(1)}, u32[]{:S(2)}, u32[]{:S(2)}) collective-permute-start(bf16[128,1152]{1,0:T(8,128)(2,1)S(1)} %collective-permute-done.4.refs_0_), channel_id=1, source_target_pairs={{0,64},{64,128},{128,192},{192,0},{1,65},{65,129},{129,193},{193,1... | collective-permute-start | bytes 884744 | tf_op jit(solution)/shard_map/ppermute | solution.py:38
  165.7 23.3 %collective-permute-start.12 = (bf16[128,1152]{1,0:T(8,128)(2,1)S(1)}, bf16[128,1152]{1,0:T(8,128)(2,1)S(1)}, u32[]{:S(2)}, u32[]{:S(2)}) collective-permute-start(bf16[128,1152]{1,0:T(8,128)(2,1)S(1)} %collective-permute-done.4.refs_0_), channel_id=1, source_target_pairs={{0,192},{64,0},{128,64},{192,128},{1,193},{65,1},{129,65},{193,129... | collective-permute-start | bytes 884744 | tf_op jit(solution)/shard_map/ppermute | solution.py:38
  171.6 13.9 %collective-permute-start.8 = (bf16[128,1152]{1,0:T(8,128)(2,1)S(1)}, bf16[128,1152]{1,0:T(8,128)(2,1)S(1)}, u32[]{:S(2)}, u32[]{:S(2)}) collective-permute-start(bf16[128,1152]{1,0:T(8,128)(2,1)S(1)} %collective-permute-done.7.refs_0_), channel_id=1, source_target_pairs={{0,192},{64,0},{128,64},{192,128},{1,193},{65,1},{129,65},{193,129... | collective-permute-start | bytes 884744 | tf_op jit(solution)/shard_map/ppermute | solution.py:38
  179.5 31.0 %all-to-all-start.5 = ((bf16[8,16,896]{2,1,0:T(8,128)(2,1)}), bf16[8,16,896]{2,1,0:T(8,128)(2,1)S(1)}, u32[]{:S(2)}, u32[]{:S(2)}) async-start(bf16[8,16,896]{2,1,0:T(8,128)(2,1)} %bitcast.11), calls=%async_computation.6 | async-start | bytes 458752 | tf_op jit(solution)/shard_map/all_to_all | solution.py:285
  184.8 8.6 %collective-permute-start.11 = (bf16[128,1152]{1,0:T(8,128)(2,1)S(1)}, bf16[128,1152]{1,0:T(8,128)(2,1)S(1)}, u32[]{:S(2)}, u32[]{:S(2)}) collective-permute-start(bf16[128,1152]{1,0:T(8,128)(2,1)S(1)} %collective-permute-done.7.refs_0_), channel_id=1, source_target_pairs={{0,64},{64,128},{128,192},{192,0},{1,65},{65,129},{129,193},{193,1... | collective-permute-start | bytes 884744 | tf_op jit(solution)/shard_map/ppermute | solution.py:38
  184.9 14.5 %collective-permute-start.6 = (bf16[128,1152]{1,0:T(8,128)(2,1)S(1)}, bf16[128,1152]{1,0:T(8,128)(2,1)S(1)}, u32[]{:S(2)}, u32[]{:S(2)}) collective-permute-start(bf16[128,1152]{1,0:T(8,128)(2,1)S(1)} %collective-permute-done.5.refs_1_), channel_id=1, source_target_pairs={{0,64},{64,128},{128,192},{192,0},{1,65},{65,129},{129,193},{193,1... | collective-permute-start | bytes 884744 | tf_op jit(solution)/shard_map/ppermute | solution.py:38
  185.6 13.9 %collective-permute-start.9 = (bf16[128,1152]{1,0:T(8,128)(2,1)S(1)}, bf16[128,1152]{1,0:T(8,128)(2,1)S(1)}, u32[]{:S(2)}, u32[]{:S(2)}) collective-permute-start(bf16[128,1152]{1,0:T(8,128)(2,1)S(1)} %collective-permute-done.8.refs_1_), channel_id=1, source_target_pairs={{0,192},{64,0},{128,64},{192,128},{1,193},{65,1},{129,65},{193,129... | collective-permute-start | bytes 884744 | tf_op jit(solution)/shard_map/ppermute | solution.py:38
  202.7 8.5 %collective-permute-start.13 = (f32[128,1024]{1,0:T(8,128)S(1)}, f32[128,1024]{1,0:T(8,128)S(1)}, u32[]{:S(2)}, u32[]{:S(2)}) collective-permute-start(f32[128,1024]{1,0:T(8,128)S(1)} %get-tuple-element.22), channel_id=1, source_target_pairs={{0,16},{16,0},{1,17},{17,1},{2,18},{18,2},{3,19},{19,3},{4,20},{20... | collective-permute-start | bytes 1572872 | tf_op jit(solution)/shard_map/ppermute | solution.py:34
  205.3 4.4 %collective-permute-start.3 = (bf16[128,96]{1,0:T(8,128)(2,1)S(1)}, bf16[128,96]{1,0:T(8,128)(2,1)S(1)}, u32[]{:S(2)}, u32[]{:S(2)}) collective-permute-start(bf16[128,96]{1,0:T(8,128)(2,1)S(1)} %constant_dynamic-slice_fusion), channel_id=1, source_target_pairs={{0,1},{1,0},{2,3},{3,2},{4,5},{5,4},{6,7},{7,6},{8,9},{9,8},{10,11... | collective-permute-start | bytes 73736 | tf_op jit(solution)/shard_map/ppermute | solution.py:34
  (4 other events, 4.1 us)
Sparse Core Ops, SparseCore 0:
  16.0 57.9 reduce-scatter.1

commit v3 on v2

--- a/solution.py
+++ b/solution.py
@@ -21,7 +21,7 @@
 HEAD = ("z", "yh")
 HALF = 128
 SLOTS = 1024
-WIDE = 1024 + 128
+WIDE = 1024
 
 
 def rms_round(values, gain):
@@ -104,56 +104,59 @@
     )(core, kept, got, residual, gain, mine, other)
 
 
-def query_kernel(latent_ref, own_ref, other_ref, pick_ref, o_ref):
+def query_kernel(latent_ref, own_ref, other_ref, first_ref, second_ref):
     latent = latent_ref[:, :QL]
-    o_ref[:, :512] = jnp.dot(latent, own_ref[...], preferred_element_type=jnp.float32).astype(jnp.bfloat16)
-    o_ref[:, 512:1024] = jnp.dot(latent, other_ref[...], preferred_element_type=jnp.float32).astype(
-        jnp.bfloat16
-    )
-    o_ref[:, 1024:] = jnp.dot(
-        latent_ref[:, QL:], pick_ref[...], preferred_element_type=jnp.float32
-    ).astype(jnp.bfloat16)
-
-
-def make_queries(latent, own, other, pick):
+    first_ref[...] = jnp.dot(latent, own_ref[...], preferred_element_type=jnp.float32).astype(jnp.bfloat16)
+    second_ref[...] = jnp.dot(latent, other_ref[...], preferred_element_type=jnp.float32).astype(jnp.bfloat16)
+
+
+def make_queries(latent, own, other):
     whole = pl.BlockSpec(memory_space=pltpu.VMEM)
+    shape = jax.ShapeDtypeStruct((HALF, own.shape[1]), jnp.bfloat16)
     return pl.pallas_call(
         query_kernel,
-        in_specs=[whole] * 4,
-        out_specs=whole,
-        out_shape=jax.ShapeDtypeStruct((HALF, WIDE), jnp.bfloat16),
+        in_specs=[whole] * 3,
+        out_specs=[whole, whole],
+        out_shape=[shape, shape],
         compiler_params=kernel_params(),
-    )(latent, own, other, pick)
-
-
-def score_kernel(count, first, *refs):
+    )(latent, own, other)
+
+
+def score_kernel(count, first, groups_ref, w_ref, *refs):
     pieces, k_ref = refs[:count], refs[count]
     before, o_ref = (None if first else refs[count + 1]), refs[-1]
     scale = IDIM ** (-0.5)
     rows, slots = o_ref.shape
     tile_rows, tile_slots = 64, 256
+    lane = lax.broadcasted_iota(jnp.int32, (128, 128), 1)
+    row = lax.broadcasted_iota(jnp.int32, (128, 128), 0)
+    picked = []
+    for n in range(count):
+        source = jnp.where(lane < 4, groups_ref[2 * n] * 4 + lane, groups_ref[2 * n + 1] * 4 + lane - 4)
+        pick = jnp.where((row == source) & (lane < 8), 1.0, 0.0).astype(jnp.bfloat16)
+        picked.append(jnp.dot(w_ref[...], pick, preferred_element_type=jnp.float32) * scale)
     for at in range(0, rows, tile_rows):
-        weights = [piece[at : at + tile_rows, 1024:].astype(jnp.float32) * scale for piece in pieces]
         for slot in range(0, slots, tile_slots):
             here = (slice(at, at + tile_rows), slice(slot, slot + tile_slots))
             total = jnp.zeros((tile_rows, tile_slots), jnp.float32) if first else before[here]
-            for piece, weight in zip(pieces, weights):
+            for piece, weight in zip(pieces, picked):
                 for j in range(8):
                     logits = jnp.dot(
                         piece[at : at + tile_rows, j * IDIM : (j + 1) * IDIM],
                         k_ref[:, slot : slot + tile_slots],
                         preferred_element_type=jnp.float32,
                     )
-                    total = total + jnp.maximum(logits, 0.0) * weight[:, j : j + 1]
+                    total = total + jnp.maximum(logits, 0.0) * weight[at : at + tile_rows, j : j + 1]
             o_ref[here] = total
 
 
-def add_scores(pieces, keys_t, before):
+def add_scores(pieces, groups, head_weights, keys_t, before):
     count, slots, block = len(pieces), keys_t.shape[1], 512
     tile = pl.BlockSpec((HALF, block), lambda i: (0, i))
-    specs = [pl.BlockSpec((HALF, WIDE), lambda i: (0, 0))] * count
+    specs = [pl.BlockSpec(memory_space=pltpu.SMEM), pl.BlockSpec((HALF, 128), lambda i: (0, 0))]
+    specs += [pl.BlockSpec((HALF, WIDE), lambda i: (0, 0))] * count
     specs += [pl.BlockSpec((IDIM, block), lambda i: (0, i))]
-    args = list(pieces) + [keys_t]
+    args = [jnp.stack(groups).astype(jnp.int32), head_weights] + list(pieces) + [keys_t]
     if before is not None:
         specs.append(tile)
         args.append(before)
@@ -165,7 +168,7 @@
         out_shape=jax.ShapeDtypeStruct((HALF, slots), jnp.float32),
         compiler_params=kernel_params(),
         cost_estimate=pl.CostEstimate(
-            flops=2 * count * 8 * HALF * slots * IDIM * 2, bytes_accessed=2 * HALF * slots * 4, transcendentals=0
+            flops=4 * count * 8 * HALF * slots * IDIM, bytes_accessed=2 * HALF * slots * 4, transcendentals=0
         ),
     )(*args)
 
@@ -217,14 +220,21 @@
     return half, swap(half, "c")
 
 
-def turn(queries):
+def spread(values, flip):
     moves = []
     for at in range(N_SEQ * N_HEAD):
         s, h = divmod(at, N_HEAD)
-        pair, core = divmod(s, 2)
-        level, high = divmod(h, 2)
-        moves.append((at, ((pair ^ level) * 2 + high) * N_HEAD + pair * 2 + core))
-    return lax.ppermute(queries, SEQ + HEAD, moves)
+        moves.append((at, ((((s // 2) ^ (h // 2) ^ flip) * 2) + s % 2) * N_HEAD + h))
+    return lax.ppermute(values, SEQ + HEAD, moves)
+
+
+def cross(values, flip):
+    moves = []
+    for at in range(N_SEQ * N_HEAD):
+        s, h = divmod(at, N_HEAD)
+        (pair, core), (z, high) = divmod(s, 2), divmod(h, 2)
+        moves.append((at, (pair * 2 + high) * N_HEAD + (pair ^ z ^ flip) * 2 + core))
+    return lax.ppermute(values, SEQ + HEAD, moves)
 
 
 def shards(
@@ -257,6 +267,9 @@
     keys_other = swap(index_keys, "c")
     keys_t = jnp.concatenate([index_keys, keys_other], axis=0).T
 
+    summed, residual_cols, down_mine, down_other, weight_other, keys_t = lax.optimization_barrier(
+        (summed, residual_cols, down_mine, down_other, weight_other, keys_t)
+    )
     kept = lax.dynamic_index_in_dim(summed, yh, 0, keepdims=False)
     got = swap(lax.dynamic_index_in_dim(summed, 1 - yh, 0, keepdims=False), "yh")
     gain = lax.dynamic_slice_in_dim(norm_gain, z * DZ, DZ).reshape(1, DZ)
@@ -275,30 +288,42 @@
     everyone = lax.all_to_all(jnp.broadcast_to(packed[None], (NZ,) + packed.shape), "z", 0, 0)
     everyone = everyone.reshape(HALF, packed.shape[1])
 
-    lane = lax.broadcasted_iota(jnp.int32, (128, 128), 1)
-    source = jnp.where(lane < 4, head * 4 + lane, (head ^ 1) * 4 + lane - 4)
-    pick = (lax.broadcasted_iota(jnp.int32, (128, 128), 0) == source) & (lane < 8)
-    queries = make_queries(everyone, index_weight, weight_other, pick.astype(jnp.bfloat16))
-    queries, everyone, hidden = lax.optimization_barrier((queries, everyone, hidden))
-
-    piece = turn(queries)
+    first, second = make_queries(everyone, index_weight, weight_other)
+    first, second, everyone, hidden = lax.optimization_barrier((first, second, everyone, hidden))
+    all_weights = everyone[:, QL:]
+    moved = (spread(first, 0), spread(second, 4), spread(all_weights, 0))
     hidden_rows = lax.all_to_all(hidden.reshape(NZ, own, DZ), "z", 0, 0).transpose(1, 0, 2).reshape(own, D)
     latent_mine = lax.dynamic_slice_in_dim(everyone, head * local, local, 1).reshape(NZ, own, local)
     latent_give = lax.dynamic_slice_in_dim(everyone, (head ^ 1) * local, local, 1)
     latent_got = swap(latent_give, "yh").reshape(NZ, own, local)
+    first, second, all_weights = cross(moved[0], 0), cross(moved[1], 4), cross(moved[2], 0)
+    first, second, all_weights, hidden_rows, latent_got = lax.optimization_barrier(
+        (first, second, all_weights, hidden_rows, latent_got)
+    )
     latent_out = jnp.stack(
         [jnp.where(yh == 0, latent_mine, latent_got), jnp.where(yh == 0, latent_got, latent_mine)], axis=1
     ).reshape(rows, local)
 
+    def groups(*steps):
+        out = []
+        for dx, dy in steps:
+            level = (((x + dx) % 4) * 2 + (yl ^ dy)) ^ z
+            out += [level * 2 + c, (level ^ 4) * 2 + (c ^ 1)]
+        return out
+
+    def add(pieces, steps, before):
+        return add_scores(pieces, groups(*steps), all_weights, keys_t, before)
+
+    piece = jnp.concatenate([first, second], axis=1)
     beside = swap(piece, "yl")
     right, left = shift(piece, "x", 4, 1), shift(piece, "x", 4, -1)
-    scores = add_scores([piece], keys_t, None)
+    scores = add([piece], [(0, 0)], None)
     beside_right, beside_left = shift(beside, "x", 4, 1), shift(beside, "x", 4, -1)
     across = shift(right, "x", 4, 1)
-    scores = add_scores([beside, right, left], keys_t, scores)
+    scores = add([beside, right, left], [(0, 1), (-1, 0), (1, 0)], scores)
     beside_across = shift(beside_left, "x", 4, -1)
-    scores = add_scores([beside_right, beside_left], keys_t, scores)
-    scores = add_scores([across, beside_across], keys_t, scores)
+    scores = add([beside_right, beside_left], [(-1, 1), (1, 1)], scores)
+    scores = add([across, beside_across], [(2, 0), (2, 1)], scores)
     got_scores = swap(scores[:, SLOTS:], "c")
     own_positions = lax.dynamic_slice_in_dim(positions, head * rows, rows).reshape(rows, 1)
     numbers = jnp.stack([c, cache_len[0], seq * SLOTS]).astype(jnp.int32)

time: 221 us -> 239 us (1.081)
  waiting for transfers between devices: 45.1 us -> 63.5 us
  blocking collectives: 44.7 us -> 38 us
  Pallas kernels: 27 us -> 32.5 us
    ppermute x1 -> x6, starting transfers between devices: 5.45 us -> 39.3 us  [the longest x3 28.1 us: cross(): return lax.ppermute(values, SEQ + HEAD, moves)]
    ppermute x7, starting transfers between devices: 30.7 us -> 11.1 us  [swap(): return lax.ppermute(values, axis, [(0, 1), (1, 0)])]
    all_to_all x1, waiting for transfers between devices: 0.01 us -> 18.6 us  [down_weight_rows(): lax.all_to_all(jnp.broadcast_to(wide[None], (8,) + wide.shape), ('x', 'yl...]
    ppermute x6, starting transfers between devices: 23.3 us -> 7.51 us  [shift(): lax.ppermute(values, axis, [(i, (i + by) % size) for i in range(size)])]
    all_to_all x1, blocking collectives: 20.6 us -> 13.9 us  [shards(): lax.all_to_all(jnp.broadcast_to(packed[None], (NZ,) + packed.shape), 'z',...]
    pallas_call x4, Pallas kernels: 12.7 us -> 17.6 us  [add_scores(): pl.pallas_call(functools.partial(score_kernel, count, before is None), gr...]
    ppermute x1 -> x6, waiting for transfers between devices: 4.86 us -> 0.02 us  [the longest x3 0.01 us: cross(): return lax.ppermute(values, SEQ + HEAD, moves)]
    ppermute x7, waiting for transfers between devices: 18.4 us -> 21.9 us  [swap(): return lax.ppermute(values, axis, [(0, 1), (1, 0)])]
  transfers between devices with their start and end apart: 19 -> 24, of which waited for: 7 -> 8; matrix products, arithmetic and copies ran while one was open for 4% -> 4% of each run, Pallas kernels for 6% -> 6%
where the time goes in v3:
time: 239 us; the launch traced here: 237 us
  starting transfers between devices  73.2 us (31%)
  waiting for transfers between devices  63.5 us (27%)
  blocking collectives  38 us (16%)
  Pallas kernels  32.5 us (14%)
  between operations  15.2 us (6%)
  local copies, waits for them, and re-layouts  11.9 us (5%)
  other arithmetic  2.78 us (1%)
    ppermute x3, starting transfers between devices, cross(): return lax.ppermute(values, SEQ + HEAD, moves)  28.1 us
    all_to_all x1, blocking collectives, down_weight_rows(): lax.all_to_all(jnp.repeat(own, 2, axis=0), HEAD, 0, 0).transpose(1, 0, 2)  24.1 us
    ppermute x7, waiting for transfers between devices, swap(): return lax.ppermute(values, axis, [(0, 1), (1, 0)])  21.9 us
    all_to_all x1, waiting for transfers between devices, down_weight_rows(): lax.all_to_all(jnp.broadcast_to(wide[None], (8,) + wide.shape), ('x', 'yl...  18.6 us
    pallas_call x4, Pallas kernels, add_scores(): pl.pallas_call(functools.partial(score_kernel, count, before is None), gr...  17.6 us
    all_to_all x1, blocking collectives, shards(): lax.all_to_all(jnp.broadcast_to(packed[None], (NZ,) + packed.shape), 'z',...  13.9 us
    all_to_all x1, waiting for transfers between devices, shards(): parts = lax.all_to_all(lifted.reshape(NZ, own, lifted.shape[1]), 'z', 0, 0)  11.9 us
    ppermute x3, starting transfers between devices, spread(): return lax.ppermute(values, SEQ + HEAD, moves)  11.2 us
  transfers between devices with their start and end apart: 24, of which 8 were waited for; matrix products, arithmetic and copies ran while one was open for 4% of the time, Pallas kernels for 6%

profile of v3, /device:TPU:1, one launch (start us, length us, event | category | flops | bytes accessed | tf_op | source)
XLA Modules:
  0.0 237.0 jit_solution(16362300662585806883)
XLA Ops:
  7.2 8.7 %shard_map.130 = bf16[8,2,128,896]{3,2,1,0:T(8,128)(2,1)} custom-call(bf16[256,512]{1,0:T(8,128)(2,1)} %a_ref.1, bf16[512,7168]{1,0:T(8,128)(2,1)} %b_ref.1), custom_call_target="tpu_custom_call" | custom-call | tf_op jit(solution)/shard_map/pallas_call | solution.py:56
  18.0 24.1 %all_to_all.30 = bf16[16,56,100]{2,1,0:T(8,128)(2,1)S(1)} all-to-all(bf16[16,56,100]{2,1,0:T(8,128)(2,1)S(1)} %bitcast.77), channel_id=1, replica_groups=mesh['x'=4,'yl'=2,'c'=2,'z'=8,'yh'=2] {'z','yh'}, dimensions={0} | all-to-all | bytes 358400 | tf_op jit(solution)/shard_map/all_to_all | solution.py:208
  44.1 4.8 %all-to-all-start.2 = ((bf16[8,56,1664]{2,1,0:T(8,128)(2,1)}), bf16[8,56,1664]{2,1,0:T(8,128)(2,1)S(1)}, u32[]{:S(2)}, u32[]{:S(2)}) async-start(bf16[8,56,1664]{2,1,0:T(8,128)(2,1)} %broadcast_in_dim.12), calls=%async_computation.3 | async-start | bytes 2981888 | tf_op jit(solution)/shard_map/all_to_all | solution.py:218
  49.0 18.6 %all-to-all-done.2 = bf16[8,56,1664]{2,1,0:T(8,128)(2,1)S(1)} async-done(((bf16[8,56,1664]{2,1,0:T(8,128)(2,1)}), bf16[8,56,1664]{2,1,0:T(8,128)(2,1)S(1)}, u32[]{:S(2)}, u32[]{:S(2)}) %all-to-all-start.2) | async-done | bytes 1490976 | tf_op jit(solution)/shard_map/all_to_all | solution.py:218
  67.6 3.3 %collective-permute-start = (bf16[448,1664]{1,0:T(8,128)(2,1)S(1)}, bf16[448,1664]{1,0:T(8,128)(2,1)}, u32[]{:S(2)}, u32[]{:S(2)}) collective-permute-start(bf16[448,1664]{1,0:T(8,128)(2,1)S(1)} %bitcast.64), channel_id=1, source_target_pairs={{0,16},{16,0},{1,17},{17,1},{2,18},{18,2},{3,19},{19,3},{4,20},{20... | collective-permute-start | bytes 4472840 | tf_op jit(solution)/shard_map/ppermute | solution.py:34
  72.9 3.4 %all-to-all-start = ((bf16[8,16,896]{2,1,0:T(8,128)(2,1)}), bf16[8,16,896]{2,1,0:T(8,128)(2,1)S(1)}, u32[]{:S(2)}, u32[]{:S(2)}) async-start(bf16[8,16,896]{2,1,0:T(8,128)(2,1)} %bitcast.76), calls=%async_computation.1 | async-start | bytes 458752 | tf_op jit(solution)/shard_map/all_to_all | solution.py:265
  78.1 8.3 %all-to-all-done = bf16[8,16,896]{2,1,0:T(8,128)(2,1)S(1)} async-done(((bf16[8,16,896]{2,1,0:T(8,128)(2,1)}), bf16[8,16,896]{2,1,0:T(8,128)(2,1)S(1)}, u32[]{:S(2)}, u32[]{:S(2)}) %all-to-all-start) | async-done | bytes 229408 | tf_op jit(solution)/shard_map/all_to_all | solution.py:265
  86.4 12.1 %collective-permute-done.1.other_ref = bf16[1536,512]{1,0:T(8,128)(2,1)} collective-permute-done((bf16[1536,512]{1,0:T(8,128)(2,1)S(1)}, bf16[1536,512]{1,0:T(8,128)(2,1)}, u32[]{:S(2)}, u32[]{:S(2)}) %collective-permute-start.1) | collective-permute-done | bytes 1572896 | tf_op jit(solution)/shard_map/ppermute | solution.py:34
  100.3 3.2 %collective-permute-start.3 = (bf16[128,896]{1,0:T(8,128)(2,1)}, bf16[128,896]{1,0:T(8,128)(2,1)}, u32[]{:S(2)}, u32[]{:S(2)}) collective-permute-start(bf16[128,896]{1,0:T(8,128)(2,1)} %get-tuple-element.52), channel_id=1, source_target_pairs={{0,1},{1,0},{2,3},{3,2},{4,5},{5,4},{6,7},{7,6},{8,9},{9,8},{10,11... | collective-permute-start | bytes 688136 | tf_op jit(solution)/shard_map/ppermute | solution.py:34
  104.3 3.7 %collective-permute-done.3.got_ref = bf16[128,896]{1,0:T(8,128)(2,1)} collective-permute-done((bf16[128,896]{1,0:T(8,128)(2,1)}, bf16[128,896]{1,0:T(8,128)(2,1)}, u32[]{:S(2)}, u32[]{:S(2)}) %collective-permute-start.3) | collective-permute-done | bytes 229408 | tf_op jit(solution)/shard_map/ppermute | solution.py:34
  111.4 3.5 %all-to-all-start.3 = ((bf16[8,16,1664]{2,1,0:T(8,128)(2,1)}), bf16[8,16,1664]{2,1,0:T(8,128)(2,1)S(1)}, u32[]{:S(2)}, u32[]{:S(2)}) async-start(bf16[8,16,1664]{2,1,0:T(8,128)(2,1)} %bitcast.70), calls=%async_computation.4 | async-start | bytes 851968 | tf_op jit(solution)/shard_map/all_to_all | solution.py:280
  114.9 11.9 %all-to-all-done.3 = bf16[8,16,1664]{2,1,0:T(8,128)(2,1)S(1)} async-done(((bf16[8,16,1664]{2,1,0:T(8,128)(2,1)}), bf16[8,16,1664]{2,1,0:T(8,128)(2,1)S(1)}, u32[]{:S(2)}, u32[]{:S(2)}) %all-to-all-start.3) | async-done | bytes 426016 | tf_op jit(solution)/shard_map/all_to_all | solution.py:280
  127.6 13.9 %all_to_all.31 = bf16[8,16,1664]{2,1,0:T(8,128)(2,1)S(1)} all-to-all(bf16[8,16,1664]{2,1,0:T(8,128)(2,1)S(1)} %broadcast_in_dim.27), channel_id=1, replica_groups=mesh['x'=4,'yl'=2,'c'=2,'z'=8,'yh'=2] {'z'}, dimensions={0} | all-to-all | bytes 851968 | tf_op jit(solution)/shard_map/all_to_all | solution.py:288
  143.5 3.5 %all-to-all-start.5 = ((bf16[8,16,896]{2,1,0:T(8,128)(2,1)}), bf16[8,16,896]{2,1,0:T(8,128)(2,1)S(1)}, u32[]{:S(2)}, u32[]{:S(2)}) async-start(bf16[8,16,896]{2,1,0:T(8,128)(2,1)} %bitcast.13), calls=%async_computation.6 | async-start | bytes 458752 | tf_op jit(solution)/shard_map/all_to_all | solution.py:295
  147.7 9.9 %collective-permute-start.6 = (bf16[128,512]{1,0:T(8,128)(2,1)S(1)}, bf16[128,512]{1,0:T(8,128)(2,1)S(1)}, u32[]{:S(2)}, u32[]{:S(2)}) collective-permute-start(bf16[128,512]{1,0:T(8,128)(2,1)S(1)} %get-tuple-element.32), channel_id=1, source_target_pairs={{0,128},{1,129},{2,162},{3,163},{4,196},{5,197},{6,230},{7,231},{8... | collective-permute-start | bytes 393224 | tf_op jit(solution)/shard_map/ppermute | solution.py:228
  158.3 9.2 %collective-permute-start.9 = (bf16[128,128]{1,0:T(8,128)(2,1)S(1)}, bf16[128,128]{1,0:T(8,128)(2,1)S(1)}, u32[]{:S(2)}, u32[]{:S(2)}) collective-permute-start(bf16[128,128]{1,0:T(8,128)(2,1)S(1)} %collective-permute-done.8), channel_id=1, source_target_pairs={{0,0},{1,16},{2,2},{3,18},{4,4},{5,20},{6,6},{7,22},{8,8},{9,24},{... | collective-permute-start | bytes 98312 | tf_op jit(solution)/shard_map/ppermute | solution.py:237
  169.5 17.0 %collective-permute-start.7 = (bf16[128,512]{1,0:T(8,128)(2,1)S(1)}, bf16[128,512]{1,0:T(8,128)(2,1)S(1)}, u32[]{:S(2)}, u32[]{:S(2)}) collective-permute-start(bf16[128,512]{1,0:T(8,128)(2,1)S(1)} %collective-permute-done.6), channel_id=1, source_target_pairs={{0,8},{1,24},{2,10},{3,26},{4,12},{5,28},{6,14},{7,30},{8,0},{9,16... | collective-permute-start | bytes 393224 | tf_op jit(solution)/shard_map/ppermute | solution.py:237
  187.4 3.5 %collective-permute-done.10 = bf16[128,96]{1,0:T(8,128)(2,1)S(1)} collective-permute-done((bf16[128,96]{1,0:T(8,128)(2,1)S(1)}, bf16[128,96]{1,0:T(8,128)(2,1)S(1)}, u32[]{:S(2)}, u32[]{:S(2)}) %collective-permute-start.10) | collective-permute-done | bytes 24608 | tf_op jit(solution)/shard_map/ppermute | solution.py:34
  191.0 2.8 %collective-permute-start.13 = (bf16[128,1024]{1,0:T(8,128)(2,1)S(1)}, bf16[128,1024]{1,0:T(8,128)(2,1)S(1)}, u32[]{:S(2)}, u32[]{:S(2)}) collective-permute-start(bf16[128,1024]{1,0:T(8,128)(2,1)S(1)} %constant_dynamic-update-slice_fusion.refs_0_), channel_id=1, source_target_pairs={{0,32},{32,0},{1,33},{33,1},{2,34},{34,2},{3,35},{35,3},{4,36},{36... | collective-permute-start | bytes 786440 | tf_op jit(solution)/shard_map/ppermute | solution.py:34
  199.8 2.7 %shard_map.133.refs_4_ = f32[128,2048]{1,0:T(8,128)S(1)} custom-call(s32[2]{0:T(128)S(1)} %pad_add_fusion.3.groups_ref, bf16[128,128]{1,0:T(8,128)(2,1)S(1)} %collective-permute-done.9.w_ref, bf16[128,1024]{1,0:T(8,128)(2,1)S(1)} %constant_dynamic-update-slice_fusion.refs_0_, bf16[128,2048]{1,0:T(8,128)(2,1)S(1)} %copy-done.1), custom_call_target="tpu_custom_call" | custom-call | flops 1073741824 | bytes 2097152 | tf_op jit(solution)/shard_map/pallas_call | solution.py:163
  206.6 3.0 %collective-permute-start.15 = (bf16[128,1024]{1,0:T(8,128)(2,1)S(1)}, bf16[128,1024]{1,0:T(8,128)(2,1)S(1)}, u32[]{:S(2)}, u32[]{:S(2)}) collective-permute-start(bf16[128,1024]{1,0:T(8,128)(2,1)S(1)} %collective-permute-done.14.refs_1_), channel_id=1, source_target_pairs={{0,192},{64,0},{128,64},{192,128},{1,193},{65,1},{129,65},{193,129... | collective-permute-start | bytes 786440 | tf_op jit(solution)/shard_map/ppermute | solution.py:38
  209.6 5.8 %shard_map.134.refs_3_ = f32[128,2048]{1,0:T(8,128)S(1)} custom-call(s32[6]{0:T(128)S(1)} %stack.101.groups_ref, bf16[128,128]{1,0:T(8,128)(2,1)S(1)} %collective-permute-done.9.w_ref, bf16[128,1024]{1,0:T(8,128)(2,1)S(1)} %collective-permute-done.13.refs_0_, bf16[128,1024]{1,0:T(8,128)(2,1)S(1)} %collective-permute-done.11.refs_1_, ...), custom_call_target="tpu_custom_call" | custom-call | flops 3221225472 | bytes 2097152 | tf_op jit(solution)/shard_map/pallas_call | solution.py:163
  215.5 4.5 %shard_map.135.refs_3_ = f32[128,2048]{1,0:T(8,128)S(1)} custom-call(s32[4]{0:T(128)S(1)} %pad_add_fusion.2.groups_ref, bf16[128,128]{1,0:T(8,128)(2,1)S(1)} %collective-permute-done.9.w_ref, bf16[128,1024]{1,0:T(8,128)(2,1)S(1)} %collective-permute-done.16.refs_0_, bf16[128,1024]{1,0:T(8,128)(2,1)S(1)} %collective-permute-done.14.refs_1_, ...), custom_call_target="tpu_custom_call" | custom-call | flops 2147483648 | bytes 2097152 | tf_op jit(solution)/shard_map/pallas_call | solution.py:163
  220.0 4.5 %shard_map.136 = f32[128,2048]{1,0:T(8,128)S(1)} custom-call(s32[4]{0:T(128)S(1)} %pad_add_fusion.1.groups_ref, bf16[128,128]{1,0:T(8,128)(2,1)S(1)} %collective-permute-done.9.w_ref, bf16[128,1024]{1,0:T(8,128)(2,1)S(1)} %collective-permute-done.12.refs_0_, bf16[128,1024]{1,0:T(8,128)(2,1)S(1)} %collective-permute-done.15.refs_1_, ...), custom_call_target="tpu_custom_call" | custom-call | flops 2147483648 | bytes 2097152 | tf_op jit(solution)/shard_map/pallas_call | solution.py:163
  (96 shorter events, 35.6 us)
Async XLA Ops:
  7.2 91.4 %reduce-scatter.2.cloned.1.call-start = ((), (), s32[]{:S(2)}) async-start(), calls=%async_computation.7 | async-start | bytes 4128768 | tf_op jit(solution)/shard_map/reduce_scatter | solution.py:262
  44.1 23.5 %all-to-all-start.2 = ((bf16[8,56,1664]{2,1,0:T(8,128)(2,1)}), bf16[8,56,1664]{2,1,0:T(8,128)(2,1)S(1)}, u32[]{:S(2)}, u32[]{:S(2)}) async-start(bf16[8,56,1664]{2,1,0:T(8,128)(2,1)} %broadcast_in_dim.12), calls=%async_computation.3 | async-start | bytes 2981888 | tf_op jit(solution)/shard_map/all_to_all | solution.py:218
  48.9 49.6 %collective-permute-start.1 = (bf16[1536,512]{1,0:T(8,128)(2,1)S(1)}, bf16[1536,512]{1,0:T(8,128)(2,1)}, u32[]{:S(2)}, u32[]{:S(2)}) collective-permute-start(bf16[1536,512]{1,0:T(8,128)(2,1)S(1)} %copy-done), channel_id=1, source_target_pairs={{0,1},{1,0},{2,3},{3,2},{4,5},{5,4},{6,7},{7,6},{8,9},{9,8},{10,11... | collective-permute-start | bytes 4718600 | tf_op jit(solution)/shard_map/ppermute | solution.py:34
  67.6 30.9 %collective-permute-start = (bf16[448,1664]{1,0:T(8,128)(2,1)S(1)}, bf16[448,1664]{1,0:T(8,128)(2,1)}, u32[]{:S(2)}, u32[]{:S(2)}) collective-permute-start(bf16[448,1664]{1,0:T(8,128)(2,1)S(1)} %bitcast.64), channel_id=1, source_target_pairs={{0,16},{16,0},{1,17},{17,1},{2,18},{18,2},{3,19},{19,3},{4,20},{20... | collective-permute-start | bytes 4472840 | tf_op jit(solution)/shard_map/ppermute | solution.py:34
  72.0 4.2 %collective-permute-start.2 = (bf16[1024,128]{0,1:T(8,128)(2,1)S(1)}, bf16[1024,128]{0,1:T(8,128)(2,1)}, u32[]{:S(2)}, u32[]{:S(2)}) collective-permute-start(bf16[1024,128]{0,1:T(8,128)(2,1)S(1)} %copy.47), channel_id=1, source_target_pairs={{0,16},{16,0},{1,17},{17,1},{2,18},{18,2},{3,19},{19,3},{4,20},{20... | collective-permute-start | bytes 786440 | tf_op jit(solution)/shard_map/ppermute | solution.py:34
  72.9 13.5 %all-to-all-start = ((bf16[8,16,896]{2,1,0:T(8,128)(2,1)}), bf16[8,16,896]{2,1,0:T(8,128)(2,1)S(1)}, u32[]{:S(2)}, u32[]{:S(2)}) async-start(bf16[8,16,896]{2,1,0:T(8,128)(2,1)} %bitcast.76), calls=%async_computation.1 | async-start | bytes 458752 | tf_op jit(solution)/shard_map/all_to_all | solution.py:265
  100.3 7.7 %collective-permute-start.3 = (bf16[128,896]{1,0:T(8,128)(2,1)}, bf16[128,896]{1,0:T(8,128)(2,1)}, u32[]{:S(2)}, u32[]{:S(2)}) collective-permute-start(bf16[128,896]{1,0:T(8,128)(2,1)} %get-tuple-element.52), channel_id=1, source_target_pairs={{0,1},{1,0},{2,3},{3,2},{4,5},{5,4},{6,7},{7,6},{8,9},{9,8},{10,11... | collective-permute-start | bytes 688136 | tf_op jit(solution)/shard_map/ppermute | solution.py:34
  111.4 15.5 %all-to-all-start.3 = ((bf16[8,16,1664]{2,1,0:T(8,128)(2,1)}), bf16[8,16,1664]{2,1,0:T(8,128)(2,1)S(1)}, u32[]{:S(2)}, u32[]{:S(2)}) async-start(bf16[8,16,1664]{2,1,0:T(8,128)(2,1)} %bitcast.70), calls=%async_computation.4 | async-start | bytes 851968 | tf_op jit(solution)/shard_map/all_to_all | solution.py:280
  143.5 43.2 %all-to-all-start.5 = ((bf16[8,16,896]{2,1,0:T(8,128)(2,1)}), bf16[8,16,896]{2,1,0:T(8,128)(2,1)S(1)}, u32[]{:S(2)}, u32[]{:S(2)}) async-start(bf16[8,16,896]{2,1,0:T(8,128)(2,1)} %bitcast.13), calls=%async_computation.6 | async-start | bytes 458752 | tf_op jit(solution)/shard_map/all_to_all | solution.py:295
  147.1 20.5 %collective-permute-start.4 = (bf16[128,512]{1,0:T(8,128)(2,1)S(1)}, bf16[128,512]{1,0:T(8,128)(2,1)S(1)}, u32[]{:S(2)}, u32[]{:S(2)}) collective-permute-start(bf16[128,512]{1,0:T(8,128)(2,1)S(1)} %get-tuple-element.31), channel_id=1, source_target_pairs={{0,0},{1,1},{2,34},{3,35},{4,68},{5,69},{6,102},{7,103},{8,136},{9... | collective-permute-start | bytes 393224 | tf_op jit(solution)/shard_map/ppermute | solution.py:228
  147.7 21.7 %collective-permute-start.6 = (bf16[128,512]{1,0:T(8,128)(2,1)S(1)}, bf16[128,512]{1,0:T(8,128)(2,1)S(1)}, u32[]{:S(2)}, u32[]{:S(2)}) collective-permute-start(bf16[128,512]{1,0:T(8,128)(2,1)S(1)} %get-tuple-element.32), channel_id=1, source_target_pairs={{0,128},{1,129},{2,162},{3,163},{4,196},{5,197},{6,230},{7,231},{8... | collective-permute-start | bytes 393224 | tf_op jit(solution)/shard_map/ppermute | solution.py:228
  157.6 0.7 collective-permute-start.8
  158.3 32.7 %collective-permute-start.9 = (bf16[128,128]{1,0:T(8,128)(2,1)S(1)}, bf16[128,128]{1,0:T(8,128)(2,1)S(1)}, u32[]{:S(2)}, u32[]{:S(2)}) collective-permute-start(bf16[128,128]{1,0:T(8,128)(2,1)S(1)} %collective-permute-done.8), channel_id=1, source_target_pairs={{0,0},{1,16},{2,2},{3,18},{4,4},{5,20},{6,6},{7,22},{8,8},{9,24},{... | collective-permute-start | bytes 98312 | tf_op jit(solution)/shard_map/ppermute | solution.py:237
  167.5 23.4 %collective-permute-start.5 = (bf16[128,512]{1,0:T(8,128)(2,1)S(1)}, bf16[128,512]{1,0:T(8,128)(2,1)S(1)}, u32[]{:S(2)}, u32[]{:S(2)}) collective-permute-start(bf16[128,512]{1,0:T(8,128)(2,1)S(1)} %collective-permute-done.4), channel_id=1, source_target_pairs={{0,0},{1,16},{2,2},{3,18},{4,4},{5,20},{6,6},{7,22},{8,8},{9,24},{... | collective-permute-start | bytes 393224 | tf_op jit(solution)/shard_map/ppermute | solution.py:237
  169.5 21.5 %collective-permute-start.7 = (bf16[128,512]{1,0:T(8,128)(2,1)S(1)}, bf16[128,512]{1,0:T(8,128)(2,1)S(1)}, u32[]{:S(2)}, u32[]{:S(2)}) collective-permute-start(bf16[128,512]{1,0:T(8,128)(2,1)S(1)} %collective-permute-done.6), channel_id=1, source_target_pairs={{0,8},{1,24},{2,10},{3,26},{4,12},{5,28},{6,14},{7,30},{8,0},{9,16... | collective-permute-start | bytes 393224 | tf_op jit(solution)/shard_map/ppermute | solution.py:237
  186.6 4.4 %collective-permute-start.10 = (bf16[128,96]{1,0:T(8,128)(2,1)S(1)}, bf16[128,96]{1,0:T(8,128)(2,1)S(1)}, u32[]{:S(2)}, u32[]{:S(2)}) collective-permute-start(bf16[128,96]{1,0:T(8,128)(2,1)S(1)} %get-tuple-element.55), channel_id=1, source_target_pairs={{0,1},{1,0},{2,3},{3,2},{4,5},{5,4},{6,7},{7,6},{8,9},{9,8},{10,11... | collective-permute-start | bytes 73736 | tf_op jit(solution)/shard_map/ppermute | solution.py:34
  191.0 8.1 %collective-permute-start.13 = (bf16[128,1024]{1,0:T(8,128)(2,1)S(1)}, bf16[128,1024]{1,0:T(8,128)(2,1)S(1)}, u32[]{:S(2)}, u32[]{:S(2)}) collective-permute-start(bf16[128,1024]{1,0:T(8,128)(2,1)S(1)} %constant_dynamic-update-slice_fusion.refs_0_), channel_id=1, source_target_pairs={{0,32},{32,0},{1,33},{33,1},{2,34},{34,2},{3,35},{35,3},{4,36},{36... | collective-permute-start | bytes 786440 | tf_op jit(solution)/shard_map/ppermute | solution.py:34
  193.9 9.9 %collective-permute-start.11 = (bf16[128,1024]{1,0:T(8,128)(2,1)S(1)}, bf16[128,1024]{1,0:T(8,128)(2,1)S(1)}, u32[]{:S(2)}, u32[]{:S(2)}) collective-permute-start(bf16[128,1024]{1,0:T(8,128)(2,1)S(1)} %constant_dynamic-update-slice_fusion.refs_0_), channel_id=1, source_target_pairs={{0,64},{64,128},{128,192},{192,0},{1,65},{65,129},{129,193},{193,1... | collective-permute-start | bytes 786440 | tf_op jit(solution)/shard_map/ppermute | solution.py:38
  193.9 15.7 %collective-permute-start.17 = (bf16[128,1024]{1,0:T(8,128)(2,1)S(1)}, bf16[128,1024]{1,0:T(8,128)(2,1)S(1)}, u32[]{:S(2)}, u32[]{:S(2)}) collective-permute-start(bf16[128,1024]{1,0:T(8,128)(2,1)S(1)} %constant_dynamic-update-slice_fusion.refs_0_), channel_id=1, source_target_pairs={{0,192},{64,0},{128,64},{192,128},{1,193},{65,1},{129,65},{193,129... | collective-permute-start | bytes 786440 | tf_op jit(solution)/shard_map/ppermute | solution.py:38
  199.1 7.5 %collective-permute-start.14 = (bf16[128,1024]{1,0:T(8,128)(2,1)S(1)}, bf16[128,1024]{1,0:T(8,128)(2,1)S(1)}, u32[]{:S(2)}, u32[]{:S(2)}) collective-permute-start(bf16[128,1024]{1,0:T(8,128)(2,1)S(1)} %collective-permute-done.13.refs_0_), channel_id=1, source_target_pairs={{0,192},{64,0},{128,64},{192,128},{1,193},{65,1},{129,65},{193,129... | collective-permute-start | bytes 786440 | tf_op jit(solution)/shard_map/ppermute | solution.py:38
  202.6 12.9 %collective-permute-start.16 = (bf16[128,1024]{1,0:T(8,128)(2,1)S(1)}, bf16[128,1024]{1,0:T(8,128)(2,1)S(1)}, u32[]{:S(2)}, u32[]{:S(2)}) collective-permute-start(bf16[128,1024]{1,0:T(8,128)(2,1)S(1)} %collective-permute-done.13.refs_0_), channel_id=1, source_target_pairs={{0,64},{64,128},{128,192},{192,0},{1,65},{65,129},{129,193},{193,1... | collective-permute-start | bytes 786440 | tf_op jit(solution)/shard_map/ppermute | solution.py:38
  203.8 16.2 %collective-permute-start.12 = (bf16[128,1024]{1,0:T(8,128)(2,1)S(1)}, bf16[128,1024]{1,0:T(8,128)(2,1)S(1)}, u32[]{:S(2)}, u32[]{:S(2)}) collective-permute-start(bf16[128,1024]{1,0:T(8,128)(2,1)S(1)} %collective-permute-done.11.refs_1_), channel_id=1, source_target_pairs={{0,64},{64,128},{128,192},{192,0},{1,65},{65,129},{129,193},{193,1... | collective-permute-start | bytes 786440 | tf_op jit(solution)/shard_map/ppermute | solution.py:38
  206.6 13.4 %collective-permute-start.15 = (bf16[128,1024]{1,0:T(8,128)(2,1)S(1)}, bf16[128,1024]{1,0:T(8,128)(2,1)S(1)}, u32[]{:S(2)}, u32[]{:S(2)}) collective-permute-start(bf16[128,1024]{1,0:T(8,128)(2,1)S(1)} %collective-permute-done.14.refs_1_), channel_id=1, source_target_pairs={{0,192},{64,0},{128,64},{192,128},{1,193},{65,1},{129,65},{193,129... | collective-permute-start | bytes 786440 | tf_op jit(solution)/shard_map/ppermute | solution.py:38
  224.6 3.8 %collective-permute-start.18 = (f32[128,1024]{1,0:T(8,128)S(1)}, f32[128,1024]{1,0:T(8,128)S(1)}, u32[]{:S(2)}, u32[]{:S(2)}) collective-permute-start(f32[128,1024]{1,0:T(8,128)S(1)} %get-tuple-element.50), channel_id=1, source_target_pairs={{0,16},{16,0},{1,17},{17,1},{2,18},{18,2},{3,19},{19,3},{4,20},{20... | collective-permute-start | bytes 1572872 | tf_op jit(solution)/shard_map/ppermute | solution.py:34
  (7 other events, 98.9 us)
Sparse Core Ops, SparseCore 0:
  16.0 57.9 reduce-scatter.1

commit v4 on v2

v4 whole, which is shorter than its diff:
```python
import functools

import jax
import jax.numpy as jnp
from jax import lax
from jax.experimental import pallas as pl
from jax.experimental.pallas import tpu as pltpu
from jax.sharding import Mesh
from jax.sharding import PartitionSpec as P

D = 7168
QL = 1536
IHEADS = 64
IDIM = 128
N_SEQ = 16
N_HEAD = 16
NZ = 8
DZ = D // NZ
EPSILON = 1e-06
SEQ = ("x", "yl", "c")
HEAD = ("z", "yh")
HALF = 128
SLOTS = 1024


def rms_round(values, gain):
    widened = values.astype(jnp.float32)
    inverse = lax.rsqrt(jnp.mean(widened * widened, axis=-1, keepdims=True) + EPSILON)
    return (widened * inverse * gain.astype(jnp.float32)).astype(jnp.bfloat16)


def swap(values, axis):
    return lax.ppermute(values, axis, [(0, 1), (1, 0)])


def shift(values, axis, size, by):
    return lax.ppermute(values, axis, [(i, (i + by) % size) for i in range(size)])


def kernel_params():
    return pltpu.CompilerParams(vmem_limit_bytes=48 * 1024 * 1024)


def project_kernel(a_ref, b_ref, o_ref):
    product = jnp.dot(a_ref[...], b_ref[...], preferred_element_type=jnp.float32).astype(o_ref.dtype)
    for group in range(NZ):
        for half in range(2):
            o_ref[0, half, group * 16 : (group + 1) * 16, :] = product[
                group * 32 + half * 16 : group * 32 + (half + 1) * 16, :
            ]


def project(attn_out, out_weight):
    rows, depth = attn_out.shape
    return pl.pallas_call(
        project_kernel,
        grid=(NZ,),
        in_specs=[
            pl.BlockSpec((rows, depth), lambda i: (0, 0)),
            pl.BlockSpec((depth, DZ), lambda i: (0, i)),
        ],
        out_specs=pl.BlockSpec((1, 2, HALF, DZ), lambda i: (i, 0, 0, 0)),
        out_shape=jax.ShapeDtypeStruct((NZ, 2, HALF, DZ), jnp.bfloat16),
        compiler_params=pltpu.CompilerParams(vmem_limit_bytes=60 * 1024 * 1024),
    )(attn_out, out_weight)


def lift_kernel(core_ref, kept_ref, got_ref, res_ref, gain_ref, mine_ref, other_ref, hidden_ref, o_ref):
    hidden = (
        kept_ref[...].astype(jnp.float32)
        + got_ref[...].astype(jnp.float32)
        + res_ref[...].astype(jnp.float32)
    ).astype(jnp.bfloat16)
    hidden_ref[...] = hidden
    wide = hidden.astype(jnp.float32)
    squares = jnp.sum(wide * wide, axis=1, keepdims=True)
    high = squares.astype(jnp.bfloat16).astype(jnp.float32)
    scaled = wide * gain_ref[...].astype(jnp.float32)
    first, second = scaled[:, : DZ // 2], scaled[:, DZ // 2 :]
    is_first = core_ref[0] == 0
    mine = jnp.where(is_first, first, second).astype(jnp.bfloat16)
    other = jnp.where(is_first, second, first).astype(jnp.bfloat16)
    lifted = jnp.dot(mine, mine_ref[...], preferred_element_type=jnp.float32) + jnp.dot(
        other, other_ref[...], preferred_element_type=jnp.float32
    )
    lane = lax.broadcasted_iota(jnp.int32, (HALF, 128), 1)
    tail = jnp.where(lane == IHEADS, high, jnp.where(lane == IHEADS + 1, squares - high, 0.0))
    o_ref[:, :QL] = lifted[:, :QL].astype(jnp.bfloat16)
    o_ref[:, QL:] = jnp.where(lane < IHEADS, lifted[:, QL:], tail).astype(jnp.bfloat16)


def lift(core, kept, got, residual, gain, mine, other):
    whole = pl.BlockSpec(memory_space=pltpu.VMEM)
    return pl.pallas_call(
        lift_kernel,
        in_specs=[pl.BlockSpec(memory_space=pltpu.SMEM)] + [whole] * 6,
        out_specs=[whole, whole],
        out_shape=[
            jax.ShapeDtypeStruct((HALF, DZ), jnp.bfloat16),
            jax.ShapeDtypeStruct((HALF, QL + 128), jnp.bfloat16),
        ],
        compiler_params=kernel_params(),
    )(core, kept, got, residual, gain, mine, other)


def query_kernel(place_ref, latent_ref, own_ref, mine_ref, theirs_ref, o_ref):
    core, high = place_ref[0], place_ref[1]
    is_first = core == 0
    left, right = latent_ref[:, : QL // 2], latent_ref[:, QL // 2 : QL]
    here = jnp.where(is_first, left, right)
    there = jnp.where(is_first, right, left)
    own = jnp.dot(latent_ref[:, :QL], own_ref[...], preferred_element_type=jnp.float32)
    other = jnp.dot(here, mine_ref[...], preferred_element_type=jnp.float32) + jnp.dot(
        there, theirs_ref[...], preferred_element_type=jnp.float32
    )
    for at, part in ((high * 4, own), ((1 - high) * 4, other)):
        part = part.astype(jnp.bfloat16)
        for j in range(4):
            for block in range(NZ):
                o_ref[block, at + j] = part[block * 16 : (block + 1) * 16, j * IDIM : (j + 1) * IDIM]


def make_queries(place, latent, own, mine, theirs):
    whole = pl.BlockSpec(memory_space=pltpu.VMEM)
    return pl.pallas_call(
        query_kernel,
        in_specs=[pl.BlockSpec(memory_space=pltpu.SMEM)] + [whole] * 4,
        out_specs=whole,
        out_shape=jax.ShapeDtypeStruct((NZ, 8, 16, IDIM), jnp.bfloat16),
        compiler_params=kernel_params(),
    )(place, latent, own, mine, theirs)


def score_kernel(q_ref, w_ref, k_ref, o_ref, wide_ref):
    scale = IDIM ** (-0.5)
    tile = 256

    @pl.when(pl.program_id(0) == 0)
    def _():
        weights = w_ref[...].astype(jnp.float32) * scale
        for j in range(IHEADS):
            wide_ref[j * 16 : (j + 1) * 16, :] = jnp.broadcast_to(weights[:, j : j + 1], (16, 128))

    blocks, _, slots = o_ref.shape
    for block in range(blocks):
        for slot in range(0, slots, tile):
            at = block * slots + slot
            logits = lax.dot_general(
                q_ref[...],
                k_ref[at : at + tile, :],
                (((1,), (1,)), ((), ())),
                preferred_element_type=jnp.float32,
            )
            halves = [jnp.zeros((16, 128), jnp.float32), jnp.zeros((16, 128), jnp.float32)]
            for j in range(IHEADS):
                weight = wide_ref[j * 16 : (j + 1) * 16, :]
                for n in range(2):
                    halves[n] += (
                        jnp.maximum(logits[j * 16 : (j + 1) * 16, n * 128 : (n + 1) * 128], 0.0) * weight
                    )
            for n in range(2):
                o_ref[block, :, slot + n * 128 : slot + (n + 1) * 128] = halves[n].astype(o_ref.dtype)


def make_scores(queries, head_weights, keys):
    per_step = 2
    return pl.pallas_call(
        score_kernel,
        grid=(N_SEQ // per_step,),
        in_specs=[
            pl.BlockSpec((IHEADS * 16, IDIM), lambda i: (0, 0)),
            pl.BlockSpec((16, 128), lambda i: (0, 0)),
            pl.BlockSpec((per_step * SLOTS, IDIM), lambda i: (i, 0)),
        ],
        out_specs=pl.BlockSpec((per_step, 16, SLOTS), lambda i: (i, 0, 0)),
        out_shape=jax.ShapeDtypeStruct((N_SEQ, 16, SLOTS), jnp.bfloat16),
        scratch_shapes=[pltpu.VMEM((IHEADS * 16, 128), jnp.float32)],
        compiler_params=kernel_params(),
    )(queries, head_weights, keys)


def finish_kernel(numbers_ref, s_ref, pos_ref, o_ref):
    local = lax.broadcasted_iota(jnp.int32, (16, SLOTS), 1)
    filled, base = numbers_ref[0], numbers_ref[1]
    for group in range(N_SEQ):
        here = slice(group * 16, (group + 1) * 16)
        reach = jnp.minimum(filled, pos_ref[here, :] - base + 1)
        o_ref[here, :] = jnp.where(local < reach, s_ref[group].astype(jnp.float32), 0.0)


def finish(numbers, scores, own_positions):
    whole = pl.BlockSpec(memory_space=pltpu.VMEM)
    return pl.pallas_call(
        finish_kernel,
        in_specs=[pl.BlockSpec(memory_space=pltpu.SMEM), whole, whole],
        out_specs=whole,
        out_shape=jax.ShapeDtypeStruct((N_SEQ * 16, SLOTS), jnp.float32),
        compiler_params=kernel_params(),
    )(numbers, scores, own_positions)


def down_weight_rows(latent_weight, index_proj, x, yl, c):
    piece = c * 8 + x * 2 + yl
    share = DZ // N_SEQ

    def own_rows(weight):
        return lax.dynamic_slice_in_dim(weight.reshape(NZ, DZ, weight.shape[1]), piece * share, share, 1)

    own = jnp.concatenate([own_rows(latent_weight), own_rows(index_proj)], axis=2)
    by_head = lax.all_to_all(jnp.repeat(own, 2, axis=0), HEAD, 0, 0).transpose(1, 0, 2)
    local = latent_weight.shape[1]
    wide = jnp.concatenate(
        [
            by_head[:, :, :local].reshape(share, QL),
            by_head[:, :, local:].reshape(share, IHEADS),
            jnp.zeros((share, 64), jnp.bfloat16),
        ],
        axis=1,
    )
    half = lax.all_to_all(jnp.broadcast_to(wide[None], (8,) + wide.shape), ("x", "yl"), 0, 0)
    half = half.reshape(8 * share, wide.shape[1])
    return half, swap(half, "c")


def turn(values):
    moves = [(s * N_HEAD + h, h * N_HEAD + s) for s in range(N_SEQ) for h in range(N_HEAD)]
    return lax.ppermute(values, SEQ + HEAD, moves)


def shards(
    attn_out,
    out_weight,
    residual,
    norm_gain,
    latent_weight,
    index_proj,
    latent_gain,
    index_weight,
    index_keys,
    positions,
    cache_len,
):
    x, yl, c = (lax.axis_index(a) for a in SEQ)
    z, yh = (lax.axis_index(a) for a in HEAD)
    seq = (x * 2 + yl) * 2 + c
    head = z * 2 + yh
    rows = attn_out.shape[0]
    own = rows // N_HEAD
    local = latent_weight.shape[1]

    partial = project(attn_out, out_weight)
    summed = lax.psum_scatter(partial, "z", scatter_dimension=0, tiled=False)

    down_mine, down_other = down_weight_rows(latent_weight, index_proj, x, yl, c)
    residual_cols = lax.all_to_all(residual.reshape(own, NZ, DZ).transpose(1, 0, 2), "z", 0, 0)
    depth = QL // 2
    weight_mine = swap(lax.dynamic_slice_in_dim(index_weight, c * depth, depth, 0), "yh")
    weight_theirs = swap(weight_mine, "c")
    (summed, residual_cols, down_mine, down_other, weight_mine, weight_theirs, index_keys) = (
        lax.optimization_barrier(
            (summed, residual_cols, down_mine, down_other, weight_mine, weight_theirs, index_keys)
        )
    )
    all_keys = lax.all_gather(index_keys, SEQ, axis=0, tiled=True)
    kept = lax.dynamic_index_in_dim(summed, yh, 0, keepdims=False)
    got = swap(lax.dynamic_index_in_dim(summed, 1 - yh, 0, keepdims=False), "yh")
    gain = lax.dynamic_slice_in_dim(norm_gain, z * DZ, DZ).reshape(1, DZ)
    core = jnp.stack([c]).astype(jnp.int32)
    hidden, lifted = lift(
        core, kept, got, residual_cols.reshape(HALF, DZ), gain, down_mine, down_other
    )
    parts = lax.all_to_all(lifted.reshape(NZ, own, lifted.shape[1]), "z", 0, 0)
    total = jnp.sum(parts.astype(jnp.float32), axis=0)
    mean = (total[:, 1600:1601] + total[:, 1601:1602]) / D
    inverse = lax.rsqrt(mean + EPSILON)
    latent_raw = (total[:, :QL] * inverse).astype(jnp.bfloat16)
    head_weights = (total[:, QL:1600] * inverse * IHEADS ** (-0.5)).astype(jnp.bfloat16)
    latent = rms_round(latent_raw, latent_gain)
    packed = jnp.concatenate([latent, head_weights, jnp.zeros((own, 64), jnp.bfloat16)], axis=1)
    turned = turn(packed)
    everyone = lax.all_to_all(jnp.broadcast_to(turned[None], (NZ,) + turned.shape), "z", 0, 0)
    place = jnp.stack([c, yh]).astype(jnp.int32)
    queries = make_queries(
        place, everyone.reshape(HALF, packed.shape[1]), index_weight, weight_mine, weight_theirs
    )
    queries = lax.all_to_all(queries, "z", 0, 0).reshape(IHEADS * own, IDIM)
    scores = make_scores(queries, turned[:, QL:], all_keys)
    latent, hidden, scores = lax.optimization_barrier((latent, hidden, scores))
    scores = lax.all_to_all(scores, SEQ, 0, 0)

    payload = jnp.concatenate(
        [hidden.reshape(NZ, own, DZ), latent.reshape(own, NZ, 2 * local).transpose(1, 0, 2)], axis=2
    )
    payload = lax.all_to_all(payload, "z", 0, 0)
    hidden_rows = payload[:, :, :DZ].transpose(1, 0, 2).reshape(own, D)
    latent_cols = payload[:, :, DZ:].reshape(NZ, own, 2, local)
    latent_mine = lax.dynamic_index_in_dim(latent_cols, yh, 2, keepdims=False)
    latent_got = swap(lax.dynamic_index_in_dim(latent_cols, 1 - yh, 2, keepdims=False), "yh")
    latent_out = jnp.stack(
        [jnp.where(yh == 0, latent_mine, latent_got), jnp.where(yh == 0, latent_got, latent_mine)], axis=1
    ).reshape(rows, local)

    own_positions = lax.dynamic_slice_in_dim(positions, head * rows, rows).reshape(rows, 1)
    numbers = jnp.stack([cache_len[0], seq * SLOTS]).astype(jnp.int32)
    return (hidden_rows, latent_out, finish(numbers, scores, own_positions))


def solution(mesh):
    fine = Mesh(mesh.devices.reshape(4, 2, 2, 8, 2), SEQ + HEAD)
    in_specs = (
        P(SEQ, HEAD),
        P(HEAD, None),
        P(SEQ + HEAD, None),
        P(),
        P(None, HEAD),
        P(None, HEAD),
        P(),
        P(None, HEAD),
        P(SEQ, None),
        P(),
        P(SEQ),
    )
    out_specs = (P(SEQ + HEAD, None), P(SEQ, HEAD), P(HEAD, SEQ))
    return jax.shard_map(shards, mesh=fine, in_specs=in_specs, out_specs=out_specs, check_vma=False)
```

time: 221 us -> 241 us (1.090)
  waiting for transfers between devices: 45.1 us -> 83.8 us
  starting transfers between devices: 74.1 us -> 41.6 us
  blocking collectives: 44.7 us -> 54.3 us
  local copies, waits for them, and re-layouts: 12.9 us -> 18.2 us
    all_to_all x3 -> x4, waiting for transfers between devices: 5.24 us -> 52.6 us  [the longest x1 17.7 us: down_weight_rows(): lax.all_to_all(jnp.broadcast_to(wide[None], (8,) + wide.shape), ('x', 'yl...]
    ppermute x7 -> x5, starting transfers between devices: 30.7 us -> 7.27 us  [swap(): return lax.ppermute(values, axis, [(0, 1), (1, 0)])]
    ppermute x7 -> x1, starting transfers between devices: 28.8 us -> 7.32 us  [turn(): return lax.ppermute(values, SEQ + HEAD, moves)]
    all_to_all x3 -> x4, starting transfers between devices: 10.3 us -> 23.3 us  [the longest x1 9.16 us: shards(): lax.all_to_all(jnp.broadcast_to(turned[None], (NZ,) + turned.shape), 'z',...]
    all_to_all x1 -> x2, blocking collectives: 20.6 us -> 30.2 us  [the longest x1 15.5 us: shards(): lax.all_to_all(residual.reshape(own, NZ, DZ).transpose(1, 0, 2), 'z', 0, 0)]
    ppermute x7 -> x1, waiting for transfers between devices: 7.75 us -> 1.8 us  [turn(): return lax.ppermute(values, SEQ + HEAD, moves)]
    unnamed x22 -> x31, local copies, waits for them, and re-layouts: 5.71 us -> 9.38 us
    ppermute x7 -> x5, waiting for transfers between devices: 18.4 us -> 16.4 us  [swap(): return lax.ppermute(values, axis, [(0, 1), (1, 0)])]
  transfers between devices with their start and end apart: 19 -> 13, of which waited for: 7 -> 8; matrix products, arithmetic and copies ran while one was open for 4% -> 4% of each run, Pallas kernels for 6% -> 2%
where the time goes in v4:
time: 241 us; the launch traced here: 239 us
  waiting for transfers between devices  83.8 us (35%)
  blocking collectives  54.3 us (23%)
  starting transfers between devices  41.6 us (17%)
  Pallas kernels  25.7 us (11%)
  local copies, waits for them, and re-layouts  18.2 us (8%)
  between operations  15 us (6%)
    all_to_all x1, blocking collectives, down_weight_rows(): lax.all_to_all(jnp.repeat(own, 2, axis=0), HEAD, 0, 0).transpose(1, 0, 2)  24.1 us
    all_to_all x1, waiting for transfers between devices, down_weight_rows(): lax.all_to_all(jnp.broadcast_to(wide[None], (8,) + wide.shape), ('x', 'yl...  17.7 us
    ppermute x5, waiting for transfers between devices, swap(): return lax.ppermute(values, axis, [(0, 1), (1, 0)])  16.4 us
    all_to_all x1, waiting for transfers between devices, shards(): lax.all_to_all(jnp.broadcast_to(turned[None], (NZ,) + turned.shape), 'z',...  15.9 us
    all_to_all x1, blocking collectives, shards(): lax.all_to_all(residual.reshape(own, NZ, DZ).transpose(1, 0, 2), 'z', 0, 0)  15.5 us
    all_to_all x1, blocking collectives, shards(): payload = lax.all_to_all(payload, 'z', 0, 0)  14.7 us
    all_to_all x1, waiting for transfers between devices, shards(): parts = lax.all_to_all(lifted.reshape(NZ, own, lifted.shape[1]), 'z', 0, 0)  13 us
    all_to_all x1, waiting for transfers between devices, shards(): queries = lax.all_to_all(queries, 'z', 0, 0).reshape(IHEADS * own, IDIM)  12.2 us
  transfers between devices with their start and end apart: 13, of which 8 were waited for; matrix products, arithmetic and copies ran while one was open for 4% of the time, Pallas kernels for 2%

profile of v4, /device:TPU:1, one launch (start us, length us, event | category | flops | bytes accessed | tf_op | source)
XLA Modules:
  0.0 239.5 jit_solution(854250408042584791)
XLA Ops:
  7.2 8.7 %shard_map.130 = bf16[8,2,128,896]{3,2,1,0:T(8,128)(2,1)} custom-call(bf16[256,512]{1,0:T(8,128)(2,1)} %a_ref.1, bf16[512,7168]{1,0:T(8,128)(2,1)} %b_ref.1), custom_call_target="tpu_custom_call" | custom-call | tf_op jit(solution)/shard_map/pallas_call | solution.py:55
  18.0 24.1 %all_to_all.40 = bf16[16,56,100]{2,1,0:T(8,128)(2,1)S(1)} all-to-all(bf16[16,56,100]{2,1,0:T(8,128)(2,1)S(1)} %bitcast.67), channel_id=1, replica_groups=mesh['x'=4,'yl'=2,'c'=2,'z'=8,'yh'=2] {'z','yh'}, dimensions={0} | all-to-all | bytes 358400 | tf_op jit(solution)/shard_map/all_to_all | solution.py:210
  44.1 4.8 %all-to-all-start.2 = ((bf16[8,56,1664]{2,1,0:T(8,128)(2,1)}), bf16[8,56,1664]{2,1,0:T(8,128)(2,1)S(1)}, u32[]{:S(2)}, u32[]{:S(2)}) async-start(bf16[8,56,1664]{2,1,0:T(8,128)(2,1)} %broadcast_in_dim.12), calls=%async_computation.3 | async-start | bytes 2981888 | tf_op jit(solution)/shard_map/all_to_all | solution.py:220
  49.9 17.7 %all-to-all-done.2 = bf16[8,56,1664]{2,1,0:T(8,128)(2,1)S(1)} async-done(((bf16[8,56,1664]{2,1,0:T(8,128)(2,1)}), bf16[8,56,1664]{2,1,0:T(8,128)(2,1)S(1)}, u32[]{:S(2)}, u32[]{:S(2)}) %all-to-all-start.2) | async-done | bytes 1490976 | tf_op jit(solution)/shard_map/all_to_all | solution.py:220
  67.6 3.3 %collective-permute-start = (bf16[448,1664]{1,0:T(8,128)(2,1)S(1)}, bf16[448,1664]{1,0:T(8,128)(2,1)S(1)}, u32[]{:S(2)}, u32[]{:S(2)}) collective-permute-start(bf16[448,1664]{1,0:T(8,128)(2,1)S(1)} %bitcast.55), channel_id=1, source_target_pairs={{0,16},{16,0},{1,17},{17,1},{2,18},{18,2},{3,19},{19,3},{4,20},{20... | collective-permute-start | bytes 4472840 | tf_op jit(solution)/shard_map/ppermute | solution.py:33
  70.9 10.8 %collective-permute-done.1.mine_ref = bf16[768,512]{1,0:T(8,128)(2,1)} collective-permute-done((bf16[768,512]{1,0:T(8,128)(2,1)}, bf16[768,512]{1,0:T(8,128)(2,1)}, u32[]{:S(2)}, u32[]{:S(2)}) %collective-permute-start.1) | collective-permute-done | bytes 786464 | tf_op jit(solution)/shard_map/ppermute | solution.py:33
  83.4 15.5 %all_to_all.41 = bf16[8,16,896]{2,1,0:T(8,128)(2,1)S(1)} all-to-all(bf16[8,16,896]{2,1,0:T(8,128)(2,1)S(1)} %bitcast.66), channel_id=1, replica_groups=mesh['x'=4,'yl'=2,'c'=2,'z'=8,'yh'=2] {'z'}, dimensions={0} | all-to-all | bytes 458752 | tf_op jit(solution)/shard_map/all_to_all | solution.py:255
  102.8 2.1 collective-permute-start.3
  105.7 5.6 %collective-permute-done.3.got_ref = bf16[128,896]{1,0:T(8,128)(2,1)} collective-permute-done((bf16[128,896]{1,0:T(8,128)(2,1)}, bf16[128,896]{1,0:T(8,128)(2,1)}, u32[]{:S(2)}, u32[]{:S(2)}) %collective-permute-start.3) | collective-permute-done | bytes 229408 | tf_op jit(solution)/shard_map/ppermute | solution.py:33
  112.7 1.8 shard_map.131
  115.9 3.6 %all-to-all-start.3 = ((bf16[8,16,1664]{2,1,0:T(8,128)(2,1)}), bf16[8,16,1664]{2,1,0:T(8,128)(2,1)S(1)}, u32[]{:S(2)}, u32[]{:S(2)}) async-start(bf16[8,16,1664]{2,1,0:T(8,128)(2,1)} %bitcast.60), calls=%async_computation.4 | async-start | bytes 851968 | tf_op jit(solution)/shard_map/all_to_all | solution.py:272
  119.6 13.0 %all-to-all-done.3 = bf16[8,16,1664]{2,1,0:T(8,128)(2,1)S(1)} async-done(((bf16[8,16,1664]{2,1,0:T(8,128)(2,1)}), bf16[8,16,1664]{2,1,0:T(8,128)(2,1)S(1)}, u32[]{:S(2)}, u32[]{:S(2)}) %all-to-all-start.3) | async-done | bytes 426016 | tf_op jit(solution)/shard_map/all_to_all | solution.py:272
  133.3 7.3 %collective-permute-start.4 = (bf16[16,1664]{1,0:T(8,128)(2,1)S(1)}, bf16[16,1664]{1,0:T(8,128)(2,1)S(1)}, u32[]{:S(2)}, u32[]{:S(2)}) collective-permute-start(bf16[16,1664]{1,0:T(8,128)(2,1)S(1)} %concatenate.14), channel_id=1, source_target_pairs={{0,0},{1,16},{2,32},{3,48},{4,64},{5,80},{6,96},{7,112},{8,128},{9... | collective-permute-start | bytes 159752 | tf_op jit(solution)/shard_map/ppermute | solution.py:227
  140.6 1.8 collective-permute-done.4
  143.2 9.2 %all-to-all-start.4 = ((bf16[8,16,1664]{2,1,0:T(8,128)(2,1)}), bf16[8,16,1664]{2,1,0:T(8,128)(2,1)S(1)}, u32[]{:S(2)}, u32[]{:S(2)}) async-start(bf16[8,16,1664]{2,1,0:T(8,128)(2,1)} %broadcast_in_dim.27), calls=%async_computation.5 | async-start | bytes 851968 | tf_op jit(solution)/shard_map/all_to_all | solution.py:281
  152.4 15.9 %all-to-all-done.4 = bf16[8,16,1664]{2,1,0:T(8,128)(2,1)S(1)} async-done(((bf16[8,16,1664]{2,1,0:T(8,128)(2,1)}), bf16[8,16,1664]{2,1,0:T(8,128)(2,1)S(1)}, u32[]{:S(2)}, u32[]{:S(2)}) %all-to-all-start.4) | async-done | bytes 426016 | tf_op jit(solution)/shard_map/all_to_all | solution.py:281
  168.3 2.4 %shard_map.132 = bf16[8,8,16,128]{3,2,1,0:T(8,128)(2,1)} custom-call(s32[2]{0:T(128)S(1)} %pad_add_fusion.place_ref, bf16[128,1664]{1,0:T(8,128)(2,1)S(1)} %bitcast.57, bf16[1536,512]{1,0:T(8,128)(2,1)S(1)} %copy-done.1, bf16[768,512]{1,0:T(8,128)(2,1)} %collective-permute-done.1.mine_ref, bf16[768,512]{1,0:T(8,128)(2,1)S(1)} %copy-done.5), custom_call_target="tpu_custom_call" | custom-call | tf_op jit(solution)/shard_map/pallas_call | solution.py:125
  170.7 3.4 %all-to-all-start.5 = ((bf16[8,8,16,128]{3,2,1,0:T(8,128)(2,1)}), bf16[8,8,16,128]{3,2,1,0:T(8,128)(2,1)S(1)}, u32[]{:S(2)}, u32[]{:S(2)}) async-start(bf16[8,8,16,128]{3,2,1,0:T(8,128)(2,1)} %shard_map.132), calls=%async_computation.6 | async-start | bytes 524288 | tf_op jit(solution)/shard_map/all_to_all | solution.py:286
  174.2 12.2 %all-to-all-done.5 = bf16[8,8,16,128]{3,2,1,0:T(8,128)(2,1)S(1)} async-done(((bf16[8,8,16,128]{3,2,1,0:T(8,128)(2,1)}), bf16[8,8,16,128]{3,2,1,0:T(8,128)(2,1)S(1)}, u32[]{:S(2)}, u32[]{:S(2)}) %all-to-all-start.5) | async-done | bytes 262176 | tf_op jit(solution)/shard_map/all_to_all | solution.py:286
  186.4 2.2 copy-done
  188.5 11.1 %shard_map.133 = bf16[16,16,1024]{2,1,0:T(8,128)(2,1)} custom-call(bf16[1024,128]{1,0:T(8,128)(2,1)S(1)} %bitcast.58, bf16[16,128]{1,0:T(8,128)(2,1)S(1)} %slice.42.w_ref, bf16[16384,128]{1,0:T(8,128)(2,1)S(1)} %copy-done), custom_call_target="tpu_custom_call" | custom-call | tf_op jit(solution)/shard_map/pallas_call | solution.py:167
  199.8 14.7 %all_to_all.42 = bf16[8,16,1088]{2,1,0:T(8,128)(2,1)S(1)} all-to-all(bf16[8,16,1088]{2,1,0:T(8,128)(2,1)S(1)} %pad_maximum_fusion), channel_id=1, replica_groups=mesh['x'=4,'yl'=2,'c'=2,'z'=8,'yh'=2] {'z'}, dimensions={0} | all-to-all | bytes 557056 | tf_op jit(solution)/shard_map/all_to_all | solution.py:294
  214.6 6.0 %all-to-all-start.7 = ((bf16[16,16,1024]{2,1,0:T(8,128)(2,1)}), bf16[16,16,1024]{2,1,0:T(8,128)(2,1)S(1)}, u32[]{:S(2)}, u32[]{:S(2)}) async-start(bf16[16,16,1024]{2,1,0:T(8,128)(2,1)} %shard_map.133), calls=%async_computation.8 | async-start | bytes 1048576 | tf_op jit(solution)/shard_map/all_to_all | solution.py:289
  223.3 6.9 %all-to-all-done.7.s_ref = bf16[16,16,1024]{2,1,0:T(8,128)(2,1)S(1)} async-done(((bf16[16,16,1024]{2,1,0:T(8,128)(2,1)}), bf16[16,16,1024]{2,1,0:T(8,128)(2,1)S(1)}, u32[]{:S(2)}, u32[]{:S(2)}) %all-to-all-start.7) | async-done | bytes 524320 | tf_op jit(solution)/shard_map/all_to_all | solution.py:289
  (86 shorter events, 20.6 us)
Async XLA Ops:
  7.2 93.8 %reduce-scatter.2.cloned.1.call-start = ((), (), s32[]{:S(2)}) async-start(), calls=%async_computation.9 | async-start | bytes 4128768 | tf_op jit(solution)/shard_map/reduce_scatter | solution.py:252
  15.9 0.8 copy-start.11
  15.9 1.4 copy-start.9
  44.1 4.8 %copy-start.1 = (bf16[1536,512]{1,0:T(8,128)(2,1)S(1)}, bf16[1536,512]{1,0:T(8,128)(2,1)}, u32[]{:S(2)}) copy-start(bf16[1536,512]{1,0:T(8,128)(2,1)} %own_ref.1) | copy-start | bytes 4718596
  44.1 23.5 %all-to-all-start.2 = ((bf16[8,56,1664]{2,1,0:T(8,128)(2,1)}), bf16[8,56,1664]{2,1,0:T(8,128)(2,1)S(1)}, u32[]{:S(2)}, u32[]{:S(2)}) async-start(bf16[8,56,1664]{2,1,0:T(8,128)(2,1)} %broadcast_in_dim.12), calls=%async_computation.3 | async-start | bytes 2981888 | tf_op jit(solution)/shard_map/all_to_all | solution.py:220
  48.9 34.5 %copy-start.10 = (bf16[16,7168]{1,0:T(8,128)(2,1)S(1)}, bf16[16,7168]{1,0:T(8,128)(2,1)}, u32[]{:S(2)}) copy-start(bf16[16,7168]{1,0:T(8,128)(2,1)} %param.13) | copy-start | bytes 688132
  48.9 137.5 %all-gather.2.cloned.1.call-start = ((), (), s32[]{:S(2)}) async-start(), calls=%async_computation.10 | async-start | bytes 4456448 | tf_op jit(solution)/shard_map/all_gather | solution.py:264
  49.9 31.8 %collective-permute-start.1 = (bf16[768,512]{1,0:T(8,128)(2,1)}, bf16[768,512]{1,0:T(8,128)(2,1)}, u32[]{:S(2)}, u32[]{:S(2)}) collective-permute-start(bf16[768,512]{1,0:T(8,128)(2,1)} %constant_dynamic-slice_fusion.2), channel_id=1, source_target_pairs={{0,1},{1,0},{2,3},{3,2},{4,5},{5,4},{6,7},{7,6},{8,9},{9,8},{10,11... | collective-permute-start | bytes 2359304 | tf_op jit(solution)/shard_map/ppermute | solution.py:33
  67.6 32.2 %collective-permute-start = (bf16[448,1664]{1,0:T(8,128)(2,1)S(1)}, bf16[448,1664]{1,0:T(8,128)(2,1)S(1)}, u32[]{:S(2)}, u32[]{:S(2)}) collective-permute-start(bf16[448,1664]{1,0:T(8,128)(2,1)S(1)} %bitcast.55), channel_id=1, source_target_pairs={{0,16},{16,0},{1,17},{17,1},{2,18},{18,2},{3,19},{19,3},{4,20},{20... | collective-permute-start | bytes 4472840 | tf_op jit(solution)/shard_map/ppermute | solution.py:33
  81.7 17.3 %collective-permute-start.2 = (bf16[768,512]{1,0:T(8,128)(2,1)}, bf16[768,512]{1,0:T(8,128)(2,1)S(1)}, u32[]{:S(2)}, u32[]{:S(2)}) collective-permute-start(bf16[768,512]{1,0:T(8,128)(2,1)} %collective-permute-done.1.mine_ref), channel_id=1, source_target_pairs={{0,16},{16,0},{1,17},{17,1},{2,18},{18,2},{3,19},{19,3},{4,20},{20... | collective-permute-start | bytes 2359304 | tf_op jit(solution)/shard_map/ppermute | solution.py:33
  98.9 0.9 copy-start.4
  99.8 1.2 copy-start.2
  102.8 8.5 %collective-permute-start.3 = (bf16[128,896]{1,0:T(8,128)(2,1)}, bf16[128,896]{1,0:T(8,128)(2,1)}, u32[]{:S(2)}, u32[]{:S(2)}) collective-permute-start(bf16[128,896]{1,0:T(8,128)(2,1)} %get-tuple-element.36), channel_id=1, source_target_pairs={{0,1},{1,0},{2,3},{3,2},{4,5},{5,4},{6,7},{7,6},{8,9},{9,8},{10,11... | collective-permute-start | bytes 688136 | tf_op jit(solution)/shard_map/ppermute | solution.py:33
  111.3 1.4 copy-start.3
  112.7 6.9 %copy-start.12 = (bf16[1536]{0:T(1024)(128)(2,1)S(1)}, bf16[1536]{0:T(1024)(128)(2,1)}, u32[]{:S(2)}) copy-start(bf16[1536]{0:T(1024)(128)(2,1)} %param.17) | copy-start | bytes 9220
  115.9 52.4 %copy-start.5 = (bf16[768,512]{1,0:T(8,128)(2,1)S(1)}, bf16[768,512]{1,0:T(8,128)(2,1)}, u32[]{:S(2)}) copy-start(bf16[768,512]{1,0:T(8,128)(2,1)} %copy-done.4) | copy-start | bytes 2359300
  115.9 16.6 %all-to-all-start.3 = ((bf16[8,16,1664]{2,1,0:T(8,128)(2,1)}), bf16[8,16,1664]{2,1,0:T(8,128)(2,1)S(1)}, u32[]{:S(2)}, u32[]{:S(2)}) async-start(bf16[8,16,1664]{2,1,0:T(8,128)(2,1)} %bitcast.60), calls=%async_computation.4 | async-start | bytes 851968 | tf_op jit(solution)/shard_map/all_to_all | solution.py:272
  133.3 9.1 %collective-permute-start.4 = (bf16[16,1664]{1,0:T(8,128)(2,1)S(1)}, bf16[16,1664]{1,0:T(8,128)(2,1)S(1)}, u32[]{:S(2)}, u32[]{:S(2)}) collective-permute-start(bf16[16,1664]{1,0:T(8,128)(2,1)S(1)} %concatenate.14), channel_id=1, source_target_pairs={{0,0},{1,16},{2,32},{3,48},{4,64},{5,80},{6,96},{7,112},{8,128},{9... | collective-permute-start | bytes 159752 | tf_op jit(solution)/shard_map/ppermute | solution.py:227
  143.2 25.1 %all-to-all-start.4 = ((bf16[8,16,1664]{2,1,0:T(8,128)(2,1)}), bf16[8,16,1664]{2,1,0:T(8,128)(2,1)S(1)}, u32[]{:S(2)}, u32[]{:S(2)}) async-start(bf16[8,16,1664]{2,1,0:T(8,128)(2,1)} %broadcast_in_dim.27), calls=%async_computation.5 | async-start | bytes 851968 | tf_op jit(solution)/shard_map/all_to_all | solution.py:281
  170.7 15.6 %all-to-all-start.5 = ((bf16[8,8,16,128]{3,2,1,0:T(8,128)(2,1)}), bf16[8,8,16,128]{3,2,1,0:T(8,128)(2,1)S(1)}, u32[]{:S(2)}, u32[]{:S(2)}) async-start(bf16[8,8,16,128]{3,2,1,0:T(8,128)(2,1)} %shard_map.132), calls=%async_computation.6 | async-start | bytes 524288 | tf_op jit(solution)/shard_map/all_to_all | solution.py:286
  186.3 2.2 copy-start
  188.5 11.2 %copy-start.8 = (bf16[128,896]{1,0:T(8,128)(2,1)S(1)}, bf16[128,896]{1,0:T(8,128)(2,1)}, u32[]{:S(2)}) copy-start(bf16[128,896]{1,0:T(8,128)(2,1)} %copy-done.7) | copy-start | bytes 688132
  214.6 15.6 %all-to-all-start.7 = ((bf16[16,16,1024]{2,1,0:T(8,128)(2,1)}), bf16[16,16,1024]{2,1,0:T(8,128)(2,1)S(1)}, u32[]{:S(2)}, u32[]{:S(2)}) async-start(bf16[16,16,1024]{2,1,0:T(8,128)(2,1)} %shard_map.133), calls=%async_computation.8 | async-start | bytes 1048576 | tf_op jit(solution)/shard_map/all_to_all | solution.py:289
  222.4 9.4 %collective-permute-start.5 = (bf16[8,16,96]{2,1,0:T(8,128)(2,1)S(1)}, bf16[8,16,96]{2,1,0:T(8,128)(2,1)S(1)}, u32[]{:S(2)}, u32[]{:S(2)}) collective-permute-start(bf16[8,16,96]{2,1,0:T(8,128)(2,1)S(1)} %bitcast.76), channel_id=1, source_target_pairs={{0,1},{1,0},{2,3},{3,2},{4,5},{5,4},{6,7},{7,6},{8,9},{9,8},{10,11... | collective-permute-start | bytes 73736 | tf_op jit(solution)/shard_map/ppermute | solution.py:33
  (2 other events, 1.5 us)
Sparse Core Ops, SparseCore 0:
  16.0 57.9 reduce-scatter.1
  101.1 37.3 all-gather.1

commit v5 on v4

--- a/solution.py
+++ b/solution.py
@@ -41,37 +41,67 @@
     return pltpu.CompilerParams(vmem_limit_bytes=48 * 1024 * 1024)
 
 
-def project_kernel(a_ref, b_ref, o_ref):
-    product = jnp.dot(a_ref[...], b_ref[...], preferred_element_type=jnp.float32).astype(o_ref.dtype)
-    for group in range(NZ):
-        for half in range(2):
-            o_ref[0, half, group * 16 : (group + 1) * 16, :] = product[
-                group * 32 + half * 16 : group * 32 + (half + 1) * 16, :
-            ]
-
-
-def project(attn_out, out_weight):
+def big_params():
+    return pltpu.CompilerParams(vmem_limit_bytes=60 * 1024 * 1024)
+
+
+def project_kernel(head_ref, a_ref, b_ref, res_ref, o_ref, b_held, o_held, in_sems, out_sems):
+    rows = a_ref.shape[0]
+
+    def fetch(i):
+        columns = pl.ds(pl.multiple_of(i * DZ, 128), DZ)
+        return pltpu.make_async_copy(b_ref.at[:, columns], b_held.at[i], in_sems.at[i])
+
+    def store(i):
+        return pltpu.make_async_copy(o_held.at[i], o_ref.at[i], out_sems.at[i])
+
+    for i in range(NZ):
+        fetch(i).start()
+    own = lax.broadcasted_iota(jnp.int32, (rows, 16), 1) + head_ref[0] * 16
+    place = lax.broadcasted_iota(jnp.int32, (rows, 16), 0) == own
+    place = jnp.where(place, 1.0, 0.0).astype(jnp.bfloat16)
+
+    @pl.loop(0, NZ)
+    def _(i):
+        columns = pl.ds(pl.multiple_of(i * DZ, 128), DZ)
+        fetch(i).wait()
+        product = jnp.dot(a_ref[...], b_held[i], preferred_element_type=jnp.float32)
+        product = product + jnp.dot(place, res_ref[:, columns], preferred_element_type=jnp.float32)
+        product = product.astype(o_ref.dtype)
+        for group in range(NZ):
+            for half in range(2):
+                o_held[i, half, group * 16 : (group + 1) * 16, :] = product[
+                    group * 32 + half * 16 : group * 32 + (half + 1) * 16, :
+                ]
+        store(i).start()
+
+    for i in range(NZ):
+        store(i).wait()
+
+
+def project(head, attn_out, out_weight, residual):
     rows, depth = attn_out.shape
+    whole = pl.BlockSpec(memory_space=pltpu.VMEM)
+    apart = pl.BlockSpec(memory_space=pl.ANY)
+    shape = (NZ, 2, HALF, DZ)
     return pl.pallas_call(
         project_kernel,
-        grid=(NZ,),
-        in_specs=[
-            pl.BlockSpec((rows, depth), lambda i: (0, 0)),
-            pl.BlockSpec((depth, DZ), lambda i: (0, i)),
+        in_specs=[pl.BlockSpec(memory_space=pltpu.SMEM), whole, apart, whole],
+        out_specs=apart,
+        out_shape=jax.ShapeDtypeStruct(shape, jnp.bfloat16),
+        scratch_shapes=[
+            pltpu.VMEM((NZ, depth, DZ), jnp.bfloat16),
+            pltpu.VMEM(shape, jnp.bfloat16),
+            pltpu.SemaphoreType.DMA((NZ,)),
+            pltpu.SemaphoreType.DMA((NZ,)),
         ],
-        out_specs=pl.BlockSpec((1, 2, HALF, DZ), lambda i: (i, 0, 0, 0)),
-        out_shape=jax.ShapeDtypeStruct((NZ, 2, HALF, DZ), jnp.bfloat16),
-        compiler_params=pltpu.CompilerParams(vmem_limit_bytes=60 * 1024 * 1024),
-    )(attn_out, out_weight)
-
-
-def lift_kernel(core_ref, kept_ref, got_ref, res_ref, gain_ref, mine_ref, other_ref, hidden_ref, o_ref):
-    hidden = (
-        kept_ref[...].astype(jnp.float32)
-        + got_ref[...].astype(jnp.float32)
-        + res_ref[...].astype(jnp.float32)
-    ).astype(jnp.bfloat16)
-    hidden_ref[...] = hidden
+        compiler_params=big_params(),
+    )(head, attn_out, out_weight, residual)
+
+
+def lift_kernel(core_ref, kept_ref, got_ref, gain_ref, mine_ref, other_ref, o_ref):
+    hidden = (kept_ref[...].astype(jnp.float32) + got_ref[...].astype(jnp.float32)).astype(jnp.bfloat16)
+    o_ref[:, QL + 128 :] = hidden
     wide = hidden.astype(jnp.float32)
     squares = jnp.sum(wide * wide, axis=1, keepdims=True)
     high = squares.astype(jnp.bfloat16).astype(jnp.float32)
@@ -86,24 +116,21 @@
     lane = lax.broadcasted_iota(jnp.int32, (HALF, 128), 1)
     tail = jnp.where(lane == IHEADS, high, jnp.where(lane == IHEADS + 1, squares - high, 0.0))
     o_ref[:, :QL] = lifted[:, :QL].astype(jnp.bfloat16)
-    o_ref[:, QL:] = jnp.where(lane < IHEADS, lifted[:, QL:], tail).astype(jnp.bfloat16)
-
-
-def lift(core, kept, got, residual, gain, mine, other):
+    o_ref[:, QL : QL + 128] = jnp.where(lane < IHEADS, lifted[:, QL:], tail).astype(jnp.bfloat16)
+
+
+def lift(core, kept, got, gain, mine, other):
     whole = pl.BlockSpec(memory_space=pltpu.VMEM)
     return pl.pallas_call(
         lift_kernel,
-        in_specs=[pl.BlockSpec(memory_space=pltpu.SMEM)] + [whole] * 6,
-        out_specs=[whole, whole],
-        out_shape=[
-            jax.ShapeDtypeStruct((HALF, DZ), jnp.bfloat16),
-            jax.ShapeDtypeStruct((HALF, QL + 128), jnp.bfloat16),
-        ],
+        in_specs=[pl.BlockSpec(memory_space=pltpu.SMEM)] + [whole] * 5,
+        out_specs=whole,
+        out_shape=jax.ShapeDtypeStruct((HALF, QL + 128 + DZ), jnp.bfloat16),
         compiler_params=kernel_params(),
-    )(core, kept, got, residual, gain, mine, other)
-
-
-def query_kernel(place_ref, latent_ref, own_ref, mine_ref, theirs_ref, o_ref):
+    )(core, kept, got, gain, mine, other)
+
+
+def query_kernel(place_ref, latent_ref, own_ref, mine_ref, theirs_ref, final_ref, o_ref):
     core, high = place_ref[0], place_ref[1]
     is_first = core == 0
     left, right = latent_ref[:, : QL // 2], latent_ref[:, QL // 2 : QL]
@@ -118,20 +145,25 @@
         for j in range(4):
             for block in range(NZ):
                 o_ref[block, at + j] = part[block * 16 : (block + 1) * 16, j * IDIM : (j + 1) * IDIM]
-
-
-def make_queries(place, latent, own, mine, theirs):
+    o_ref[:, 8:] = jnp.zeros((NZ, 2, 16, IDIM), jnp.bfloat16)
+    for block in range(NZ):
+        for half in range(2):
+            at = (block * 2 + half) * 96
+            o_ref[block, 8 + half, :, :96] = final_ref[:, at : at + 96]
+
+
+def make_queries(place, latent, own, mine, theirs, final):
     whole = pl.BlockSpec(memory_space=pltpu.VMEM)
     return pl.pallas_call(
         query_kernel,
-        in_specs=[pl.BlockSpec(memory_space=pltpu.SMEM)] + [whole] * 4,
+        in_specs=[pl.BlockSpec(memory_space=pltpu.SMEM)] + [whole] * 5,
         out_specs=whole,
-        out_shape=jax.ShapeDtypeStruct((NZ, 8, 16, IDIM), jnp.bfloat16),
+        out_shape=jax.ShapeDtypeStruct((NZ, 10, 16, IDIM), jnp.bfloat16),
         compiler_params=kernel_params(),
-    )(place, latent, own, mine, theirs)
-
-
-def score_kernel(q_ref, w_ref, k_ref, o_ref, wide_ref):
+    )(place, latent, own, mine, theirs, final)
+
+
+def score_kernel(q_ref, w_ref, k_ref, o_ref, wide_ref, rows_ref):
     scale = IDIM ** (-0.5)
     tile = 256
 
@@ -140,13 +172,14 @@
         weights = w_ref[...].astype(jnp.float32) * scale
         for j in range(IHEADS):
             wide_ref[j * 16 : (j + 1) * 16, :] = jnp.broadcast_to(weights[:, j : j + 1], (16, 128))
+            rows_ref[j * 16 : (j + 1) * 16, :] = q_ref[j // 8, j % 8]
 
     blocks, _, slots = o_ref.shape
     for block in range(blocks):
         for slot in range(0, slots, tile):
             at = block * slots + slot
             logits = lax.dot_general(
-                q_ref[...],
+                rows_ref[...],
                 k_ref[at : at + tile, :],
                 (((1,), (1,)), ((), ())),
                 preferred_element_type=jnp.float32,
@@ -168,14 +201,17 @@
         score_kernel,
         grid=(N_SEQ // per_step,),
         in_specs=[
-            pl.BlockSpec((IHEADS * 16, IDIM), lambda i: (0, 0)),
+            pl.BlockSpec(queries.shape, lambda i: (0, 0, 0, 0)),
             pl.BlockSpec((16, 128), lambda i: (0, 0)),
             pl.BlockSpec((per_step * SLOTS, IDIM), lambda i: (i, 0)),
         ],
         out_specs=pl.BlockSpec((per_step, 16, SLOTS), lambda i: (i, 0, 0)),
         out_shape=jax.ShapeDtypeStruct((N_SEQ, 16, SLOTS), jnp.bfloat16),
-        scratch_shapes=[pltpu.VMEM((IHEADS * 16, 128), jnp.float32)],
-        compiler_params=kernel_params(),
+        scratch_shapes=[
+            pltpu.VMEM((IHEADS * 16, 128), jnp.float32),
+            pltpu.VMEM((IHEADS * 16, IDIM), jnp.bfloat16),
+        ],
+        compiler_params=big_params(),
     )(queries, head_weights, keys)
 
 
@@ -199,8 +235,7 @@
     )(numbers, scores, own_positions)
 
 
-def down_weight_rows(latent_weight, index_proj, x, yl, c):
-    piece = c * 8 + x * 2 + yl
+def down_weight_rows(latent_weight, index_proj, piece, early):
     share = DZ // N_SEQ
 
     def own_rows(weight):
@@ -217,9 +252,10 @@
         ],
         axis=1,
     )
+    wide, early = lax.optimization_barrier((wide, early))
     half = lax.all_to_all(jnp.broadcast_to(wide[None], (8,) + wide.shape), ("x", "yl"), 0, 0)
     half = half.reshape(8 * share, wide.shape[1])
-    return half, swap(half, "c")
+    return half, swap(half, "c"), early
 
 
 def turn(values):
@@ -248,29 +284,26 @@
     own = rows // N_HEAD
     local = latent_weight.shape[1]
 
-    partial = project(attn_out, out_weight)
+    partial = project(jnp.stack([head]).astype(jnp.int32), attn_out, out_weight, residual)
     summed = lax.psum_scatter(partial, "z", scatter_dimension=0, tiled=False)
 
-    down_mine, down_other = down_weight_rows(latent_weight, index_proj, x, yl, c)
-    residual_cols = lax.all_to_all(residual.reshape(own, NZ, DZ).transpose(1, 0, 2), "z", 0, 0)
     depth = QL // 2
     weight_mine = swap(lax.dynamic_slice_in_dim(index_weight, c * depth, depth, 0), "yh")
+    down_mine, down_other, weight_mine = down_weight_rows(
+        latent_weight, index_proj, c * 8 + x * 2 + yl, weight_mine
+    )
     weight_theirs = swap(weight_mine, "c")
-    (summed, residual_cols, down_mine, down_other, weight_mine, weight_theirs, index_keys) = (
-        lax.optimization_barrier(
-            (summed, residual_cols, down_mine, down_other, weight_mine, weight_theirs, index_keys)
-        )
+    summed, down_mine, down_other, weight_mine, weight_theirs, index_keys = lax.optimization_barrier(
+        (summed, down_mine, down_other, weight_mine, weight_theirs, index_keys)
     )
     all_keys = lax.all_gather(index_keys, SEQ, axis=0, tiled=True)
     kept = lax.dynamic_index_in_dim(summed, yh, 0, keepdims=False)
     got = swap(lax.dynamic_index_in_dim(summed, 1 - yh, 0, keepdims=False), "yh")
     gain = lax.dynamic_slice_in_dim(norm_gain, z * DZ, DZ).reshape(1, DZ)
-    core = jnp.stack([c]).astype(jnp.int32)
-    hidden, lifted = lift(
-        core, kept, got, residual_cols.reshape(HALF, DZ), gain, down_mine, down_other
-    )
+    lifted = lift(jnp.stack([c]).astype(jnp.int32), kept, got, gain, down_mine, down_other)
     parts = lax.all_to_all(lifted.reshape(NZ, own, lifted.shape[1]), "z", 0, 0)
-    total = jnp.sum(parts.astype(jnp.float32), axis=0)
+    hidden_rows = parts[:, :, QL + 128 :].transpose(1, 0, 2).reshape(own, D)
+    total = jnp.sum(parts[:, :, : QL + 128].astype(jnp.float32), axis=0)
     mean = (total[:, 1600:1601] + total[:, 1601:1602]) / D
     inverse = lax.rsqrt(mean + EPSILON)
     latent_raw = (total[:, :QL] * inverse).astype(jnp.bfloat16)
@@ -281,21 +314,15 @@
     everyone = lax.all_to_all(jnp.broadcast_to(turned[None], (NZ,) + turned.shape), "z", 0, 0)
     place = jnp.stack([c, yh]).astype(jnp.int32)
     queries = make_queries(
-        place, everyone.reshape(HALF, packed.shape[1]), index_weight, weight_mine, weight_theirs
-    )
-    queries = lax.all_to_all(queries, "z", 0, 0).reshape(IHEADS * own, IDIM)
+        place, everyone.reshape(HALF, packed.shape[1]), index_weight, weight_mine, weight_theirs, latent
+    )
+    queries = lax.all_to_all(queries, "z", 0, 0)
     scores = make_scores(queries, turned[:, QL:], all_keys)
-    latent, hidden, scores = lax.optimization_barrier((latent, hidden, scores))
     scores = lax.all_to_all(scores, SEQ, 0, 0)
 
-    payload = jnp.concatenate(
-        [hidden.reshape(NZ, own, DZ), latent.reshape(own, NZ, 2 * local).transpose(1, 0, 2)], axis=2
-    )
-    payload = lax.all_to_all(payload, "z", 0, 0)
-    hidden_rows = payload[:, :, :DZ].transpose(1, 0, 2).reshape(own, D)
-    latent_cols = payload[:, :, DZ:].reshape(NZ, own, 2, local)
-    latent_mine = lax.dynamic_index_in_dim(latent_cols, yh, 2, keepdims=False)
-    latent_got = swap(lax.dynamic_index_in_dim(latent_cols, 1 - yh, 2, keepdims=False), "yh")
+    latent_mine = lax.dynamic_index_in_dim(queries, 8 + yh, 1, keepdims=False)[:, :, :local]
+    latent_give = lax.dynamic_index_in_dim(queries, 9 - yh, 1, keepdims=False)[:, :, :local]
+    latent_got = swap(latent_give, "yh")
     latent_out = jnp.stack(
         [jnp.where(yh == 0, latent_mine, latent_got), jnp.where(yh == 0, latent_got, latent_mine)], axis=1
     ).reshape(rows, local)

time: 241 us -> 209 us (0.87)
  waiting for transfers between devices: 83.8 us -> 59.9 us
  blocking collectives: 54.3 us -> 44.1 us
  starting transfers between devices: 41.6 us -> 44.1 us
    all_to_all x2 -> x1, waiting for transfers between devices: 29.9 us -> 7.79 us  [shards(): queries = lax.all_to_all(queries, 'z', 0, 0)]
    all_to_all x2 -> x1, blocking collectives: 30.2 us -> 21.3 us  [down_weight_rows(): lax.all_to_all(jnp.broadcast_to(wide[None], (8,) + wide.shape), ('x', 'yl...]
    all_to_all x1, starting transfers between devices: 5.95 us -> 13.1 us  [shards(): scores = lax.all_to_all(scores, SEQ, 0, 0)]
    all_to_all x1, waiting for transfers between devices: 13 us -> 17.9 us  [shards(): parts = lax.all_to_all(lifted.reshape(NZ, own, lifted.shape[1]), 'z', 0, 0)]
    ppermute x5, waiting for transfers between devices: 16.4 us -> 11.5 us  [swap(): return lax.ppermute(values, axis, [(0, 1), (1, 0)])]
    all_to_all x2 -> x1, starting transfers between devices: 8.18 us -> 3.43 us  [shards(): queries = lax.all_to_all(queries, 'z', 0, 0)]
    all_to_all x1, waiting for transfers between devices: 15.9 us -> 12.6 us  [shards(): lax.all_to_all(jnp.broadcast_to(turned[None], (NZ,) + turned.shape), 'z',...]
    unnamed x31 -> x28, local copies, waits for them, and re-layouts: 9.38 us -> 11.6 us
  transfers between devices with their start and end apart: 13 -> 12, of which waited for: 8 -> 7; matrix products, arithmetic and copies ran while one was open for 4% -> 6% of each run, Pallas kernels for 2% -> 7%
where the time goes in v5:
time: 209 us; the launch traced here: 208 us
  waiting for transfers between devices  59.9 us (29%)
  starting transfers between devices  44.1 us (21%)
  blocking collectives  44.1 us (21%)
  Pallas kernels  24.1 us (12%)
  local copies, waits for them, and re-layouts  20.5 us (10%)
  between operations  15 us (7%)
    all_to_all x1, blocking collectives, down_weight_rows(): lax.all_to_all(jnp.repeat(own, 2, axis=0), HEAD, 0, 0).transpose(1, 0, 2)  22.8 us
    all_to_all x1, blocking collectives, down_weight_rows(): lax.all_to_all(jnp.broadcast_to(wide[None], (8,) + wide.shape), ('x', 'yl...  21.3 us
    all_to_all x1, waiting for transfers between devices, shards(): parts = lax.all_to_all(lifted.reshape(NZ, own, lifted.shape[1]), 'z', 0, 0)  17.9 us
    all_to_all x1, starting transfers between devices, shards(): scores = lax.all_to_all(scores, SEQ, 0, 0)  13.1 us
    all_to_all x1, waiting for transfers between devices, shards(): lax.all_to_all(jnp.broadcast_to(turned[None], (NZ,) + turned.shape), 'z',...  12.6 us
    pallas_call x1, Pallas kernels, make_scores(): pl.pallas_call(score_kernel, grid=(N_SEQ // per_step,), in_specs=[pl.Bloc...  12.3 us
    unnamed x28, local copies, waits for them, and re-layouts  11.6 us
    ppermute x5, waiting for transfers between devices, swap(): return lax.ppermute(values, axis, [(0, 1), (1, 0)])  11.5 us
  transfers between devices with their start and end apart: 12, of which 7 were waited for; matrix products, arithmetic and copies ran while one was open for 6% of the time, Pallas kernels for 7%

profile of v5, /device:TPU:1, one launch (start us, length us, event | category | flops | bytes accessed | tf_op | source)
XLA Modules:
  0.0 208.4 jit_solution(11849866853855442835)
XLA Ops:
  7.2 7.4 %shard_map.130 = bf16[8,2,128,896]{3,2,1,0:T(8,128)(2,1)} custom-call(s32[1]{0:T(128)} %bitcast.1.head_ref, bf16[256,512]{1,0:T(8,128)(2,1)} %a_ref.1, bf16[512,7168]{1,0:T(8,128)(2,1)} %b_ref.1, bf16[16,7168]{1,0:T(8,128)(2,1)} %res_ref.1), custom_call_target="tpu_custom_call" | custom-call | tf_op jit(solution)/shard_map/pallas_call | solution.py:87
  14.7 1.3 copy-done
  16.9 3.8 %collective-permute-start = (bf16[768,512]{1,0:T(8,128)(2,1)}, bf16[768,512]{1,0:T(8,128)(2,1)S(1)}, u32[]{:S(2)}, u32[]{:S(2)}) collective-permute-start(bf16[768,512]{1,0:T(8,128)(2,1)} %constant_dynamic-slice_fusion), channel_id=1, source_target_pairs={{0,1},{1,0},{2,3},{3,2},{4,5},{5,4},{6,7},{7,6},{8,9},{9,8},{10,11... | collective-permute-start | bytes 2359304 | tf_op jit(solution)/shard_map/ppermute | solution.py:33
  20.7 2.6 %copy.39 = bf16[12,8,8,896]{3,2,1,0:T(8,128)(2,1)} copy(bf16[12,8,8,896]{3,1,2,0:T(8,128)(2,1)} %bitcast.48) | data formatting | bytes 2752512
  24.9 22.8 %all_to_all.30 = bf16[16,56,100]{2,1,0:T(8,128)(2,1)S(1)} all-to-all(bf16[16,56,100]{2,1,0:T(8,128)(2,1)S(1)} %bitcast.49), channel_id=1, replica_groups=mesh['x'=4,'yl'=2,'c'=2,'z'=8,'yh'=2] {'z','yh'}, dimensions={0} | all-to-all | bytes 358400 | tf_op jit(solution)/shard_map/all_to_all | solution.py:245
  49.5 21.3 %all_to_all.31 = bf16[8,56,1664]{2,1,0:T(8,128)(2,1)S(1)} all-to-all(bf16[8,56,1664]{2,1,0:T(8,128)(2,1)S(1)} %broadcast_in_dim.12), channel_id=1, replica_groups=mesh['x'=4,'yl'=2,'c'=2,'z'=8,'yh'=2] {'x','yl'}, dimensions={0} | all-to-all | bytes 2981888 | tf_op jit(solution)/shard_map/all_to_all | solution.py:256
  70.8 4.5 %collective-permute-start.1 = (bf16[448,1664]{1,0:T(8,128)(2,1)S(1)}, bf16[448,1664]{1,0:T(8,128)(2,1)S(1)}, u32[]{:S(2)}, u32[]{:S(2)}) collective-permute-start(bf16[448,1664]{1,0:T(8,128)(2,1)S(1)} %bitcast.41), channel_id=1, source_target_pairs={{0,16},{16,0},{1,17},{17,1},{2,18},{18,2},{3,19},{19,3},{4,20},{20... | collective-permute-start | bytes 4472840 | tf_op jit(solution)/shard_map/ppermute | solution.py:33
  75.3 4.0 %collective-permute-done.2.theirs_ref = bf16[768,512]{1,0:T(8,128)(2,1)S(1)} collective-permute-done((bf16[768,512]{1,0:T(8,128)(2,1)S(1)}, bf16[768,512]{1,0:T(8,128)(2,1)S(1)}, u32[]{:S(2)}, u32[]{:S(2)}) %collective-permute-start.2) | collective-permute-done | bytes 786464 | tf_op jit(solution)/shard_map/ppermute | solution.py:33
  81.4 1.8 dynamic-slice_bitcast_fusion
  85.0 7.5 %collective-permute-done.3.got_ref = bf16[128,896]{1,0:T(8,128)(2,1)S(1)} collective-permute-done((bf16[128,896]{1,0:T(8,128)(2,1)}, bf16[128,896]{1,0:T(8,128)(2,1)S(1)}, u32[]{:S(2)}, u32[]{:S(2)}) %collective-permute-start.3) | collective-permute-done | bytes 229408 | tf_op jit(solution)/shard_map/ppermute | solution.py:33
  92.5 1.4 copy-done.3
  95.5 3.7 %all-to-all-start.2 = ((bf16[8,16,2560]{2,1,0:T(8,128)(2,1)}), bf16[8,16,2560]{2,1,0:T(8,128)(2,1)S(1)}, u32[]{:S(2)}, u32[]{:S(2)}) async-start(bf16[8,16,2560]{2,1,0:T(8,128)(2,1)} %bitcast.43), calls=%async_computation.3 | async-start | bytes 1310720 | tf_op jit(solution)/shard_map/all_to_all | solution.py:304
  99.2 17.9 %all-to-all-done.2 = bf16[8,16,2560]{2,1,0:T(8,128)(2,1)S(1)} async-done(((bf16[8,16,2560]{2,1,0:T(8,128)(2,1)}), bf16[8,16,2560]{2,1,0:T(8,128)(2,1)S(1)}, u32[]{:S(2)}, u32[]{:S(2)}) %all-to-all-start.2) | async-done | bytes 655392 | tf_op jit(solution)/shard_map/all_to_all | solution.py:304
  117.9 6.9 %collective-permute-start.4 = (bf16[16,1664]{1,0:T(8,128)(2,1)S(1)}, bf16[16,1664]{1,0:T(8,128)(2,1)S(1)}, u32[]{:S(2)}, u32[]{:S(2)}) collective-permute-start(bf16[16,1664]{1,0:T(8,128)(2,1)S(1)} %concatenate.11), channel_id=1, source_target_pairs={{0,0},{1,16},{2,32},{3,48},{4,64},{5,80},{6,96},{7,112},{8,128},{9... | collective-permute-start | bytes 159752 | tf_op jit(solution)/shard_map/ppermute | solution.py:263
  124.8 1.8 collective-permute-done.4
  127.4 7.5 %all-to-all-start.3 = ((bf16[8,16,1664]{2,1,0:T(8,128)(2,1)}), bf16[8,16,1664]{2,1,0:T(8,128)(2,1)S(1)}, u32[]{:S(2)}, u32[]{:S(2)}) async-start(bf16[8,16,1664]{2,1,0:T(8,128)(2,1)} %broadcast_in_dim.27), calls=%async_computation.4 | async-start | bytes 851968 | tf_op jit(solution)/shard_map/all_to_all | solution.py:314
  135.0 12.6 %all-to-all-done.3 = bf16[8,16,1664]{2,1,0:T(8,128)(2,1)S(1)} async-done(((bf16[8,16,1664]{2,1,0:T(8,128)(2,1)}), bf16[8,16,1664]{2,1,0:T(8,128)(2,1)S(1)}, u32[]{:S(2)}, u32[]{:S(2)}) %all-to-all-start.3) | async-done | bytes 426016 | tf_op jit(solution)/shard_map/all_to_all | solution.py:314
  148.8 1.9 shard_map.132
  150.7 3.4 %all-to-all-start.4 = ((bf16[8,10,16,128]{3,2,1,0:T(8,128)(2,1)}), bf16[8,10,16,128]{3,2,1,0:T(8,128)(2,1)S(1)}, u32[]{:S(2)}, u32[]{:S(2)}) async-start(bf16[8,10,16,128]{3,2,1,0:T(8,128)(2,1)} %shard_map.132), calls=%async_computation.5 | async-start | bytes 655360 | tf_op jit(solution)/shard_map/all_to_all | solution.py:319
  156.3 7.8 %all-to-all-done.4.q_ref = bf16[8,10,16,128]{3,2,1,0:T(8,128)(2,1)S(1)} async-done(((bf16[8,10,16,128]{3,2,1,0:T(8,128)(2,1)}), bf16[8,10,16,128]{3,2,1,0:T(8,128)(2,1)S(1)}, u32[]{:S(2)}, u32[]{:S(2)}) %all-to-all-start.4) | async-done | bytes 327712 | tf_op jit(solution)/shard_map/all_to_all | solution.py:319
  164.9 12.3 %shard_map.133 = bf16[16,16,1024]{2,1,0:T(8,128)(2,1)} custom-call(bf16[8,10,16,128]{3,2,1,0:T(8,128)(2,1)} %copy-done.9, bf16[16,128]{1,0:T(8,128)(2,1)} %slice.54.w_ref, bf16[16384,128]{1,0:T(8,128)(2,1)} %all-gather.2.cloned.1.call-done.k_ref), custom_call_target="tpu_custom_call" | custom-call | tf_op jit(solution)/shard_map/pallas_call | solution.py:200
  177.1 13.1 %all-to-all-start.5 = ((bf16[16,16,1024]{2,1,0:T(8,128)(2,1)}), bf16[16,16,1024]{2,1,0:T(8,128)(2,1)S(1)}, u32[]{:S(2)}, u32[]{:S(2)}) async-start(bf16[16,16,1024]{2,1,0:T(8,128)(2,1)} %shard_map.133), calls=%async_computation.6 | async-start | bytes 1048576 | tf_op jit(solution)/shard_map/all_to_all | solution.py:321
  191.8 8.1 %all-to-all-done.5.s_ref = bf16[16,16,1024]{2,1,0:T(8,128)(2,1)S(1)} async-done(((bf16[16,16,1024]{2,1,0:T(8,128)(2,1)}), bf16[16,16,1024]{2,1,0:T(8,128)(2,1)S(1)}, u32[]{:S(2)}, u32[]{:S(2)}) %all-to-all-start.5) | async-done | bytes 524320 | tf_op jit(solution)/shard_map/all_to_all | solution.py:321
  199.9 1.7 shard_map.134
  (74 shorter events, 16.3 us)
Async XLA Ops:
  7.2 74.2 %reduce-scatter.2.cloned.1.call-start = ((), (), s32[]{:S(2)}) async-start(), calls=%async_computation.7 | async-start | bytes 4128768 | tf_op jit(solution)/shard_map/reduce_scatter | solution.py:288
  14.6 1.4 copy-start
  14.6 6.1 %copy-start.10 = (bf16[7168,4]{0,1:T(4,128)(2,1)S(1)}, bf16[7168,4]{0,1:T(4,128)(2,1)}, u32[]{:S(2)}) copy-start(bf16[7168,4]{0,1:T(4,128)(2,1)} %param.16) | copy-start | bytes 172036
  14.7 149.6 %all-gather.2.cloned.1.call-start = ((), (), s32[]{:S(2)}) async-start(), calls=%async_computation.8 | async-start | bytes 4456448 | tf_op jit(solution)/shard_map/all_gather | solution.py:299
  16.9 31.5 %collective-permute-start = (bf16[768,512]{1,0:T(8,128)(2,1)}, bf16[768,512]{1,0:T(8,128)(2,1)S(1)}, u32[]{:S(2)}, u32[]{:S(2)}) collective-permute-start(bf16[768,512]{1,0:T(8,128)(2,1)} %constant_dynamic-slice_fusion), channel_id=1, source_target_pairs={{0,1},{1,0},{2,3},{3,2},{4,5},{5,4},{6,7},{7,6},{8,9},{9,8},{10,11... | collective-permute-start | bytes 2359304 | tf_op jit(solution)/shard_map/ppermute | solution.py:33
  48.5 0.9 copy-start.4
  49.5 25.8 %copy-start.5 = (bf16[768,512]{1,0:T(8,128)(2,1)S(1)}, bf16[768,512]{1,0:T(8,128)(2,1)}, u32[]{:S(2)}) copy-start(bf16[768,512]{1,0:T(8,128)(2,1)} %copy-done.4) | copy-start | bytes 2359300
  70.8 9.4 %collective-permute-start.1 = (bf16[448,1664]{1,0:T(8,128)(2,1)S(1)}, bf16[448,1664]{1,0:T(8,128)(2,1)S(1)}, u32[]{:S(2)}, u32[]{:S(2)}) collective-permute-start(bf16[448,1664]{1,0:T(8,128)(2,1)S(1)} %bitcast.41), channel_id=1, source_target_pairs={{0,16},{16,0},{1,17},{17,1},{2,18},{18,2},{3,19},{19,3},{4,20},{20... | collective-permute-start | bytes 4472840 | tf_op jit(solution)/shard_map/ppermute | solution.py:33
  75.3 4.0 %collective-permute-start.2 = (bf16[768,512]{1,0:T(8,128)(2,1)S(1)}, bf16[768,512]{1,0:T(8,128)(2,1)S(1)}, u32[]{:S(2)}, u32[]{:S(2)}) collective-permute-start(bf16[768,512]{1,0:T(8,128)(2,1)S(1)} %copy-done.5), channel_id=1, source_target_pairs={{0,16},{16,0},{1,17},{17,1},{2,18},{18,2},{3,19},{19,3},{4,20},{20... | collective-permute-start | bytes 2359304 | tf_op jit(solution)/shard_map/ppermute | solution.py:33
  79.3 0.9 copy-start.7
  80.2 1.2 copy-start.2
  83.2 9.3 %collective-permute-start.3 = (bf16[128,896]{1,0:T(8,128)(2,1)}, bf16[128,896]{1,0:T(8,128)(2,1)S(1)}, u32[]{:S(2)}, u32[]{:S(2)}) collective-permute-start(bf16[128,896]{1,0:T(8,128)(2,1)} %get-tuple-element.28), channel_id=1, source_target_pairs={{0,1},{1,0},{2,3},{3,2},{4,5},{5,4},{6,7},{7,6},{8,9},{9,8},{10,11... | collective-permute-start | bytes 688136 | tf_op jit(solution)/shard_map/ppermute | solution.py:33
  92.5 1.4 copy-start.3
  93.9 5.4 %copy-start.11 = (bf16[1536]{0:T(1024)(128)(2,1)S(1)}, bf16[1536]{0:T(1024)(128)(2,1)}, u32[]{:S(2)}) copy-start(bf16[1536]{0:T(1024)(128)(2,1)} %param.17) | copy-start | bytes 9220
  94.7 0.9 copy-start.1
  95.5 52.1 %copy-start.6 = (bf16[768,512]{1,0:T(8,128)(2,1)S(1)}, bf16[768,512]{1,0:T(8,128)(2,1)}, u32[]{:S(2)}) copy-start(bf16[768,512]{1,0:T(8,128)(2,1)} %copy-done.4) | copy-start | bytes 2359300
  95.5 21.6 %all-to-all-start.2 = ((bf16[8,16,2560]{2,1,0:T(8,128)(2,1)}), bf16[8,16,2560]{2,1,0:T(8,128)(2,1)S(1)}, u32[]{:S(2)}, u32[]{:S(2)}) async-start(bf16[8,16,2560]{2,1,0:T(8,128)(2,1)} %bitcast.43), calls=%async_computation.3 | async-start | bytes 1310720 | tf_op jit(solution)/shard_map/all_to_all | solution.py:304
  117.9 8.7 %collective-permute-start.4 = (bf16[16,1664]{1,0:T(8,128)(2,1)S(1)}, bf16[16,1664]{1,0:T(8,128)(2,1)S(1)}, u32[]{:S(2)}, u32[]{:S(2)}) collective-permute-start(bf16[16,1664]{1,0:T(8,128)(2,1)S(1)} %concatenate.11), channel_id=1, source_target_pairs={{0,0},{1,16},{2,32},{3,48},{4,64},{5,80},{6,96},{7,112},{8,128},{9... | collective-permute-start | bytes 159752 | tf_op jit(solution)/shard_map/ppermute | solution.py:263
  127.4 20.2 %all-to-all-start.3 = ((bf16[8,16,1664]{2,1,0:T(8,128)(2,1)}), bf16[8,16,1664]{2,1,0:T(8,128)(2,1)S(1)}, u32[]{:S(2)}, u32[]{:S(2)}) async-start(bf16[8,16,1664]{2,1,0:T(8,128)(2,1)} %broadcast_in_dim.27), calls=%async_computation.4 | async-start | bytes 851968 | tf_op jit(solution)/shard_map/all_to_all | solution.py:314
  147.7 1.1 copy-start.8
  150.7 13.5 %all-to-all-start.4 = ((bf16[8,10,16,128]{3,2,1,0:T(8,128)(2,1)}), bf16[8,10,16,128]{3,2,1,0:T(8,128)(2,1)S(1)}, u32[]{:S(2)}, u32[]{:S(2)}) async-start(bf16[8,10,16,128]{3,2,1,0:T(8,128)(2,1)} %shard_map.132), calls=%async_computation.5 | async-start | bytes 655360 | tf_op jit(solution)/shard_map/all_to_all | solution.py:319
  164.1 0.7 copy-start.9
  164.1 26.8 %collective-permute-start.5 = (bf16[8,16,96]{2,1,0:T(8,128)(2,1)S(1)}, bf16[8,16,96]{2,1,0:T(8,128)(2,1)S(1)}, u32[]{:S(2)}, u32[]{:S(2)}) collective-permute-start(bf16[8,16,96]{2,1,0:T(8,128)(2,1)S(1)} %bitcast.56), channel_id=1, source_target_pairs={{0,1},{1,0},{2,3},{3,2},{4,5},{5,4},{6,7},{7,6},{8,9},{9,8},{10,11... | collective-permute-start | bytes 73736 | tf_op jit(solution)/shard_map/ppermute | solution.py:33
  177.1 22.7 %all-to-all-start.5 = ((bf16[16,16,1024]{2,1,0:T(8,128)(2,1)}), bf16[16,16,1024]{2,1,0:T(8,128)(2,1)S(1)}, u32[]{:S(2)}, u32[]{:S(2)}) async-start(bf16[16,16,1024]{2,1,0:T(8,128)(2,1)} %shard_map.133), calls=%async_computation.6 | async-start | bytes 1048576 | tf_op jit(solution)/shard_map/all_to_all | solution.py:321
Sparse Core Ops, SparseCore 0:
  14.8 59.1 reduce-scatter.1
  81.5 34.6 all-gather.1

commit v6 on v5

--- a/solution.py
+++ b/solution.py
@@ -38,7 +38,7 @@
 
 
 def kernel_params():
-    return pltpu.CompilerParams(vmem_limit_bytes=48 * 1024 * 1024)
+    return pltpu.CompilerParams(vmem_limit_bytes=20 * 1024 * 1024)
 
 
 def big_params():
@@ -130,21 +130,24 @@
     )(core, kept, got, gain, mine, other)
 
 
-def query_kernel(place_ref, latent_ref, own_ref, mine_ref, theirs_ref, final_ref, o_ref):
-    core, high = place_ref[0], place_ref[1]
+def query_kernel(place_ref, own_ref, mine_ref, theirs_ref, final_ref, *refs):
+    pieces, o_ref, latent_ref = refs[:NZ], refs[NZ], refs[NZ + 1]
+    core, high, level = place_ref[0], place_ref[1], place_ref[2]
+    for k in range(NZ):
+        latent_ref[k * 16 : (k + 1) * 16, :] = pieces[k][:, :QL]
     is_first = core == 0
-    left, right = latent_ref[:, : QL // 2], latent_ref[:, QL // 2 : QL]
+    left, right = latent_ref[:, : QL // 2], latent_ref[:, QL // 2 :]
     here = jnp.where(is_first, left, right)
     there = jnp.where(is_first, right, left)
-    own = jnp.dot(latent_ref[:, :QL], own_ref[...], preferred_element_type=jnp.float32)
+    own = jnp.dot(latent_ref[...], own_ref[...], preferred_element_type=jnp.float32)
     other = jnp.dot(here, mine_ref[...], preferred_element_type=jnp.float32) + jnp.dot(
         there, theirs_ref[...], preferred_element_type=jnp.float32
     )
     for at, part in ((high * 4, own), ((1 - high) * 4, other)):
         part = part.astype(jnp.bfloat16)
         for j in range(4):
-            for block in range(NZ):
-                o_ref[block, at + j] = part[block * 16 : (block + 1) * 16, j * IDIM : (j + 1) * IDIM]
+            for k in range(NZ):
+                o_ref[level ^ k, at + j] = part[k * 16 : (k + 1) * 16, j * IDIM : (j + 1) * IDIM]
     o_ref[:, 8:] = jnp.zeros((NZ, 2, 16, IDIM), jnp.bfloat16)
     for block in range(NZ):
         for half in range(2):
@@ -152,15 +155,16 @@
             o_ref[block, 8 + half, :, :96] = final_ref[:, at : at + 96]
 
 
-def make_queries(place, latent, own, mine, theirs, final):
+def make_queries(place, pieces, own, mine, theirs, final):
     whole = pl.BlockSpec(memory_space=pltpu.VMEM)
     return pl.pallas_call(
         query_kernel,
-        in_specs=[pl.BlockSpec(memory_space=pltpu.SMEM)] + [whole] * 5,
+        in_specs=[pl.BlockSpec(memory_space=pltpu.SMEM)] + [whole] * (4 + NZ),
         out_specs=whole,
         out_shape=jax.ShapeDtypeStruct((NZ, 10, 16, IDIM), jnp.bfloat16),
+        scratch_shapes=[pltpu.VMEM((HALF, QL), jnp.bfloat16)],
         compiler_params=kernel_params(),
-    )(place, latent, own, mine, theirs, final)
+    )(place, own, mine, theirs, final, *pieces)
 
 
 def score_kernel(q_ref, w_ref, k_ref, o_ref, wide_ref, rows_ref):
@@ -258,8 +262,11 @@
     return half, swap(half, "c"), early
 
 
-def turn(values):
-    moves = [(s * N_HEAD + h, h * N_HEAD + s) for s in range(N_SEQ) for h in range(N_HEAD)]
+def turn(values, flip):
+    moves = []
+    for s in range(N_SEQ):
+        for h in range(N_HEAD):
+            moves.append((s * N_HEAD + h, h * N_HEAD + (s ^ (flip * 2))))
     return lax.ppermute(values, SEQ + HEAD, moves)
 
 
@@ -293,8 +300,8 @@
         latent_weight, index_proj, c * 8 + x * 2 + yl, weight_mine
     )
     weight_theirs = swap(weight_mine, "c")
-    summed, down_mine, down_other, weight_mine, weight_theirs, index_keys = lax.optimization_barrier(
-        (summed, down_mine, down_other, weight_mine, weight_theirs, index_keys)
+    summed, down_mine, down_other, index_keys = lax.optimization_barrier(
+        (summed, down_mine, down_other, index_keys)
     )
     all_keys = lax.all_gather(index_keys, SEQ, axis=0, tiled=True)
     kept = lax.dynamic_index_in_dim(summed, yh, 0, keepdims=False)
@@ -310,14 +317,12 @@
     head_weights = (total[:, QL:1600] * inverse * IHEADS ** (-0.5)).astype(jnp.bfloat16)
     latent = rms_round(latent_raw, latent_gain)
     packed = jnp.concatenate([latent, head_weights, jnp.zeros((own, 64), jnp.bfloat16)], axis=1)
-    turned = turn(packed)
-    everyone = lax.all_to_all(jnp.broadcast_to(turned[None], (NZ,) + turned.shape), "z", 0, 0)
-    place = jnp.stack([c, yh]).astype(jnp.int32)
-    queries = make_queries(
-        place, everyone.reshape(HALF, packed.shape[1]), index_weight, weight_mine, weight_theirs, latent
-    )
+    pieces = [turn(packed, k) for k in range(NZ)]
+    place = jnp.stack([c, yh, z]).astype(jnp.int32)
+    queries = make_queries(place, pieces, index_weight, weight_mine, weight_theirs, latent)
     queries = lax.all_to_all(queries, "z", 0, 0)
-    scores = make_scores(queries, turned[:, QL:], all_keys)
+    scores = make_scores(queries, pieces[0][:, QL:], all_keys)
+    scores, queries = lax.optimization_barrier((scores, queries))
     scores = lax.all_to_all(scores, SEQ, 0, 0)
 
     latent_mine = lax.dynamic_index_in_dim(queries, 8 + yh, 1, keepdims=False)[:, :, :local]

time: 209 us -> 213 us (1.019)
  starting transfers between devices: 44.1 us -> 60.1 us
  waiting for transfers between devices: 59.9 us -> 47.3 us
    ppermute x1 -> x8, starting transfers between devices: 6.93 us -> 30.2 us  [turn(): return lax.ppermute(values, SEQ + HEAD, moves)]
    all_to_all x1 -> x0, waiting for transfers between devices: 12.6 us -> none  [shards(): lax.all_to_all(jnp.broadcast_to(turned[None], (NZ,) + turned.shape), 'z',...]
    all_to_all x1, starting transfers between devices: 13.1 us -> 4.27 us  [shards(): scores = lax.all_to_all(scores, SEQ, 0, 0)]
    all_to_all x1 -> x0, starting transfers between devices: 7.52 us -> none  [shards(): lax.all_to_all(jnp.broadcast_to(turned[None], (NZ,) + turned.shape), 'z',...]
    all_to_all x1, starting transfers between devices: 3.43 us -> 10.3 us  [shards(): queries = lax.all_to_all(queries, 'z', 0, 0)]
    ppermute x1 -> x8, waiting for transfers between devices: 1.8 us -> 4.92 us  [turn(): return lax.ppermute(values, SEQ + HEAD, moves)]
    unnamed x28 -> x22, local copies, waits for them, and re-layouts: 11.6 us -> 10.7 us
  transfers between devices with their start and end apart: 12 -> 18, of which waited for: 7 -> 8; matrix products, arithmetic and copies ran while one was open for 6% -> 7% of each run, Pallas kernels for 7% -> 1%
where the time goes in v6:
time: 213 us; the launch traced here: 212 us
  starting transfers between devices  60.1 us (28%)
  waiting for transfers between devices  47.3 us (22%)
  blocking collectives  44 us (21%)
  Pallas kernels  24.1 us (11%)
  local copies, waits for them, and re-layouts  19.5 us (9%)
  between operations  15 us (7%)
    ppermute x8, starting transfers between devices, turn(): return lax.ppermute(values, SEQ + HEAD, moves)  30.2 us
    all_to_all x1, blocking collectives, down_weight_rows(): lax.all_to_all(jnp.repeat(own, 2, axis=0), HEAD, 0, 0).transpose(1, 0, 2)  22.8 us
    all_to_all x1, blocking collectives, down_weight_rows(): lax.all_to_all(jnp.broadcast_to(wide[None], (8,) + wide.shape), ('x', 'yl...  21.2 us
    all_to_all x1, waiting for transfers between devices, shards(): parts = lax.all_to_all(lifted.reshape(NZ, own, lifted.shape[1]), 'z', 0, 0)  17.6 us
    pallas_call x1, Pallas kernels, make_scores(): pl.pallas_call(score_kernel, grid=(N_SEQ // per_step,), in_specs=[pl.Bloc...  12.3 us
    ppermute x5, starting transfers between devices, swap(): return lax.ppermute(values, axis, [(0, 1), (1, 0)])  10.9 us
    unnamed x22, local copies, waits for them, and re-layouts  10.7 us
    all_to_all x1, starting transfers between devices, shards(): queries = lax.all_to_all(queries, 'z', 0, 0)  10.3 us
  transfers between devices with their start and end apart: 18, of which 8 were waited for; matrix products, arithmetic and copies ran while one was open for 7% of the time, Pallas kernels for 1%

profile of v6, /device:TPU:1, one launch (start us, length us, event | category | flops | bytes accessed | tf_op | source)
XLA Modules:
  0.0 212.0 jit_solution(10931725757883985134)
XLA Ops:
  7.2 7.4 %shard_map.130 = bf16[8,2,128,896]{3,2,1,0:T(8,128)(2,1)} custom-call(s32[1]{0:T(128)} %bitcast.1.head_ref, bf16[256,512]{1,0:T(8,128)(2,1)} %a_ref.1, bf16[512,7168]{1,0:T(8,128)(2,1)} %b_ref.1, bf16[16,7168]{1,0:T(8,128)(2,1)} %res_ref.1), custom_call_target="tpu_custom_call" | custom-call | tf_op jit(solution)/shard_map/pallas_call | solution.py:87
  17.0 3.8 %collective-permute-start = (bf16[768,512]{1,0:T(8,128)(2,1)}, bf16[768,512]{1,0:T(8,128)(2,1)S(1)}, u32[]{:S(2)}, u32[]{:S(2)}) collective-permute-start(bf16[768,512]{1,0:T(8,128)(2,1)} %constant_dynamic-slice_fusion), channel_id=1, source_target_pairs={{0,1},{1,0},{2,3},{3,2},{4,5},{5,4},{6,7},{7,6},{8,9},{9,8},{10,11... | collective-permute-start | bytes 2359304 | tf_op jit(solution)/shard_map/ppermute | solution.py:33
  20.7 2.6 %copy.39 = bf16[12,8,8,896]{3,2,1,0:T(8,128)(2,1)} copy(bf16[12,8,8,896]{3,1,2,0:T(8,128)(2,1)} %bitcast.47) | data formatting | bytes 2752512
  24.9 22.8 %all_to_all.25 = bf16[16,56,100]{2,1,0:T(8,128)(2,1)S(1)} all-to-all(bf16[16,56,100]{2,1,0:T(8,128)(2,1)S(1)} %bitcast.48), channel_id=1, replica_groups=mesh['x'=4,'yl'=2,'c'=2,'z'=8,'yh'=2] {'z','yh'}, dimensions={0} | all-to-all | bytes 358400 | tf_op jit(solution)/shard_map/all_to_all | solution.py:249
  49.5 21.2 %all_to_all.26 = bf16[8,56,1664]{2,1,0:T(8,128)(2,1)S(1)} all-to-all(bf16[8,56,1664]{2,1,0:T(8,128)(2,1)S(1)} %broadcast_in_dim.19), channel_id=1, replica_groups=mesh['x'=4,'yl'=2,'c'=2,'z'=8,'yh'=2] {'x','yl'}, dimensions={0} | all-to-all | bytes 2981888 | tf_op jit(solution)/shard_map/all_to_all | solution.py:260
  70.7 4.4 %collective-permute-start.1 = (bf16[448,1664]{1,0:T(8,128)(2,1)S(1)}, bf16[448,1664]{1,0:T(8,128)(2,1)S(1)}, u32[]{:S(2)}, u32[]{:S(2)}) collective-permute-start(bf16[448,1664]{1,0:T(8,128)(2,1)S(1)} %bitcast.41), channel_id=1, source_target_pairs={{0,16},{16,0},{1,17},{17,1},{2,18},{18,2},{3,19},{19,3},{4,20},{20... | collective-permute-start | bytes 4472840 | tf_op jit(solution)/shard_map/ppermute | solution.py:33
  75.2 2.9 %collective-permute-done.1.other_ref = bf16[448,1664]{1,0:T(8,128)(2,1)S(1)} collective-permute-done((bf16[448,1664]{1,0:T(8,128)(2,1)S(1)}, bf16[448,1664]{1,0:T(8,128)(2,1)S(1)}, u32[]{:S(2)}, u32[]{:S(2)}) %collective-permute-start.1) | collective-permute-done | bytes 1490976 | tf_op jit(solution)/shard_map/ppermute | solution.py:33
  79.3 1.8 dynamic-slice_bitcast_fusion
  82.8 6.8 %collective-permute-done.2.got_ref = bf16[128,896]{1,0:T(8,128)(2,1)S(1)} collective-permute-done((bf16[128,896]{1,0:T(8,128)(2,1)}, bf16[128,896]{1,0:T(8,128)(2,1)S(1)}, u32[]{:S(2)}, u32[]{:S(2)}) %collective-permute-start.2) | collective-permute-done | bytes 229408 | tf_op jit(solution)/shard_map/ppermute | solution.py:33
  92.7 4.3 %all-to-all-start.2 = ((bf16[8,16,2560]{2,1,0:T(8,128)(2,1)}), bf16[8,16,2560]{2,1,0:T(8,128)(2,1)}, u32[]{:S(2)}, u32[]{:S(2)}) async-start(bf16[8,16,2560]{2,1,0:T(8,128)(2,1)} %bitcast.43), calls=%async_computation.3 | async-start | bytes 1310720 | tf_op jit(solution)/shard_map/all_to_all | solution.py:311
  97.1 1.7 collective-permute-start.3
  98.8 17.6 %all-to-all-done.2 = bf16[8,16,2560]{2,1,0:T(8,128)(2,1)} async-done(((bf16[8,16,2560]{2,1,0:T(8,128)(2,1)}), bf16[8,16,2560]{2,1,0:T(8,128)(2,1)}, u32[]{:S(2)}, u32[]{:S(2)}) %all-to-all-start.2) | async-done | bytes 655392 | tf_op jit(solution)/shard_map/all_to_all | solution.py:311
  118.2 4.8 %collective-permute-start.4 = (bf16[16,1664]{1,0:T(8,128)(2,1)S(1)}, bf16[16,1664]{1,0:T(8,128)(2,1)S(1)}, u32[]{:S(2)}, u32[]{:S(2)}) collective-permute-start(bf16[16,1664]{1,0:T(8,128)(2,1)S(1)} %concatenate.11), channel_id=1, source_target_pairs={{0,0},{1,16},{2,32},{3,48},{4,64},{5,80},{6,96},{7,112},{8,128},{9... | collective-permute-start | bytes 159752 | tf_op jit(solution)/shard_map/ppermute | solution.py:270
  123.1 3.3 %collective-permute-start.6 = (bf16[16,1664]{1,0:T(8,128)(2,1)S(1)}, bf16[16,1664]{1,0:T(8,128)(2,1)S(1)}, u32[]{:S(2)}, u32[]{:S(2)}) collective-permute-start(bf16[16,1664]{1,0:T(8,128)(2,1)S(1)} %concatenate.11), channel_id=1, source_target_pairs={{0,4},{1,20},{2,36},{3,52},{4,68},{5,84},{6,100},{7,116},{8,132},{... | collective-permute-start | bytes 159752 | tf_op jit(solution)/shard_map/ppermute | solution.py:270
  127.3 14.1 %collective-permute-start.8 = (bf16[16,1664]{1,0:T(8,128)(2,1)S(1)}, bf16[16,1664]{1,0:T(8,128)(2,1)S(1)}, u32[]{:S(2)}, u32[]{:S(2)}) collective-permute-start(bf16[16,1664]{1,0:T(8,128)(2,1)S(1)} %concatenate.11), channel_id=1, source_target_pairs={{0,8},{1,24},{2,40},{3,56},{4,72},{5,88},{6,104},{7,120},{8,136},{... | collective-permute-start | bytes 159752 | tf_op jit(solution)/shard_map/ppermute | solution.py:270
  141.4 5.1 %collective-permute-start.10 = (bf16[16,1664]{1,0:T(8,128)(2,1)S(1)}, bf16[16,1664]{1,0:T(8,128)(2,1)S(1)}, u32[]{:S(2)}, u32[]{:S(2)}) collective-permute-start(bf16[16,1664]{1,0:T(8,128)(2,1)S(1)} %concatenate.11), channel_id=1, source_target_pairs={{0,12},{1,28},{2,44},{3,60},{4,76},{5,92},{6,108},{7,124},{8,140},... | collective-permute-start | bytes 159752 | tf_op jit(solution)/shard_map/ppermute | solution.py:270
  146.5 1.9 collective-permute-start.11
  149.1 4.3 %collective-permute-done.11.refs_7_ = bf16[16,1664]{1,0:T(8,128)(2,1)S(1)} collective-permute-done((bf16[16,1664]{1,0:T(8,128)(2,1)S(1)}, bf16[16,1664]{1,0:T(8,128)(2,1)S(1)}, u32[]{:S(2)}, u32[]{:S(2)}) %collective-permute-start.11) | collective-permute-done | bytes 53280 | tf_op jit(solution)/shard_map/ppermute | solution.py:270
  153.4 1.9 shard_map.132
  155.3 10.3 %all-to-all-start.3 = ((bf16[8,10,16,128]{3,2,1,0:T(8,128)(2,1)}), bf16[8,10,16,128]{3,2,1,0:T(8,128)(2,1)S(1)}, u32[]{:S(2)}, u32[]{:S(2)}) async-start(bf16[8,10,16,128]{3,2,1,0:T(8,128)(2,1)} %shard_map.132), calls=%async_computation.4 | async-start | bytes 655360 | tf_op jit(solution)/shard_map/all_to_all | solution.py:323
  167.9 7.8 %all-to-all-done.3.q_ref = bf16[8,10,16,128]{3,2,1,0:T(8,128)(2,1)S(1)} async-done(((bf16[8,10,16,128]{3,2,1,0:T(8,128)(2,1)}), bf16[8,10,16,128]{3,2,1,0:T(8,128)(2,1)S(1)}, u32[]{:S(2)}, u32[]{:S(2)}) %all-to-all-start.3) | async-done | bytes 327712 | tf_op jit(solution)/shard_map/all_to_all | solution.py:323
  176.4 12.3 %shard_map.133 = bf16[16,16,1024]{2,1,0:T(8,128)(2,1)} custom-call(bf16[8,10,16,128]{3,2,1,0:T(8,128)(2,1)} %copy-done.6, bf16[16,128]{1,0:T(8,128)(2,1)} %slice.52.w_ref, bf16[16384,128]{1,0:T(8,128)(2,1)} %all-gather.2.cloned.1.call-done.k_ref), custom_call_target="tpu_custom_call" | custom-call | tf_op jit(solution)/shard_map/pallas_call | solution.py:204
  189.4 4.3 %all-to-all-start.4 = ((bf16[16,16,1024]{2,1,0:T(8,128)(2,1)}), bf16[16,16,1024]{2,1,0:T(8,128)(2,1)S(1)}, u32[]{:S(2)}, u32[]{:S(2)}) async-start(bf16[16,16,1024]{2,1,0:T(8,128)(2,1)} %shard_map.133), calls=%async_computation.5 | async-start | bytes 1048576 | tf_op jit(solution)/shard_map/all_to_all | solution.py:326
  196.2 7.2 %all-to-all-done.4.s_ref = bf16[16,16,1024]{2,1,0:T(8,128)(2,1)S(1)} async-done(((bf16[16,16,1024]{2,1,0:T(8,128)(2,1)}), bf16[16,16,1024]{2,1,0:T(8,128)(2,1)S(1)}, u32[]{:S(2)}, u32[]{:S(2)}) %all-to-all-start.4) | async-done | bytes 524320 | tf_op jit(solution)/shard_map/all_to_all | solution.py:326
  (79 shorter events, 22.1 us)
Async XLA Ops:
  7.2 72.1 %reduce-scatter.2.cloned.1.call-start = ((), (), s32[]{:S(2)}) async-start(), calls=%async_computation.6 | async-start | bytes 4128768 | tf_op jit(solution)/shard_map/reduce_scatter | solution.py:295
  14.6 1.4 copy-start
  14.7 6.1 %copy-start.7 = (bf16[7168,4]{0,1:T(4,128)(2,1)S(1)}, bf16[7168,4]{0,1:T(4,128)(2,1)}, u32[]{:S(2)}) copy-start(bf16[7168,4]{0,1:T(4,128)(2,1)} %param.16) | copy-start | bytes 172036
  14.7 161.0 %all-gather.2.cloned.1.call-start = ((), (), s32[]{:S(2)}) async-start(), calls=%async_computation.7 | async-start | bytes 4456448 | tf_op jit(solution)/shard_map/all_gather | solution.py:306
  17.0 31.5 %collective-permute-start = (bf16[768,512]{1,0:T(8,128)(2,1)}, bf16[768,512]{1,0:T(8,128)(2,1)S(1)}, u32[]{:S(2)}, u32[]{:S(2)}) collective-permute-start(bf16[768,512]{1,0:T(8,128)(2,1)} %constant_dynamic-slice_fusion), channel_id=1, source_target_pairs={{0,1},{1,0},{2,3},{3,2},{4,5},{5,4},{6,7},{7,6},{8,9},{9,8},{10,11... | collective-permute-start | bytes 2359304 | tf_op jit(solution)/shard_map/ppermute | solution.py:33
  70.7 7.4 %collective-permute-start.1 = (bf16[448,1664]{1,0:T(8,128)(2,1)S(1)}, bf16[448,1664]{1,0:T(8,128)(2,1)S(1)}, u32[]{:S(2)}, u32[]{:S(2)}) collective-permute-start(bf16[448,1664]{1,0:T(8,128)(2,1)S(1)} %bitcast.41), channel_id=1, source_target_pairs={{0,16},{16,0},{1,17},{17,1},{2,18},{18,2},{3,19},{19,3},{4,20},{20... | collective-permute-start | bytes 4472840 | tf_op jit(solution)/shard_map/ppermute | solution.py:33
  78.1 1.2 copy-start.2
  81.1 8.5 %collective-permute-start.2 = (bf16[128,896]{1,0:T(8,128)(2,1)}, bf16[128,896]{1,0:T(8,128)(2,1)S(1)}, u32[]{:S(2)}, u32[]{:S(2)}) collective-permute-start(bf16[128,896]{1,0:T(8,128)(2,1)} %get-tuple-element.28), channel_id=1, source_target_pairs={{0,1},{1,0},{2,3},{3,2},{4,5},{5,4},{6,7},{7,6},{8,9},{9,8},{10,11... | collective-permute-start | bytes 688136 | tf_op jit(solution)/shard_map/ppermute | solution.py:33
  89.6 1.4 copy-start.3
  91.0 6.0 %copy-start.8 = (bf16[1536]{0:T(1024)(128)(2,1)S(1)}, bf16[1536]{0:T(1024)(128)(2,1)}, u32[]{:S(2)}) copy-start(bf16[1536]{0:T(1024)(128)(2,1)} %param.17) | copy-start | bytes 9220
  92.7 60.7 %copy-start.5 = (bf16[768,512]{1,0:T(8,128)(2,1)S(1)}, bf16[768,512]{1,0:T(8,128)(2,1)}, u32[]{:S(2)}) copy-start(bf16[768,512]{1,0:T(8,128)(2,1)} %copy-done.4) | copy-start | bytes 2359300
  92.7 23.7 %all-to-all-start.2 = ((bf16[8,16,2560]{2,1,0:T(8,128)(2,1)}), bf16[8,16,2560]{2,1,0:T(8,128)(2,1)}, u32[]{:S(2)}, u32[]{:S(2)}) async-start(bf16[8,16,2560]{2,1,0:T(8,128)(2,1)} %bitcast.43), calls=%async_computation.3 | async-start | bytes 1310720 | tf_op jit(solution)/shard_map/all_to_all | solution.py:311
  97.1 30.2 %collective-permute-start.3 = (bf16[768,512]{1,0:T(8,128)(2,1)}, bf16[768,512]{1,0:T(8,128)(2,1)S(1)}, u32[]{:S(2)}, u32[]{:S(2)}) collective-permute-start(bf16[768,512]{1,0:T(8,128)(2,1)} %copy-done.4), channel_id=1, source_target_pairs={{0,16},{16,0},{1,17},{17,1},{2,18},{18,2},{3,19},{19,3},{4,20},{20... | collective-permute-start | bytes 2359304 | tf_op jit(solution)/shard_map/ppermute | solution.py:33
  118.2 23.2 %collective-permute-start.4 = (bf16[16,1664]{1,0:T(8,128)(2,1)S(1)}, bf16[16,1664]{1,0:T(8,128)(2,1)S(1)}, u32[]{:S(2)}, u32[]{:S(2)}) collective-permute-start(bf16[16,1664]{1,0:T(8,128)(2,1)S(1)} %concatenate.11), channel_id=1, source_target_pairs={{0,0},{1,16},{2,32},{3,48},{4,64},{5,80},{6,96},{7,112},{8,128},{9... | collective-permute-start | bytes 159752 | tf_op jit(solution)/shard_map/ppermute | solution.py:270
  123.0 18.3 %collective-permute-start.5 = (bf16[16,1664]{1,0:T(8,128)(2,1)S(1)}, bf16[16,1664]{1,0:T(8,128)(2,1)S(1)}, u32[]{:S(2)}, u32[]{:S(2)}) collective-permute-start(bf16[16,1664]{1,0:T(8,128)(2,1)S(1)} %concatenate.11), channel_id=1, source_target_pairs={{0,2},{1,18},{2,34},{3,50},{4,66},{5,82},{6,98},{7,114},{8,130},{9... | collective-permute-start | bytes 159752 | tf_op jit(solution)/shard_map/ppermute | solution.py:270
  123.1 23.4 %collective-permute-start.6 = (bf16[16,1664]{1,0:T(8,128)(2,1)S(1)}, bf16[16,1664]{1,0:T(8,128)(2,1)S(1)}, u32[]{:S(2)}, u32[]{:S(2)}) collective-permute-start(bf16[16,1664]{1,0:T(8,128)(2,1)S(1)} %concatenate.11), channel_id=1, source_target_pairs={{0,4},{1,20},{2,36},{3,52},{4,68},{5,84},{6,100},{7,116},{8,132},{... | collective-permute-start | bytes 159752 | tf_op jit(solution)/shard_map/ppermute | solution.py:270
  126.5 22.0 %collective-permute-start.7 = (bf16[16,1664]{1,0:T(8,128)(2,1)S(1)}, bf16[16,1664]{1,0:T(8,128)(2,1)S(1)}, u32[]{:S(2)}, u32[]{:S(2)}) collective-permute-start(bf16[16,1664]{1,0:T(8,128)(2,1)S(1)} %concatenate.11), channel_id=1, source_target_pairs={{0,6},{1,22},{2,38},{3,54},{4,70},{5,86},{6,102},{7,118},{8,134},{... | collective-permute-start | bytes 159752 | tf_op jit(solution)/shard_map/ppermute | solution.py:270
  127.3 21.2 %collective-permute-start.8 = (bf16[16,1664]{1,0:T(8,128)(2,1)S(1)}, bf16[16,1664]{1,0:T(8,128)(2,1)S(1)}, u32[]{:S(2)}, u32[]{:S(2)}) collective-permute-start(bf16[16,1664]{1,0:T(8,128)(2,1)S(1)} %concatenate.11), channel_id=1, source_target_pairs={{0,8},{1,24},{2,40},{3,56},{4,72},{5,88},{6,104},{7,120},{8,136},{... | collective-permute-start | bytes 159752 | tf_op jit(solution)/shard_map/ppermute | solution.py:270
  141.4 7.6 %collective-permute-start.9 = (bf16[16,1664]{1,0:T(8,128)(2,1)S(1)}, bf16[16,1664]{1,0:T(8,128)(2,1)S(1)}, u32[]{:S(2)}, u32[]{:S(2)}) collective-permute-start(bf16[16,1664]{1,0:T(8,128)(2,1)S(1)} %concatenate.11), channel_id=1, source_target_pairs={{0,10},{1,26},{2,42},{3,58},{4,74},{5,90},{6,106},{7,122},{8,138},... | collective-permute-start | bytes 159752 | tf_op jit(solution)/shard_map/ppermute | solution.py:270
  141.4 7.7 %collective-permute-start.10 = (bf16[16,1664]{1,0:T(8,128)(2,1)S(1)}, bf16[16,1664]{1,0:T(8,128)(2,1)S(1)}, u32[]{:S(2)}, u32[]{:S(2)}) collective-permute-start(bf16[16,1664]{1,0:T(8,128)(2,1)S(1)} %concatenate.11), channel_id=1, source_target_pairs={{0,12},{1,28},{2,44},{3,60},{4,76},{5,92},{6,108},{7,124},{8,140},... | collective-permute-start | bytes 159752 | tf_op jit(solution)/shard_map/ppermute | solution.py:270
  146.5 6.9 %collective-permute-start.11 = (bf16[16,1664]{1,0:T(8,128)(2,1)S(1)}, bf16[16,1664]{1,0:T(8,128)(2,1)S(1)}, u32[]{:S(2)}, u32[]{:S(2)}) collective-permute-start(bf16[16,1664]{1,0:T(8,128)(2,1)S(1)} %concatenate.11), channel_id=1, source_target_pairs={{0,14},{1,30},{2,46},{3,62},{4,78},{5,94},{6,110},{7,126},{8,142},... | collective-permute-start | bytes 159752 | tf_op jit(solution)/shard_map/ppermute | solution.py:270
  155.3 20.4 %all-to-all-start.3 = ((bf16[8,10,16,128]{3,2,1,0:T(8,128)(2,1)}), bf16[8,10,16,128]{3,2,1,0:T(8,128)(2,1)S(1)}, u32[]{:S(2)}, u32[]{:S(2)}) async-start(bf16[8,10,16,128]{3,2,1,0:T(8,128)(2,1)} %shard_map.132), calls=%async_computation.4 | async-start | bytes 655360 | tf_op jit(solution)/shard_map/all_to_all | solution.py:323
  189.4 5.9 %collective-permute-start.12 = (bf16[8,16,96]{2,1,0:T(8,128)(2,1)S(1)}, bf16[8,16,96]{2,1,0:T(8,128)(2,1)S(1)}, u32[]{:S(2)}, u32[]{:S(2)}) collective-permute-start(bf16[8,16,96]{2,1,0:T(8,128)(2,1)S(1)} %bitcast.55), channel_id=1, source_target_pairs={{0,1},{1,0},{2,3},{3,2},{4,5},{5,4},{6,7},{7,6},{8,9},{9,8},{10,11... | collective-permute-start | bytes 73736 | tf_op jit(solution)/shard_map/ppermute | solution.py:33
  189.4 14.0 %all-to-all-start.4 = ((bf16[16,16,1024]{2,1,0:T(8,128)(2,1)}), bf16[16,16,1024]{2,1,0:T(8,128)(2,1)S(1)}, u32[]{:S(2)}, u32[]{:S(2)}) async-start(bf16[16,16,1024]{2,1,0:T(8,128)(2,1)} %shard_map.133), calls=%async_computation.5 | async-start | bytes 1048576 | tf_op jit(solution)/shard_map/all_to_all | solution.py:326
  (3 other events, 2.5 us)
Sparse Core Ops, SparseCore 0:
  14.8 59.0 reduce-scatter.1
  79.4 35.5 all-gather.1

commit v7 on v5

--- a/solution.py
+++ b/solution.py
@@ -38,7 +38,7 @@
 
 
 def kernel_params():
-    return pltpu.CompilerParams(vmem_limit_bytes=48 * 1024 * 1024)
+    return pltpu.CompilerParams(vmem_limit_bytes=20 * 1024 * 1024)
 
 
 def big_params():
@@ -70,7 +70,7 @@
         product = product.astype(o_ref.dtype)
         for group in range(NZ):
             for half in range(2):
-                o_held[i, half, group * 16 : (group + 1) * 16, :] = product[
+                o_held[i, half ^ head_ref[1], group * 16 : (group + 1) * 16, :] = product[
                     group * 32 + half * 16 : group * 32 + (half + 1) * 16, :
                 ]
         store(i).start()
@@ -130,7 +130,7 @@
     )(core, kept, got, gain, mine, other)
 
 
-def query_kernel(place_ref, latent_ref, own_ref, mine_ref, theirs_ref, final_ref, o_ref):
+def query_kernel(place_ref, latent_ref, own_ref, mine_ref, theirs_ref, final_ref, beside_ref, o_ref):
     core, high = place_ref[0], place_ref[1]
     is_first = core == 0
     left, right = latent_ref[:, : QL // 2], latent_ref[:, QL // 2 : QL]
@@ -147,20 +147,21 @@
                 o_ref[block, at + j] = part[block * 16 : (block + 1) * 16, j * IDIM : (j + 1) * IDIM]
     o_ref[:, 8:] = jnp.zeros((NZ, 2, 16, IDIM), jnp.bfloat16)
     for block in range(NZ):
-        for half in range(2):
-            at = (block * 2 + half) * 96
-            o_ref[block, 8 + half, :, :96] = final_ref[:, at : at + 96]
-
-
-def make_queries(place, latent, own, mine, theirs, final):
+        low = final_ref[:, block * 192 : block * 192 + 96]
+        top = final_ref[:, block * 192 + 96 : block * 192 + 192]
+        o_ref[block, 8 + high, :, :96] = jnp.where(high == 0, low, top)
+        o_ref[block, 9 - high, :, :96] = beside_ref[:, block * 96 : (block + 1) * 96]
+
+
+def make_queries(place, latent, own, mine, theirs, final, beside):
     whole = pl.BlockSpec(memory_space=pltpu.VMEM)
     return pl.pallas_call(
         query_kernel,
-        in_specs=[pl.BlockSpec(memory_space=pltpu.SMEM)] + [whole] * 5,
+        in_specs=[pl.BlockSpec(memory_space=pltpu.SMEM)] + [whole] * 6,
         out_specs=whole,
         out_shape=jax.ShapeDtypeStruct((NZ, 10, 16, IDIM), jnp.bfloat16),
         compiler_params=kernel_params(),
-    )(place, latent, own, mine, theirs, final)
+    )(place, latent, own, mine, theirs, final, beside)
 
 
 def score_kernel(q_ref, w_ref, k_ref, o_ref, wide_ref, rows_ref):
@@ -235,7 +236,7 @@
     )(numbers, scores, own_positions)
 
 
-def down_weight_rows(latent_weight, index_proj, piece, early):
+def down_weight_rows(latent_weight, index_proj, piece):
     share = DZ // N_SEQ
 
     def own_rows(weight):
@@ -252,10 +253,9 @@
         ],
         axis=1,
     )
-    wide, early = lax.optimization_barrier((wide, early))
     half = lax.all_to_all(jnp.broadcast_to(wide[None], (8,) + wide.shape), ("x", "yl"), 0, 0)
     half = half.reshape(8 * share, wide.shape[1])
-    return half, swap(half, "c"), early
+    return half, swap(half, "c")
 
 
 def turn(values):
@@ -284,21 +284,16 @@
     own = rows // N_HEAD
     local = latent_weight.shape[1]
 
-    partial = project(jnp.stack([head]).astype(jnp.int32), attn_out, out_weight, residual)
+    partial = project(jnp.stack([head, yh]).astype(jnp.int32), attn_out, out_weight, residual)
     summed = lax.psum_scatter(partial, "z", scatter_dimension=0, tiled=False)
 
     depth = QL // 2
     weight_mine = swap(lax.dynamic_slice_in_dim(index_weight, c * depth, depth, 0), "yh")
-    down_mine, down_other, weight_mine = down_weight_rows(
-        latent_weight, index_proj, c * 8 + x * 2 + yl, weight_mine
-    )
     weight_theirs = swap(weight_mine, "c")
-    summed, down_mine, down_other, weight_mine, weight_theirs, index_keys = lax.optimization_barrier(
-        (summed, down_mine, down_other, weight_mine, weight_theirs, index_keys)
-    )
+    down_mine, down_other = down_weight_rows(latent_weight, index_proj, c * 8 + x * 2 + yl)
+    summed, index_keys = lax.optimization_barrier((summed, index_keys))
     all_keys = lax.all_gather(index_keys, SEQ, axis=0, tiled=True)
-    kept = lax.dynamic_index_in_dim(summed, yh, 0, keepdims=False)
-    got = swap(lax.dynamic_index_in_dim(summed, 1 - yh, 0, keepdims=False), "yh")
+    kept, got = summed[0], swap(summed[1], "yh")
     gain = lax.dynamic_slice_in_dim(norm_gain, z * DZ, DZ).reshape(1, DZ)
     lifted = lift(jnp.stack([c]).astype(jnp.int32), kept, got, gain, down_mine, down_other)
     parts = lax.all_to_all(lifted.reshape(NZ, own, lifted.shape[1]), "z", 0, 0)
@@ -311,21 +306,16 @@
     latent = rms_round(latent_raw, latent_gain)
     packed = jnp.concatenate([latent, head_weights, jnp.zeros((own, 64), jnp.bfloat16)], axis=1)
     turned = turn(packed)
+    give = lax.dynamic_index_in_dim(latent.reshape(own, NZ, 2, local), 1 - yh, 2, keepdims=False)
+    beside = swap(give.reshape(own, NZ * local), "yh")
     everyone = lax.all_to_all(jnp.broadcast_to(turned[None], (NZ,) + turned.shape), "z", 0, 0)
+    everyone = everyone.reshape(HALF, packed.shape[1])
     place = jnp.stack([c, yh]).astype(jnp.int32)
-    queries = make_queries(
-        place, everyone.reshape(HALF, packed.shape[1]), index_weight, weight_mine, weight_theirs, latent
-    )
+    queries = make_queries(place, everyone, index_weight, weight_mine, weight_theirs, latent, beside)
     queries = lax.all_to_all(queries, "z", 0, 0)
+    latent_out = queries[:, 8:, :, :local].reshape(rows, local)
     scores = make_scores(queries, turned[:, QL:], all_keys)
     scores = lax.all_to_all(scores, SEQ, 0, 0)
-
-    latent_mine = lax.dynamic_index_in_dim(queries, 8 + yh, 1, keepdims=False)[:, :, :local]
-    latent_give = lax.dynamic_index_in_dim(queries, 9 - yh, 1, keepdims=False)[:, :, :local]
-    latent_got = swap(latent_give, "yh")
-    latent_out = jnp.stack(
-        [jnp.where(yh == 0, latent_mine, latent_got), jnp.where(yh == 0, latent_got, latent_mine)], axis=1
-    ).reshape(rows, local)
 
     own_positions = lax.dynamic_slice_in_dim(positions, head * rows, rows).reshape(rows, 1)
     numbers = jnp.stack([cache_len[0], seq * SLOTS]).astype(jnp.int32)

time: 209 us -> 251 us (1.20)
  waiting for transfers between devices: 59.9 us -> 107 us
  starting transfers between devices: 44.1 us -> 36.2 us
  blocking collectives: 44.1 us -> 50.2 us
  local copies, waits for them, and re-layouts: 20.5 us -> 16 us
    reduce_scatter x1, waiting for transfers between devices: 0.01 us -> 54.3 us  [shards(): summed = lax.psum_scatter(partial, 'z', scatter_dimension=0, tiled=False)]
    all_to_all x1, blocking collectives: 21.3 us -> 32.6 us  [down_weight_rows(): lax.all_to_all(jnp.broadcast_to(wide[None], (8,) + wide.shape), ('x', 'yl...]
    unnamed x28 -> x24, local copies, waits for them, and re-layouts: 11.6 us -> 5.12 us
    all_to_all x1, waiting for transfers between devices: 12.6 us -> 7.24 us  [shards(): lax.all_to_all(jnp.broadcast_to(turned[None], (NZ,) + turned.shape), 'z',...]
    all_to_all x1, blocking collectives: 22.8 us -> 17.7 us  [down_weight_rows(): lax.all_to_all(jnp.repeat(own, 2, axis=0), HEAD, 0, 0).transpose(1, 0, 2)]
    ppermute x5, starting transfers between devices: 9.36 us -> 6.15 us  [swap(): return lax.ppermute(values, axis, [(0, 1), (1, 0)])]
    ppermute x1, starting transfers between devices: 6.93 us -> 3.98 us  [turn(): return lax.ppermute(values, SEQ + HEAD, moves)]
  transfers between devices with their start and end apart: 12 -> 12, of which waited for: 7 -> 8; matrix products, arithmetic and copies ran while one was open for 6% -> 5% of each run, Pallas kernels for 7% -> 1%
where the time goes in v7:
time: 251 us; the launch traced here: 250 us
  waiting for transfers between devices  107 us (43%)
  blocking collectives  50.2 us (20%)
  starting transfers between devices  36.2 us (14%)
  Pallas kernels  24.7 us (10%)
  local copies, waits for them, and re-layouts  16 us (6%)
  between operations  15 us (6%)
    reduce_scatter x1, waiting for transfers between devices, shards(): summed = lax.psum_scatter(partial, 'z', scatter_dimension=0, tiled=False)  54.3 us
    all_to_all x1, blocking collectives, down_weight_rows(): lax.all_to_all(jnp.broadcast_to(wide[None], (8,) + wide.shape), ('x', 'yl...  32.6 us
    all_to_all x1, waiting for transfers between devices, shards(): parts = lax.all_to_all(lifted.reshape(NZ, own, lifted.shape[1]), 'z', 0, 0)  18.1 us
    all_to_all x1, blocking collectives, down_weight_rows(): lax.all_to_all(jnp.repeat(own, 2, axis=0), HEAD, 0, 0).transpose(1, 0, 2)  17.7 us
    pallas_call x1, Pallas kernels, make_scores(): pl.pallas_call(score_kernel, grid=(N_SEQ // per_step,), in_specs=[pl.Bloc...  12.3 us
    all_to_all x1, starting transfers between devices, shards(): scores = lax.all_to_all(scores, SEQ, 0, 0)  11.9 us
    ppermute x5, waiting for transfers between devices, swap(): return lax.ppermute(values, axis, [(0, 1), (1, 0)])  9.31 us
    all_to_all x1, waiting for transfers between devices, shards(): queries = lax.all_to_all(queries, 'z', 0, 0)  8.97 us
  transfers between devices with their start and end apart: 12, of which 8 were waited for; matrix products, arithmetic and copies ran while one was open for 5% of the time, Pallas kernels for 1%

profile of v7, /device:TPU:1, one launch (start us, length us, event | category | flops | bytes accessed | tf_op | source)
XLA Modules:
  0.0 250.0 jit_solution(11240451461950637579)
XLA Ops:
  7.8 7.4 %shard_map.130 = bf16[8,2,128,896]{3,2,1,0:T(8,128)(2,1)} custom-call(s32[2]{0:T(128)} %pad_add_fusion.head_ref, bf16[256,512]{1,0:T(8,128)(2,1)} %a_ref.1, bf16[512,7168]{1,0:T(8,128)(2,1)} %b_ref.1, bf16[16,7168]{1,0:T(8,128)(2,1)} %res_ref.1), custom_call_target="tpu_custom_call" | custom-call | tf_op jit(solution)/shard_map/pallas_call | solution.py:87
  15.3 54.3 %reduce-scatter.2.cloned.1.call-done = bf16[1,2,128,896]{3,2,1,0:T(8,128)(2,1)} async-done(((bf16[8,2,128,896]{3,2,1,0:T(8,128)(2,1)}), bf16[1,2,128,896]{3,2,1,0:T(8,128)(2,1)}) %reduce-scatter.2.cloned.1.call-update) | async-done | bytes 458768 | tf_op jit(solution)/shard_map/reduce_scatter | solution.py:288
  70.5 17.7 %all_to_all.30 = bf16[16,56,100]{2,1,0:T(8,128)(2,1)S(1)} all-to-all(bf16[16,56,100]{2,1,0:T(8,128)(2,1)S(1)} %bitcast.40), channel_id=1, replica_groups=mesh['x'=4,'yl'=2,'c'=2,'z'=8,'yh'=2] {'z','yh'}, dimensions={0} | all-to-all | bytes 358400 | tf_op jit(solution)/shard_map/all_to_all | solution.py:246
  89.1 32.6 %all_to_all.31 = bf16[8,56,1664]{2,1,0:T(8,128)(2,1)S(1)} all-to-all(bf16[8,56,1664]{2,1,0:T(8,128)(2,1)S(1)} %broadcast_in_dim.12), channel_id=1, replica_groups=mesh['x'=4,'yl'=2,'c'=2,'z'=8,'yh'=2] {'x','yl'}, dimensions={0} | all-to-all | bytes 2981888 | tf_op jit(solution)/shard_map/all_to_all | solution.py:256
  121.6 2.3 collective-permute-start.1
  124.7 2.0 collective-permute-start
  128.6 5.0 %collective-permute-done.got_ref = bf16[128,896]{1,0:T(8,128)(2,1)S(1)} collective-permute-done((bf16[128,896]{1,0:T(8,128)(2,1)}, bf16[128,896]{1,0:T(8,128)(2,1)S(1)}, u32[]{:S(2)}, u32[]{:S(2)}) %collective-permute-start) | collective-permute-done | bytes 229408 | tf_op jit(solution)/shard_map/ppermute | solution.py:33
  133.6 1.4 copy-done.3
  136.7 4.1 %all-to-all-start.2 = ((bf16[8,16,2560]{2,1,0:T(8,128)(2,1)}), bf16[8,16,2560]{2,1,0:T(8,128)(2,1)S(1)}, u32[]{:S(2)}, u32[]{:S(2)}) async-start(bf16[8,16,2560]{2,1,0:T(8,128)(2,1)} %bitcast.34), calls=%async_computation.3 | async-start | bytes 1310720 | tf_op jit(solution)/shard_map/all_to_all | solution.py:299
  141.8 1.7 collective-permute-start.3
  143.5 18.1 %all-to-all-done.2 = bf16[8,16,2560]{2,1,0:T(8,128)(2,1)S(1)} async-done(((bf16[8,16,2560]{2,1,0:T(8,128)(2,1)}), bf16[8,16,2560]{2,1,0:T(8,128)(2,1)S(1)}, u32[]{:S(2)}, u32[]{:S(2)}) %all-to-all-start.2) | async-done | bytes 655392 | tf_op jit(solution)/shard_map/all_to_all | solution.py:299
  162.3 4.0 %collective-permute-start.2 = (bf16[16,1664]{1,0:T(8,128)(2,1)S(1)}, bf16[16,1664]{1,0:T(8,128)(2,1)S(1)}, u32[]{:S(2)}, u32[]{:S(2)}) collective-permute-start(bf16[16,1664]{1,0:T(8,128)(2,1)S(1)} %concatenate.11), channel_id=1, source_target_pairs={{0,0},{1,16},{2,32},{3,48},{4,64},{5,80},{6,96},{7,112},{8,128},{9... | collective-permute-start | bytes 159752 | tf_op jit(solution)/shard_map/ppermute | solution.py:263
  166.4 2.8 %collective-permute-done.2 = bf16[16,1664]{1,0:T(8,128)(2,1)S(1)} collective-permute-done((bf16[16,1664]{1,0:T(8,128)(2,1)S(1)}, bf16[16,1664]{1,0:T(8,128)(2,1)S(1)}, u32[]{:S(2)}, u32[]{:S(2)}) %collective-permute-start.2) | collective-permute-done | bytes 53280 | tf_op jit(solution)/shard_map/ppermute | solution.py:263
  170.1 6.5 %all-to-all-start.3 = ((bf16[8,16,1664]{2,1,0:T(8,128)(2,1)}), bf16[8,16,1664]{2,1,0:T(8,128)(2,1)S(1)}, u32[]{:S(2)}, u32[]{:S(2)}) async-start(bf16[8,16,1664]{2,1,0:T(8,128)(2,1)} %broadcast_in_dim.27), calls=%async_computation.4 | async-start | bytes 851968 | tf_op jit(solution)/shard_map/all_to_all | solution.py:311
  179.2 4.3 %collective-permute-done.5.beside_ref = bf16[16,768]{1,0:T(8,128)(2,1)S(1)} collective-permute-done((bf16[16,768]{1,0:T(8,128)(2,1)}, bf16[16,768]{1,0:T(8,128)(2,1)S(1)}, u32[]{:S(2)}, u32[]{:S(2)}) %collective-permute-start.5) | collective-permute-done | bytes 24608 | tf_op jit(solution)/shard_map/ppermute | solution.py:33
  183.5 7.2 %all-to-all-done.3 = bf16[8,16,1664]{2,1,0:T(8,128)(2,1)S(1)} async-done(((bf16[8,16,1664]{2,1,0:T(8,128)(2,1)}), bf16[8,16,1664]{2,1,0:T(8,128)(2,1)S(1)}, u32[]{:S(2)}, u32[]{:S(2)}) %all-to-all-start.3) | async-done | bytes 426016 | tf_op jit(solution)/shard_map/all_to_all | solution.py:311
  190.7 2.5 shard_map.132
  193.2 3.4 %all-to-all-start.4 = ((bf16[8,10,16,128]{3,2,1,0:T(8,128)(2,1)}), bf16[8,10,16,128]{3,2,1,0:T(8,128)(2,1)S(1)}, u32[]{:S(2)}, u32[]{:S(2)}) async-start(bf16[8,10,16,128]{3,2,1,0:T(8,128)(2,1)} %shard_map.132), calls=%async_computation.5 | async-start | bytes 655360 | tf_op jit(solution)/shard_map/all_to_all | solution.py:315
  196.6 1.3 slice.57.w_ref
  197.9 9.0 %all-to-all-done.4.q_ref = bf16[8,10,16,128]{3,2,1,0:T(8,128)(2,1)S(1)} async-done(((bf16[8,10,16,128]{3,2,1,0:T(8,128)(2,1)}), bf16[8,10,16,128]{3,2,1,0:T(8,128)(2,1)S(1)}, u32[]{:S(2)}, u32[]{:S(2)}) %all-to-all-start.4) | async-done | bytes 327712 | tf_op jit(solution)/shard_map/all_to_all | solution.py:315
  207.6 12.3 %shard_map.133 = bf16[16,16,1024]{2,1,0:T(8,128)(2,1)} custom-call(bf16[8,10,16,128]{3,2,1,0:T(8,128)(2,1)} %copy-done.4, bf16[16,128]{1,0:T(8,128)(2,1)} %slice.57.w_ref, bf16[16384,128]{1,0:T(8,128)(2,1)} %all-gather.2.cloned.1.call-done.k_ref), custom_call_target="tpu_custom_call" | custom-call | tf_op jit(solution)/shard_map/pallas_call | solution.py:201
  219.9 11.9 %all-to-all-start.5 = ((bf16[16,16,1024]{2,1,0:T(8,128)(2,1)}), bf16[16,16,1024]{2,1,0:T(8,128)(2,1)S(1)}, u32[]{:S(2)}, u32[]{:S(2)}) async-start(bf16[16,16,1024]{2,1,0:T(8,128)(2,1)} %shard_map.133), calls=%async_computation.6 | async-start | bytes 1048576 | tf_op jit(solution)/shard_map/all_to_all | solution.py:318
  235.8 5.7 %all-to-all-done.5.s_ref = bf16[16,16,1024]{2,1,0:T(8,128)(2,1)S(1)} async-done(((bf16[16,16,1024]{2,1,0:T(8,128)(2,1)}), bf16[16,16,1024]{2,1,0:T(8,128)(2,1)S(1)}, u32[]{:S(2)}, u32[]{:S(2)}) %all-to-all-start.5) | async-done | bytes 524320 | tf_op jit(solution)/shard_map/all_to_all | solution.py:318
  241.5 1.7 shard_map.134
  (71 shorter events, 15.8 us)
Async XLA Ops:
  7.2 62.5 %reduce-scatter.2.cloned.1.call-start = ((), (), s32[]{:S(2)}) async-start(), calls=%async_computation.7 | async-start | bytes 4128768 | tf_op jit(solution)/shard_map/reduce_scatter | solution.py:288
  15.2 54.5 %copy-start.8 = (bf16[7168,4]{0,1:T(4,128)(2,1)S(1)}, bf16[7168,4]{0,1:T(4,128)(2,1)}, u32[]{:S(2)}) copy-start(bf16[7168,4]{0,1:T(4,128)(2,1)} %param.16) | copy-start | bytes 172036
  15.2 54.5 %copy-start.5 = (bf16[7168,96]{0,1:T(8,128)(2,1)S(1)}, bf16[7168,96]{0,1:T(8,128)(2,1)}, u32[]{:S(2)}) copy-start(bf16[7168,96]{0,1:T(8,128)(2,1)} %param.15) | copy-start | bytes 4128772
  15.3 191.6 %all-gather.2.cloned.1.call-start = ((), (), s32[]{:S(2)}) async-start(), calls=%async_computation.8 | async-start | bytes 4456448 | tf_op jit(solution)/shard_map/all_gather | solution.py:295
  89.1 34.9 %copy-start.6 = (bf16[1,2,128,896]{3,2,1,0:T(8,128)(2,1)S(1)}, bf16[1,2,128,896]{3,2,1,0:T(8,128)(2,1)}, u32[]{:S(2)}) copy-start(bf16[1,2,128,896]{3,2,1,0:T(8,128)(2,1)} %reduce-scatter.2.cloned.1.call-done) | copy-start | bytes 1376260
  121.6 5.8 %collective-permute-start.1 = (bf16[448,1664]{1,0:T(8,128)(2,1)S(1)}, bf16[448,1664]{1,0:T(8,128)(2,1)S(1)}, u32[]{:S(2)}, u32[]{:S(2)}) collective-permute-start(bf16[448,1664]{1,0:T(8,128)(2,1)S(1)} %bitcast.32), channel_id=1, source_target_pairs={{0,16},{16,0},{1,17},{17,1},{2,18},{18,2},{3,19},{19,3},{4,20},{20... | collective-permute-start | bytes 4472840 | tf_op jit(solution)/shard_map/ppermute | solution.py:33
  124.7 8.9 %collective-permute-start = (bf16[128,896]{1,0:T(8,128)(2,1)}, bf16[128,896]{1,0:T(8,128)(2,1)S(1)}, u32[]{:S(2)}, u32[]{:S(2)}) collective-permute-start(bf16[128,896]{1,0:T(8,128)(2,1)} %get-tuple-element.19), channel_id=1, source_target_pairs={{0,1},{1,0},{2,3},{3,2},{4,5},{5,4},{6,7},{7,6},{8,9},{9,8},{10,11... | collective-permute-start | bytes 688136 | tf_op jit(solution)/shard_map/ppermute | solution.py:33
  127.5 1.1 copy-start.2
  133.6 1.4 copy-start.3
  135.0 5.8 %copy-start = (bf16[1536,512]{1,0:T(8,128)(2,1)S(1)}, bf16[1536,512]{1,0:T(8,128)(2,1)}, u32[]{:S(2)}) copy-start(bf16[1536,512]{1,0:T(8,128)(2,1)} %own_ref.1) | copy-start | bytes 4718596
  135.8 0.8 copy-start.1
  136.7 6.8 %copy-start.9 = (bf16[1536]{0:T(1024)(128)(2,1)S(1)}, bf16[1536]{0:T(1024)(128)(2,1)}, u32[]{:S(2)}) copy-start(bf16[1536]{0:T(1024)(128)(2,1)} %param.17) | copy-start | bytes 9220
  136.7 24.9 %all-to-all-start.2 = ((bf16[8,16,2560]{2,1,0:T(8,128)(2,1)}), bf16[8,16,2560]{2,1,0:T(8,128)(2,1)S(1)}, u32[]{:S(2)}, u32[]{:S(2)}) async-start(bf16[8,16,2560]{2,1,0:T(8,128)(2,1)} %bitcast.34), calls=%async_computation.3 | async-start | bytes 1310720 | tf_op jit(solution)/shard_map/all_to_all | solution.py:299
  141.8 24.6 %collective-permute-start.3 = (bf16[768,512]{1,0:T(8,128)(2,1)}, bf16[768,512]{1,0:T(8,128)(2,1)S(1)}, u32[]{:S(2)}, u32[]{:S(2)}) collective-permute-start(bf16[768,512]{1,0:T(8,128)(2,1)} %constant_dynamic-slice_fusion), channel_id=1, source_target_pairs={{0,1},{1,0},{2,3},{3,2},{4,5},{5,4},{6,7},{7,6},{8,9},{9,8},{10,11... | collective-permute-start | bytes 2359304 | tf_op jit(solution)/shard_map/ppermute | solution.py:33
  162.3 6.9 %collective-permute-start.2 = (bf16[16,1664]{1,0:T(8,128)(2,1)S(1)}, bf16[16,1664]{1,0:T(8,128)(2,1)S(1)}, u32[]{:S(2)}, u32[]{:S(2)}) collective-permute-start(bf16[16,1664]{1,0:T(8,128)(2,1)S(1)} %concatenate.11), channel_id=1, source_target_pairs={{0,0},{1,16},{2,32},{3,48},{4,64},{5,80},{6,96},{7,112},{8,128},{9... | collective-permute-start | bytes 159752 | tf_op jit(solution)/shard_map/ppermute | solution.py:263
  166.3 12.8 %collective-permute-start.4 = (bf16[768,512]{1,0:T(8,128)(2,1)S(1)}, bf16[768,512]{1,0:T(8,128)(2,1)}, u32[]{:S(2)}, u32[]{:S(2)}) collective-permute-start(bf16[768,512]{1,0:T(8,128)(2,1)S(1)} %collective-permute-done.3.mine_ref), channel_id=1, source_target_pairs={{0,16},{16,0},{1,17},{17,1},{2,18},{18,2},{3,19},{19,3},{4,20},{20... | collective-permute-start | bytes 2359304 | tf_op jit(solution)/shard_map/ppermute | solution.py:33
  169.3 0.8 copy-start.7
  170.1 20.6 %all-to-all-start.3 = ((bf16[8,16,1664]{2,1,0:T(8,128)(2,1)}), bf16[8,16,1664]{2,1,0:T(8,128)(2,1)S(1)}, u32[]{:S(2)}, u32[]{:S(2)}) async-start(bf16[8,16,1664]{2,1,0:T(8,128)(2,1)} %broadcast_in_dim.27), calls=%async_computation.4 | async-start | bytes 851968 | tf_op jit(solution)/shard_map/all_to_all | solution.py:311
  179.1 4.4 %collective-permute-start.5 = (bf16[16,768]{1,0:T(8,128)(2,1)}, bf16[16,768]{1,0:T(8,128)(2,1)S(1)}, u32[]{:S(2)}, u32[]{:S(2)}) collective-permute-start(bf16[16,768]{1,0:T(8,128)(2,1)} %reshape.71), channel_id=1, source_target_pairs={{0,1},{1,0},{2,3},{3,2},{4,5},{5,4},{6,7},{7,6},{8,9},{9,8},{10,11... | collective-permute-start | bytes 73736 | tf_op jit(solution)/shard_map/ppermute | solution.py:33
  193.2 13.7 %all-to-all-start.4 = ((bf16[8,10,16,128]{3,2,1,0:T(8,128)(2,1)}), bf16[8,10,16,128]{3,2,1,0:T(8,128)(2,1)S(1)}, u32[]{:S(2)}, u32[]{:S(2)}) async-start(bf16[8,10,16,128]{3,2,1,0:T(8,128)(2,1)} %shard_map.132), calls=%async_computation.5 | async-start | bytes 655360 | tf_op jit(solution)/shard_map/all_to_all | solution.py:315
  206.9 0.7 copy-start.4
  219.9 21.6 %all-to-all-start.5 = ((bf16[16,16,1024]{2,1,0:T(8,128)(2,1)}), bf16[16,16,1024]{2,1,0:T(8,128)(2,1)S(1)}, u32[]{:S(2)}, u32[]{:S(2)}) async-start(bf16[16,16,1024]{2,1,0:T(8,128)(2,1)} %shard_map.133), calls=%async_computation.6 | async-start | bytes 1048576 | tf_op jit(solution)/shard_map/all_to_all | solution.py:318
Sparse Core Ops, SparseCore 0:
  15.4 54.2 reduce-scatter.1
  71.5 52.2 all-gather.1

commit v8 on v7

--- a/solution.py
+++ b/solution.py
@@ -70,7 +70,7 @@
         product = product.astype(o_ref.dtype)
         for group in range(NZ):
             for half in range(2):
-                o_held[i, half ^ head_ref[1], group * 16 : (group + 1) * 16, :] = product[
+                o_held[i, half ^ (head_ref[0] % 2), group * 16 : (group + 1) * 16, :] = product[
                     group * 32 + half * 16 : group * 32 + (half + 1) * 16, :
                 ]
         store(i).start()
@@ -99,9 +99,9 @@
     )(head, attn_out, out_weight, residual)
 
 
-def lift_kernel(core_ref, kept_ref, got_ref, gain_ref, mine_ref, other_ref, o_ref):
+def lift_kernel(core_ref, kept_ref, got_ref, gain_ref, mine_ref, other_ref, hidden_ref, o_ref):
     hidden = (kept_ref[...].astype(jnp.float32) + got_ref[...].astype(jnp.float32)).astype(jnp.bfloat16)
-    o_ref[:, QL + 128 :] = hidden
+    hidden_ref[...] = hidden
     wide = hidden.astype(jnp.float32)
     squares = jnp.sum(wide * wide, axis=1, keepdims=True)
     high = squares.astype(jnp.bfloat16).astype(jnp.float32)
@@ -116,7 +116,7 @@
     lane = lax.broadcasted_iota(jnp.int32, (HALF, 128), 1)
     tail = jnp.where(lane == IHEADS, high, jnp.where(lane == IHEADS + 1, squares - high, 0.0))
     o_ref[:, :QL] = lifted[:, :QL].astype(jnp.bfloat16)
-    o_ref[:, QL : QL + 128] = jnp.where(lane < IHEADS, lifted[:, QL:], tail).astype(jnp.bfloat16)
+    o_ref[:, QL:] = jnp.where(lane < IHEADS, lifted[:, QL:], tail).astype(jnp.bfloat16)
 
 
 def lift(core, kept, got, gain, mine, other):
@@ -124,8 +124,11 @@
     return pl.pallas_call(
         lift_kernel,
         in_specs=[pl.BlockSpec(memory_space=pltpu.SMEM)] + [whole] * 5,
-        out_specs=whole,
-        out_shape=jax.ShapeDtypeStruct((HALF, QL + 128 + DZ), jnp.bfloat16),
+        out_specs=[whole, whole],
+        out_shape=[
+            jax.ShapeDtypeStruct((HALF, DZ), jnp.bfloat16),
+            jax.ShapeDtypeStruct((HALF, QL + 128), jnp.bfloat16),
+        ],
         compiler_params=kernel_params(),
     )(core, kept, got, gain, mine, other)
 
@@ -284,21 +287,22 @@
     own = rows // N_HEAD
     local = latent_weight.shape[1]
 
-    partial = project(jnp.stack([head, yh]).astype(jnp.int32), attn_out, out_weight, residual)
+    partial = project(jnp.stack([head]).astype(jnp.int32), attn_out, out_weight, residual)
     summed = lax.psum_scatter(partial, "z", scatter_dimension=0, tiled=False)
 
     depth = QL // 2
     weight_mine = swap(lax.dynamic_slice_in_dim(index_weight, c * depth, depth, 0), "yh")
     weight_theirs = swap(weight_mine, "c")
     down_mine, down_other = down_weight_rows(latent_weight, index_proj, c * 8 + x * 2 + yl)
-    summed, index_keys = lax.optimization_barrier((summed, index_keys))
+    summed, index_keys, down_mine, down_other = lax.optimization_barrier(
+        (summed, index_keys, down_mine, down_other)
+    )
     all_keys = lax.all_gather(index_keys, SEQ, axis=0, tiled=True)
     kept, got = summed[0], swap(summed[1], "yh")
     gain = lax.dynamic_slice_in_dim(norm_gain, z * DZ, DZ).reshape(1, DZ)
-    lifted = lift(jnp.stack([c]).astype(jnp.int32), kept, got, gain, down_mine, down_other)
+    hidden, lifted = lift(jnp.stack([c]).astype(jnp.int32), kept, got, gain, down_mine, down_other)
     parts = lax.all_to_all(lifted.reshape(NZ, own, lifted.shape[1]), "z", 0, 0)
-    hidden_rows = parts[:, :, QL + 128 :].transpose(1, 0, 2).reshape(own, D)
-    total = jnp.sum(parts[:, :, : QL + 128].astype(jnp.float32), axis=0)
+    total = jnp.sum(parts.astype(jnp.float32), axis=0)
     mean = (total[:, 1600:1601] + total[:, 1601:1602]) / D
     inverse = lax.rsqrt(mean + EPSILON)
     latent_raw = (total[:, :QL] * inverse).astype(jnp.bfloat16)
@@ -310,6 +314,10 @@
     beside = swap(give.reshape(own, NZ * local), "yh")
     everyone = lax.all_to_all(jnp.broadcast_to(turned[None], (NZ,) + turned.shape), "z", 0, 0)
     everyone = everyone.reshape(HALF, packed.shape[1])
+    everyone, hidden = lax.optimization_barrier((everyone, hidden))
+    all_hidden = lax.all_gather(hidden, "z", axis=0, tiled=False)
+    hidden_rows = lax.dynamic_slice_in_dim(all_hidden, z * own, own, 1)
+    hidden_rows = hidden_rows.transpose(1, 0, 2).reshape(own, D)
     place = jnp.stack([c, yh]).astype(jnp.int32)
     queries = make_queries(place, everyone, index_weight, weight_mine, weight_theirs, latent, beside)
     queries = lax.all_to_all(queries, "z", 0, 0)

time: 251 us -> 219 us (0.87)
  waiting for transfers between devices: 107 us -> 66.7 us
  blocking collectives: 50.2 us -> 68.6 us
  starting transfers between devices: 36.2 us -> 30 us
  local copies, waits for them, and re-layouts: 16 us -> 12.2 us
    reduce_scatter x1, waiting for transfers between devices: 54.3 us -> 2.57 us  [shards(): summed = lax.psum_scatter(partial, 'z', scatter_dimension=0, tiled=False)]
    all_to_all x0 -> x1, blocking collectives: none -> 24.2 us  [shards(): lax.all_to_all(jnp.broadcast_to(turned[None], (NZ,) + turned.shape), 'z',...]
    ppermute x5, waiting for transfers between devices: 9.31 us -> 32.3 us  [swap(): return lax.ppermute(values, axis, [(0, 1), (1, 0)])]
    all_to_all x1, blocking collectives: 32.6 us -> 20.4 us  [down_weight_rows(): lax.all_to_all(jnp.broadcast_to(wide[None], (8,) + wide.shape), ('x', 'yl...]
    all_to_all x1 -> x0, waiting for transfers between devices: 7.24 us -> none  [shards(): lax.all_to_all(jnp.broadcast_to(turned[None], (NZ,) + turned.shape), 'z',...]
    all_to_all x1 -> x0, starting transfers between devices: 6.49 us -> none  [shards(): lax.all_to_all(jnp.broadcast_to(turned[None], (NZ,) + turned.shape), 'z',...]
    all_to_all x1, blocking collectives: 17.7 us -> 24 us  [down_weight_rows(): lax.all_to_all(jnp.repeat(own, 2, axis=0), HEAD, 0, 0).transpose(1, 0, 2)]
    all_to_all x1, starting transfers between devices: 11.9 us -> 5.95 us  [shards(): scores = lax.all_to_all(scores, SEQ, 0, 0)]
  transfers between devices with their start and end apart: 12 -> 12, of which waited for: 8 -> 10; matrix products, arithmetic and copies ran while one was open for 5% -> 5% of each run, Pallas kernels for 1% -> 7%
where the time goes in v8:
time: 219 us; the launch traced here: 218 us
  blocking collectives  68.6 us (31%)
  waiting for transfers between devices  66.7 us (30%)
  starting transfers between devices  30 us (14%)
  Pallas kernels  24.8 us (11%)
  between operations  14.7 us (7%)
  local copies, waits for them, and re-layouts  12.2 us (6%)
    ppermute x5, waiting for transfers between devices, swap(): return lax.ppermute(values, axis, [(0, 1), (1, 0)])  32.3 us
    all_to_all x1, blocking collectives, shards(): lax.all_to_all(jnp.broadcast_to(turned[None], (NZ,) + turned.shape), 'z',...  24.2 us
    all_to_all x1, blocking collectives, down_weight_rows(): lax.all_to_all(jnp.repeat(own, 2, axis=0), HEAD, 0, 0).transpose(1, 0, 2)  24 us
    all_to_all x1, blocking collectives, down_weight_rows(): lax.all_to_all(jnp.broadcast_to(wide[None], (8,) + wide.shape), ('x', 'yl...  20.4 us
    all_to_all x1, waiting for transfers between devices, shards(): parts = lax.all_to_all(lifted.reshape(NZ, own, lifted.shape[1]), 'z', 0, 0)  13.8 us
    pallas_call x1, Pallas kernels, make_scores(): pl.pallas_call(score_kernel, grid=(N_SEQ // per_step,), in_specs=[pl.Bloc...  12.3 us
    all_to_all x1, waiting for transfers between devices, shards(): queries = lax.all_to_all(queries, 'z', 0, 0)  11 us
    ppermute x5, starting transfers between devices, swap(): return lax.ppermute(values, axis, [(0, 1), (1, 0)])  9.28 us
  transfers between devices with their start and end apart: 12, of which 10 were waited for; matrix products, arithmetic and copies ran while one was open for 5% of the time, Pallas kernels for 7%

profile of v8, /device:TPU:1, one launch (start us, length us, event | category | flops | bytes accessed | tf_op | source)
XLA Modules:
  0.0 217.9 jit_solution(10100026569506174771)
XLA Ops:
  7.2 7.4 %shard_map.130 = bf16[8,2,128,896]{3,2,1,0:T(8,128)(2,1)} custom-call(s32[1]{0:T(128)} %bitcast.1.head_ref, bf16[256,512]{1,0:T(8,128)(2,1)} %a_ref.1, bf16[512,7168]{1,0:T(8,128)(2,1)} %b_ref.1, bf16[16,7168]{1,0:T(8,128)(2,1)} %res_ref.1), custom_call_target="tpu_custom_call" | custom-call | tf_op jit(solution)/shard_map/pallas_call | solution.py:87
  16.8 24.0 %all_to_all.30 = bf16[16,56,100]{2,1,0:T(8,128)(2,1)S(1)} all-to-all(bf16[16,56,100]{2,1,0:T(8,128)(2,1)S(1)} %bitcast.41), channel_id=1, replica_groups=mesh['x'=4,'yl'=2,'c'=2,'z'=8,'yh'=2] {'z','yh'}, dimensions={0} | all-to-all | bytes 358400 | tf_op jit(solution)/shard_map/all_to_all | solution.py:249
  41.7 20.4 %all_to_all.31 = bf16[8,56,1664]{2,1,0:T(8,128)(2,1)S(1)} all-to-all(bf16[8,56,1664]{2,1,0:T(8,128)(2,1)S(1)} %broadcast_in_dim.12), channel_id=1, replica_groups=mesh['x'=4,'yl'=2,'c'=2,'z'=8,'yh'=2] {'x','yl'}, dimensions={0} | all-to-all | bytes 2981888 | tf_op jit(solution)/shard_map/all_to_all | solution.py:259
  62.1 5.1 %collective-permute-start = (bf16[448,1664]{1,0:T(8,128)(2,1)S(1)}, bf16[448,1664]{1,0:T(8,128)(2,1)S(1)}, u32[]{:S(2)}, u32[]{:S(2)}) collective-permute-start(bf16[448,1664]{1,0:T(8,128)(2,1)S(1)} %bitcast.33), channel_id=1, source_target_pairs={{0,16},{16,0},{1,17},{17,1},{2,18},{18,2},{3,19},{19,3},{4,20},{20... | collective-permute-start | bytes 4472840 | tf_op jit(solution)/shard_map/ppermute | solution.py:33
  67.3 2.9 %collective-permute-done.other_ref = bf16[448,1664]{1,0:T(8,128)(2,1)S(1)} collective-permute-done((bf16[448,1664]{1,0:T(8,128)(2,1)S(1)}, bf16[448,1664]{1,0:T(8,128)(2,1)S(1)}, u32[]{:S(2)}, u32[]{:S(2)}) %collective-permute-start) | collective-permute-done | bytes 1490976 | tf_op jit(solution)/shard_map/ppermute | solution.py:33
  70.2 2.6 %reduce-scatter.2.cloned.1.call-done = bf16[1,2,128,896]{3,2,1,0:T(8,128)(2,1)} async-done(((bf16[8,2,128,896]{3,2,1,0:T(8,128)(2,1)}), bf16[1,2,128,896]{3,2,1,0:T(8,128)(2,1)}) %reduce-scatter.2.cloned.1.call-update) | async-done | bytes 458768 | tf_op jit(solution)/shard_map/reduce_scatter | solution.py:291
  72.8 1.8 slice_bitcast_fusion
  74.6 2.7 %collective-permute-start.1 = (bf16[128,896]{1,0:T(8,128)(2,1)}, bf16[128,896]{1,0:T(8,128)(2,1)S(1)}, u32[]{:S(2)}, u32[]{:S(2)}) collective-permute-start(bf16[128,896]{1,0:T(8,128)(2,1)} %get-tuple-element.31), channel_id=1, source_target_pairs={{0,1},{1,0},{2,3},{3,2},{4,5},{5,4},{6,7},{7,6},{8,9},{9,8},{10,11... | collective-permute-start | bytes 688136 | tf_op jit(solution)/shard_map/ppermute | solution.py:33
  78.0 5.0 %collective-permute-done.1.got_ref = bf16[128,896]{1,0:T(8,128)(2,1)S(1)} collective-permute-done((bf16[128,896]{1,0:T(8,128)(2,1)}, bf16[128,896]{1,0:T(8,128)(2,1)S(1)}, u32[]{:S(2)}, u32[]{:S(2)}) %collective-permute-start.1) | collective-permute-done | bytes 229408 | tf_op jit(solution)/shard_map/ppermute | solution.py:33
  84.7 4.3 %all-to-all-start.2 = ((bf16[8,16,1664]{2,1,0:T(8,128)(2,1)}), bf16[8,16,1664]{2,1,0:T(8,128)(2,1)S(1)}, u32[]{:S(2)}, u32[]{:S(2)}) async-start(bf16[8,16,1664]{2,1,0:T(8,128)(2,1)} %bitcast.36), calls=%async_computation.3 | async-start | bytes 851968 | tf_op jit(solution)/shard_map/all_to_all | solution.py:304
  89.1 13.8 %all-to-all-done.2 = bf16[8,16,1664]{2,1,0:T(8,128)(2,1)S(1)} async-done(((bf16[8,16,1664]{2,1,0:T(8,128)(2,1)}), bf16[8,16,1664]{2,1,0:T(8,128)(2,1)S(1)}, u32[]{:S(2)}, u32[]{:S(2)}) %all-to-all-start.2) | async-done | bytes 426016 | tf_op jit(solution)/shard_map/all_to_all | solution.py:304
  103.7 7.0 %collective-permute-start.2 = (bf16[16,1664]{1,0:T(8,128)(2,1)S(1)}, bf16[16,1664]{1,0:T(8,128)(2,1)S(1)}, u32[]{:S(2)}, u32[]{:S(2)}) collective-permute-start(bf16[16,1664]{1,0:T(8,128)(2,1)S(1)} %concatenate.11), channel_id=1, source_target_pairs={{0,0},{1,16},{2,32},{3,48},{4,64},{5,80},{6,96},{7,112},{8,128},{9... | collective-permute-start | bytes 159752 | tf_op jit(solution)/shard_map/ppermute | solution.py:266
  110.6 2.2 %collective-permute-done.2 = bf16[16,1664]{1,0:T(8,128)(2,1)S(1)} collective-permute-done((bf16[16,1664]{1,0:T(8,128)(2,1)S(1)}, bf16[16,1664]{1,0:T(8,128)(2,1)S(1)}, u32[]{:S(2)}, u32[]{:S(2)}) %collective-permute-start.2) | collective-permute-done | bytes 53280 | tf_op jit(solution)/shard_map/ppermute | solution.py:266
  112.9 24.2 %all_to_all.32 = bf16[8,16,1664]{2,1,0:T(8,128)(2,1)S(1)} all-to-all(bf16[8,16,1664]{2,1,0:T(8,128)(2,1)S(1)} %broadcast_in_dim.27), channel_id=1, replica_groups=mesh['x'=4,'yl'=2,'c'=2,'z'=8,'yh'=2] {'z'}, dimensions={0} | all-to-all | bytes 851968 | tf_op jit(solution)/shard_map/all_to_all | solution.py:315
  137.3 20.2 %collective-permute-done.3.mine_ref = bf16[768,512]{1,0:T(8,128)(2,1)S(1)} collective-permute-done((bf16[768,512]{1,0:T(8,128)(2,1)S(1)}, bf16[768,512]{1,0:T(8,128)(2,1)S(1)}, u32[]{:S(2)}, u32[]{:S(2)}) %collective-permute-start.3) | collective-permute-done | bytes 786464 | tf_op jit(solution)/shard_map/ppermute | solution.py:33
  159.4 1.4 collective-permute-done.4.theirs_ref
  160.8 2.7 %collective-permute-done.5.beside_ref = bf16[16,768]{1,0:T(8,128)(2,1)S(1)} collective-permute-done((bf16[16,768]{1,0:T(8,128)(2,1)S(1)}, bf16[16,768]{1,0:T(8,128)(2,1)S(1)}, u32[]{:S(2)}, u32[]{:S(2)}) %collective-permute-start.5) | collective-permute-done | bytes 24608 | tf_op jit(solution)/shard_map/ppermute | solution.py:33
  163.5 2.5 %shard_map.132 = bf16[8,10,16,128]{3,2,1,0:T(8,128)(2,1)} custom-call(s32[2]{0:T(128)S(1)} %pad_add_fusion.place_ref, bf16[128,1664]{1,0:T(8,128)(2,1)S(1)} %bitcast.35, bf16[1536,512]{1,0:T(8,128)(2,1)S(1)} %copy-done, bf16[768,512]{1,0:T(8,128)(2,1)S(1)} %collective-permute-done.3.mine_ref, bf16[768,512]{1,0:T(8,128)(2,1)} %collective-permute-done.4.theirs_ref, ...), custom_call_target="tpu_custom_call" | custom-call | tf_op jit(solution)/shard_map/pallas_call | solution.py:161
  166.0 3.4 %all-to-all-start.4 = ((bf16[8,10,16,128]{3,2,1,0:T(8,128)(2,1)}), bf16[8,10,16,128]{3,2,1,0:T(8,128)(2,1)S(1)}, u32[]{:S(2)}, u32[]{:S(2)}) async-start(bf16[8,10,16,128]{3,2,1,0:T(8,128)(2,1)} %shard_map.132), calls=%async_computation.5 | async-start | bytes 655360 | tf_op jit(solution)/shard_map/all_to_all | solution.py:323
  170.0 11.0 %all-to-all-done.4.q_ref = bf16[8,10,16,128]{3,2,1,0:T(8,128)(2,1)S(1)} async-done(((bf16[8,10,16,128]{3,2,1,0:T(8,128)(2,1)}), bf16[8,10,16,128]{3,2,1,0:T(8,128)(2,1)S(1)}, u32[]{:S(2)}, u32[]{:S(2)}) %all-to-all-start.4) | async-done | bytes 327712 | tf_op jit(solution)/shard_map/all_to_all | solution.py:323
  181.7 12.3 %shard_map.133 = bf16[16,16,1024]{2,1,0:T(8,128)(2,1)} custom-call(bf16[8,10,16,128]{3,2,1,0:T(8,128)(2,1)} %copy-done.2, bf16[16,128]{1,0:T(8,128)(2,1)} %slice.47.w_ref, bf16[16384,128]{1,0:T(8,128)(2,1)} %all-gather.4.cloned.1.call-done.k_ref), custom_call_target="tpu_custom_call" | custom-call | tf_op jit(solution)/shard_map/pallas_call | solution.py:204
  194.0 5.9 %all-to-all-start.5 = ((bf16[16,16,1024]{2,1,0:T(8,128)(2,1)}), bf16[16,16,1024]{2,1,0:T(8,128)(2,1)S(1)}, u32[]{:S(2)}, u32[]{:S(2)}) async-start(bf16[16,16,1024]{2,1,0:T(8,128)(2,1)} %shard_map.133), calls=%async_computation.6 | async-start | bytes 1048576 | tf_op jit(solution)/shard_map/all_to_all | solution.py:326
  204.8 4.8 %all-to-all-done.5.s_ref = bf16[16,16,1024]{2,1,0:T(8,128)(2,1)S(1)} async-done(((bf16[16,16,1024]{2,1,0:T(8,128)(2,1)}), bf16[16,16,1024]{2,1,0:T(8,128)(2,1)S(1)}, u32[]{:S(2)}, u32[]{:S(2)}) %all-to-all-start.5) | async-done | bytes 524320 | tf_op jit(solution)/shard_map/all_to_all | solution.py:326
  209.6 1.7 shard_map.134
  (64 shorter events, 13.8 us)
Async XLA Ops:
  7.2 65.6 %reduce-scatter.2.cloned.1.call-start = ((), (), s32[]{:S(2)}) async-start(), calls=%async_computation.7 | async-start | bytes 4128768 | tf_op jit(solution)/shard_map/reduce_scatter | solution.py:291
  14.7 0.8 copy-start.4
  14.7 1.4 copy-start.3
  14.7 166.3 %all-gather.4.cloned.1.call-start = ((), (), s32[]{:S(2)}) async-start(), calls=%async_computation.8 | async-start | bytes 4456448 | tf_op jit(solution)/shard_map/all_gather | solution.py:300
  62.1 8.1 %collective-permute-start = (bf16[448,1664]{1,0:T(8,128)(2,1)S(1)}, bf16[448,1664]{1,0:T(8,128)(2,1)S(1)}, u32[]{:S(2)}, u32[]{:S(2)}) collective-permute-start(bf16[448,1664]{1,0:T(8,128)(2,1)S(1)} %bitcast.33), channel_id=1, source_target_pairs={{0,16},{16,0},{1,17},{17,1},{2,18},{18,2},{3,19},{19,3},{4,20},{20... | collective-permute-start | bytes 4472840 | tf_op jit(solution)/shard_map/ppermute | solution.py:33
  74.6 8.5 %collective-permute-start.1 = (bf16[128,896]{1,0:T(8,128)(2,1)}, bf16[128,896]{1,0:T(8,128)(2,1)S(1)}, u32[]{:S(2)}, u32[]{:S(2)}) collective-permute-start(bf16[128,896]{1,0:T(8,128)(2,1)} %get-tuple-element.31), channel_id=1, source_target_pairs={{0,1},{1,0},{2,3},{3,2},{4,5},{5,4},{6,7},{7,6},{8,9},{9,8},{10,11... | collective-permute-start | bytes 688136 | tf_op jit(solution)/shard_map/ppermute | solution.py:33
  83.1 6.0 %copy-start.5 = (bf16[1536]{0:T(1024)(128)(2,1)S(1)}, bf16[1536]{0:T(1024)(128)(2,1)}, u32[]{:S(2)}) copy-start(bf16[1536]{0:T(1024)(128)(2,1)} %param.17) | copy-start | bytes 9220
  84.0 0.8 copy-start.1
  84.7 52.4 %copy-start = (bf16[1536,512]{1,0:T(8,128)(2,1)S(1)}, bf16[1536,512]{1,0:T(8,128)(2,1)}, u32[]{:S(2)}) copy-start(bf16[1536,512]{1,0:T(8,128)(2,1)} %own_ref.1) | copy-start | bytes 4718596
  84.7 18.2 %all-to-all-start.2 = ((bf16[8,16,1664]{2,1,0:T(8,128)(2,1)}), bf16[8,16,1664]{2,1,0:T(8,128)(2,1)S(1)}, u32[]{:S(2)}, u32[]{:S(2)}) async-start(bf16[8,16,1664]{2,1,0:T(8,128)(2,1)} %bitcast.36), calls=%async_computation.3 | async-start | bytes 851968 | tf_op jit(solution)/shard_map/all_to_all | solution.py:304
  89.0 114.1 %all-gather.6.cloned.1.call-start = ((), (), s32[]{:S(2)}) async-start(), calls=%async_computation.9 | async-start | bytes 2064384 | tf_op jit(solution)/shard_map/all_gather | solution.py:318
  103.7 9.2 %collective-permute-start.2 = (bf16[16,1664]{1,0:T(8,128)(2,1)S(1)}, bf16[16,1664]{1,0:T(8,128)(2,1)S(1)}, u32[]{:S(2)}, u32[]{:S(2)}) collective-permute-start(bf16[16,1664]{1,0:T(8,128)(2,1)S(1)} %concatenate.11), channel_id=1, source_target_pairs={{0,0},{1,16},{2,32},{3,48},{4,64},{5,80},{6,96},{7,112},{8,128},{9... | collective-permute-start | bytes 159752 | tf_op jit(solution)/shard_map/ppermute | solution.py:266
  137.2 20.3 %collective-permute-start.3 = (bf16[768,512]{1,0:T(8,128)(2,1)S(1)}, bf16[768,512]{1,0:T(8,128)(2,1)S(1)}, u32[]{:S(2)}, u32[]{:S(2)}) collective-permute-start(bf16[768,512]{1,0:T(8,128)(2,1)S(1)} %constant_dynamic-slice_fusion), channel_id=1, source_target_pairs={{0,1},{1,0},{2,3},{3,2},{4,5},{5,4},{6,7},{7,6},{8,9},{9,8},{10,11... | collective-permute-start | bytes 2359304 | tf_op jit(solution)/shard_map/ppermute | solution.py:33
  157.5 3.3 %collective-permute-start.4 = (bf16[768,512]{1,0:T(8,128)(2,1)S(1)}, bf16[768,512]{1,0:T(8,128)(2,1)}, u32[]{:S(2)}, u32[]{:S(2)}) collective-permute-start(bf16[768,512]{1,0:T(8,128)(2,1)S(1)} %collective-permute-done.3.mine_ref), channel_id=1, source_target_pairs={{0,16},{16,0},{1,17},{17,1},{2,18},{18,2},{3,19},{19,3},{4,20},{20... | collective-permute-start | bytes 2359304 | tf_op jit(solution)/shard_map/ppermute | solution.py:33
  159.2 4.3 %collective-permute-start.5 = (bf16[16,768]{1,0:T(8,128)(2,1)S(1)}, bf16[16,768]{1,0:T(8,128)(2,1)S(1)}, u32[]{:S(2)}, u32[]{:S(2)}) collective-permute-start(bf16[16,768]{1,0:T(8,128)(2,1)S(1)} %reshape.71), channel_id=1, source_target_pairs={{0,1},{1,0},{2,3},{3,2},{4,5},{5,4},{6,7},{7,6},{8,9},{9,8},{10,11... | collective-permute-start | bytes 73736 | tf_op jit(solution)/shard_map/ppermute | solution.py:33
  166.0 15.0 %all-to-all-start.4 = ((bf16[8,10,16,128]{3,2,1,0:T(8,128)(2,1)}), bf16[8,10,16,128]{3,2,1,0:T(8,128)(2,1)S(1)}, u32[]{:S(2)}, u32[]{:S(2)}) async-start(bf16[8,10,16,128]{3,2,1,0:T(8,128)(2,1)} %shard_map.132), calls=%async_computation.5 | async-start | bytes 655360 | tf_op jit(solution)/shard_map/all_to_all | solution.py:323
  181.0 0.7 copy-start.2
  194.0 15.6 %all-to-all-start.5 = ((bf16[16,16,1024]{2,1,0:T(8,128)(2,1)}), bf16[16,16,1024]{2,1,0:T(8,128)(2,1)S(1)}, u32[]{:S(2)}, u32[]{:S(2)}) async-start(bf16[16,16,1024]{2,1,0:T(8,128)(2,1)} %shard_map.133), calls=%async_computation.6 | async-start | bytes 1048576 | tf_op jit(solution)/shard_map/all_to_all | solution.py:326
Sparse Core Ops, SparseCore 0:
  14.8 57.9 reduce-scatter.1
  74.6 39.0 all-gather.3
  137.2 30.3 all-gather.5

commit v9 on v8

--- a/solution.py
+++ b/solution.py
@@ -23,12 +23,6 @@
 SLOTS = 1024
 
 
-def rms_round(values, gain):
-    widened = values.astype(jnp.float32)
-    inverse = lax.rsqrt(jnp.mean(widened * widened, axis=-1, keepdims=True) + EPSILON)
-    return (widened * inverse * gain.astype(jnp.float32)).astype(jnp.bfloat16)
-
-
 def swap(values, axis):
     return lax.ppermute(values, axis, [(0, 1), (1, 0)])
 
@@ -100,7 +94,7 @@
 
 
 def lift_kernel(core_ref, kept_ref, got_ref, gain_ref, mine_ref, other_ref, hidden_ref, o_ref):
-    hidden = (kept_ref[...].astype(jnp.float32) + got_ref[...].astype(jnp.float32)).astype(jnp.bfloat16)
+    hidden = (kept_ref[0].astype(jnp.float32) + got_ref[...].astype(jnp.float32)).astype(jnp.bfloat16)
     hidden_ref[...] = hidden
     wide = hidden.astype(jnp.float32)
     squares = jnp.sum(wide * wide, axis=1, keepdims=True)
@@ -131,6 +125,39 @@
         ],
         compiler_params=kernel_params(),
     )(core, kept, got, gain, mine, other)
+
+
+def norm_kernel(high_ref, parts_ref, gain_ref, o_ref, give_ref):
+    total = parts_ref[0].astype(jnp.float32)
+    for n in range(1, NZ):
+        total = total + parts_ref[n].astype(jnp.float32)
+    mean = (total[:, 1600:1601] + total[:, 1601:1602]) / D
+    inverse = lax.rsqrt(mean + EPSILON)
+    raw = (total[:, :QL] * inverse).astype(jnp.bfloat16).astype(jnp.float32)
+    level = lax.rsqrt(jnp.mean(raw * raw, axis=-1, keepdims=True) + EPSILON)
+    latent = (raw * level * gain_ref[...].astype(jnp.float32)).astype(jnp.bfloat16)
+    lane = lax.broadcasted_iota(jnp.int32, (16, 128), 1)
+    weights = jnp.where(lane < IHEADS, total[:, QL:] * inverse * IHEADS ** (-0.5), 0.0)
+    o_ref[:, :QL] = latent
+    o_ref[:, QL:] = weights.astype(jnp.bfloat16)
+    for block in range(NZ):
+        low = latent[:, block * 192 : block * 192 + 96]
+        top = latent[:, block * 192 + 96 : block * 192 + 192]
+        give_ref[:, block * 96 : (block + 1) * 96] = jnp.where(high_ref[0] == 0, top, low)
+
+
+def normalize(high, parts, gain):
+    whole = pl.BlockSpec(memory_space=pltpu.VMEM)
+    return pl.pallas_call(
+        norm_kernel,
+        in_specs=[pl.BlockSpec(memory_space=pltpu.SMEM), whole, whole],
+        out_specs=[whole, whole],
+        out_shape=[
+            jax.ShapeDtypeStruct((16, QL + 128), jnp.bfloat16),
+            jax.ShapeDtypeStruct((16, QL // 2), jnp.bfloat16),
+        ],
+        compiler_params=kernel_params(),
+    )(high, parts, gain)
 
 
 def query_kernel(place_ref, latent_ref, own_ref, mine_ref, theirs_ref, final_ref, beside_ref, o_ref):
@@ -239,7 +266,7 @@
     )(numbers, scores, own_positions)
 
 
-def down_weight_rows(latent_weight, index_proj, piece):
+def down_weight_rows(latent_weight, index_proj, piece, early):
     share = DZ // N_SEQ
 
     def own_rows(weight):
@@ -256,9 +283,10 @@
         ],
         axis=1,
     )
+    wide, early = lax.optimization_barrier((wide, early))
     half = lax.all_to_all(jnp.broadcast_to(wide[None], (8,) + wide.shape), ("x", "yl"), 0, 0)
     half = half.reshape(8 * share, wide.shape[1])
-    return half, swap(half, "c")
+    return half, swap(half, "c"), early
 
 
 def turn(values):
@@ -292,26 +320,20 @@
 
     depth = QL // 2
     weight_mine = swap(lax.dynamic_slice_in_dim(index_weight, c * depth, depth, 0), "yh")
+    down_mine, down_other, weight_mine = down_weight_rows(
+        latent_weight, index_proj, c * 8 + x * 2 + yl, weight_mine
+    )
     weight_theirs = swap(weight_mine, "c")
-    down_mine, down_other = down_weight_rows(latent_weight, index_proj, c * 8 + x * 2 + yl)
     summed, index_keys, down_mine, down_other = lax.optimization_barrier(
         (summed, index_keys, down_mine, down_other)
     )
     all_keys = lax.all_gather(index_keys, SEQ, axis=0, tiled=True)
-    kept, got = summed[0], swap(summed[1], "yh")
+    got = swap(summed[1], "yh")
     gain = lax.dynamic_slice_in_dim(norm_gain, z * DZ, DZ).reshape(1, DZ)
-    hidden, lifted = lift(jnp.stack([c]).astype(jnp.int32), kept, got, gain, down_mine, down_other)
+    hidden, lifted = lift(jnp.stack([c]).astype(jnp.int32), summed, got, gain, down_mine, down_other)
     parts = lax.all_to_all(lifted.reshape(NZ, own, lifted.shape[1]), "z", 0, 0)
-    total = jnp.sum(parts.astype(jnp.float32), axis=0)
-    mean = (total[:, 1600:1601] + total[:, 1601:1602]) / D
-    inverse = lax.rsqrt(mean + EPSILON)
-    latent_raw = (total[:, :QL] * inverse).astype(jnp.bfloat16)
-    head_weights = (total[:, QL:1600] * inverse * IHEADS ** (-0.5)).astype(jnp.bfloat16)
-    latent = rms_round(latent_raw, latent_gain)
-    packed = jnp.concatenate([latent, head_weights, jnp.zeros((own, 64), jnp.bfloat16)], axis=1)
-    turned = turn(packed)
-    give = lax.dynamic_index_in_dim(latent.reshape(own, NZ, 2, local), 1 - yh, 2, keepdims=False)
-    beside = swap(give.reshape(own, NZ * local), "yh")
+    packed, give = normalize(jnp.stack([yh]).astype(jnp.int32), parts, latent_gain.reshape(1, QL))
+    turned, beside = lax.optimization_barrier((turn(packed), swap(give, "yh")))
     everyone = lax.all_to_all(jnp.broadcast_to(turned[None], (NZ,) + turned.shape), "z", 0, 0)
     everyone = everyone.reshape(HALF, packed.shape[1])
     everyone, hidden = lax.optimization_barrier((everyone, hidden))
@@ -319,7 +341,7 @@
     hidden_rows = lax.dynamic_slice_in_dim(all_hidden, z * own, own, 1)
     hidden_rows = hidden_rows.transpose(1, 0, 2).reshape(own, D)
     place = jnp.stack([c, yh]).astype(jnp.int32)
-    queries = make_queries(place, everyone, index_weight, weight_mine, weight_theirs, latent, beside)
+    queries = make_queries(place, everyone, index_weight, weight_mine, weight_theirs, packed, beside)
     queries = lax.all_to_all(queries, "z", 0, 0)
     latent_out = queries[:, 8:, :, :local].reshape(rows, local)
     scores = make_scores(queries, turned[:, QL:], all_keys)

time: 219 us -> 203 us (0.927)
  waiting for transfers between devices: 66.7 us -> 48.6 us
  local copies, waits for them, and re-layouts: 12.2 us -> 18.9 us
  blocking collectives: 68.6 us -> 65.5 us
    ppermute x5, waiting for transfers between devices: 32.3 us -> 15.5 us  [swap(): return lax.ppermute(values, axis, [(0, 1), (1, 0)])]
    unnamed x16 -> x22, local copies, waits for them, and re-layouts: 4.67 us -> 10.8 us
    all_to_all x1, waiting for transfers between devices: 11 us -> 14.2 us  [shards(): queries = lax.all_to_all(queries, 'z', 0, 0)]
    all_to_all x1, blocking collectives: 24.2 us -> 21.6 us  [shards(): lax.all_to_all(jnp.broadcast_to(turned[None], (NZ,) + turned.shape), 'z',...]
    reduce_scatter x1, waiting for transfers between devices: 2.57 us -> 0.01 us  [shards(): summed = lax.psum_scatter(partial, 'z', scatter_dimension=0, tiled=False)]
    ppermute x5, starting transfers between devices: 9.28 us -> 11.8 us  [swap(): return lax.ppermute(values, axis, [(0, 1), (1, 0)])]
    ppermute x1, waiting for transfers between devices: 2.24 us -> 0.01 us  [turn(): return lax.ppermute(values, SEQ + HEAD, moves)]
  transfers between devices with their start and end apart: 12 -> 12, of which waited for: 10 -> 7; matrix products, arithmetic and copies ran while one was open for 5% -> 6% of each run, Pallas kernels for 7% -> 8%
where the time goes in v9:
time: 203 us; the launch traced here: 202 us
  blocking collectives  65.5 us (32%)
  waiting for transfers between devices  48.6 us (24%)
  starting transfers between devices  29 us (14%)
  Pallas kernels  25.3 us (12%)
  local copies, waits for them, and re-layouts  18.9 us (9%)
  between operations  14.6 us (7%)
    all_to_all x1, blocking collectives, down_weight_rows(): lax.all_to_all(jnp.repeat(own, 2, axis=0), HEAD, 0, 0).transpose(1, 0, 2)  22.8 us
    all_to_all x1, blocking collectives, shards(): lax.all_to_all(jnp.broadcast_to(turned[None], (NZ,) + turned.shape), 'z',...  21.6 us
    all_to_all x1, blocking collectives, down_weight_rows(): lax.all_to_all(jnp.broadcast_to(wide[None], (8,) + wide.shape), ('x', 'yl...  21.2 us
    ppermute x5, waiting for transfers between devices, swap(): return lax.ppermute(values, axis, [(0, 1), (1, 0)])  15.5 us
    all_to_all x1, waiting for transfers between devices, shards(): queries = lax.all_to_all(queries, 'z', 0, 0)  14.2 us
    all_to_all x1, waiting for transfers between devices, shards(): parts = lax.all_to_all(lifted.reshape(NZ, own, lifted.shape[1]), 'z', 0, 0)  14.1 us
    pallas_call x1, Pallas kernels, make_scores(): pl.pallas_call(score_kernel, grid=(N_SEQ // per_step,), in_specs=[pl.Bloc...  12.3 us
    ppermute x5, starting transfers between devices, swap(): return lax.ppermute(values, axis, [(0, 1), (1, 0)])  11.8 us
  transfers between devices with their start and end apart: 12, of which 7 were waited for; matrix products, arithmetic and copies ran while one was open for 6% of the time, Pallas kernels for 8%

profile of v9, /device:TPU:1, one launch (start us, length us, event | category | flops | bytes accessed | tf_op | source)
XLA Modules:
  0.0 202.2 jit_solution(16647771264342863385)
XLA Ops:
  7.2 7.4 %shard_map.130 = bf16[8,2,128,896]{3,2,1,0:T(8,128)(2,1)} custom-call(s32[1]{0:T(128)} %bitcast.2.head_ref, bf16[256,512]{1,0:T(8,128)(2,1)} %a_ref.1, bf16[512,7168]{1,0:T(8,128)(2,1)} %b_ref.1, bf16[16,7168]{1,0:T(8,128)(2,1)} %res_ref.1), custom_call_target="tpu_custom_call" | custom-call | tf_op jit(solution)/shard_map/pallas_call | solution.py:81
  17.0 3.8 %collective-permute-start = (bf16[768,512]{1,0:T(8,128)(2,1)}, bf16[768,512]{1,0:T(8,128)(2,1)S(1)}, u32[]{:S(2)}, u32[]{:S(2)}) collective-permute-start(bf16[768,512]{1,0:T(8,128)(2,1)} %constant_dynamic-slice_fusion), channel_id=1, source_target_pairs={{0,1},{1,0},{2,3},{3,2},{4,5},{5,4},{6,7},{7,6},{8,9},{9,8},{10,11... | collective-permute-start | bytes 2359304 | tf_op jit(solution)/shard_map/ppermute | solution.py:27
  20.8 2.7 %copy.36 = bf16[12,8,8,896]{3,2,1,0:T(8,128)(2,1)} copy(bf16[12,8,8,896]{3,1,2,0:T(8,128)(2,1)} %bitcast.39) | data formatting | bytes 2752512
  24.9 22.8 %all_to_all.30 = bf16[16,56,100]{2,1,0:T(8,128)(2,1)S(1)} all-to-all(bf16[16,56,100]{2,1,0:T(8,128)(2,1)S(1)} %bitcast.40), channel_id=1, replica_groups=mesh['x'=4,'yl'=2,'c'=2,'z'=8,'yh'=2] {'z','yh'}, dimensions={0} | all-to-all | bytes 358400 | tf_op jit(solution)/shard_map/all_to_all | solution.py:276
  49.5 21.2 %all_to_all.31 = bf16[8,56,1664]{2,1,0:T(8,128)(2,1)S(1)} all-to-all(bf16[8,56,1664]{2,1,0:T(8,128)(2,1)S(1)} %broadcast_in_dim.20), channel_id=1, replica_groups=mesh['x'=4,'yl'=2,'c'=2,'z'=8,'yh'=2] {'x','yl'}, dimensions={0} | all-to-all | bytes 2981888 | tf_op jit(solution)/shard_map/all_to_all | solution.py:287
  70.7 4.5 %collective-permute-start.1 = (bf16[448,1664]{1,0:T(8,128)(2,1)S(1)}, bf16[448,1664]{1,0:T(8,128)(2,1)S(1)}, u32[]{:S(2)}, u32[]{:S(2)}) collective-permute-start(bf16[448,1664]{1,0:T(8,128)(2,1)S(1)} %bitcast.31), channel_id=1, source_target_pairs={{0,16},{16,0},{1,17},{17,1},{2,18},{18,2},{3,19},{19,3},{4,20},{20... | collective-permute-start | bytes 4472840 | tf_op jit(solution)/shard_map/ppermute | solution.py:27
  75.2 2.9 %collective-permute-done.1.other_ref = bf16[448,1664]{1,0:T(8,128)(2,1)S(1)} collective-permute-done((bf16[448,1664]{1,0:T(8,128)(2,1)S(1)}, bf16[448,1664]{1,0:T(8,128)(2,1)S(1)}, u32[]{:S(2)}, u32[]{:S(2)}) %collective-permute-start.1) | collective-permute-done | bytes 1490976 | tf_op jit(solution)/shard_map/ppermute | solution.py:27
  82.1 6.6 %collective-permute-done.2.got_ref = bf16[128,896]{1,0:T(8,128)(2,1)S(1)} collective-permute-done((bf16[128,896]{1,0:T(8,128)(2,1)S(1)}, bf16[128,896]{1,0:T(8,128)(2,1)S(1)}, u32[]{:S(2)}, u32[]{:S(2)}) %collective-permute-start.2) | collective-permute-done | bytes 229408 | tf_op jit(solution)/shard_map/ppermute | solution.py:27
  88.6 1.4 copy-done.2
  91.0 1.6 shard_map.131
  92.6 3.6 %all-to-all-start.2 = ((bf16[8,16,1664]{2,1,0:T(8,128)(2,1)}), bf16[8,16,1664]{2,1,0:T(8,128)(2,1)S(1)}, u32[]{:S(2)}, u32[]{:S(2)}) async-start(bf16[8,16,1664]{2,1,0:T(8,128)(2,1)} %bitcast.9), calls=%async_computation.3 | async-start | bytes 851968 | tf_op jit(solution)/shard_map/all_to_all | solution.py:334
  96.3 14.1 %all-to-all-done.2.parts_ref = bf16[8,16,1664]{2,1,0:T(8,128)(2,1)S(1)} async-done(((bf16[8,16,1664]{2,1,0:T(8,128)(2,1)}), bf16[8,16,1664]{2,1,0:T(8,128)(2,1)S(1)}, u32[]{:S(2)}, u32[]{:S(2)}) %all-to-all-start.2) | async-done | bytes 426016 | tf_op jit(solution)/shard_map/all_to_all | solution.py:334
  110.8 4.9 %collective-permute-start.3 = (bf16[16,1664]{1,0:T(8,128)(2,1)S(1)}, bf16[16,1664]{1,0:T(8,128)(2,1)S(1)}, u32[]{:S(2)}, u32[]{:S(2)}) collective-permute-start(bf16[16,1664]{1,0:T(8,128)(2,1)S(1)} %get-tuple-element.22.final_ref), channel_id=1, source_target_pairs={{0,0},{1,16},{2,32},{3,48},{4,64},{5,80},{6,96},{7,112},{8,128},{9... | collective-permute-start | bytes 159752 | tf_op jit(solution)/shard_map/ppermute | solution.py:294
  115.8 4.2 %collective-permute-done.4.beside_ref = bf16[16,768]{1,0:T(8,128)(2,1)S(1)} collective-permute-done((bf16[16,768]{1,0:T(8,128)(2,1)S(1)}, bf16[16,768]{1,0:T(8,128)(2,1)S(1)}, u32[]{:S(2)}, u32[]{:S(2)}) %collective-permute-start.4) | collective-permute-done | bytes 24608 | tf_op jit(solution)/shard_map/ppermute | solution.py:27
  120.0 21.6 %all_to_all.32 = bf16[8,16,1664]{2,1,0:T(8,128)(2,1)S(1)} all-to-all(bf16[8,16,1664]{2,1,0:T(8,128)(2,1)S(1)} %broadcast_in_dim.21), channel_id=1, replica_groups=mesh['x'=4,'yl'=2,'c'=2,'z'=8,'yh'=2] {'z'}, dimensions={0} | all-to-all | bytes 851968 | tf_op jit(solution)/shard_map/all_to_all | solution.py:337
  141.6 2.3 %collective-permute-start.5 = (bf16[768,512]{1,0:T(8,128)(2,1)S(1)}, bf16[768,512]{1,0:T(8,128)(2,1)S(1)}, u32[]{:S(2)}, u32[]{:S(2)}) collective-permute-start(bf16[768,512]{1,0:T(8,128)(2,1)S(1)} %copy-done.5), channel_id=1, source_target_pairs={{0,16},{16,0},{1,17},{17,1},{2,18},{18,2},{3,19},{19,3},{4,20},{20... | collective-permute-start | bytes 2359304 | tf_op jit(solution)/shard_map/ppermute | solution.py:27
  144.0 1.8 collective-permute-done.5.theirs_ref
  145.9 1.9 shard_map.133
  147.8 3.4 %all-to-all-start.4 = ((bf16[8,10,16,128]{3,2,1,0:T(8,128)(2,1)}), bf16[8,10,16,128]{3,2,1,0:T(8,128)(2,1)S(1)}, u32[]{:S(2)}, u32[]{:S(2)}) async-start(bf16[8,10,16,128]{3,2,1,0:T(8,128)(2,1)} %shard_map.133), calls=%async_computation.5 | async-start | bytes 655360 | tf_op jit(solution)/shard_map/all_to_all | solution.py:345
  151.8 14.2 %all-to-all-done.4.q_ref = bf16[8,10,16,128]{3,2,1,0:T(8,128)(2,1)S(1)} async-done(((bf16[8,10,16,128]{3,2,1,0:T(8,128)(2,1)}), bf16[8,10,16,128]{3,2,1,0:T(8,128)(2,1)S(1)}, u32[]{:S(2)}, u32[]{:S(2)}) %all-to-all-start.4) | async-done | bytes 327712 | tf_op jit(solution)/shard_map/all_to_all | solution.py:345
  166.8 12.3 %shard_map.134 = bf16[16,16,1024]{2,1,0:T(8,128)(2,1)} custom-call(bf16[8,10,16,128]{3,2,1,0:T(8,128)(2,1)} %copy-done.6, bf16[16,128]{1,0:T(8,128)(2,1)} %slice.19.w_ref, bf16[16384,128]{1,0:T(8,128)(2,1)} %all-gather.4.cloned.1.call-done.k_ref), custom_call_target="tpu_custom_call" | custom-call | tf_op jit(solution)/shard_map/pallas_call | solution.py:231
  179.1 5.2 %all-to-all-start.5 = ((bf16[16,16,1024]{2,1,0:T(8,128)(2,1)}), bf16[16,16,1024]{2,1,0:T(8,128)(2,1)S(1)}, u32[]{:S(2)}, u32[]{:S(2)}) async-start(bf16[16,16,1024]{2,1,0:T(8,128)(2,1)} %shard_map.134), calls=%async_computation.6 | async-start | bytes 1048576 | tf_op jit(solution)/shard_map/all_to_all | solution.py:348
  189.2 4.7 %all-to-all-done.5.s_ref = bf16[16,16,1024]{2,1,0:T(8,128)(2,1)S(1)} async-done(((bf16[16,16,1024]{2,1,0:T(8,128)(2,1)}), bf16[16,16,1024]{2,1,0:T(8,128)(2,1)S(1)}, u32[]{:S(2)}, u32[]{:S(2)}) %all-to-all-start.5) | async-done | bytes 524320 | tf_op jit(solution)/shard_map/all_to_all | solution.py:348
  193.9 1.7 shard_map.135
  (60 shorter events, 16.8 us)
Async XLA Ops:
  7.2 72.1 %reduce-scatter.2.cloned.1.call-start = ((), (), s32[]{:S(2)}) async-start(), calls=%async_computation.7 | async-start | bytes 4128768 | tf_op jit(solution)/shard_map/reduce_scatter | solution.py:319
  14.6 1.4 copy-start
  14.7 6.1 %copy-start.7 = (bf16[7168,4]{0,1:T(4,128)(2,1)S(1)}, bf16[7168,4]{0,1:T(4,128)(2,1)}, u32[]{:S(2)}) copy-start(bf16[7168,4]{0,1:T(4,128)(2,1)} %param.16) | copy-start | bytes 172036
  14.7 151.4 %all-gather.4.cloned.1.call-start = ((), (), s32[]{:S(2)}) async-start(), calls=%async_computation.8 | async-start | bytes 4456448 | tf_op jit(solution)/shard_map/all_gather | solution.py:330
  17.0 31.6 %collective-permute-start = (bf16[768,512]{1,0:T(8,128)(2,1)}, bf16[768,512]{1,0:T(8,128)(2,1)S(1)}, u32[]{:S(2)}, u32[]{:S(2)}) collective-permute-start(bf16[768,512]{1,0:T(8,128)(2,1)} %constant_dynamic-slice_fusion), channel_id=1, source_target_pairs={{0,1},{1,0},{2,3},{3,2},{4,5},{5,4},{6,7},{7,6},{8,9},{9,8},{10,11... | collective-permute-start | bytes 2359304 | tf_op jit(solution)/shard_map/ppermute | solution.py:27
  48.5 0.9 copy-start.4
  70.7 7.4 %collective-permute-start.1 = (bf16[448,1664]{1,0:T(8,128)(2,1)S(1)}, bf16[448,1664]{1,0:T(8,128)(2,1)S(1)}, u32[]{:S(2)}, u32[]{:S(2)}) collective-permute-start(bf16[448,1664]{1,0:T(8,128)(2,1)S(1)} %bitcast.31), channel_id=1, source_target_pairs={{0,16},{16,0},{1,17},{17,1},{2,18},{18,2},{3,19},{19,3},{4,20},{20... | collective-permute-start | bytes 4472840 | tf_op jit(solution)/shard_map/ppermute | solution.py:27
  78.1 1.2 copy-start.1
  80.2 8.4 %collective-permute-start.2 = (bf16[128,896]{1,0:T(8,128)(2,1)S(1)}, bf16[128,896]{1,0:T(8,128)(2,1)S(1)}, u32[]{:S(2)}, u32[]{:S(2)}) collective-permute-start(bf16[128,896]{1,0:T(8,128)(2,1)S(1)} %slice_bitcast_fusion), channel_id=1, source_target_pairs={{0,1},{1,0},{2,3},{3,2},{4,5},{5,4},{6,7},{7,6},{8,9},{9,8},{10,11... | collective-permute-start | bytes 688136 | tf_op jit(solution)/shard_map/ppermute | solution.py:27
  88.6 1.4 copy-start.2
  90.0 1.0 copy-start.3
  91.0 5.3 %copy-start.8 = (bf16[1536]{0:T(1024)(128)(2,1)S(1)}, bf16[1536]{0:T(1024)(128)(2,1)}, u32[]{:S(2)}) copy-start(bf16[1536]{0:T(1024)(128)(2,1)} %param.17) | copy-start | bytes 9220
  92.6 49.0 %copy-start.5 = (bf16[768,512]{1,0:T(8,128)(2,1)S(1)}, bf16[768,512]{1,0:T(8,128)(2,1)}, u32[]{:S(2)}) copy-start(bf16[768,512]{1,0:T(8,128)(2,1)} %copy-done.4) | copy-start | bytes 2359300
  92.6 17.8 %all-to-all-start.2 = ((bf16[8,16,1664]{2,1,0:T(8,128)(2,1)}), bf16[8,16,1664]{2,1,0:T(8,128)(2,1)S(1)}, u32[]{:S(2)}, u32[]{:S(2)}) async-start(bf16[8,16,1664]{2,1,0:T(8,128)(2,1)} %bitcast.9), calls=%async_computation.3 | async-start | bytes 851968 | tf_op jit(solution)/shard_map/all_to_all | solution.py:334
  96.2 91.3 %all-gather.6.cloned.1.call-start = ((), (), s32[]{:S(2)}) async-start(), calls=%async_computation.9 | async-start | bytes 2064384 | tf_op jit(solution)/shard_map/all_gather | solution.py:340
  110.8 9.2 %collective-permute-start.3 = (bf16[16,1664]{1,0:T(8,128)(2,1)S(1)}, bf16[16,1664]{1,0:T(8,128)(2,1)S(1)}, u32[]{:S(2)}, u32[]{:S(2)}) collective-permute-start(bf16[16,1664]{1,0:T(8,128)(2,1)S(1)} %get-tuple-element.22.final_ref), channel_id=1, source_target_pairs={{0,0},{1,16},{2,32},{3,48},{4,64},{5,80},{6,96},{7,112},{8,128},{9... | collective-permute-start | bytes 159752 | tf_op jit(solution)/shard_map/ppermute | solution.py:294
  115.7 4.3 %collective-permute-start.4 = (bf16[16,768]{1,0:T(8,128)(2,1)S(1)}, bf16[16,768]{1,0:T(8,128)(2,1)S(1)}, u32[]{:S(2)}, u32[]{:S(2)}) collective-permute-start(bf16[16,768]{1,0:T(8,128)(2,1)S(1)} %get-tuple-element.23), channel_id=1, source_target_pairs={{0,1},{1,0},{2,3},{3,2},{4,5},{5,4},{6,7},{7,6},{8,9},{9,8},{10,11... | collective-permute-start | bytes 73736 | tf_op jit(solution)/shard_map/ppermute | solution.py:27
  141.6 4.2 %collective-permute-start.5 = (bf16[768,512]{1,0:T(8,128)(2,1)S(1)}, bf16[768,512]{1,0:T(8,128)(2,1)S(1)}, u32[]{:S(2)}, u32[]{:S(2)}) collective-permute-start(bf16[768,512]{1,0:T(8,128)(2,1)S(1)} %copy-done.5), channel_id=1, source_target_pairs={{0,16},{16,0},{1,17},{17,1},{2,18},{18,2},{3,19},{19,3},{4,20},{20... | collective-permute-start | bytes 2359304 | tf_op jit(solution)/shard_map/ppermute | solution.py:27
  147.8 18.3 %all-to-all-start.4 = ((bf16[8,10,16,128]{3,2,1,0:T(8,128)(2,1)}), bf16[8,10,16,128]{3,2,1,0:T(8,128)(2,1)S(1)}, u32[]{:S(2)}, u32[]{:S(2)}) async-start(bf16[8,10,16,128]{3,2,1,0:T(8,128)(2,1)} %shard_map.133), calls=%async_computation.5 | async-start | bytes 655360 | tf_op jit(solution)/shard_map/all_to_all | solution.py:345
  166.0 0.7 copy-start.6
  179.1 14.9 %all-to-all-start.5 = ((bf16[16,16,1024]{2,1,0:T(8,128)(2,1)}), bf16[16,16,1024]{2,1,0:T(8,128)(2,1)S(1)}, u32[]{:S(2)}, u32[]{:S(2)}) async-start(bf16[16,16,1024]{2,1,0:T(8,128)(2,1)} %shard_map.134), calls=%async_computation.6 | async-start | bytes 1048576 | tf_op jit(solution)/shard_map/all_to_all | solution.py:348
Sparse Core Ops, SparseCore 0:
  14.8 59.1 reduce-scatter.1
  79.4 35.5 all-gather.3
  141.7 36.6 all-gather.5

commit v10 on v9

--- a/solution.py
+++ b/solution.py
@@ -40,7 +40,8 @@
 
 
 def project_kernel(head_ref, a_ref, b_ref, res_ref, o_ref, b_held, o_held, in_sems, out_sems):
-    rows = a_ref.shape[0]
+    head = head_ref[0]
+    own = pl.ds(pl.multiple_of(head // 2 * 16, 16), 16)
 
     def fetch(i):
         columns = pl.ds(pl.multiple_of(i * DZ, 128), DZ)
@@ -51,22 +52,19 @@
 
     for i in range(NZ):
         fetch(i).start()
-    own = lax.broadcasted_iota(jnp.int32, (rows, 16), 1) + head_ref[0] * 16
-    place = lax.broadcasted_iota(jnp.int32, (rows, 16), 0) == own
-    place = jnp.where(place, 1.0, 0.0).astype(jnp.bfloat16)
-
     @pl.loop(0, NZ)
     def _(i):
         columns = pl.ds(pl.multiple_of(i * DZ, 128), DZ)
         fetch(i).wait()
         product = jnp.dot(a_ref[...], b_held[i], preferred_element_type=jnp.float32)
-        product = product + jnp.dot(place, res_ref[:, columns], preferred_element_type=jnp.float32)
         product = product.astype(o_ref.dtype)
         for group in range(NZ):
             for half in range(2):
-                o_held[i, half ^ (head_ref[0] % 2), group * 16 : (group + 1) * 16, :] = product[
+                o_held[i, half ^ (head % 2), group * 16 : (group + 1) * 16, :] = product[
                     group * 32 + half * 16 : group * 32 + (half + 1) * 16, :
                 ]
+        added = o_held[i, 0, own, :].astype(jnp.float32) + res_ref[:, columns].astype(jnp.float32)
+        o_held[i, 0, own, :] = added.astype(o_ref.dtype)
         store(i).start()
 
     for i in range(NZ):
@@ -94,7 +92,7 @@
 
 
 def lift_kernel(core_ref, kept_ref, got_ref, gain_ref, mine_ref, other_ref, hidden_ref, o_ref):
-    hidden = (kept_ref[0].astype(jnp.float32) + got_ref[...].astype(jnp.float32)).astype(jnp.bfloat16)
+    hidden = (kept_ref[...].astype(jnp.float32) + got_ref[...].astype(jnp.float32)).astype(jnp.bfloat16)
     hidden_ref[...] = hidden
     wide = hidden.astype(jnp.float32)
     squares = jnp.sum(wide * wide, axis=1, keepdims=True)
@@ -243,6 +241,9 @@
             pltpu.VMEM((IHEADS * 16, IDIM), jnp.bfloat16),
         ],
         compiler_params=big_params(),
+        cost_estimate=pl.CostEstimate(
+            flops=4 * IHEADS * 16 * keys.shape[0] * IDIM, bytes_accessed=2 * keys.size * 2, transcendentals=0
+        ),
     )(queries, head_weights, keys)
 
 
@@ -266,7 +267,7 @@
     )(numbers, scores, own_positions)
 
 
-def down_weight_rows(latent_weight, index_proj, piece, early):
+def down_weight_rows(latent_weight, index_proj, piece):
     share = DZ // N_SEQ
 
     def own_rows(weight):
@@ -283,10 +284,9 @@
         ],
         axis=1,
     )
-    wide, early = lax.optimization_barrier((wide, early))
     half = lax.all_to_all(jnp.broadcast_to(wide[None], (8,) + wide.shape), ("x", "yl"), 0, 0)
     half = half.reshape(8 * share, wide.shape[1])
-    return half, swap(half, "c"), early
+    return half, swap(half, "c")
 
 
 def turn(values):
@@ -318,33 +318,34 @@
     partial = project(jnp.stack([head]).astype(jnp.int32), attn_out, out_weight, residual)
     summed = lax.psum_scatter(partial, "z", scatter_dimension=0, tiled=False)
 
+    down_mine, down_other = down_weight_rows(latent_weight, index_proj, c * 8 + x * 2 + yl)
+    summed, index_keys, down_mine, down_other = lax.optimization_barrier(
+        (summed, index_keys, down_mine, down_other)
+    )
+    all_keys = lax.all_gather(index_keys, SEQ, axis=0, tiled=True)
+    kept, got = summed[0], swap(summed[1], "yh")
+    gain = lax.dynamic_slice_in_dim(norm_gain, z * DZ, DZ).reshape(1, DZ)
+    hidden, lifted = lift(jnp.stack([c]).astype(jnp.int32), kept, got, gain, down_mine, down_other)
+    lifted, index_weight = lax.optimization_barrier((lifted, index_weight))
+    parts = lax.all_to_all(lifted.reshape(NZ, own, lifted.shape[1]), "z", 0, 0)
     depth = QL // 2
     weight_mine = swap(lax.dynamic_slice_in_dim(index_weight, c * depth, depth, 0), "yh")
-    down_mine, down_other, weight_mine = down_weight_rows(
-        latent_weight, index_proj, c * 8 + x * 2 + yl, weight_mine
-    )
     weight_theirs = swap(weight_mine, "c")
-    summed, index_keys, down_mine, down_other = lax.optimization_barrier(
-        (summed, index_keys, down_mine, down_other)
-    )
-    all_keys = lax.all_gather(index_keys, SEQ, axis=0, tiled=True)
-    got = swap(summed[1], "yh")
-    gain = lax.dynamic_slice_in_dim(norm_gain, z * DZ, DZ).reshape(1, DZ)
-    hidden, lifted = lift(jnp.stack([c]).astype(jnp.int32), summed, got, gain, down_mine, down_other)
-    parts = lax.all_to_all(lifted.reshape(NZ, own, lifted.shape[1]), "z", 0, 0)
     packed, give = normalize(jnp.stack([yh]).astype(jnp.int32), parts, latent_gain.reshape(1, QL))
-    turned, beside = lax.optimization_barrier((turn(packed), swap(give, "yh")))
+    turned, beside, weight_mine, weight_theirs = lax.optimization_barrier(
+        (turn(packed), swap(give, "yh"), weight_mine, weight_theirs)
+    )
     everyone = lax.all_to_all(jnp.broadcast_to(turned[None], (NZ,) + turned.shape), "z", 0, 0)
     everyone = everyone.reshape(HALF, packed.shape[1])
-    everyone, hidden = lax.optimization_barrier((everyone, hidden))
-    all_hidden = lax.all_gather(hidden, "z", axis=0, tiled=False)
-    hidden_rows = lax.dynamic_slice_in_dim(all_hidden, z * own, own, 1)
-    hidden_rows = hidden_rows.transpose(1, 0, 2).reshape(own, D)
     place = jnp.stack([c, yh]).astype(jnp.int32)
     queries = make_queries(place, everyone, index_weight, weight_mine, weight_theirs, packed, beside)
     queries = lax.all_to_all(queries, "z", 0, 0)
     latent_out = queries[:, 8:, :, :local].reshape(rows, local)
+    queries, hidden = lax.optimization_barrier((queries, hidden))
+    hidden_rows = lax.all_to_all(hidden.reshape(NZ, own, DZ), "z", 0, 0)
     scores = make_scores(queries, turned[:, QL:], all_keys)
+    scores, hidden_rows = lax.optimization_barrier((scores, hidden_rows))
+    hidden_rows = hidden_rows.transpose(1, 0, 2).reshape(own, D)
     scores = lax.all_to_all(scores, SEQ, 0, 0)
 
     own_positions = lax.dynamic_slice_in_dim(positions, head * rows, rows).reshape(rows, 1)

time: 203 us -> 219 us (1.079)
  waiting for transfers between devices: 48.6 us -> 79 us
  blocking collectives: 65.5 us -> 44.4 us
  starting transfers between devices: 29 us -> 41.5 us
  local copies, waits for them, and re-layouts: 18.9 us -> 13.3 us
    ppermute x5, waiting for transfers between devices: 15.5 us -> 42.9 us  [swap(): return lax.ppermute(values, axis, [(0, 1), (1, 0)])]
    all_to_all x1 -> x0, blocking collectives: 21.6 us -> none  [shards(): lax.all_to_all(jnp.broadcast_to(turned[None], (NZ,) + turned.shape), 'z',...]
    all_to_all x0 -> x2, waiting for transfers between devices: none -> 15.8 us  [the longest x1 15.8 us: shards(): lax.all_to_all(jnp.broadcast_to(turned[None], (NZ,) + turned.shape), 'z',...]
    all_to_all x1, waiting for transfers between devices: 14.1 us -> 0.01 us  [shards(): parts = lax.all_to_all(lifted.reshape(NZ, own, lifted.shape[1]), 'z', 0, 0)]
    all_to_all x0 -> x2, starting transfers between devices: none -> 13.9 us  [the longest x1 10.5 us: shards(): lax.all_to_all(jnp.broadcast_to(turned[None], (NZ,) + turned.shape), 'z',...]
    unnamed x22 -> x19, local copies, waits for them, and re-layouts: 10.8 us -> 5.35 us
  transfers between devices with their start and end apart: 12 -> 13, of which waited for: 7 -> 8; matrix products, arithmetic and copies ran while one was open for 6% -> 4% of each run, Pallas kernels for 8% -> 7%
where the time goes in v10:
time: 219 us; the launch traced here: 218 us
  waiting for transfers between devices  79 us (36%)
  blocking collectives  44.4 us (20%)
  starting transfers between devices  41.5 us (19%)
  Pallas kernels  24.6 us (11%)
  between operations  14.9 us (7%)
  local copies, waits for them, and re-layouts  13.3 us (6%)
    ppermute x5, waiting for transfers between devices, swap(): return lax.ppermute(values, axis, [(0, 1), (1, 0)])  42.9 us
    all_to_all x1, blocking collectives, down_weight_rows(): lax.all_to_all(jnp.repeat(own, 2, axis=0), HEAD, 0, 0).transpose(1, 0, 2)  24 us
    all_to_all x1, blocking collectives, down_weight_rows(): lax.all_to_all(jnp.broadcast_to(wide[None], (8,) + wide.shape), ('x', 'yl...  20.4 us
    all_to_all x1, waiting for transfers between devices, shards(): lax.all_to_all(jnp.broadcast_to(turned[None], (NZ,) + turned.shape), 'z',...  15.8 us
    all_to_all x1, waiting for transfers between devices, shards(): queries = lax.all_to_all(queries, 'z', 0, 0)  13.1 us
    ppermute x5, starting transfers between devices, swap(): return lax.ppermute(values, axis, [(0, 1), (1, 0)])  12.8 us
    pallas_call x1, Pallas kernels, make_scores(): pl.pallas_call(score_kernel, grid=(N_SEQ // per_step,), in_specs=[pl.Bloc...  12.3 us
    all_to_all x1, starting transfers between devices, shards(): lax.all_to_all(jnp.broadcast_to(turned[None], (NZ,) + turned.shape), 'z',...  10.5 us
  transfers between devices with their start and end apart: 13, of which 8 were waited for; matrix products, arithmetic and copies ran while one was open for 4% of the time, Pallas kernels for 7%

profile of v10, /device:TPU:1, one launch (start us, length us, event | category | flops | bytes accessed | tf_op | source)
XLA Modules:
  0.0 217.8 jit_solution(9545464507449827673)
XLA Ops:
  7.2 6.7 %shard_map.130 = bf16[8,2,128,896]{3,2,1,0:T(8,128)(2,1)} custom-call(s32[1]{0:T(128)} %bitcast.2.head_ref, bf16[256,512]{1,0:T(8,128)(2,1)} %a_ref.1, bf16[512,7168]{1,0:T(8,128)(2,1)} %b_ref.1, bf16[16,7168]{1,0:T(8,128)(2,1)} %res_ref.1), custom_call_target="tpu_custom_call" | custom-call | tf_op jit(solution)/shard_map/pallas_call | solution.py:79
  16.1 24.0 %all_to_all.35 = bf16[16,56,100]{2,1,0:T(8,128)(2,1)S(1)} all-to-all(bf16[16,56,100]{2,1,0:T(8,128)(2,1)S(1)} %bitcast.41), channel_id=1, replica_groups=mesh['x'=4,'yl'=2,'c'=2,'z'=8,'yh'=2] {'z','yh'}, dimensions={0} | all-to-all | bytes 358400 | tf_op jit(solution)/shard_map/all_to_all | solution.py:277
  41.0 20.4 %all_to_all.36 = bf16[8,56,1664]{2,1,0:T(8,128)(2,1)S(1)} all-to-all(bf16[8,56,1664]{2,1,0:T(8,128)(2,1)S(1)} %broadcast_in_dim.20), channel_id=1, replica_groups=mesh['x'=4,'yl'=2,'c'=2,'z'=8,'yh'=2] {'x','yl'}, dimensions={0} | all-to-all | bytes 2981888 | tf_op jit(solution)/shard_map/all_to_all | solution.py:287
  61.5 5.1 %collective-permute-start = (bf16[448,1664]{1,0:T(8,128)(2,1)S(1)}, bf16[448,1664]{1,0:T(8,128)(2,1)S(1)}, u32[]{:S(2)}, u32[]{:S(2)}) collective-permute-start(bf16[448,1664]{1,0:T(8,128)(2,1)S(1)} %bitcast.32), channel_id=1, source_target_pairs={{0,16},{16,0},{1,17},{17,1},{2,18},{18,2},{3,19},{19,3},{4,20},{20... | collective-permute-start | bytes 4472840 | tf_op jit(solution)/shard_map/ppermute | solution.py:27
  66.6 2.9 %collective-permute-done.other_ref = bf16[448,1664]{1,0:T(8,128)(2,1)S(1)} collective-permute-done((bf16[448,1664]{1,0:T(8,128)(2,1)S(1)}, bf16[448,1664]{1,0:T(8,128)(2,1)S(1)}, u32[]{:S(2)}, u32[]{:S(2)}) %collective-permute-start) | collective-permute-done | bytes 1490976 | tf_op jit(solution)/shard_map/ppermute | solution.py:27
  70.7 1.4 reduce-scatter.2.cloned.1.call-done
  73.2 2.8 %collective-permute-start.1 = (bf16[128,896]{1,0:T(8,128)(2,1)S(1)}, bf16[128,896]{1,0:T(8,128)(2,1)S(1)}, u32[]{:S(2)}, u32[]{:S(2)}) collective-permute-start(bf16[128,896]{1,0:T(8,128)(2,1)S(1)} %get-tuple-element.51), channel_id=1, source_target_pairs={{0,1},{1,0},{2,3},{3,2},{4,5},{5,4},{6,7},{7,6},{8,9},{9,8},{10,11... | collective-permute-start | bytes 688136 | tf_op jit(solution)/shard_map/ppermute | solution.py:27
  76.8 4.8 %collective-permute-done.1.got_ref = bf16[128,896]{1,0:T(8,128)(2,1)S(1)} collective-permute-done((bf16[128,896]{1,0:T(8,128)(2,1)S(1)}, bf16[128,896]{1,0:T(8,128)(2,1)S(1)}, u32[]{:S(2)}, u32[]{:S(2)}) %collective-permute-start.1) | collective-permute-done | bytes 229408 | tf_op jit(solution)/shard_map/ppermute | solution.py:27
  85.4 2.7 %collective-permute-start.4 = (bf16[768,512]{1,0:T(8,128)(2,1)}, bf16[768,512]{1,0:T(8,128)(2,1)S(1)}, u32[]{:S(2)}, u32[]{:S(2)}) collective-permute-start(bf16[768,512]{1,0:T(8,128)(2,1)} %constant_dynamic-slice_fusion), channel_id=1, source_target_pairs={{0,1},{1,0},{2,3},{3,2},{4,5},{5,4},{6,7},{7,6},{8,9},{9,8},{10,11... | collective-permute-start | bytes 2359304 | tf_op jit(solution)/shard_map/ppermute | solution.py:27
  88.1 4.2 %all-to-all-start.2 = ((bf16[8,16,1664]{2,1,0:T(8,128)(2,1)}), bf16[8,16,1664]{2,1,0:T(8,128)(2,1)S(1)}, u32[]{:S(2)}, u32[]{:S(2)}) async-start(bf16[8,16,1664]{2,1,0:T(8,128)(2,1)} %bitcast.35), calls=%async_computation.3 | async-start | bytes 851968 | tf_op jit(solution)/shard_map/all_to_all | solution.py:330
  92.3 30.5 %collective-permute-done.4.mine_ref = bf16[768,512]{1,0:T(8,128)(2,1)S(1)} collective-permute-done((bf16[768,512]{1,0:T(8,128)(2,1)}, bf16[768,512]{1,0:T(8,128)(2,1)S(1)}, u32[]{:S(2)}, u32[]{:S(2)}) %collective-permute-start.4) | collective-permute-done | bytes 786464 | tf_op jit(solution)/shard_map/ppermute | solution.py:27
  122.8 2.1 collective-permute-start.5
  125.3 3.1 %collective-permute-start.2 = (bf16[16,1664]{1,0:T(8,128)(2,1)S(1)}, bf16[16,1664]{1,0:T(8,128)(2,1)S(1)}, u32[]{:S(2)}, u32[]{:S(2)}) collective-permute-start(bf16[16,1664]{1,0:T(8,128)(2,1)S(1)} %get-tuple-element.26.final_ref), channel_id=1, source_target_pairs={{0,0},{1,16},{2,32},{3,48},{4,64},{5,80},{6,96},{7,112},{8,128},{9... | collective-permute-start | bytes 159752 | tf_op jit(solution)/shard_map/ppermute | solution.py:294
  128.5 4.7 %collective-permute-done.3.beside_ref = bf16[16,768]{1,0:T(8,128)(2,1)S(1)} collective-permute-done((bf16[16,768]{1,0:T(8,128)(2,1)S(1)}, bf16[16,768]{1,0:T(8,128)(2,1)S(1)}, u32[]{:S(2)}, u32[]{:S(2)}) %collective-permute-start.3) | collective-permute-done | bytes 24608 | tf_op jit(solution)/shard_map/ppermute | solution.py:27
  134.0 10.5 %all-to-all-start.3 = ((bf16[8,16,1664]{2,1,0:T(8,128)(2,1)}), bf16[8,16,1664]{2,1,0:T(8,128)(2,1)S(1)}, u32[]{:S(2)}, u32[]{:S(2)}) async-start(bf16[8,16,1664]{2,1,0:T(8,128)(2,1)} %broadcast_in_dim.21), calls=%async_computation.4 | async-start | bytes 851968 | tf_op jit(solution)/shard_map/all_to_all | solution.py:338
  144.6 15.8 %all-to-all-done.3 = bf16[8,16,1664]{2,1,0:T(8,128)(2,1)S(1)} async-done(((bf16[8,16,1664]{2,1,0:T(8,128)(2,1)}), bf16[8,16,1664]{2,1,0:T(8,128)(2,1)S(1)}, u32[]{:S(2)}, u32[]{:S(2)}) %all-to-all-start.3) | async-done | bytes 426016 | tf_op jit(solution)/shard_map/all_to_all | solution.py:338
  160.4 2.5 %shard_map.133 = bf16[8,10,16,128]{3,2,1,0:T(8,128)(2,1)} custom-call(s32[2]{0:T(128)S(1)} %pad_add_fusion.place_ref, bf16[128,1664]{1,0:T(8,128)(2,1)S(1)} %bitcast.34, bf16[1536,512]{1,0:T(8,128)(2,1)S(1)} %copy-done, bf16[768,512]{1,0:T(8,128)(2,1)S(1)} %collective-permute-done.4.mine_ref, bf16[768,512]{1,0:T(8,128)(2,1)} %collective-permute-done.5.theirs_ref, ...), custom_call_target="tpu_custom_call" | custom-call | tf_op jit(solution)/shard_map/pallas_call | solution.py:186
  162.9 3.4 %all-to-all-start.4 = ((bf16[8,10,16,128]{3,2,1,0:T(8,128)(2,1)}), bf16[8,10,16,128]{3,2,1,0:T(8,128)(2,1)S(1)}, u32[]{:S(2)}, u32[]{:S(2)}) async-start(bf16[8,10,16,128]{3,2,1,0:T(8,128)(2,1)} %shard_map.133), calls=%async_computation.5 | async-start | bytes 655360 | tf_op jit(solution)/shard_map/all_to_all | solution.py:342
  166.9 13.1 %all-to-all-done.4.q_ref = bf16[8,10,16,128]{3,2,1,0:T(8,128)(2,1)S(1)} async-done(((bf16[8,10,16,128]{3,2,1,0:T(8,128)(2,1)}), bf16[8,10,16,128]{3,2,1,0:T(8,128)(2,1)S(1)}, u32[]{:S(2)}, u32[]{:S(2)}) %all-to-all-start.4) | async-done | bytes 327712 | tf_op jit(solution)/shard_map/all_to_all | solution.py:342
  180.0 3.4 %all-to-all-start.5 = ((bf16[8,16,896]{2,1,0:T(8,128)(2,1)}), bf16[8,16,896]{2,1,0:T(8,128)(2,1)S(1)}, u32[]{:S(2)}, u32[]{:S(2)}) async-start(bf16[8,16,896]{2,1,0:T(8,128)(2,1)} %bitcast.12), calls=%async_computation.6 | async-start | bytes 458752 | tf_op jit(solution)/shard_map/all_to_all | solution.py:345
  183.5 12.3 %shard_map.134 = bf16[16,16,1024]{2,1,0:T(8,128)(2,1)} custom-call(bf16[8,10,16,128]{3,2,1,0:T(8,128)(2,1)} %copy-done.5, bf16[16,128]{1,0:T(8,128)(2,1)} %slice.22.w_ref, bf16[16384,128]{1,0:T(8,128)(2,1)} %all-gather.2.cloned.1.call-done.k_ref), custom_call_target="tpu_custom_call" | custom-call | flops 8589934592 | bytes 8388608 | tf_op jit(solution)/shard_map/pallas_call | solution.py:229
  195.8 3.8 %all-to-all-start.6 = ((bf16[16,16,1024]{2,1,0:T(8,128)(2,1)}), bf16[16,16,1024]{2,1,0:T(8,128)(2,1)S(1)}, u32[]{:S(2)}, u32[]{:S(2)}) async-start(bf16[16,16,1024]{2,1,0:T(8,128)(2,1)} %shard_map.134), calls=%async_computation.7 | async-start | bytes 1048576 | tf_op jit(solution)/shard_map/all_to_all | solution.py:349
  203.5 5.8 %all-to-all-done.6.s_ref = bf16[16,16,1024]{2,1,0:T(8,128)(2,1)S(1)} async-done(((bf16[16,16,1024]{2,1,0:T(8,128)(2,1)}), bf16[16,16,1024]{2,1,0:T(8,128)(2,1)S(1)}, u32[]{:S(2)}, u32[]{:S(2)}) %all-to-all-start.6) | async-done | bytes 524320 | tf_op jit(solution)/shard_map/all_to_all | solution.py:349
  209.3 1.7 shard_map.135
  (57 shorter events, 15.0 us)
Async XLA Ops:
  7.2 64.9 %reduce-scatter.2.cloned.1.call-start = ((), (), s32[]{:S(2)}) async-start(), calls=%async_computation.8 | async-start | bytes 4128768 | tf_op jit(solution)/shard_map/reduce_scatter | solution.py:319
  14.0 0.8 copy-start.6
  14.0 1.4 copy-start.4
  14.0 169.4 %all-gather.2.cloned.1.call-start = ((), (), s32[]{:S(2)}) async-start(), calls=%async_computation.9 | async-start | bytes 4456448 | tf_op jit(solution)/shard_map/all_gather | solution.py:325
  61.5 8.1 %collective-permute-start = (bf16[448,1664]{1,0:T(8,128)(2,1)S(1)}, bf16[448,1664]{1,0:T(8,128)(2,1)S(1)}, u32[]{:S(2)}, u32[]{:S(2)}) collective-permute-start(bf16[448,1664]{1,0:T(8,128)(2,1)S(1)} %bitcast.32), channel_id=1, source_target_pairs={{0,16},{16,0},{1,17},{17,1},{2,18},{18,2},{3,19},{19,3},{4,20},{20... | collective-permute-start | bytes 4472840 | tf_op jit(solution)/shard_map/ppermute | solution.py:27
  69.5 1.1 copy-start.1
  73.2 8.4 %collective-permute-start.1 = (bf16[128,896]{1,0:T(8,128)(2,1)S(1)}, bf16[128,896]{1,0:T(8,128)(2,1)S(1)}, u32[]{:S(2)}, u32[]{:S(2)}) collective-permute-start(bf16[128,896]{1,0:T(8,128)(2,1)S(1)} %get-tuple-element.51), channel_id=1, source_target_pairs={{0,1},{1,0},{2,3},{3,2},{4,5},{5,4},{6,7},{7,6},{8,9},{9,8},{10,11... | collective-permute-start | bytes 688136 | tf_op jit(solution)/shard_map/ppermute | solution.py:27
  81.6 1.4 copy-start.2
  82.9 1.5 copy-start
  83.8 4.2 %copy-start.3 = (bf16[128,1664]{1,0:T(8,128)(2,1)}, bf16[128,1664]{1,0:T(8,128)(2,1)S(1)}, u32[]{:S(2)}) copy-start(bf16[128,1664]{1,0:T(8,128)(2,1)S(1)} %get-tuple-element.25) | copy-start | bytes 1277956
  83.8 41.0 %copy-start.7 = (bf16[1536]{0:T(1024)(128)(2,1)S(1)}, bf16[1536]{0:T(1024)(128)(2,1)}, u32[]{:S(2)}) copy-start(bf16[1536]{0:T(1024)(128)(2,1)} %param.17) | copy-start | bytes 9220
  85.4 37.4 %collective-permute-start.4 = (bf16[768,512]{1,0:T(8,128)(2,1)}, bf16[768,512]{1,0:T(8,128)(2,1)S(1)}, u32[]{:S(2)}, u32[]{:S(2)}) collective-permute-start(bf16[768,512]{1,0:T(8,128)(2,1)} %constant_dynamic-slice_fusion), channel_id=1, source_target_pairs={{0,1},{1,0},{2,3},{3,2},{4,5},{5,4},{6,7},{7,6},{8,9},{9,8},{10,11... | collective-permute-start | bytes 2359304 | tf_op jit(solution)/shard_map/ppermute | solution.py:27
  88.1 36.8 %all-to-all-start.2 = ((bf16[8,16,1664]{2,1,0:T(8,128)(2,1)}), bf16[8,16,1664]{2,1,0:T(8,128)(2,1)S(1)}, u32[]{:S(2)}, u32[]{:S(2)}) async-start(bf16[8,16,1664]{2,1,0:T(8,128)(2,1)} %bitcast.35), calls=%async_computation.3 | async-start | bytes 851968 | tf_op jit(solution)/shard_map/all_to_all | solution.py:330
  122.8 10.4 %collective-permute-start.5 = (bf16[768,512]{1,0:T(8,128)(2,1)S(1)}, bf16[768,512]{1,0:T(8,128)(2,1)}, u32[]{:S(2)}, u32[]{:S(2)}) collective-permute-start(bf16[768,512]{1,0:T(8,128)(2,1)S(1)} %collective-permute-done.4.mine_ref), channel_id=1, source_target_pairs={{0,16},{16,0},{1,17},{17,1},{2,18},{18,2},{3,19},{19,3},{4,20},{20... | collective-permute-start | bytes 2359304 | tf_op jit(solution)/shard_map/ppermute | solution.py:27
  125.3 7.9 %collective-permute-start.2 = (bf16[16,1664]{1,0:T(8,128)(2,1)S(1)}, bf16[16,1664]{1,0:T(8,128)(2,1)S(1)}, u32[]{:S(2)}, u32[]{:S(2)}) collective-permute-start(bf16[16,1664]{1,0:T(8,128)(2,1)S(1)} %get-tuple-element.26.final_ref), channel_id=1, source_target_pairs={{0,0},{1,16},{2,32},{3,48},{4,64},{5,80},{6,96},{7,112},{8,128},{9... | collective-permute-start | bytes 159752 | tf_op jit(solution)/shard_map/ppermute | solution.py:294
  128.4 4.8 %collective-permute-start.3 = (bf16[16,768]{1,0:T(8,128)(2,1)S(1)}, bf16[16,768]{1,0:T(8,128)(2,1)S(1)}, u32[]{:S(2)}, u32[]{:S(2)}) collective-permute-start(bf16[16,768]{1,0:T(8,128)(2,1)S(1)} %get-tuple-element.27), channel_id=1, source_target_pairs={{0,1},{1,0},{2,3},{3,2},{4,5},{5,4},{6,7},{7,6},{8,9},{9,8},{10,11... | collective-permute-start | bytes 73736 | tf_op jit(solution)/shard_map/ppermute | solution.py:27
  134.0 26.4 %all-to-all-start.3 = ((bf16[8,16,1664]{2,1,0:T(8,128)(2,1)}), bf16[8,16,1664]{2,1,0:T(8,128)(2,1)S(1)}, u32[]{:S(2)}, u32[]{:S(2)}) async-start(bf16[8,16,1664]{2,1,0:T(8,128)(2,1)} %broadcast_in_dim.21), calls=%async_computation.4 | async-start | bytes 851968 | tf_op jit(solution)/shard_map/all_to_all | solution.py:338
  162.9 17.1 %all-to-all-start.4 = ((bf16[8,10,16,128]{3,2,1,0:T(8,128)(2,1)}), bf16[8,10,16,128]{3,2,1,0:T(8,128)(2,1)S(1)}, u32[]{:S(2)}, u32[]{:S(2)}) async-start(bf16[8,10,16,128]{3,2,1,0:T(8,128)(2,1)} %shard_map.133), calls=%async_computation.5 | async-start | bytes 655360 | tf_op jit(solution)/shard_map/all_to_all | solution.py:342
  180.0 3.4 %copy-start.5 = (bf16[8,10,16,128]{3,2,1,0:T(8,128)(2,1)}, bf16[8,10,16,128]{3,2,1,0:T(8,128)(2,1)S(1)}, u32[]{:S(2)}) copy-start(bf16[8,10,16,128]{3,2,1,0:T(8,128)(2,1)S(1)} %all-to-all-done.4.q_ref) | copy-start | bytes 983044
  180.0 15.7 %all-to-all-start.5 = ((bf16[8,16,896]{2,1,0:T(8,128)(2,1)}), bf16[8,16,896]{2,1,0:T(8,128)(2,1)S(1)}, u32[]{:S(2)}, u32[]{:S(2)}) async-start(bf16[8,16,896]{2,1,0:T(8,128)(2,1)} %bitcast.12), calls=%async_computation.6 | async-start | bytes 458752 | tf_op jit(solution)/shard_map/all_to_all | solution.py:345
  195.8 13.5 %all-to-all-start.6 = ((bf16[16,16,1024]{2,1,0:T(8,128)(2,1)}), bf16[16,16,1024]{2,1,0:T(8,128)(2,1)S(1)}, u32[]{:S(2)}, u32[]{:S(2)}) async-start(bf16[16,16,1024]{2,1,0:T(8,128)(2,1)} %shard_map.134), calls=%async_computation.7 | async-start | bytes 1048576 | tf_op jit(solution)/shard_map/all_to_all | solution.py:349
Sparse Core Ops, SparseCore 0:
  14.1 57.9 reduce-scatter.1
  73.9 50.9 all-gather.1

commit v11 on v10

--- a/solution.py
+++ b/solution.py
@@ -39,9 +39,13 @@
     return pltpu.CompilerParams(vmem_limit_bytes=60 * 1024 * 1024)
 
 
-def project_kernel(head_ref, a_ref, b_ref, res_ref, o_ref, b_held, o_held, in_sems, out_sems):
-    head = head_ref[0]
+def project_kernel(place_ref, a_ref, b_ref, res_ref, w_ref, o_ref, half_ref, b_held, o_held, in_sems, out_sems, half_sem):
+    head, core = place_ref[0] // 2, place_ref[0] % 2
     own = pl.ds(pl.multiple_of(head // 2 * 16, 16), 16)
+    depth = half_ref.shape[0]
+    half_copy = pltpu.make_async_copy(
+        w_ref.at[pl.ds(pl.multiple_of(core * depth, 16), depth), :], half_ref, half_sem
+    )
 
     def fetch(i):
         columns = pl.ds(pl.multiple_of(i * DZ, 128), DZ)
@@ -52,6 +56,8 @@
 
     for i in range(NZ):
         fetch(i).start()
+    half_copy.start()
+
     @pl.loop(0, NZ)
     def _(i):
         columns = pl.ds(pl.multiple_of(i * DZ, 128), DZ)
@@ -69,31 +75,36 @@
 
     for i in range(NZ):
         store(i).wait()
-
-
-def project(head, attn_out, out_weight, residual):
+    half_copy.wait()
+
+
+def project(place, attn_out, out_weight, residual, index_weight):
     rows, depth = attn_out.shape
     whole = pl.BlockSpec(memory_space=pltpu.VMEM)
     apart = pl.BlockSpec(memory_space=pl.ANY)
     shape = (NZ, 2, HALF, DZ)
     return pl.pallas_call(
         project_kernel,
-        in_specs=[pl.BlockSpec(memory_space=pltpu.SMEM), whole, apart, whole],
-        out_specs=apart,
-        out_shape=jax.ShapeDtypeStruct(shape, jnp.bfloat16),
+        in_specs=[pl.BlockSpec(memory_space=pltpu.SMEM), whole, apart, whole, apart],
+        out_specs=[apart, apart],
+        out_shape=[
+            jax.ShapeDtypeStruct(shape, jnp.bfloat16),
+            jax.ShapeDtypeStruct((QL // 2, index_weight.shape[1]), jnp.bfloat16),
+        ],
         scratch_shapes=[
             pltpu.VMEM((NZ, depth, DZ), jnp.bfloat16),
             pltpu.VMEM(shape, jnp.bfloat16),
             pltpu.SemaphoreType.DMA((NZ,)),
             pltpu.SemaphoreType.DMA((NZ,)),
+            pltpu.SemaphoreType.DMA,
         ],
         compiler_params=big_params(),
-    )(head, attn_out, out_weight, residual)
-
-
-def lift_kernel(core_ref, kept_ref, got_ref, gain_ref, mine_ref, other_ref, hidden_ref, o_ref):
+    )(place, attn_out, out_weight, residual, index_weight)
+
+
+def lift_kernel(core_ref, kept_ref, got_ref, gain_ref, mine_ref, other_ref, o_ref):
     hidden = (kept_ref[...].astype(jnp.float32) + got_ref[...].astype(jnp.float32)).astype(jnp.bfloat16)
-    hidden_ref[...] = hidden
+    o_ref[:, QL + 128 :] = hidden
     wide = hidden.astype(jnp.float32)
     squares = jnp.sum(wide * wide, axis=1, keepdims=True)
     high = squares.astype(jnp.bfloat16).astype(jnp.float32)
@@ -108,7 +119,7 @@
     lane = lax.broadcasted_iota(jnp.int32, (HALF, 128), 1)
     tail = jnp.where(lane == IHEADS, high, jnp.where(lane == IHEADS + 1, squares - high, 0.0))
     o_ref[:, :QL] = lifted[:, :QL].astype(jnp.bfloat16)
-    o_ref[:, QL:] = jnp.where(lane < IHEADS, lifted[:, QL:], tail).astype(jnp.bfloat16)
+    o_ref[:, QL : QL + 128] = jnp.where(lane < IHEADS, lifted[:, QL:], tail).astype(jnp.bfloat16)
 
 
 def lift(core, kept, got, gain, mine, other):
@@ -116,19 +127,18 @@
     return pl.pallas_call(
         lift_kernel,
         in_specs=[pl.BlockSpec(memory_space=pltpu.SMEM)] + [whole] * 5,
-        out_specs=[whole, whole],
-        out_shape=[
-            jax.ShapeDtypeStruct((HALF, DZ), jnp.bfloat16),
-            jax.ShapeDtypeStruct((HALF, QL + 128), jnp.bfloat16),
-        ],
+        out_specs=whole,
+        out_shape=jax.ShapeDtypeStruct((HALF, QL + 128 + DZ), jnp.bfloat16),
         compiler_params=kernel_params(),
     )(core, kept, got, gain, mine, other)
 
 
-def norm_kernel(high_ref, parts_ref, gain_ref, o_ref, give_ref):
-    total = parts_ref[0].astype(jnp.float32)
+def norm_kernel(high_ref, parts_ref, gain_ref, o_ref, give_ref, hidden_ref):
+    total = parts_ref[0, :, : QL + 128].astype(jnp.float32)
     for n in range(1, NZ):
-        total = total + parts_ref[n].astype(jnp.float32)
+        total = total + parts_ref[n, :, : QL + 128].astype(jnp.float32)
+    for n in range(NZ):
+        hidden_ref[:, n * DZ : (n + 1) * DZ] = parts_ref[n, :, QL + 128 :]
     mean = (total[:, 1600:1601] + total[:, 1601:1602]) / D
     inverse = lax.rsqrt(mean + EPSILON)
     raw = (total[:, :QL] * inverse).astype(jnp.bfloat16).astype(jnp.float32)
@@ -149,10 +159,11 @@
     return pl.pallas_call(
         norm_kernel,
         in_specs=[pl.BlockSpec(memory_space=pltpu.SMEM), whole, whole],
-        out_specs=[whole, whole],
+        out_specs=[whole] * 3,
         out_shape=[
             jax.ShapeDtypeStruct((16, QL + 128), jnp.bfloat16),
             jax.ShapeDtypeStruct((16, QL // 2), jnp.bfloat16),
+            jax.ShapeDtypeStruct((16, D), jnp.bfloat16),
         ],
         compiler_params=kernel_params(),
     )(high, parts, gain)
@@ -267,7 +278,7 @@
     )(numbers, scores, own_positions)
 
 
-def down_weight_rows(latent_weight, index_proj, piece):
+def down_weight_rows(latent_weight, index_proj, piece, early):
     share = DZ // N_SEQ
 
     def own_rows(weight):
@@ -284,9 +295,10 @@
         ],
         axis=1,
     )
+    wide, early = lax.optimization_barrier((wide, early))
     half = lax.all_to_all(jnp.broadcast_to(wide[None], (8,) + wide.shape), ("x", "yl"), 0, 0)
     half = half.reshape(8 * share, wide.shape[1])
-    return half, swap(half, "c")
+    return half, swap(half, "c"), early
 
 
 def turn(values):
@@ -315,37 +327,36 @@
     own = rows // N_HEAD
     local = latent_weight.shape[1]
 
-    partial = project(jnp.stack([head]).astype(jnp.int32), attn_out, out_weight, residual)
+    partial, half_weight = project(
+        jnp.stack([head * 2 + c]).astype(jnp.int32), attn_out, out_weight, residual, index_weight
+    )
     summed = lax.psum_scatter(partial, "z", scatter_dimension=0, tiled=False)
 
-    down_mine, down_other = down_weight_rows(latent_weight, index_proj, c * 8 + x * 2 + yl)
+    weight_mine = swap(half_weight, "yh")
+    down_mine, down_other, weight_mine = down_weight_rows(
+        latent_weight, index_proj, c * 8 + x * 2 + yl, weight_mine
+    )
+    weight_theirs = swap(weight_mine, "c")
     summed, index_keys, down_mine, down_other = lax.optimization_barrier(
         (summed, index_keys, down_mine, down_other)
     )
     all_keys = lax.all_gather(index_keys, SEQ, axis=0, tiled=True)
     kept, got = summed[0], swap(summed[1], "yh")
     gain = lax.dynamic_slice_in_dim(norm_gain, z * DZ, DZ).reshape(1, DZ)
-    hidden, lifted = lift(jnp.stack([c]).astype(jnp.int32), kept, got, gain, down_mine, down_other)
-    lifted, index_weight = lax.optimization_barrier((lifted, index_weight))
+    lifted = lift(jnp.stack([c]).astype(jnp.int32), kept, got, gain, down_mine, down_other)
+    lifted, weight_theirs = lax.optimization_barrier((lifted, weight_theirs))
     parts = lax.all_to_all(lifted.reshape(NZ, own, lifted.shape[1]), "z", 0, 0)
-    depth = QL // 2
-    weight_mine = swap(lax.dynamic_slice_in_dim(index_weight, c * depth, depth, 0), "yh")
-    weight_theirs = swap(weight_mine, "c")
-    packed, give = normalize(jnp.stack([yh]).astype(jnp.int32), parts, latent_gain.reshape(1, QL))
-    turned, beside, weight_mine, weight_theirs = lax.optimization_barrier(
-        (turn(packed), swap(give, "yh"), weight_mine, weight_theirs)
-    )
+    packed, give, hidden_rows = normalize(
+        jnp.stack([yh]).astype(jnp.int32), parts, latent_gain.reshape(1, QL)
+    )
+    turned, beside = lax.optimization_barrier((turn(packed), swap(give, "yh")))
     everyone = lax.all_to_all(jnp.broadcast_to(turned[None], (NZ,) + turned.shape), "z", 0, 0)
     everyone = everyone.reshape(HALF, packed.shape[1])
     place = jnp.stack([c, yh]).astype(jnp.int32)
     queries = make_queries(place, everyone, index_weight, weight_mine, weight_theirs, packed, beside)
     queries = lax.all_to_all(queries, "z", 0, 0)
     latent_out = queries[:, 8:, :, :local].reshape(rows, local)
-    queries, hidden = lax.optimization_barrier((queries, hidden))
-    hidden_rows = lax.all_to_all(hidden.reshape(NZ, own, DZ), "z", 0, 0)
     scores = make_scores(queries, turned[:, QL:], all_keys)
-    scores, hidden_rows = lax.optimization_barrier((scores, hidden_rows))
-    hidden_rows = hidden_rows.transpose(1, 0, 2).reshape(own, D)
     scores = lax.all_to_all(scores, SEQ, 0, 0)
 
     own_positions = lax.dynamic_slice_in_dim(positions, head * rows, rows).reshape(rows, 1)

time: 219 us -> 222 us (1.014)
  Pallas kernels: 24.6 us -> 45.3 us
  waiting for transfers between devices: 79 us -> 69 us
  starting transfers between devices: 41.5 us -> 35.7 us
  local copies, waits for them, and re-layouts: 13.3 us -> 10.9 us
    ppermute x5, waiting for transfers between devices: 42.9 us -> 12.9 us  [swap(): return lax.ppermute(values, axis, [(0, 1), (1, 0)])]
    all_to_all x1, waiting for transfers between devices: 0.01 us -> 20.7 us  [shards(): parts = lax.all_to_all(lifted.reshape(NZ, own, lifted.shape[1]), 'z', 0, 0)]
    pallas_call x1, Pallas kernels: 6.73 us -> 26.1 us  [project(): pl.pallas_call(project_kernel, in_specs=[pl.BlockSpec(memory_space=pltpu....]
    all_to_all x1 -> x0, starting transfers between devices: 3.4 us -> none  [shards(): hidden_rows = lax.all_to_all(hidden.reshape(NZ, own, DZ), 'z', 0, 0)]
    ppermute x5, starting transfers between devices: 12.8 us -> 10.3 us  [swap(): return lax.ppermute(values, axis, [(0, 1), (1, 0)])]
    unnamed x19 -> x17, local copies, waits for them, and re-layouts: 5.35 us -> 3.21 us
  transfers between devices with their start and end apart: 13 -> 12, of which waited for: 8 -> 7; matrix products, arithmetic and copies ran while one was open for 4% -> 4% of each run, Pallas kernels for 7% -> 2%
where the time goes in v11:
time: 222 us; the launch traced here: 221 us
  waiting for transfers between devices  69 us (31%)
  Pallas kernels  45.3 us (20%)
  blocking collectives  45 us (20%)
  starting transfers between devices  35.7 us (16%)
  between operations  14.9 us (7%)
  local copies, waits for them, and re-layouts  10.9 us (5%)
    pallas_call x1, Pallas kernels, project(): pl.pallas_call(project_kernel, in_specs=[pl.BlockSpec(memory_space=pltpu....  26.1 us
    all_to_all x1, blocking collectives, down_weight_rows(): lax.all_to_all(jnp.repeat(own, 2, axis=0), HEAD, 0, 0).transpose(1, 0, 2)  22.9 us
    all_to_all x1, blocking collectives, down_weight_rows(): lax.all_to_all(jnp.broadcast_to(wide[None], (8,) + wide.shape), ('x', 'yl...  22 us
    all_to_all x1, waiting for transfers between devices, shards(): parts = lax.all_to_all(lifted.reshape(NZ, own, lifted.shape[1]), 'z', 0, 0)  20.7 us
    all_to_all x1, waiting for transfers between devices, shards(): lax.all_to_all(jnp.broadcast_to(turned[None], (NZ,) + turned.shape), 'z',...  15.8 us
    all_to_all x1, waiting for transfers between devices, shards(): queries = lax.all_to_all(queries, 'z', 0, 0)  13.1 us
    ppermute x5, waiting for transfers between devices, swap(): return lax.ppermute(values, axis, [(0, 1), (1, 0)])  12.9 us
    pallas_call x1, Pallas kernels, make_scores(): pl.pallas_call(score_kernel, grid=(N_SEQ // per_step,), in_specs=[pl.Bloc...  12.3 us
  transfers between devices with their start and end apart: 12, of which 7 were waited for; matrix products, arithmetic and copies ran while one was open for 4% of the time, Pallas kernels for 2%

profile of v11, /device:TPU:1, one launch (start us, length us, event | category | flops | bytes accessed | tf_op | source)
XLA Modules:
  0.0 221.0 jit_solution(11462796308565280673)
XLA Ops:
  7.2 26.1 %shard_map.130 = (bf16[8,2,128,896]{3,2,1,0:T(8,128)(2,1)}, bf16[768,512]{1,0:T(8,128)(2,1)}) custom-call(s32[1]{0:T(128)} %bitcast.2.place_ref, bf16[256,512]{1,0:T(8,128)(2,1)} %a_ref.1, bf16[512,7168]{1,0:T(8,128)(2,1)} %b_ref.1, bf16[16,7168]{1,0:T(8,128)(2,1)} %res_ref.1, bf16[1536,512]{1,0:T(8,128)(2,1)} %own_ref.1), custom_call_target="tpu_custom_call" | custom-call | tf_op jit(solution)/shard_map/pallas_call | solution.py:86
  33.4 3.8 %collective-permute-start = (bf16[768,512]{1,0:T(8,128)(2,1)}, bf16[768,512]{1,0:T(8,128)(2,1)S(1)}, u32[]{:S(2)}, u32[]{:S(2)}) collective-permute-start(bf16[768,512]{1,0:T(8,128)(2,1)} %get-tuple-element.19), channel_id=1, source_target_pairs={{0,1},{1,0},{2,3},{3,2},{4,5},{5,4},{6,7},{7,6},{8,9},{9,8},{10,11... | collective-permute-start | bytes 2359304 | tf_op jit(solution)/shard_map/ppermute | solution.py:27
  39.4 22.9 %all_to_all.30 = bf16[16,56,100]{2,1,0:T(8,128)(2,1)S(1)} all-to-all(bf16[16,56,100]{2,1,0:T(8,128)(2,1)S(1)} %bitcast.35), channel_id=1, replica_groups=mesh['x'=4,'yl'=2,'c'=2,'z'=8,'yh'=2] {'z','yh'}, dimensions={0} | all-to-all | bytes 358400 | tf_op jit(solution)/shard_map/all_to_all | solution.py:288
  64.1 22.0 %all_to_all.31 = bf16[8,56,1664]{2,1,0:T(8,128)(2,1)S(1)} all-to-all(bf16[8,56,1664]{2,1,0:T(8,128)(2,1)S(1)} %broadcast_in_dim.20), channel_id=1, replica_groups=mesh['x'=4,'yl'=2,'c'=2,'z'=8,'yh'=2] {'x','yl'}, dimensions={0} | all-to-all | bytes 2981888 | tf_op jit(solution)/shard_map/all_to_all | solution.py:299
  86.1 3.7 %collective-permute-start.1 = (bf16[448,1664]{1,0:T(8,128)(2,1)S(1)}, bf16[448,1664]{1,0:T(8,128)(2,1)S(1)}, u32[]{:S(2)}, u32[]{:S(2)}) collective-permute-start(bf16[448,1664]{1,0:T(8,128)(2,1)S(1)} %bitcast.28), channel_id=1, source_target_pairs={{0,16},{16,0},{1,17},{17,1},{2,18},{18,2},{3,19},{19,3},{4,20},{20... | collective-permute-start | bytes 4472840 | tf_op jit(solution)/shard_map/ppermute | solution.py:27
  89.9 2.9 %collective-permute-done.1.other_ref = bf16[448,1664]{1,0:T(8,128)(2,1)S(1)} collective-permute-done((bf16[448,1664]{1,0:T(8,128)(2,1)S(1)}, bf16[448,1664]{1,0:T(8,128)(2,1)S(1)}, u32[]{:S(2)}, u32[]{:S(2)}) %collective-permute-start.1) | collective-permute-done | bytes 1490976 | tf_op jit(solution)/shard_map/ppermute | solution.py:27
  93.3 1.8 slice_bitcast_fusion
  95.1 2.2 collective-permute-start.2
  98.0 5.8 %collective-permute-done.2.got_ref = bf16[128,896]{1,0:T(8,128)(2,1)S(1)} collective-permute-done((bf16[128,896]{1,0:T(8,128)(2,1)}, bf16[128,896]{1,0:T(8,128)(2,1)S(1)}, u32[]{:S(2)}, u32[]{:S(2)}) %collective-permute-start.2) | collective-permute-done | bytes 229408 | tf_op jit(solution)/shard_map/ppermute | solution.py:27
  103.8 1.7 shard_map.131
  105.5 4.3 %all-to-all-start.2 = ((bf16[8,16,2560]{2,1,0:T(8,128)(2,1)}), bf16[8,16,2560]{2,1,0:T(8,128)(2,1)S(1)}, u32[]{:S(2)}, u32[]{:S(2)}) async-start(bf16[8,16,2560]{2,1,0:T(8,128)(2,1)} %bitcast.10), calls=%async_computation.3 | async-start | bytes 1310720 | tf_op jit(solution)/shard_map/all_to_all | solution.py:348
  109.8 20.7 %all-to-all-done.2.parts_ref = bf16[8,16,2560]{2,1,0:T(8,128)(2,1)S(1)} async-done(((bf16[8,16,2560]{2,1,0:T(8,128)(2,1)}), bf16[8,16,2560]{2,1,0:T(8,128)(2,1)S(1)}, u32[]{:S(2)}, u32[]{:S(2)}) %all-to-all-start.2) | async-done | bytes 655392 | tf_op jit(solution)/shard_map/all_to_all | solution.py:348
  130.6 1.0 shard_map.132
  131.6 4.9 %collective-permute-start.4 = (bf16[16,1664]{1,0:T(8,128)(2,1)S(1)}, bf16[16,1664]{1,0:T(8,128)(2,1)S(1)}, u32[]{:S(2)}, u32[]{:S(2)}) collective-permute-start(bf16[16,1664]{1,0:T(8,128)(2,1)S(1)} %get-tuple-element.27.final_ref), channel_id=1, source_target_pairs={{0,0},{1,16},{2,32},{3,48},{4,64},{5,80},{6,96},{7,112},{8,128},{9... | collective-permute-start | bytes 159752 | tf_op jit(solution)/shard_map/ppermute | solution.py:306
  136.6 4.2 %collective-permute-done.5.beside_ref = bf16[16,768]{1,0:T(8,128)(2,1)S(1)} collective-permute-done((bf16[16,768]{1,0:T(8,128)(2,1)S(1)}, bf16[16,768]{1,0:T(8,128)(2,1)S(1)}, u32[]{:S(2)}, u32[]{:S(2)}) %collective-permute-start.5) | collective-permute-done | bytes 24608 | tf_op jit(solution)/shard_map/ppermute | solution.py:27
  141.6 8.8 %all-to-all-start.3 = ((bf16[8,16,1664]{2,1,0:T(8,128)(2,1)}), bf16[8,16,1664]{2,1,0:T(8,128)(2,1)S(1)}, u32[]{:S(2)}, u32[]{:S(2)}) async-start(bf16[8,16,1664]{2,1,0:T(8,128)(2,1)} %broadcast_in_dim.21), calls=%async_computation.4 | async-start | bytes 851968 | tf_op jit(solution)/shard_map/all_to_all | solution.py:353
  150.5 15.8 %all-to-all-done.3 = bf16[8,16,1664]{2,1,0:T(8,128)(2,1)S(1)} async-done(((bf16[8,16,1664]{2,1,0:T(8,128)(2,1)}), bf16[8,16,1664]{2,1,0:T(8,128)(2,1)S(1)}, u32[]{:S(2)}, u32[]{:S(2)}) %all-to-all-start.3) | async-done | bytes 426016 | tf_op jit(solution)/shard_map/all_to_all | solution.py:353
  166.3 2.5 %shard_map.133 = bf16[8,10,16,128]{3,2,1,0:T(8,128)(2,1)} custom-call(s32[2]{0:T(128)S(1)} %pad_add_fusion.place_ref, bf16[128,1664]{1,0:T(8,128)(2,1)S(1)} %bitcast.30, bf16[1536,512]{1,0:T(8,128)(2,1)S(1)} %copy-done, bf16[768,512]{1,0:T(8,128)(2,1)S(1)} %copy-done.2, bf16[768,512]{1,0:T(8,128)(2,1)} %collective-permute-done.3.theirs_ref, ...), custom_call_target="tpu_custom_call" | custom-call | tf_op jit(solution)/shard_map/pallas_call | solution.py:197
  168.8 3.4 %all-to-all-start.4 = ((bf16[8,10,16,128]{3,2,1,0:T(8,128)(2,1)}), bf16[8,10,16,128]{3,2,1,0:T(8,128)(2,1)S(1)}, u32[]{:S(2)}, u32[]{:S(2)}) async-start(bf16[8,10,16,128]{3,2,1,0:T(8,128)(2,1)} %shard_map.133), calls=%async_computation.5 | async-start | bytes 655360 | tf_op jit(solution)/shard_map/all_to_all | solution.py:357
  172.9 13.1 %all-to-all-done.4.q_ref = bf16[8,10,16,128]{3,2,1,0:T(8,128)(2,1)S(1)} async-done(((bf16[8,10,16,128]{3,2,1,0:T(8,128)(2,1)}), bf16[8,10,16,128]{3,2,1,0:T(8,128)(2,1)S(1)}, u32[]{:S(2)}, u32[]{:S(2)}) %all-to-all-start.4) | async-done | bytes 327712 | tf_op jit(solution)/shard_map/all_to_all | solution.py:357
  186.7 12.3 %shard_map.134 = bf16[16,16,1024]{2,1,0:T(8,128)(2,1)} custom-call(bf16[8,10,16,128]{3,2,1,0:T(8,128)(2,1)} %copy-done.4, bf16[16,128]{1,0:T(8,128)(2,1)} %slice.23.w_ref, bf16[16384,128]{1,0:T(8,128)(2,1)} %all-gather.2.cloned.1.call-done.k_ref), custom_call_target="tpu_custom_call" | custom-call | flops 8589934592 | bytes 8388608 | tf_op jit(solution)/shard_map/pallas_call | solution.py:240
  198.9 3.8 %all-to-all-start.5 = ((bf16[16,16,1024]{2,1,0:T(8,128)(2,1)}), bf16[16,16,1024]{2,1,0:T(8,128)(2,1)S(1)}, u32[]{:S(2)}, u32[]{:S(2)}) async-start(bf16[16,16,1024]{2,1,0:T(8,128)(2,1)} %shard_map.134), calls=%async_computation.6 | async-start | bytes 1048576 | tf_op jit(solution)/shard_map/all_to_all | solution.py:360
  206.0 6.5 %all-to-all-done.5.s_ref = bf16[16,16,1024]{2,1,0:T(8,128)(2,1)S(1)} async-done(((bf16[16,16,1024]{2,1,0:T(8,128)(2,1)}), bf16[16,16,1024]{2,1,0:T(8,128)(2,1)S(1)}, u32[]{:S(2)}, u32[]{:S(2)}) %all-to-all-start.5) | async-done | bytes 524320 | tf_op jit(solution)/shard_map/all_to_all | solution.py:360
  212.5 1.7 shard_map.135
  (51 shorter events, 10.0 us)
Async XLA Ops:
  7.2 85.6 %reduce-scatter.2.cloned.1.call-start = ((), (), s32[]{:S(2)}) async-start(), calls=%async_computation.7 | async-start | bytes 4128768 | tf_op jit(solution)/shard_map/reduce_scatter | solution.py:333
  33.3 3.9 %copy-start.5 = (bf16[7168,4]{0,1:T(4,128)(2,1)S(1)}, bf16[7168,4]{0,1:T(4,128)(2,1)}, u32[]{:S(2)}) copy-start(bf16[7168,4]{0,1:T(4,128)(2,1)} %param.16) | copy-start | bytes 172036
  33.3 4.6 %copy-start.3 = (bf16[7168,96]{0,1:T(8,128)(2,1)S(1)}, bf16[7168,96]{0,1:T(8,128)(2,1)}, u32[]{:S(2)}) copy-start(bf16[7168,96]{0,1:T(8,128)(2,1)} %param.15) | copy-start | bytes 4128772
  33.4 152.6 %all-gather.2.cloned.1.call-start = ((), (), s32[]{:S(2)}) async-start(), calls=%async_computation.8 | async-start | bytes 4456448 | tf_op jit(solution)/shard_map/all_gather | solution.py:343
  33.4 29.7 %collective-permute-start = (bf16[768,512]{1,0:T(8,128)(2,1)}, bf16[768,512]{1,0:T(8,128)(2,1)S(1)}, u32[]{:S(2)}, u32[]{:S(2)}) collective-permute-start(bf16[768,512]{1,0:T(8,128)(2,1)} %get-tuple-element.19), channel_id=1, source_target_pairs={{0,1},{1,0},{2,3},{3,2},{4,5},{5,4},{6,7},{7,6},{8,9},{9,8},{10,11... | collective-permute-start | bytes 2359304 | tf_op jit(solution)/shard_map/ppermute | solution.py:27
  63.1 0.9 copy-start.1
  86.1 6.6 %collective-permute-start.1 = (bf16[448,1664]{1,0:T(8,128)(2,1)S(1)}, bf16[448,1664]{1,0:T(8,128)(2,1)S(1)}, u32[]{:S(2)}, u32[]{:S(2)}) collective-permute-start(bf16[448,1664]{1,0:T(8,128)(2,1)S(1)} %bitcast.28), channel_id=1, source_target_pairs={{0,16},{16,0},{1,17},{17,1},{2,18},{18,2},{3,19},{19,3},{4,20},{20... | collective-permute-start | bytes 4472840 | tf_op jit(solution)/shard_map/ppermute | solution.py:27
  92.8 12.7 %collective-permute-start.3 = (bf16[768,512]{1,0:T(8,128)(2,1)}, bf16[768,512]{1,0:T(8,128)(2,1)}, u32[]{:S(2)}, u32[]{:S(2)}) collective-permute-start(bf16[768,512]{1,0:T(8,128)(2,1)} %copy-done.1), channel_id=1, source_target_pairs={{0,16},{16,0},{1,17},{17,1},{2,18},{18,2},{3,19},{19,3},{4,20},{20... | collective-permute-start | bytes 2359304 | tf_op jit(solution)/shard_map/ppermute | solution.py:27
  95.1 8.8 %collective-permute-start.2 = (bf16[128,896]{1,0:T(8,128)(2,1)}, bf16[128,896]{1,0:T(8,128)(2,1)S(1)}, u32[]{:S(2)}, u32[]{:S(2)}) collective-permute-start(bf16[128,896]{1,0:T(8,128)(2,1)} %get-tuple-element.45), channel_id=1, source_target_pairs={{0,1},{1,0},{2,3},{3,2},{4,5},{5,4},{6,7},{7,6},{8,9},{9,8},{10,11... | collective-permute-start | bytes 688136 | tf_op jit(solution)/shard_map/ppermute | solution.py:27
  103.8 6.0 %copy-start.6 = (bf16[1536]{0:T(1024)(128)(2,1)S(1)}, bf16[1536]{0:T(1024)(128)(2,1)}, u32[]{:S(2)}) copy-start(bf16[1536]{0:T(1024)(128)(2,1)} %param.17) | copy-start | bytes 9220
  105.5 60.8 %copy-start = (bf16[1536,512]{1,0:T(8,128)(2,1)S(1)}, bf16[1536,512]{1,0:T(8,128)(2,1)}, u32[]{:S(2)}) copy-start(bf16[1536,512]{1,0:T(8,128)(2,1)} %own_ref.1) | copy-start | bytes 4718596
  105.5 60.8 %copy-start.2 = (bf16[768,512]{1,0:T(8,128)(2,1)S(1)}, bf16[768,512]{1,0:T(8,128)(2,1)}, u32[]{:S(2)}) copy-start(bf16[768,512]{1,0:T(8,128)(2,1)} %copy-done.1) | copy-start | bytes 2359300
  105.5 25.0 %all-to-all-start.2 = ((bf16[8,16,2560]{2,1,0:T(8,128)(2,1)}), bf16[8,16,2560]{2,1,0:T(8,128)(2,1)S(1)}, u32[]{:S(2)}, u32[]{:S(2)}) async-start(bf16[8,16,2560]{2,1,0:T(8,128)(2,1)} %bitcast.10), calls=%async_computation.3 | async-start | bytes 1310720 | tf_op jit(solution)/shard_map/all_to_all | solution.py:348
  131.6 9.2 %collective-permute-start.4 = (bf16[16,1664]{1,0:T(8,128)(2,1)S(1)}, bf16[16,1664]{1,0:T(8,128)(2,1)S(1)}, u32[]{:S(2)}, u32[]{:S(2)}) collective-permute-start(bf16[16,1664]{1,0:T(8,128)(2,1)S(1)} %get-tuple-element.27.final_ref), channel_id=1, source_target_pairs={{0,0},{1,16},{2,32},{3,48},{4,64},{5,80},{6,96},{7,112},{8,128},{9... | collective-permute-start | bytes 159752 | tf_op jit(solution)/shard_map/ppermute | solution.py:306
  136.5 4.3 %collective-permute-start.5 = (bf16[16,768]{1,0:T(8,128)(2,1)S(1)}, bf16[16,768]{1,0:T(8,128)(2,1)S(1)}, u32[]{:S(2)}, u32[]{:S(2)}) collective-permute-start(bf16[16,768]{1,0:T(8,128)(2,1)S(1)} %get-tuple-element.28), channel_id=1, source_target_pairs={{0,1},{1,0},{2,3},{3,2},{4,5},{5,4},{6,7},{7,6},{8,9},{9,8},{10,11... | collective-permute-start | bytes 73736 | tf_op jit(solution)/shard_map/ppermute | solution.py:27
  141.6 24.7 %all-to-all-start.3 = ((bf16[8,16,1664]{2,1,0:T(8,128)(2,1)}), bf16[8,16,1664]{2,1,0:T(8,128)(2,1)S(1)}, u32[]{:S(2)}, u32[]{:S(2)}) async-start(bf16[8,16,1664]{2,1,0:T(8,128)(2,1)} %broadcast_in_dim.21), calls=%async_computation.4 | async-start | bytes 851968 | tf_op jit(solution)/shard_map/all_to_all | solution.py:353
  168.8 17.1 %all-to-all-start.4 = ((bf16[8,10,16,128]{3,2,1,0:T(8,128)(2,1)}), bf16[8,10,16,128]{3,2,1,0:T(8,128)(2,1)S(1)}, u32[]{:S(2)}, u32[]{:S(2)}) async-start(bf16[8,10,16,128]{3,2,1,0:T(8,128)(2,1)} %shard_map.133), calls=%async_computation.5 | async-start | bytes 655360 | tf_op jit(solution)/shard_map/all_to_all | solution.py:357
  185.9 0.7 copy-start.4
  198.9 13.5 %all-to-all-start.5 = ((bf16[16,16,1024]{2,1,0:T(8,128)(2,1)}), bf16[16,16,1024]{2,1,0:T(8,128)(2,1)S(1)}, u32[]{:S(2)}, u32[]{:S(2)}) async-start(bf16[16,16,1024]{2,1,0:T(8,128)(2,1)} %shard_map.134), calls=%async_computation.6 | async-start | bytes 1048576 | tf_op jit(solution)/shard_map/all_to_all | solution.py:360
Sparse Core Ops, SparseCore 0:
  33.5 58.6 reduce-scatter.1
  94.1 39.2 all-gather.1

commit v12 on v11

--- a/solution.py
+++ b/solution.py
@@ -86,7 +86,7 @@
     return pl.pallas_call(
         project_kernel,
         in_specs=[pl.BlockSpec(memory_space=pltpu.SMEM), whole, apart, whole, apart],
-        out_specs=[apart, apart],
+        out_specs=[apart, whole],
         out_shape=[
             jax.ShapeDtypeStruct(shape, jnp.bfloat16),
             jax.ShapeDtypeStruct((QL // 2, index_weight.shape[1]), jnp.bfloat16),
@@ -183,13 +183,13 @@
         part = part.astype(jnp.bfloat16)
         for j in range(4):
             for block in range(NZ):
-                o_ref[block, at + j] = part[block * 16 : (block + 1) * 16, j * IDIM : (j + 1) * IDIM]
+                o_ref[NZ - 1 - block, at + j] = part[block * 16 : (block + 1) * 16, j * IDIM : (j + 1) * IDIM]
     o_ref[:, 8:] = jnp.zeros((NZ, 2, 16, IDIM), jnp.bfloat16)
     for block in range(NZ):
         low = final_ref[:, block * 192 : block * 192 + 96]
         top = final_ref[:, block * 192 + 96 : block * 192 + 192]
-        o_ref[block, 8 + high, :, :96] = jnp.where(high == 0, low, top)
-        o_ref[block, 9 - high, :, :96] = beside_ref[:, block * 96 : (block + 1) * 96]
+        o_ref[NZ - 1 - block, 8 + high, :, :96] = jnp.where(high == 0, low, top)
+        o_ref[NZ - 1 - block, 9 - high, :, :96] = beside_ref[:, block * 96 : (block + 1) * 96]
 
 
 def make_queries(place, latent, own, mine, theirs, final, beside):
@@ -212,7 +212,7 @@
         weights = w_ref[...].astype(jnp.float32) * scale
         for j in range(IHEADS):
             wide_ref[j * 16 : (j + 1) * 16, :] = jnp.broadcast_to(weights[:, j : j + 1], (16, 128))
-            rows_ref[j * 16 : (j + 1) * 16, :] = q_ref[j // 8, j % 8]
+            rows_ref[j * 16 : (j + 1) * 16, :] = q_ref[NZ - 1 - j // 8, j % 8]
 
     blocks, _, slots = o_ref.shape
     for block in range(blocks):
@@ -350,12 +350,12 @@
         jnp.stack([yh]).astype(jnp.int32), parts, latent_gain.reshape(1, QL)
     )
     turned, beside = lax.optimization_barrier((turn(packed), swap(give, "yh")))
-    everyone = lax.all_to_all(jnp.broadcast_to(turned[None], (NZ,) + turned.shape), "z", 0, 0)
-    everyone = everyone.reshape(HALF, packed.shape[1])
+    everyone = lax.all_to_all(jnp.broadcast_to(turned[None, :, :QL], (NZ, own, QL)), "z", 0, 0)
+    everyone = everyone.reshape(HALF, QL)
     place = jnp.stack([c, yh]).astype(jnp.int32)
     queries = make_queries(place, everyone, index_weight, weight_mine, weight_theirs, packed, beside)
-    queries = lax.all_to_all(queries, "z", 0, 0)
-    latent_out = queries[:, 8:, :, :local].reshape(rows, local)
+    queries = lax.all_to_all(queries, "z", 0, 0, axis_index_groups=[list(range(NZ))[::-1]])
+    latent_out = queries[::-1, 8:, :, :local].reshape(rows, local)
     scores = make_scores(queries, turned[:, QL:], all_keys)
     scores = lax.all_to_all(scores, SEQ, 0, 0)
 

time: 222 us -> 199 us (0.90)
  Pallas kernels: 45.3 us -> 26.8 us
  waiting for transfers between devices: 69 us -> 61.1 us
  starting transfers between devices: 35.7 us -> 38.6 us
    pallas_call x1, Pallas kernels: 26.1 us -> 7.6 us  [project(): pl.pallas_call(project_kernel, in_specs=[pl.BlockSpec(memory_space=pltpu....]
    all_to_all x2, waiting for transfers between devices: 28.9 us -> 20.9 us  [the longest x1 15 us: shards(): lax.all_to_all(jnp.broadcast_to(turned[None, :, :QL], (NZ, own, QL)), 'z'...]
    all_to_all x1, starting transfers between devices: 3.84 us -> 6.29 us  [shards(): scores = lax.all_to_all(scores, SEQ, 0, 0)]
  transfers between devices with their start and end apart: 12 -> 12, of which waited for: 7 -> 7; matrix products, arithmetic and copies ran while one was open for 4% -> 5% of each run, Pallas kernels for 2% -> 3%
where the time goes in v12:
time: 199 us; the launch traced here: 198 us
  waiting for transfers between devices  61.1 us (31%)
  blocking collectives  45 us (23%)
  starting transfers between devices  38.6 us (19%)
  Pallas kernels  26.8 us (13%)
  between operations  14.9 us (7%)
  local copies, waits for them, and re-layouts  10.9 us (5%)
    all_to_all x1, blocking collectives, down_weight_rows(): lax.all_to_all(jnp.repeat(own, 2, axis=0), HEAD, 0, 0).transpose(1, 0, 2)  22.9 us
    all_to_all x1, blocking collectives, down_weight_rows(): lax.all_to_all(jnp.broadcast_to(wide[None], (8,) + wide.shape), ('x', 'yl...  22 us
    all_to_all x1, waiting for transfers between devices, shards(): parts = lax.all_to_all(lifted.reshape(NZ, own, lifted.shape[1]), 'z', 0, 0)  20.7 us
    all_to_all x1, waiting for transfers between devices, shards(): lax.all_to_all(jnp.broadcast_to(turned[None, :, :QL], (NZ, own, QL)), 'z'...  15 us
    ppermute x5, waiting for transfers between devices, swap(): return lax.ppermute(values, axis, [(0, 1), (1, 0)])  13 us
    pallas_call x1, Pallas kernels, make_scores(): pl.pallas_call(score_kernel, grid=(N_SEQ // per_step,), in_specs=[pl.Bloc...  12.3 us
    ppermute x5, starting transfers between devices, swap(): return lax.ppermute(values, axis, [(0, 1), (1, 0)])  10.3 us
    all_to_all x1, starting transfers between devices, shards(): lax.all_to_all(jnp.broadcast_to(turned[None, :, :QL], (NZ, own, QL)), 'z'...  8.84 us
  transfers between devices with their start and end apart: 12, of which 7 were waited for; matrix products, arithmetic and copies ran while one was open for 5% of the time, Pallas kernels for 3%

profile of v12, /device:TPU:1, one launch (start us, length us, event | category | flops | bytes accessed | tf_op | source)
XLA Modules:
  0.0 197.5 jit_solution(10493514640551705088)
XLA Ops:
  7.2 7.6 %shard_map.130 = (bf16[8,2,128,896]{3,2,1,0:T(8,128)(2,1)}, bf16[768,512]{1,0:T(8,128)(2,1)}) custom-call(s32[1]{0:T(128)} %bitcast.2.place_ref, bf16[256,512]{1,0:T(8,128)(2,1)} %a_ref.1, bf16[512,7168]{1,0:T(8,128)(2,1)} %b_ref.1, bf16[16,7168]{1,0:T(8,128)(2,1)} %res_ref.1, bf16[1536,512]{1,0:T(8,128)(2,1)} %own_ref.1), custom_call_target="tpu_custom_call" | custom-call | tf_op jit(solution)/shard_map/pallas_call | solution.py:86
  14.9 3.8 %collective-permute-start = (bf16[768,512]{1,0:T(8,128)(2,1)}, bf16[768,512]{1,0:T(8,128)(2,1)S(1)}, u32[]{:S(2)}, u32[]{:S(2)}) collective-permute-start(bf16[768,512]{1,0:T(8,128)(2,1)} %get-tuple-element.19), channel_id=1, source_target_pairs={{0,1},{1,0},{2,3},{3,2},{4,5},{5,4},{6,7},{7,6},{8,9},{9,8},{10,11... | collective-permute-start | bytes 2359304 | tf_op jit(solution)/shard_map/ppermute | solution.py:27
  20.9 22.9 %all_to_all.30 = bf16[16,56,100]{2,1,0:T(8,128)(2,1)S(1)} all-to-all(bf16[16,56,100]{2,1,0:T(8,128)(2,1)S(1)} %bitcast.35), channel_id=1, replica_groups=mesh['x'=4,'yl'=2,'c'=2,'z'=8,'yh'=2] {'z','yh'}, dimensions={0} | all-to-all | bytes 358400 | tf_op jit(solution)/shard_map/all_to_all | solution.py:288
  45.6 22.0 %all_to_all.31 = bf16[8,56,1664]{2,1,0:T(8,128)(2,1)S(1)} all-to-all(bf16[8,56,1664]{2,1,0:T(8,128)(2,1)S(1)} %broadcast_in_dim.20), channel_id=1, replica_groups=mesh['x'=4,'yl'=2,'c'=2,'z'=8,'yh'=2] {'x','yl'}, dimensions={0} | all-to-all | bytes 2981888 | tf_op jit(solution)/shard_map/all_to_all | solution.py:299
  67.6 3.7 %collective-permute-start.1 = (bf16[448,1664]{1,0:T(8,128)(2,1)S(1)}, bf16[448,1664]{1,0:T(8,128)(2,1)S(1)}, u32[]{:S(2)}, u32[]{:S(2)}) collective-permute-start(bf16[448,1664]{1,0:T(8,128)(2,1)S(1)} %bitcast.28), channel_id=1, source_target_pairs={{0,16},{16,0},{1,17},{17,1},{2,18},{18,2},{3,19},{19,3},{4,20},{20... | collective-permute-start | bytes 4472840 | tf_op jit(solution)/shard_map/ppermute | solution.py:27
  71.4 2.9 %collective-permute-done.1.other_ref = bf16[448,1664]{1,0:T(8,128)(2,1)S(1)} collective-permute-done((bf16[448,1664]{1,0:T(8,128)(2,1)S(1)}, bf16[448,1664]{1,0:T(8,128)(2,1)S(1)}, u32[]{:S(2)}, u32[]{:S(2)}) %collective-permute-start.1) | collective-permute-done | bytes 1490976 | tf_op jit(solution)/shard_map/ppermute | solution.py:27
  74.8 1.8 slice_bitcast_fusion
  76.6 2.1 %collective-permute-start.2 = (bf16[128,896]{1,0:T(8,128)(2,1)}, bf16[128,896]{1,0:T(8,128)(2,1)S(1)}, u32[]{:S(2)}, u32[]{:S(2)}) collective-permute-start(bf16[128,896]{1,0:T(8,128)(2,1)} %get-tuple-element.45), channel_id=1, source_target_pairs={{0,1},{1,0},{2,3},{3,2},{4,5},{5,4},{6,7},{7,6},{8,9},{9,8},{10,11... | collective-permute-start | bytes 688136 | tf_op jit(solution)/shard_map/ppermute | solution.py:27
  79.5 5.9 %collective-permute-done.2.got_ref = bf16[128,896]{1,0:T(8,128)(2,1)S(1)} collective-permute-done((bf16[128,896]{1,0:T(8,128)(2,1)}, bf16[128,896]{1,0:T(8,128)(2,1)S(1)}, u32[]{:S(2)}, u32[]{:S(2)}) %collective-permute-start.2) | collective-permute-done | bytes 229408 | tf_op jit(solution)/shard_map/ppermute | solution.py:27
  85.3 1.7 shard_map.131
  87.0 4.3 %all-to-all-start.2 = ((bf16[8,16,2560]{2,1,0:T(8,128)(2,1)}), bf16[8,16,2560]{2,1,0:T(8,128)(2,1)S(1)}, u32[]{:S(2)}, u32[]{:S(2)}) async-start(bf16[8,16,2560]{2,1,0:T(8,128)(2,1)} %bitcast.10), calls=%async_computation.3 | async-start | bytes 1310720 | tf_op jit(solution)/shard_map/all_to_all | solution.py:348
  91.3 20.7 %all-to-all-done.2.parts_ref = bf16[8,16,2560]{2,1,0:T(8,128)(2,1)S(1)} async-done(((bf16[8,16,2560]{2,1,0:T(8,128)(2,1)}), bf16[8,16,2560]{2,1,0:T(8,128)(2,1)S(1)}, u32[]{:S(2)}, u32[]{:S(2)}) %all-to-all-start.2) | async-done | bytes 655392 | tf_op jit(solution)/shard_map/all_to_all | solution.py:348
  112.1 1.0 shard_map.132
  113.1 4.9 %collective-permute-start.4 = (bf16[16,1664]{1,0:T(8,128)(2,1)S(1)}, bf16[16,1664]{1,0:T(8,128)(2,1)S(1)}, u32[]{:S(2)}, u32[]{:S(2)}) collective-permute-start(bf16[16,1664]{1,0:T(8,128)(2,1)S(1)} %get-tuple-element.27.final_ref), channel_id=1, source_target_pairs={{0,0},{1,16},{2,32},{3,48},{4,64},{5,80},{6,96},{7,112},{8,128},{9... | collective-permute-start | bytes 159752 | tf_op jit(solution)/shard_map/ppermute | solution.py:306
  118.1 4.2 %collective-permute-done.5.beside_ref = bf16[16,768]{1,0:T(8,128)(2,1)S(1)} collective-permute-done((bf16[16,768]{1,0:T(8,128)(2,1)S(1)}, bf16[16,768]{1,0:T(8,128)(2,1)S(1)}, u32[]{:S(2)}, u32[]{:S(2)}) %collective-permute-start.5) | collective-permute-done | bytes 24608 | tf_op jit(solution)/shard_map/ppermute | solution.py:27
  123.1 8.8 %all-to-all-start.3 = ((bf16[8,16,1536]{2,1,0:T(8,128)(2,1)}), bf16[8,16,1536]{2,1,0:T(8,128)(2,1)S(1)}, u32[]{:S(2)}, u32[]{:S(2)}) async-start(bf16[8,16,1536]{2,1,0:T(8,128)(2,1)} %broadcast_in_dim.21), calls=%async_computation.4 | async-start | bytes 786432 | tf_op jit(solution)/shard_map/all_to_all | solution.py:353
  132.0 15.0 %all-to-all-done.3 = bf16[8,16,1536]{2,1,0:T(8,128)(2,1)S(1)} async-done(((bf16[8,16,1536]{2,1,0:T(8,128)(2,1)}), bf16[8,16,1536]{2,1,0:T(8,128)(2,1)S(1)}, u32[]{:S(2)}, u32[]{:S(2)}) %all-to-all-start.3) | async-done | bytes 393248 | tf_op jit(solution)/shard_map/all_to_all | solution.py:353
  147.1 2.5 %shard_map.133 = bf16[8,10,16,128]{3,2,1,0:T(8,128)(2,1)} custom-call(s32[2]{0:T(128)S(1)} %pad_add_fusion.place_ref, bf16[128,1536]{1,0:T(8,128)(2,1)S(1)} %bitcast.30, bf16[1536,512]{1,0:T(8,128)(2,1)S(1)} %copy-done, bf16[768,512]{1,0:T(8,128)(2,1)S(1)} %copy-done.2, bf16[768,512]{1,0:T(8,128)(2,1)} %collective-permute-done.3.theirs_ref, ...), custom_call_target="tpu_custom_call" | custom-call | tf_op jit(solution)/shard_map/pallas_call | solution.py:197
  149.6 4.0 %all-to-all-start.4 = ((bf16[8,10,16,128]{3,2,1,0:T(8,128)(2,1)}), bf16[8,10,16,128]{3,2,1,0:T(8,128)(2,1)S(1)}, u32[]{:S(2)}, u32[]{:S(2)}) async-start(bf16[8,10,16,128]{3,2,1,0:T(8,128)(2,1)} %shard_map.133), calls=%async_computation.5 | async-start | bytes 655360 | tf_op jit(solution)/shard_map/all_to_all | solution.py:357
  154.1 5.9 %all-to-all-done.4.q_ref = bf16[8,10,16,128]{3,2,1,0:T(8,128)(2,1)S(1)} async-done(((bf16[8,10,16,128]{3,2,1,0:T(8,128)(2,1)}), bf16[8,10,16,128]{3,2,1,0:T(8,128)(2,1)S(1)}, u32[]{:S(2)}, u32[]{:S(2)}) %all-to-all-start.4) | async-done | bytes 327712 | tf_op jit(solution)/shard_map/all_to_all | solution.py:357
  160.7 12.3 %shard_map.134 = bf16[16,16,1024]{2,1,0:T(8,128)(2,1)} custom-call(bf16[8,10,16,128]{3,2,1,0:T(8,128)(2,1)} %copy-done.4, bf16[16,128]{1,0:T(8,128)(2,1)} %slice.27.w_ref, bf16[16384,128]{1,0:T(8,128)(2,1)} %all-gather.2.cloned.1.call-done.k_ref), custom_call_target="tpu_custom_call" | custom-call | flops 8589934592 | bytes 8388608 | tf_op jit(solution)/shard_map/pallas_call | solution.py:240
  173.0 6.3 %all-to-all-start.5 = ((bf16[16,16,1024]{2,1,0:T(8,128)(2,1)}), bf16[16,16,1024]{2,1,0:T(8,128)(2,1)S(1)}, u32[]{:S(2)}, u32[]{:S(2)}) async-start(bf16[16,16,1024]{2,1,0:T(8,128)(2,1)} %shard_map.134), calls=%async_computation.6 | async-start | bytes 1048576 | tf_op jit(solution)/shard_map/all_to_all | solution.py:360
  182.5 6.5 %all-to-all-done.5.s_ref = bf16[16,16,1024]{2,1,0:T(8,128)(2,1)S(1)} async-done(((bf16[16,16,1024]{2,1,0:T(8,128)(2,1)}), bf16[16,16,1024]{2,1,0:T(8,128)(2,1)S(1)}, u32[]{:S(2)}, u32[]{:S(2)}) %all-to-all-start.5) | async-done | bytes 524320 | tf_op jit(solution)/shard_map/all_to_all | solution.py:360
  189.0 1.7 shard_map.135
  (53 shorter events, 10.0 us)
Async XLA Ops:
  7.2 67.1 %reduce-scatter.2.cloned.1.call-start = ((), (), s32[]{:S(2)}) async-start(), calls=%async_computation.7 | async-start | bytes 4128768 | tf_op jit(solution)/shard_map/reduce_scatter | solution.py:333
  14.8 3.9 %copy-start.5 = (bf16[7168,4]{0,1:T(4,128)(2,1)S(1)}, bf16[7168,4]{0,1:T(4,128)(2,1)}, u32[]{:S(2)}) copy-start(bf16[7168,4]{0,1:T(4,128)(2,1)} %param.16) | copy-start | bytes 172036
  14.8 4.6 %copy-start.3 = (bf16[7168,96]{0,1:T(8,128)(2,1)S(1)}, bf16[7168,96]{0,1:T(8,128)(2,1)}, u32[]{:S(2)}) copy-start(bf16[7168,96]{0,1:T(8,128)(2,1)} %param.15) | copy-start | bytes 4128772
  14.9 145.1 %all-gather.2.cloned.1.call-start = ((), (), s32[]{:S(2)}) async-start(), calls=%async_computation.8 | async-start | bytes 4456448 | tf_op jit(solution)/shard_map/all_gather | solution.py:343
  14.9 29.7 %collective-permute-start = (bf16[768,512]{1,0:T(8,128)(2,1)}, bf16[768,512]{1,0:T(8,128)(2,1)S(1)}, u32[]{:S(2)}, u32[]{:S(2)}) collective-permute-start(bf16[768,512]{1,0:T(8,128)(2,1)} %get-tuple-element.19), channel_id=1, source_target_pairs={{0,1},{1,0},{2,3},{3,2},{4,5},{5,4},{6,7},{7,6},{8,9},{9,8},{10,11... | collective-permute-start | bytes 2359304 | tf_op jit(solution)/shard_map/ppermute | solution.py:27
  44.6 0.9 copy-start.1
  67.6 6.6 %collective-permute-start.1 = (bf16[448,1664]{1,0:T(8,128)(2,1)S(1)}, bf16[448,1664]{1,0:T(8,128)(2,1)S(1)}, u32[]{:S(2)}, u32[]{:S(2)}) collective-permute-start(bf16[448,1664]{1,0:T(8,128)(2,1)S(1)} %bitcast.28), channel_id=1, source_target_pairs={{0,16},{16,0},{1,17},{17,1},{2,18},{18,2},{3,19},{19,3},{4,20},{20... | collective-permute-start | bytes 4472840 | tf_op jit(solution)/shard_map/ppermute | solution.py:27
  74.3 12.7 %collective-permute-start.3 = (bf16[768,512]{1,0:T(8,128)(2,1)}, bf16[768,512]{1,0:T(8,128)(2,1)}, u32[]{:S(2)}, u32[]{:S(2)}) collective-permute-start(bf16[768,512]{1,0:T(8,128)(2,1)} %copy-done.1), channel_id=1, source_target_pairs={{0,16},{16,0},{1,17},{17,1},{2,18},{18,2},{3,19},{19,3},{4,20},{20... | collective-permute-start | bytes 2359304 | tf_op jit(solution)/shard_map/ppermute | solution.py:27
  76.6 8.8 %collective-permute-start.2 = (bf16[128,896]{1,0:T(8,128)(2,1)}, bf16[128,896]{1,0:T(8,128)(2,1)S(1)}, u32[]{:S(2)}, u32[]{:S(2)}) collective-permute-start(bf16[128,896]{1,0:T(8,128)(2,1)} %get-tuple-element.45), channel_id=1, source_target_pairs={{0,1},{1,0},{2,3},{3,2},{4,5},{5,4},{6,7},{7,6},{8,9},{9,8},{10,11... | collective-permute-start | bytes 688136 | tf_op jit(solution)/shard_map/ppermute | solution.py:27
  85.3 6.0 %copy-start.6 = (bf16[1536]{0:T(1024)(128)(2,1)S(1)}, bf16[1536]{0:T(1024)(128)(2,1)}, u32[]{:S(2)}) copy-start(bf16[1536]{0:T(1024)(128)(2,1)} %param.17) | copy-start | bytes 9220
  87.0 60.0 %copy-start = (bf16[1536,512]{1,0:T(8,128)(2,1)S(1)}, bf16[1536,512]{1,0:T(8,128)(2,1)}, u32[]{:S(2)}) copy-start(bf16[1536,512]{1,0:T(8,128)(2,1)} %own_ref.1) | copy-start | bytes 4718596
  87.0 60.0 %copy-start.2 = (bf16[768,512]{1,0:T(8,128)(2,1)S(1)}, bf16[768,512]{1,0:T(8,128)(2,1)}, u32[]{:S(2)}) copy-start(bf16[768,512]{1,0:T(8,128)(2,1)} %copy-done.1) | copy-start | bytes 2359300
  87.0 25.0 %all-to-all-start.2 = ((bf16[8,16,2560]{2,1,0:T(8,128)(2,1)}), bf16[8,16,2560]{2,1,0:T(8,128)(2,1)S(1)}, u32[]{:S(2)}, u32[]{:S(2)}) async-start(bf16[8,16,2560]{2,1,0:T(8,128)(2,1)} %bitcast.10), calls=%async_computation.3 | async-start | bytes 1310720 | tf_op jit(solution)/shard_map/all_to_all | solution.py:348
  113.1 9.2 %collective-permute-start.4 = (bf16[16,1664]{1,0:T(8,128)(2,1)S(1)}, bf16[16,1664]{1,0:T(8,128)(2,1)S(1)}, u32[]{:S(2)}, u32[]{:S(2)}) collective-permute-start(bf16[16,1664]{1,0:T(8,128)(2,1)S(1)} %get-tuple-element.27.final_ref), channel_id=1, source_target_pairs={{0,0},{1,16},{2,32},{3,48},{4,64},{5,80},{6,96},{7,112},{8,128},{9... | collective-permute-start | bytes 159752 | tf_op jit(solution)/shard_map/ppermute | solution.py:306
  118.0 4.3 %collective-permute-start.5 = (bf16[16,768]{1,0:T(8,128)(2,1)S(1)}, bf16[16,768]{1,0:T(8,128)(2,1)S(1)}, u32[]{:S(2)}, u32[]{:S(2)}) collective-permute-start(bf16[16,768]{1,0:T(8,128)(2,1)S(1)} %get-tuple-element.28), channel_id=1, source_target_pairs={{0,1},{1,0},{2,3},{3,2},{4,5},{5,4},{6,7},{7,6},{8,9},{9,8},{10,11... | collective-permute-start | bytes 73736 | tf_op jit(solution)/shard_map/ppermute | solution.py:27
  123.1 23.9 %all-to-all-start.3 = ((bf16[8,16,1536]{2,1,0:T(8,128)(2,1)}), bf16[8,16,1536]{2,1,0:T(8,128)(2,1)S(1)}, u32[]{:S(2)}, u32[]{:S(2)}) async-start(bf16[8,16,1536]{2,1,0:T(8,128)(2,1)} %broadcast_in_dim.21), calls=%async_computation.4 | async-start | bytes 786432 | tf_op jit(solution)/shard_map/all_to_all | solution.py:353
  149.6 10.4 %all-to-all-start.4 = ((bf16[8,10,16,128]{3,2,1,0:T(8,128)(2,1)}), bf16[8,10,16,128]{3,2,1,0:T(8,128)(2,1)S(1)}, u32[]{:S(2)}, u32[]{:S(2)}) async-start(bf16[8,10,16,128]{3,2,1,0:T(8,128)(2,1)} %shard_map.133), calls=%async_computation.5 | async-start | bytes 655360 | tf_op jit(solution)/shard_map/all_to_all | solution.py:357
  160.0 0.7 copy-start.4
  173.0 16.0 %all-to-all-start.5 = ((bf16[16,16,1024]{2,1,0:T(8,128)(2,1)}), bf16[16,16,1024]{2,1,0:T(8,128)(2,1)S(1)}, u32[]{:S(2)}, u32[]{:S(2)}) async-start(bf16[16,16,1024]{2,1,0:T(8,128)(2,1)} %shard_map.134), calls=%async_computation.6 | async-start | bytes 1048576 | tf_op jit(solution)/shard_map/all_to_all | solution.py:360
Sparse Core Ops, SparseCore 0:
  15.0 58.6 reduce-scatter.1
  75.6 39.1 all-gather.1

commit v13 on v12

--- a/solution.py
+++ b/solution.py
@@ -27,8 +27,8 @@
     return lax.ppermute(values, axis, [(0, 1), (1, 0)])
 
 
-def shift(values, axis, size, by):
-    return lax.ppermute(values, axis, [(i, (i + by) % size) for i in range(size)])
+def from_last(values):
+    return lax.all_to_all(values, "z", 0, 0, axis_index_groups=[list(range(NZ))[::-1]])
 
 
 def kernel_params():
@@ -41,7 +41,7 @@
 
 def project_kernel(place_ref, a_ref, b_ref, res_ref, w_ref, o_ref, half_ref, b_held, o_held, in_sems, out_sems, half_sem):
     head, core = place_ref[0] // 2, place_ref[0] % 2
-    own = pl.ds(pl.multiple_of(head // 2 * 16, 16), 16)
+    own = pl.ds(pl.multiple_of((NZ - 1 - head // 2) * 16, 16), 16)
     depth = half_ref.shape[0]
     half_copy = pltpu.make_async_copy(
         w_ref.at[pl.ds(pl.multiple_of(core * depth, 16), depth), :], half_ref, half_sem
@@ -66,7 +66,8 @@
         product = product.astype(o_ref.dtype)
         for group in range(NZ):
             for half in range(2):
-                o_held[i, half ^ (head % 2), group * 16 : (group + 1) * 16, :] = product[
+                at = (NZ - 1 - group) * 16
+                o_held[i, half ^ (head % 2), at : at + 16, :] = product[
                     group * 32 + half * 16 : group * 32 + (half + 1) * 16, :
                 ]
         added = o_held[i, 0, own, :].astype(jnp.float32) + res_ref[:, columns].astype(jnp.float32)
@@ -138,7 +139,7 @@
     for n in range(1, NZ):
         total = total + parts_ref[n, :, : QL + 128].astype(jnp.float32)
     for n in range(NZ):
-        hidden_ref[:, n * DZ : (n + 1) * DZ] = parts_ref[n, :, QL + 128 :]
+        hidden_ref[:, n * DZ : (n + 1) * DZ] = parts_ref[NZ - 1 - n, :, QL + 128 :]
     mean = (total[:, 1600:1601] + total[:, 1601:1602]) / D
     inverse = lax.rsqrt(mean + EPSILON)
     raw = (total[:, :QL] * inverse).astype(jnp.bfloat16).astype(jnp.float32)
@@ -278,14 +279,17 @@
     )(numbers, scores, own_positions)
 
 
-def down_weight_rows(latent_weight, index_proj, piece, early):
+def down_weight_rows(latent_weight, index_proj, piece, high, early):
     share = DZ // N_SEQ
 
     def own_rows(weight):
         return lax.dynamic_slice_in_dim(weight.reshape(NZ, DZ, weight.shape[1]), piece * share, share, 1)
 
     own = jnp.concatenate([own_rows(latent_weight), own_rows(index_proj)], axis=2)
-    by_head = lax.all_to_all(jnp.repeat(own, 2, axis=0), HEAD, 0, 0).transpose(1, 0, 2)
+    mine = lax.all_to_all(own, "z", 0, 0)
+    theirs = swap(mine, "yh")
+    pair = [jnp.where(high == 0, mine, theirs), jnp.where(high == 0, theirs, mine)]
+    by_head = jnp.stack(pair, axis=1).reshape(N_HEAD, share, own.shape[2]).transpose(1, 0, 2)
     local = latent_weight.shape[1]
     wide = jnp.concatenate(
         [
@@ -334,7 +338,7 @@
 
     weight_mine = swap(half_weight, "yh")
     down_mine, down_other, weight_mine = down_weight_rows(
-        latent_weight, index_proj, c * 8 + x * 2 + yl, weight_mine
+        latent_weight, index_proj, c * 8 + x * 2 + yl, yh, weight_mine
     )
     weight_theirs = swap(weight_mine, "c")
     summed, index_keys, down_mine, down_other = lax.optimization_barrier(
@@ -345,7 +349,7 @@
     gain = lax.dynamic_slice_in_dim(norm_gain, z * DZ, DZ).reshape(1, DZ)
     lifted = lift(jnp.stack([c]).astype(jnp.int32), kept, got, gain, down_mine, down_other)
     lifted, weight_theirs = lax.optimization_barrier((lifted, weight_theirs))
-    parts = lax.all_to_all(lifted.reshape(NZ, own, lifted.shape[1]), "z", 0, 0)
+    parts = from_last(lifted.reshape(NZ, own, lifted.shape[1]))
     packed, give, hidden_rows = normalize(
         jnp.stack([yh]).astype(jnp.int32), parts, latent_gain.reshape(1, QL)
     )
@@ -354,7 +358,7 @@
     everyone = everyone.reshape(HALF, QL)
     place = jnp.stack([c, yh]).astype(jnp.int32)
     queries = make_queries(place, everyone, index_weight, weight_mine, weight_theirs, packed, beside)
-    queries = lax.all_to_all(queries, "z", 0, 0, axis_index_groups=[list(range(NZ))[::-1]])
+    queries = from_last(queries)
     latent_out = queries[::-1, 8:, :, :local].reshape(rows, local)
     scores = make_scores(queries, turned[:, QL:], all_keys)
     scores = lax.all_to_all(scores, SEQ, 0, 0)

time: 199 us -> 200 us (level)
  starting transfers between devices: 38.6 us -> 47.5 us
  waiting for transfers between devices: 61.1 us -> 54.3 us
  blocking collectives: 45 us -> 38.4 us
  local copies, waits for them, and re-layouts: 10.9 us -> 15.8 us
    all_to_all x2, waiting for transfers between devices: 26.6 us -> 16.6 us  [from_last(): lax.all_to_all(values, 'z', 0, 0, axis_index_groups=[list(range(NZ))[::-1]])]
    ppermute x5 -> x6, waiting for transfers between devices: 13 us -> 20.7 us  [swap(): return lax.ppermute(values, axis, [(0, 1), (1, 0)])]
    all_to_all x1, starting transfers between devices: 6.29 us -> 12.1 us  [shards(): scores = lax.all_to_all(scores, SEQ, 0, 0)]
    all_to_all x1, blocking collectives: 22.9 us -> 17.4 us  [down_weight_rows(): mine = lax.all_to_all(own, 'z', 0, 0)]
    unnamed x17, local copies, waits for them, and re-layouts: 3.21 us -> 8.3 us
    ppermute x1, starting transfers between devices: 4.94 us -> 9.55 us  [turn(): return lax.ppermute(values, SEQ + HEAD, moves)]
    all_to_all x1, waiting for transfers between devices: 15 us -> 10.6 us  [shards(): lax.all_to_all(jnp.broadcast_to(turned[None, :, :QL], (NZ, own, QL)), 'z'...]
    ppermute x5 -> x6, starting transfers between devices: 10.3 us -> 10 us  [swap(): return lax.ppermute(values, axis, [(0, 1), (1, 0)])]
  transfers between devices with their start and end apart: 12 -> 13, of which waited for: 7 -> 8; matrix products, arithmetic and copies ran while one was open for 5% -> 7% of each run, Pallas kernels for 3% -> 3%
where the time goes in v13:
time: 200 us; the launch traced here: 198 us
  waiting for transfers between devices  54.3 us (27%)
  starting transfers between devices  47.5 us (24%)
  blocking collectives  38.4 us (19%)
  Pallas kernels  26.8 us (13%)
  local copies, waits for them, and re-layouts  15.8 us (8%)
  between operations  14.9 us (7%)
    all_to_all x1, blocking collectives, down_weight_rows(): lax.all_to_all(jnp.broadcast_to(wide[None], (8,) + wide.shape), ('x', 'yl...  21 us
    ppermute x6, waiting for transfers between devices, swap(): return lax.ppermute(values, axis, [(0, 1), (1, 0)])  20.7 us
    all_to_all x1, blocking collectives, down_weight_rows(): mine = lax.all_to_all(own, 'z', 0, 0)  17.4 us
    all_to_all x2, waiting for transfers between devices, from_last(): lax.all_to_all(values, 'z', 0, 0, axis_index_groups=[list(range(NZ))[::-1]])  16.6 us
    pallas_call x1, Pallas kernels, make_scores(): pl.pallas_call(score_kernel, grid=(N_SEQ // per_step,), in_specs=[pl.Bloc...  12.3 us
    all_to_all x1, starting transfers between devices, shards(): scores = lax.all_to_all(scores, SEQ, 0, 0)  12.1 us
    all_to_all x1, waiting for transfers between devices, shards(): lax.all_to_all(jnp.broadcast_to(turned[None, :, :QL], (NZ, own, QL)), 'z'...  10.6 us
    ppermute x6, starting transfers between devices, swap(): return lax.ppermute(values, axis, [(0, 1), (1, 0)])  10 us
  transfers between devices with their start and end apart: 13, of which 8 were waited for; matrix products, arithmetic and copies ran while one was open for 7% of the time, Pallas kernels for 3%

profile of v13, /device:TPU:1, one launch (start us, length us, event | category | flops | bytes accessed | tf_op | source)
XLA Modules:
  0.0 198.1 jit_solution(5289798975989705129)
XLA Ops:
  7.2 7.6 %shard_map.130 = (bf16[8,2,128,896]{3,2,1,0:T(8,128)(2,1)}, bf16[768,512]{1,0:T(8,128)(2,1)}) custom-call(s32[1]{0:T(128)} %bitcast.2.place_ref, bf16[256,512]{1,0:T(8,128)(2,1)} %a_ref.1, bf16[512,7168]{1,0:T(8,128)(2,1)} %b_ref.1, bf16[16,7168]{1,0:T(8,128)(2,1)} %res_ref.1, bf16[1536,512]{1,0:T(8,128)(2,1)} %own_ref.1), custom_call_target="tpu_custom_call" | custom-call | tf_op jit(solution)/shard_map/pallas_call | solution.py:87
  16.0 3.7 %collective-permute-start.1 = (bf16[768,512]{1,0:T(8,128)(2,1)S(1)}, bf16[768,512]{1,0:T(8,128)(2,1)S(1)}, u32[]{:S(2)}, u32[]{:S(2)}) collective-permute-start(bf16[768,512]{1,0:T(8,128)(2,1)S(1)} %copy-done.6), channel_id=1, source_target_pairs={{0,1},{1,0},{2,3},{3,2},{4,5},{5,4},{6,7},{7,6},{8,9},{9,8},{10,11... | collective-permute-start | bytes 2359304 | tf_op jit(solution)/shard_map/ppermute | solution.py:27
  19.7 1.7 copy.23
  21.5 3.2 %copy.22 = bf16[7168,96]{1,0:T(8,128)(2,1)S(1)} copy(bf16[7168,96]{0,1:T(8,128)(2,1)} %param.15) | data formatting | bytes 2752512 | tf_op args[4]
  25.7 17.4 %all_to_all.30 = bf16[8,56,100]{2,1,0:T(8,128)(2,1)S(1)} all-to-all(bf16[8,56,100]{2,1,0:T(8,128)(2,1)S(1)} %pad_maximum_fusion.1), channel_id=1, replica_groups=mesh['x'=4,'yl'=2,'c'=2,'z'=8,'yh'=2] {'z'}, dimensions={0} | all-to-all | bytes 179200 | tf_op jit(solution)/shard_map/all_to_all | solution.py:289
  43.1 5.1 %collective-permute-done = bf16[8,56,100]{2,1,0:T(8,128)(2,1)S(1)} collective-permute-done((bf16[8,56,100]{2,1,0:T(8,128)(2,1)S(1)}, bf16[8,56,100]{2,1,0:T(8,128)(2,1)S(1)}, u32[]{:S(2)}, u32[]{:S(2)}) %collective-permute-start) | collective-permute-done | bytes 89632 | tf_op jit(solution)/shard_map/ppermute | solution.py:27
  50.2 21.0 %all_to_all.31 = bf16[8,56,1664]{2,1,0:T(8,128)(2,1)S(1)} all-to-all(bf16[8,56,1664]{2,1,0:T(8,128)(2,1)S(1)} %broadcast_in_dim.7), channel_id=1, replica_groups=mesh['x'=4,'yl'=2,'c'=2,'z'=8,'yh'=2] {'x','yl'}, dimensions={0} | all-to-all | bytes 2981888 | tf_op jit(solution)/shard_map/all_to_all | solution.py:303
  71.2 4.5 %collective-permute-start.2 = (bf16[448,1664]{1,0:T(8,128)(2,1)S(1)}, bf16[448,1664]{1,0:T(8,128)(2,1)S(1)}, u32[]{:S(2)}, u32[]{:S(2)}) collective-permute-start(bf16[448,1664]{1,0:T(8,128)(2,1)S(1)} %bitcast.27), channel_id=1, source_target_pairs={{0,16},{16,0},{1,17},{17,1},{2,18},{18,2},{3,19},{19,3},{4,20},{20... | collective-permute-start | bytes 4472840 | tf_op jit(solution)/shard_map/ppermute | solution.py:27
  75.7 2.9 %collective-permute-done.2.other_ref = bf16[448,1664]{1,0:T(8,128)(2,1)S(1)} collective-permute-done((bf16[448,1664]{1,0:T(8,128)(2,1)S(1)}, bf16[448,1664]{1,0:T(8,128)(2,1)S(1)}, u32[]{:S(2)}, u32[]{:S(2)}) %collective-permute-start.2) | collective-permute-done | bytes 1490976 | tf_op jit(solution)/shard_map/ppermute | solution.py:27
  79.1 1.8 slice_bitcast_fusion
  82.8 8.4 %collective-permute-done.3.got_ref = bf16[128,896]{1,0:T(8,128)(2,1)S(1)} collective-permute-done((bf16[128,896]{1,0:T(8,128)(2,1)}, bf16[128,896]{1,0:T(8,128)(2,1)S(1)}, u32[]{:S(2)}, u32[]{:S(2)}) %collective-permute-start.3) | collective-permute-done | bytes 229408 | tf_op jit(solution)/shard_map/ppermute | solution.py:27
  93.0 4.1 %all-to-all-start.2 = ((bf16[8,16,2560]{2,1,0:T(8,128)(2,1)}), bf16[8,16,2560]{2,1,0:T(8,128)(2,1)S(1)}, u32[]{:S(2)}, u32[]{:S(2)}) async-start(bf16[8,16,2560]{2,1,0:T(8,128)(2,1)} %bitcast.16), calls=%async_computation.3 | async-start | bytes 1310720 | tf_op jit(solution)/shard_map/all_to_all | solution.py:31
  97.1 11.3 %all-to-all-done.2.parts_ref = bf16[8,16,2560]{2,1,0:T(8,128)(2,1)S(1)} async-done(((bf16[8,16,2560]{2,1,0:T(8,128)(2,1)}), bf16[8,16,2560]{2,1,0:T(8,128)(2,1)S(1)}, u32[]{:S(2)}, u32[]{:S(2)}) %all-to-all-start.2) | async-done | bytes 655392 | tf_op jit(solution)/shard_map/all_to_all | solution.py:31
  109.4 9.6 %collective-permute-start.5 = (bf16[16,1664]{1,0:T(8,128)(2,1)S(1)}, bf16[16,1664]{1,0:T(8,128)(2,1)S(1)}, u32[]{:S(2)}, u32[]{:S(2)}) collective-permute-start(bf16[16,1664]{1,0:T(8,128)(2,1)S(1)} %get-tuple-element.27.final_ref), channel_id=1, source_target_pairs={{0,0},{1,16},{2,32},{3,48},{4,64},{5,80},{6,96},{7,112},{8,128},{9... | collective-permute-start | bytes 159752 | tf_op jit(solution)/shard_map/ppermute | solution.py:310
  119.1 4.2 %collective-permute-done.6.beside_ref = bf16[16,768]{1,0:T(8,128)(2,1)S(1)} collective-permute-done((bf16[16,768]{1,0:T(8,128)(2,1)S(1)}, bf16[16,768]{1,0:T(8,128)(2,1)S(1)}, u32[]{:S(2)}, u32[]{:S(2)}) %collective-permute-start.6) | collective-permute-done | bytes 24608 | tf_op jit(solution)/shard_map/ppermute | solution.py:27
  124.1 7.6 %all-to-all-start.3 = ((bf16[8,16,1536]{2,1,0:T(8,128)(2,1)}), bf16[8,16,1536]{2,1,0:T(8,128)(2,1)S(1)}, u32[]{:S(2)}, u32[]{:S(2)}) async-start(bf16[8,16,1536]{2,1,0:T(8,128)(2,1)} %broadcast_in_dim.8), calls=%async_computation.4 | async-start | bytes 786432 | tf_op jit(solution)/shard_map/all_to_all | solution.py:357
  131.7 10.6 %all-to-all-done.3 = bf16[8,16,1536]{2,1,0:T(8,128)(2,1)S(1)} async-done(((bf16[8,16,1536]{2,1,0:T(8,128)(2,1)}), bf16[8,16,1536]{2,1,0:T(8,128)(2,1)S(1)}, u32[]{:S(2)}, u32[]{:S(2)}) %all-to-all-start.3) | async-done | bytes 393248 | tf_op jit(solution)/shard_map/all_to_all | solution.py:357
  142.3 2.5 %shard_map.133 = bf16[8,10,16,128]{3,2,1,0:T(8,128)(2,1)} custom-call(s32[2]{0:T(128)S(1)} %pad_add_fusion.place_ref, bf16[128,1536]{1,0:T(8,128)(2,1)S(1)} %bitcast.29, bf16[1536,512]{1,0:T(8,128)(2,1)S(1)} %copy-done, bf16[768,512]{1,0:T(8,128)(2,1)S(1)} %copy-done.2, bf16[768,512]{1,0:T(8,128)(2,1)} %collective-permute-done.4.theirs_ref, ...), custom_call_target="tpu_custom_call" | custom-call | tf_op jit(solution)/shard_map/pallas_call | solution.py:198
  144.8 4.1 %all-to-all-start.4 = ((bf16[8,10,16,128]{3,2,1,0:T(8,128)(2,1)}), bf16[8,10,16,128]{3,2,1,0:T(8,128)(2,1)S(1)}, u32[]{:S(2)}, u32[]{:S(2)}) async-start(bf16[8,10,16,128]{3,2,1,0:T(8,128)(2,1)} %shard_map.133), calls=%async_computation.5 | async-start | bytes 655360 | tf_op jit(solution)/shard_map/all_to_all | solution.py:31
  149.5 5.3 %all-to-all-done.4.q_ref = bf16[8,10,16,128]{3,2,1,0:T(8,128)(2,1)S(1)} async-done(((bf16[8,10,16,128]{3,2,1,0:T(8,128)(2,1)}), bf16[8,10,16,128]{3,2,1,0:T(8,128)(2,1)S(1)}, u32[]{:S(2)}, u32[]{:S(2)}) %all-to-all-start.4) | async-done | bytes 327712 | tf_op jit(solution)/shard_map/all_to_all | solution.py:31
  155.5 12.3 %shard_map.134 = bf16[16,16,1024]{2,1,0:T(8,128)(2,1)} custom-call(bf16[8,10,16,128]{3,2,1,0:T(8,128)(2,1)} %copy-done.3, bf16[16,128]{1,0:T(8,128)(2,1)} %slice.27.w_ref, bf16[16384,128]{1,0:T(8,128)(2,1)} %all-gather.2.cloned.1.call-done.k_ref), custom_call_target="tpu_custom_call" | custom-call | flops 8589934592 | bytes 8388608 | tf_op jit(solution)/shard_map/pallas_call | solution.py:241
  167.8 12.1 %all-to-all-start.5 = ((bf16[16,16,1024]{2,1,0:T(8,128)(2,1)}), bf16[16,16,1024]{2,1,0:T(8,128)(2,1)S(1)}, u32[]{:S(2)}, u32[]{:S(2)}) async-start(bf16[16,16,1024]{2,1,0:T(8,128)(2,1)} %shard_map.134), calls=%async_computation.6 | async-start | bytes 1048576 | tf_op jit(solution)/shard_map/all_to_all | solution.py:364
  183.1 6.4 %all-to-all-done.5.s_ref = bf16[16,16,1024]{2,1,0:T(8,128)(2,1)S(1)} async-done(((bf16[16,16,1024]{2,1,0:T(8,128)(2,1)}), bf16[16,16,1024]{2,1,0:T(8,128)(2,1)S(1)}, u32[]{:S(2)}, u32[]{:S(2)}) %all-to-all-start.5) | async-done | bytes 524320 | tf_op jit(solution)/shard_map/all_to_all | solution.py:364
  189.6 1.7 shard_map.135
  (55 shorter events, 14.0 us)
Async XLA Ops:
  7.2 71.5 %reduce-scatter.2.cloned.1.call-start = ((), (), s32[]{:S(2)}) async-start(), calls=%async_computation.7 | async-start | bytes 4128768 | tf_op jit(solution)/shard_map/reduce_scatter | solution.py:337
  14.8 1.1 copy-start.6
  14.9 4.9 %copy-start.4 = (bf16[7168,4]{0,1:T(4,128)(2,1)S(1)}, bf16[7168,4]{0,1:T(4,128)(2,1)}, u32[]{:S(2)}) copy-start(bf16[7168,4]{0,1:T(4,128)(2,1)} %param.16) | copy-start | bytes 172036
  14.9 139.9 %all-gather.2.cloned.1.call-start = ((), (), s32[]{:S(2)}) async-start(), calls=%async_computation.8 | async-start | bytes 4456448 | tf_op jit(solution)/shard_map/all_gather | solution.py:347
  16.0 33.2 %collective-permute-start.1 = (bf16[768,512]{1,0:T(8,128)(2,1)S(1)}, bf16[768,512]{1,0:T(8,128)(2,1)S(1)}, u32[]{:S(2)}, u32[]{:S(2)}) collective-permute-start(bf16[768,512]{1,0:T(8,128)(2,1)S(1)} %copy-done.6), channel_id=1, source_target_pairs={{0,1},{1,0},{2,3},{3,2},{4,5},{5,4},{6,7},{7,6},{8,9},{9,8},{10,11... | collective-permute-start | bytes 2359304 | tf_op jit(solution)/shard_map/ppermute | solution.py:27
  43.1 5.1 %collective-permute-start = (bf16[8,56,100]{2,1,0:T(8,128)(2,1)S(1)}, bf16[8,56,100]{2,1,0:T(8,128)(2,1)S(1)}, u32[]{:S(2)}, u32[]{:S(2)}) collective-permute-start(bf16[8,56,100]{2,1,0:T(8,128)(2,1)S(1)} %all_to_all.30), channel_id=1, source_target_pairs={{0,1},{1,0},{2,3},{3,2},{4,5},{5,4},{6,7},{7,6},{8,9},{9,8},{10,11... | collective-permute-start | bytes 268808 | tf_op jit(solution)/shard_map/ppermute | solution.py:27
  49.2 0.9 copy-start.1
  71.2 7.4 %collective-permute-start.2 = (bf16[448,1664]{1,0:T(8,128)(2,1)S(1)}, bf16[448,1664]{1,0:T(8,128)(2,1)S(1)}, u32[]{:S(2)}, u32[]{:S(2)}) collective-permute-start(bf16[448,1664]{1,0:T(8,128)(2,1)S(1)} %bitcast.27), channel_id=1, source_target_pairs={{0,16},{16,0},{1,17},{17,1},{2,18},{18,2},{3,19},{19,3},{4,20},{20... | collective-permute-start | bytes 4472840 | tf_op jit(solution)/shard_map/ppermute | solution.py:27
  78.7 14.3 %collective-permute-start.4 = (bf16[768,512]{1,0:T(8,128)(2,1)}, bf16[768,512]{1,0:T(8,128)(2,1)}, u32[]{:S(2)}, u32[]{:S(2)}) collective-permute-start(bf16[768,512]{1,0:T(8,128)(2,1)} %copy-done.1), channel_id=1, source_target_pairs={{0,16},{16,0},{1,17},{17,1},{2,18},{18,2},{3,19},{19,3},{4,20},{20... | collective-permute-start | bytes 2359304 | tf_op jit(solution)/shard_map/ppermute | solution.py:27
  80.9 10.4 %collective-permute-start.3 = (bf16[128,896]{1,0:T(8,128)(2,1)}, bf16[128,896]{1,0:T(8,128)(2,1)S(1)}, u32[]{:S(2)}, u32[]{:S(2)}) collective-permute-start(bf16[128,896]{1,0:T(8,128)(2,1)} %get-tuple-element.42), channel_id=1, source_target_pairs={{0,1},{1,0},{2,3},{3,2},{4,5},{5,4},{6,7},{7,6},{8,9},{9,8},{10,11... | collective-permute-start | bytes 688136 | tf_op jit(solution)/shard_map/ppermute | solution.py:27
  91.3 5.8 %copy-start.5 = (bf16[1536]{0:T(1024)(128)(2,1)S(1)}, bf16[1536]{0:T(1024)(128)(2,1)}, u32[]{:S(2)}) copy-start(bf16[1536]{0:T(1024)(128)(2,1)} %param.17) | copy-start | bytes 9220
  93.0 49.3 %copy-start = (bf16[1536,512]{1,0:T(8,128)(2,1)S(1)}, bf16[1536,512]{1,0:T(8,128)(2,1)}, u32[]{:S(2)}) copy-start(bf16[1536,512]{1,0:T(8,128)(2,1)} %own_ref.1) | copy-start | bytes 4718596
  93.0 49.3 %copy-start.2 = (bf16[768,512]{1,0:T(8,128)(2,1)S(1)}, bf16[768,512]{1,0:T(8,128)(2,1)}, u32[]{:S(2)}) copy-start(bf16[768,512]{1,0:T(8,128)(2,1)} %copy-done.1) | copy-start | bytes 2359300
  93.0 15.4 %all-to-all-start.2 = ((bf16[8,16,2560]{2,1,0:T(8,128)(2,1)}), bf16[8,16,2560]{2,1,0:T(8,128)(2,1)S(1)}, u32[]{:S(2)}, u32[]{:S(2)}) async-start(bf16[8,16,2560]{2,1,0:T(8,128)(2,1)} %bitcast.16), calls=%async_computation.3 | async-start | bytes 1310720 | tf_op jit(solution)/shard_map/all_to_all | solution.py:31
  109.4 13.8 %collective-permute-start.5 = (bf16[16,1664]{1,0:T(8,128)(2,1)S(1)}, bf16[16,1664]{1,0:T(8,128)(2,1)S(1)}, u32[]{:S(2)}, u32[]{:S(2)}) collective-permute-start(bf16[16,1664]{1,0:T(8,128)(2,1)S(1)} %get-tuple-element.27.final_ref), channel_id=1, source_target_pairs={{0,0},{1,16},{2,32},{3,48},{4,64},{5,80},{6,96},{7,112},{8,128},{9... | collective-permute-start | bytes 159752 | tf_op jit(solution)/shard_map/ppermute | solution.py:310
  119.0 4.3 %collective-permute-start.6 = (bf16[16,768]{1,0:T(8,128)(2,1)S(1)}, bf16[16,768]{1,0:T(8,128)(2,1)S(1)}, u32[]{:S(2)}, u32[]{:S(2)}) collective-permute-start(bf16[16,768]{1,0:T(8,128)(2,1)S(1)} %get-tuple-element.28), channel_id=1, source_target_pairs={{0,1},{1,0},{2,3},{3,2},{4,5},{5,4},{6,7},{7,6},{8,9},{9,8},{10,11... | collective-permute-start | bytes 73736 | tf_op jit(solution)/shard_map/ppermute | solution.py:27
  124.1 18.2 %all-to-all-start.3 = ((bf16[8,16,1536]{2,1,0:T(8,128)(2,1)}), bf16[8,16,1536]{2,1,0:T(8,128)(2,1)S(1)}, u32[]{:S(2)}, u32[]{:S(2)}) async-start(bf16[8,16,1536]{2,1,0:T(8,128)(2,1)} %broadcast_in_dim.8), calls=%async_computation.4 | async-start | bytes 786432 | tf_op jit(solution)/shard_map/all_to_all | solution.py:357
  144.8 10.0 %all-to-all-start.4 = ((bf16[8,10,16,128]{3,2,1,0:T(8,128)(2,1)}), bf16[8,10,16,128]{3,2,1,0:T(8,128)(2,1)S(1)}, u32[]{:S(2)}, u32[]{:S(2)}) async-start(bf16[8,10,16,128]{3,2,1,0:T(8,128)(2,1)} %shard_map.133), calls=%async_computation.5 | async-start | bytes 655360 | tf_op jit(solution)/shard_map/all_to_all | solution.py:31
  154.8 0.7 copy-start.3
  167.8 21.8 %all-to-all-start.5 = ((bf16[16,16,1024]{2,1,0:T(8,128)(2,1)}), bf16[16,16,1024]{2,1,0:T(8,128)(2,1)S(1)}, u32[]{:S(2)}, u32[]{:S(2)}) async-start(bf16[16,16,1024]{2,1,0:T(8,128)(2,1)} %shard_map.134), calls=%async_computation.6 | async-start | bytes 1048576 | tf_op jit(solution)/shard_map/all_to_all | solution.py:364
Sparse Core Ops, SparseCore 0:
  15.0 56.6 reduce-scatter.1
  78.8 35.3 all-gather.1

commit v14 on v13

--- a/solution.py
+++ b/solution.py
@@ -237,7 +237,7 @@
 
 
 def make_scores(queries, head_weights, keys):
-    per_step = 2
+    per_step = 4
     return pl.pallas_call(
         score_kernel,
         grid=(N_SEQ // per_step,),
@@ -279,17 +279,14 @@
     )(numbers, scores, own_positions)
 
 
-def down_weight_rows(latent_weight, index_proj, piece, high, early):
+def down_weight_rows(latent_weight, index_proj, piece, early):
     share = DZ // N_SEQ
 
     def own_rows(weight):
         return lax.dynamic_slice_in_dim(weight.reshape(NZ, DZ, weight.shape[1]), piece * share, share, 1)
 
     own = jnp.concatenate([own_rows(latent_weight), own_rows(index_proj)], axis=2)
-    mine = lax.all_to_all(own, "z", 0, 0)
-    theirs = swap(mine, "yh")
-    pair = [jnp.where(high == 0, mine, theirs), jnp.where(high == 0, theirs, mine)]
-    by_head = jnp.stack(pair, axis=1).reshape(N_HEAD, share, own.shape[2]).transpose(1, 0, 2)
+    by_head = lax.all_to_all(jnp.repeat(own, 2, axis=0), HEAD, 0, 0).transpose(1, 0, 2)
     local = latent_weight.shape[1]
     wide = jnp.concatenate(
         [
@@ -338,7 +335,7 @@
 
     weight_mine = swap(half_weight, "yh")
     down_mine, down_other, weight_mine = down_weight_rows(
-        latent_weight, index_proj, c * 8 + x * 2 + yl, yh, weight_mine
+        latent_weight, index_proj, c * 8 + x * 2 + yl, weight_mine
     )
     weight_theirs = swap(weight_mine, "c")
     summed, index_keys, down_mine, down_other = lax.optimization_barrier(

time: 200 us -> 198 us (0.990)
  blocking collectives: 38.4 us -> 45 us
  local copies, waits for them, and re-layouts: 15.8 us -> 10.9 us
  waiting for transfers between devices: 54.3 us -> 52.3 us
    ppermute x6 -> x5, waiting for transfers between devices: 20.7 us -> 13 us  [swap(): return lax.ppermute(values, axis, [(0, 1), (1, 0)])]
    all_to_all x1, blocking collectives: 17.4 us -> 22.9 us  [down_weight_rows(): lax.all_to_all(jnp.repeat(own, 2, axis=0), HEAD, 0, 0).transpose(1, 0, 2)]
    unnamed x17, local copies, waits for them, and re-layouts: 8.3 us -> 3.21 us
    all_to_all x1, starting transfers between devices: 12.1 us -> 7.5 us  [shards(): scores = lax.all_to_all(scores, SEQ, 0, 0)]
    all_to_all x1, waiting for transfers between devices: 10.6 us -> 15.1 us  [shards(): lax.all_to_all(jnp.broadcast_to(turned[None, :, :QL], (NZ, own, QL)), 'z'...]
    all_to_all x2, starting transfers between devices: 8.19 us -> 10.3 us  [from_last(): lax.all_to_all(values, 'z', 0, 0, axis_index_groups=[list(range(NZ))[::-1]])]
    ppermute x6 -> x5, starting transfers between devices: 10 us -> 10.3 us  [swap(): return lax.ppermute(values, axis, [(0, 1), (1, 0)])]
  transfers between devices with their start and end apart: 13 -> 12, of which waited for: 8 -> 7; matrix products, arithmetic and copies ran while one was open for 7% -> 5% of each run, Pallas kernels for 3% -> 3%
where the time goes in v14:
time: 198 us; the launch traced here: 197 us
  waiting for transfers between devices  52.3 us (26%)
  starting transfers between devices  47 us (24%)
  blocking collectives  45 us (23%)
  Pallas kernels  26.2 us (13%)
  between operations  14.9 us (8%)
  local copies, waits for them, and re-layouts  10.9 us (6%)
    all_to_all x1, blocking collectives, down_weight_rows(): lax.all_to_all(jnp.repeat(own, 2, axis=0), HEAD, 0, 0).transpose(1, 0, 2)  22.9 us
    all_to_all x1, blocking collectives, down_weight_rows(): lax.all_to_all(jnp.broadcast_to(wide[None], (8,) + wide.shape), ('x', 'yl...  22 us
    all_to_all x2, waiting for transfers between devices, from_last(): lax.all_to_all(values, 'z', 0, 0, axis_index_groups=[list(range(NZ))[::-1]])  17.8 us
    all_to_all x1, waiting for transfers between devices, shards(): lax.all_to_all(jnp.broadcast_to(turned[None, :, :QL], (NZ, own, QL)), 'z'...  15.1 us
    ppermute x5, waiting for transfers between devices, swap(): return lax.ppermute(values, axis, [(0, 1), (1, 0)])  13 us
    pallas_call x1, Pallas kernels, make_scores(): pl.pallas_call(score_kernel, grid=(N_SEQ // per_step,), in_specs=[pl.Bloc...  11.7 us
    all_to_all x2, starting transfers between devices, from_last(): lax.all_to_all(values, 'z', 0, 0, axis_index_groups=[list(range(NZ))[::-1]])  10.3 us
    ppermute x5, starting transfers between devices, swap(): return lax.ppermute(values, axis, [(0, 1), (1, 0)])  10.3 us
  transfers between devices with their start and end apart: 12, of which 7 were waited for; matrix products, arithmetic and copies ran while one was open for 5% of the time, Pallas kernels for 3%

profile of v14, /device:TPU:1, one launch (start us, length us, event | category | flops | bytes accessed | tf_op | source)
XLA Modules:
  0.0 196.5 jit_solution(15273541864618140263)
XLA Ops:
  7.2 7.6 %shard_map.130 = (bf16[8,2,128,896]{3,2,1,0:T(8,128)(2,1)}, bf16[768,512]{1,0:T(8,128)(2,1)}) custom-call(s32[1]{0:T(128)} %bitcast.2.place_ref, bf16[256,512]{1,0:T(8,128)(2,1)} %a_ref.1, bf16[512,7168]{1,0:T(8,128)(2,1)} %b_ref.1, bf16[16,7168]{1,0:T(8,128)(2,1)} %res_ref.1, bf16[1536,512]{1,0:T(8,128)(2,1)} %own_ref.1), custom_call_target="tpu_custom_call" | custom-call | tf_op jit(solution)/shard_map/pallas_call | solution.py:87
  14.9 3.8 %collective-permute-start = (bf16[768,512]{1,0:T(8,128)(2,1)}, bf16[768,512]{1,0:T(8,128)(2,1)S(1)}, u32[]{:S(2)}, u32[]{:S(2)}) collective-permute-start(bf16[768,512]{1,0:T(8,128)(2,1)} %get-tuple-element.19), channel_id=1, source_target_pairs={{0,1},{1,0},{2,3},{3,2},{4,5},{5,4},{6,7},{7,6},{8,9},{9,8},{10,11... | collective-permute-start | bytes 2359304 | tf_op jit(solution)/shard_map/ppermute | solution.py:27
  20.9 22.9 %all_to_all.30 = bf16[16,56,100]{2,1,0:T(8,128)(2,1)S(1)} all-to-all(bf16[16,56,100]{2,1,0:T(8,128)(2,1)S(1)} %bitcast.35), channel_id=1, replica_groups=mesh['x'=4,'yl'=2,'c'=2,'z'=8,'yh'=2] {'z','yh'}, dimensions={0} | all-to-all | bytes 358400 | tf_op jit(solution)/shard_map/all_to_all | solution.py:289
  45.6 22.0 %all_to_all.31 = bf16[8,56,1664]{2,1,0:T(8,128)(2,1)S(1)} all-to-all(bf16[8,56,1664]{2,1,0:T(8,128)(2,1)S(1)} %broadcast_in_dim.20), channel_id=1, replica_groups=mesh['x'=4,'yl'=2,'c'=2,'z'=8,'yh'=2] {'x','yl'}, dimensions={0} | all-to-all | bytes 2981888 | tf_op jit(solution)/shard_map/all_to_all | solution.py:300
  67.6 3.7 %collective-permute-start.1 = (bf16[448,1664]{1,0:T(8,128)(2,1)S(1)}, bf16[448,1664]{1,0:T(8,128)(2,1)S(1)}, u32[]{:S(2)}, u32[]{:S(2)}) collective-permute-start(bf16[448,1664]{1,0:T(8,128)(2,1)S(1)} %bitcast.28), channel_id=1, source_target_pairs={{0,16},{16,0},{1,17},{17,1},{2,18},{18,2},{3,19},{19,3},{4,20},{20... | collective-permute-start | bytes 4472840 | tf_op jit(solution)/shard_map/ppermute | solution.py:27
  71.4 2.9 %collective-permute-done.1.other_ref = bf16[448,1664]{1,0:T(8,128)(2,1)S(1)} collective-permute-done((bf16[448,1664]{1,0:T(8,128)(2,1)S(1)}, bf16[448,1664]{1,0:T(8,128)(2,1)S(1)}, u32[]{:S(2)}, u32[]{:S(2)}) %collective-permute-start.1) | collective-permute-done | bytes 1490976 | tf_op jit(solution)/shard_map/ppermute | solution.py:27
  74.8 1.8 slice_bitcast_fusion
  76.6 2.1 %collective-permute-start.2 = (bf16[128,896]{1,0:T(8,128)(2,1)}, bf16[128,896]{1,0:T(8,128)(2,1)S(1)}, u32[]{:S(2)}, u32[]{:S(2)}) collective-permute-start(bf16[128,896]{1,0:T(8,128)(2,1)} %get-tuple-element.45), channel_id=1, source_target_pairs={{0,1},{1,0},{2,3},{3,2},{4,5},{5,4},{6,7},{7,6},{8,9},{9,8},{10,11... | collective-permute-start | bytes 688136 | tf_op jit(solution)/shard_map/ppermute | solution.py:27
  79.5 5.9 %collective-permute-done.2.got_ref = bf16[128,896]{1,0:T(8,128)(2,1)S(1)} collective-permute-done((bf16[128,896]{1,0:T(8,128)(2,1)}, bf16[128,896]{1,0:T(8,128)(2,1)S(1)}, u32[]{:S(2)}, u32[]{:S(2)}) %collective-permute-start.2) | collective-permute-done | bytes 229408 | tf_op jit(solution)/shard_map/ppermute | solution.py:27
  85.3 1.7 shard_map.131
  87.0 6.3 %all-to-all-start.2 = ((bf16[8,16,2560]{2,1,0:T(8,128)(2,1)}), bf16[8,16,2560]{2,1,0:T(8,128)(2,1)S(1)}, u32[]{:S(2)}, u32[]{:S(2)}) async-start(bf16[8,16,2560]{2,1,0:T(8,128)(2,1)} %bitcast.10), calls=%async_computation.3 | async-start | bytes 1310720 | tf_op jit(solution)/shard_map/all_to_all | solution.py:31
  93.4 11.9 %all-to-all-done.2.parts_ref = bf16[8,16,2560]{2,1,0:T(8,128)(2,1)S(1)} async-done(((bf16[8,16,2560]{2,1,0:T(8,128)(2,1)}), bf16[8,16,2560]{2,1,0:T(8,128)(2,1)S(1)}, u32[]{:S(2)}, u32[]{:S(2)}) %all-to-all-start.2) | async-done | bytes 655392 | tf_op jit(solution)/shard_map/all_to_all | solution.py:31
  105.3 1.0 shard_map.132
  106.3 9.9 %collective-permute-start.4 = (bf16[16,1664]{1,0:T(8,128)(2,1)S(1)}, bf16[16,1664]{1,0:T(8,128)(2,1)S(1)}, u32[]{:S(2)}, u32[]{:S(2)}) collective-permute-start(bf16[16,1664]{1,0:T(8,128)(2,1)S(1)} %get-tuple-element.27.final_ref), channel_id=1, source_target_pairs={{0,0},{1,16},{2,32},{3,48},{4,64},{5,80},{6,96},{7,112},{8,128},{9... | collective-permute-start | bytes 159752 | tf_op jit(solution)/shard_map/ppermute | solution.py:307
  116.4 4.2 %collective-permute-done.5.beside_ref = bf16[16,768]{1,0:T(8,128)(2,1)S(1)} collective-permute-done((bf16[16,768]{1,0:T(8,128)(2,1)S(1)}, bf16[16,768]{1,0:T(8,128)(2,1)S(1)}, u32[]{:S(2)}, u32[]{:S(2)}) %collective-permute-start.5) | collective-permute-done | bytes 24608 | tf_op jit(solution)/shard_map/ppermute | solution.py:27
  121.3 8.9 %all-to-all-start.3 = ((bf16[8,16,1536]{2,1,0:T(8,128)(2,1)}), bf16[8,16,1536]{2,1,0:T(8,128)(2,1)S(1)}, u32[]{:S(2)}, u32[]{:S(2)}) async-start(bf16[8,16,1536]{2,1,0:T(8,128)(2,1)} %broadcast_in_dim.21), calls=%async_computation.4 | async-start | bytes 786432 | tf_op jit(solution)/shard_map/all_to_all | solution.py:354
  130.4 15.1 %all-to-all-done.3 = bf16[8,16,1536]{2,1,0:T(8,128)(2,1)S(1)} async-done(((bf16[8,16,1536]{2,1,0:T(8,128)(2,1)}), bf16[8,16,1536]{2,1,0:T(8,128)(2,1)S(1)}, u32[]{:S(2)}, u32[]{:S(2)}) %all-to-all-start.3) | async-done | bytes 393248 | tf_op jit(solution)/shard_map/all_to_all | solution.py:354
  145.5 2.5 %shard_map.133 = bf16[8,10,16,128]{3,2,1,0:T(8,128)(2,1)} custom-call(s32[2]{0:T(128)S(1)} %pad_add_fusion.place_ref, bf16[128,1536]{1,0:T(8,128)(2,1)S(1)} %bitcast.30, bf16[1536,512]{1,0:T(8,128)(2,1)S(1)} %copy-done, bf16[768,512]{1,0:T(8,128)(2,1)S(1)} %copy-done.2, bf16[768,512]{1,0:T(8,128)(2,1)} %collective-permute-done.3.theirs_ref, ...), custom_call_target="tpu_custom_call" | custom-call | tf_op jit(solution)/shard_map/pallas_call | solution.py:198
  148.0 4.0 %all-to-all-start.4 = ((bf16[8,10,16,128]{3,2,1,0:T(8,128)(2,1)}), bf16[8,10,16,128]{3,2,1,0:T(8,128)(2,1)S(1)}, u32[]{:S(2)}, u32[]{:S(2)}) async-start(bf16[8,10,16,128]{3,2,1,0:T(8,128)(2,1)} %shard_map.133), calls=%async_computation.5 | async-start | bytes 655360 | tf_op jit(solution)/shard_map/all_to_all | solution.py:31
  152.5 5.8 %all-to-all-done.4.q_ref = bf16[8,10,16,128]{3,2,1,0:T(8,128)(2,1)S(1)} async-done(((bf16[8,10,16,128]{3,2,1,0:T(8,128)(2,1)}), bf16[8,10,16,128]{3,2,1,0:T(8,128)(2,1)S(1)}, u32[]{:S(2)}, u32[]{:S(2)}) %all-to-all-start.4) | async-done | bytes 327712 | tf_op jit(solution)/shard_map/all_to_all | solution.py:31
  159.1 11.7 %shard_map.134 = bf16[16,16,1024]{2,1,0:T(8,128)(2,1)} custom-call(bf16[8,10,16,128]{3,2,1,0:T(8,128)(2,1)} %copy-done.4, bf16[16,128]{1,0:T(8,128)(2,1)} %slice.27.w_ref, bf16[16384,128]{1,0:T(8,128)(2,1)} %all-gather.2.cloned.1.call-done.k_ref), custom_call_target="tpu_custom_call" | custom-call | flops 8589934592 | bytes 8388608 | tf_op jit(solution)/shard_map/pallas_call | solution.py:241
  170.8 7.5 %all-to-all-start.5 = ((bf16[16,16,1024]{2,1,0:T(8,128)(2,1)}), bf16[16,16,1024]{2,1,0:T(8,128)(2,1)S(1)}, u32[]{:S(2)}, u32[]{:S(2)}) async-start(bf16[16,16,1024]{2,1,0:T(8,128)(2,1)} %shard_map.134), calls=%async_computation.6 | async-start | bytes 1048576 | tf_op jit(solution)/shard_map/all_to_all | solution.py:361
  181.6 6.4 %all-to-all-done.5.s_ref = bf16[16,16,1024]{2,1,0:T(8,128)(2,1)S(1)} async-done(((bf16[16,16,1024]{2,1,0:T(8,128)(2,1)}), bf16[16,16,1024]{2,1,0:T(8,128)(2,1)S(1)}, u32[]{:S(2)}, u32[]{:S(2)}) %all-to-all-start.5) | async-done | bytes 524320 | tf_op jit(solution)/shard_map/all_to_all | solution.py:361
  188.0 1.7 shard_map.135
  (53 shorter events, 10.0 us)
Async XLA Ops:
  7.2 67.1 %reduce-scatter.2.cloned.1.call-start = ((), (), s32[]{:S(2)}) async-start(), calls=%async_computation.7 | async-start | bytes 4128768 | tf_op jit(solution)/shard_map/reduce_scatter | solution.py:334
  14.8 3.9 %copy-start.5 = (bf16[7168,4]{0,1:T(4,128)(2,1)S(1)}, bf16[7168,4]{0,1:T(4,128)(2,1)}, u32[]{:S(2)}) copy-start(bf16[7168,4]{0,1:T(4,128)(2,1)} %param.16) | copy-start | bytes 172036
  14.8 4.6 %copy-start.3 = (bf16[7168,96]{0,1:T(8,128)(2,1)S(1)}, bf16[7168,96]{0,1:T(8,128)(2,1)}, u32[]{:S(2)}) copy-start(bf16[7168,96]{0,1:T(8,128)(2,1)} %param.15) | copy-start | bytes 4128772
  14.9 143.5 %all-gather.2.cloned.1.call-start = ((), (), s32[]{:S(2)}) async-start(), calls=%async_computation.8 | async-start | bytes 4456448 | tf_op jit(solution)/shard_map/all_gather | solution.py:344
  14.9 29.7 %collective-permute-start = (bf16[768,512]{1,0:T(8,128)(2,1)}, bf16[768,512]{1,0:T(8,128)(2,1)S(1)}, u32[]{:S(2)}, u32[]{:S(2)}) collective-permute-start(bf16[768,512]{1,0:T(8,128)(2,1)} %get-tuple-element.19), channel_id=1, source_target_pairs={{0,1},{1,0},{2,3},{3,2},{4,5},{5,4},{6,7},{7,6},{8,9},{9,8},{10,11... | collective-permute-start | bytes 2359304 | tf_op jit(solution)/shard_map/ppermute | solution.py:27
  44.6 0.9 copy-start.1
  67.6 6.6 %collective-permute-start.1 = (bf16[448,1664]{1,0:T(8,128)(2,1)S(1)}, bf16[448,1664]{1,0:T(8,128)(2,1)S(1)}, u32[]{:S(2)}, u32[]{:S(2)}) collective-permute-start(bf16[448,1664]{1,0:T(8,128)(2,1)S(1)} %bitcast.28), channel_id=1, source_target_pairs={{0,16},{16,0},{1,17},{17,1},{2,18},{18,2},{3,19},{19,3},{4,20},{20... | collective-permute-start | bytes 4472840 | tf_op jit(solution)/shard_map/ppermute | solution.py:27
  74.3 12.7 %collective-permute-start.3 = (bf16[768,512]{1,0:T(8,128)(2,1)}, bf16[768,512]{1,0:T(8,128)(2,1)}, u32[]{:S(2)}, u32[]{:S(2)}) collective-permute-start(bf16[768,512]{1,0:T(8,128)(2,1)} %copy-done.1), channel_id=1, source_target_pairs={{0,16},{16,0},{1,17},{17,1},{2,18},{18,2},{3,19},{19,3},{4,20},{20... | collective-permute-start | bytes 2359304 | tf_op jit(solution)/shard_map/ppermute | solution.py:27
  76.6 8.8 %collective-permute-start.2 = (bf16[128,896]{1,0:T(8,128)(2,1)}, bf16[128,896]{1,0:T(8,128)(2,1)S(1)}, u32[]{:S(2)}, u32[]{:S(2)}) collective-permute-start(bf16[128,896]{1,0:T(8,128)(2,1)} %get-tuple-element.45), channel_id=1, source_target_pairs={{0,1},{1,0},{2,3},{3,2},{4,5},{5,4},{6,7},{7,6},{8,9},{9,8},{10,11... | collective-permute-start | bytes 688136 | tf_op jit(solution)/shard_map/ppermute | solution.py:27
  85.3 8.0 %copy-start.6 = (bf16[1536]{0:T(1024)(128)(2,1)S(1)}, bf16[1536]{0:T(1024)(128)(2,1)}, u32[]{:S(2)}) copy-start(bf16[1536]{0:T(1024)(128)(2,1)} %param.17) | copy-start | bytes 9220
  87.0 58.5 %copy-start = (bf16[1536,512]{1,0:T(8,128)(2,1)S(1)}, bf16[1536,512]{1,0:T(8,128)(2,1)}, u32[]{:S(2)}) copy-start(bf16[1536,512]{1,0:T(8,128)(2,1)} %own_ref.1) | copy-start | bytes 4718596
  87.0 58.5 %copy-start.2 = (bf16[768,512]{1,0:T(8,128)(2,1)S(1)}, bf16[768,512]{1,0:T(8,128)(2,1)}, u32[]{:S(2)}) copy-start(bf16[768,512]{1,0:T(8,128)(2,1)} %copy-done.1) | copy-start | bytes 2359300
  87.0 18.3 %all-to-all-start.2 = ((bf16[8,16,2560]{2,1,0:T(8,128)(2,1)}), bf16[8,16,2560]{2,1,0:T(8,128)(2,1)S(1)}, u32[]{:S(2)}, u32[]{:S(2)}) async-start(bf16[8,16,2560]{2,1,0:T(8,128)(2,1)} %bitcast.10), calls=%async_computation.3 | async-start | bytes 1310720 | tf_op jit(solution)/shard_map/all_to_all | solution.py:31
  106.3 14.2 %collective-permute-start.4 = (bf16[16,1664]{1,0:T(8,128)(2,1)S(1)}, bf16[16,1664]{1,0:T(8,128)(2,1)S(1)}, u32[]{:S(2)}, u32[]{:S(2)}) collective-permute-start(bf16[16,1664]{1,0:T(8,128)(2,1)S(1)} %get-tuple-element.27.final_ref), channel_id=1, source_target_pairs={{0,0},{1,16},{2,32},{3,48},{4,64},{5,80},{6,96},{7,112},{8,128},{9... | collective-permute-start | bytes 159752 | tf_op jit(solution)/shard_map/ppermute | solution.py:307
  116.3 4.3 %collective-permute-start.5 = (bf16[16,768]{1,0:T(8,128)(2,1)S(1)}, bf16[16,768]{1,0:T(8,128)(2,1)S(1)}, u32[]{:S(2)}, u32[]{:S(2)}) collective-permute-start(bf16[16,768]{1,0:T(8,128)(2,1)S(1)} %get-tuple-element.28), channel_id=1, source_target_pairs={{0,1},{1,0},{2,3},{3,2},{4,5},{5,4},{6,7},{7,6},{8,9},{9,8},{10,11... | collective-permute-start | bytes 73736 | tf_op jit(solution)/shard_map/ppermute | solution.py:27
  121.3 24.1 %all-to-all-start.3 = ((bf16[8,16,1536]{2,1,0:T(8,128)(2,1)}), bf16[8,16,1536]{2,1,0:T(8,128)(2,1)S(1)}, u32[]{:S(2)}, u32[]{:S(2)}) async-start(bf16[8,16,1536]{2,1,0:T(8,128)(2,1)} %broadcast_in_dim.21), calls=%async_computation.4 | async-start | bytes 786432 | tf_op jit(solution)/shard_map/all_to_all | solution.py:354
  148.0 10.4 %all-to-all-start.4 = ((bf16[8,10,16,128]{3,2,1,0:T(8,128)(2,1)}), bf16[8,10,16,128]{3,2,1,0:T(8,128)(2,1)S(1)}, u32[]{:S(2)}, u32[]{:S(2)}) async-start(bf16[8,10,16,128]{3,2,1,0:T(8,128)(2,1)} %shard_map.133), calls=%async_computation.5 | async-start | bytes 655360 | tf_op jit(solution)/shard_map/all_to_all | solution.py:31
  158.4 0.7 copy-start.4
  170.8 17.1 %all-to-all-start.5 = ((bf16[16,16,1024]{2,1,0:T(8,128)(2,1)}), bf16[16,16,1024]{2,1,0:T(8,128)(2,1)S(1)}, u32[]{:S(2)}, u32[]{:S(2)}) async-start(bf16[16,16,1024]{2,1,0:T(8,128)(2,1)} %shard_map.134), calls=%async_computation.6 | async-start | bytes 1048576 | tf_op jit(solution)/shard_map/all_to_all | solution.py:361
Sparse Core Ops, SparseCore 0:
  15.0 58.6 reduce-scatter.1
  75.6 39.1 all-gather.1

commit v15 on v14

--- a/solution.py
+++ b/solution.py
@@ -184,7 +184,7 @@
         part = part.astype(jnp.bfloat16)
         for j in range(4):
             for block in range(NZ):
-                o_ref[NZ - 1 - block, at + j] = part[block * 16 : (block + 1) * 16, j * IDIM : (j + 1) * IDIM]
+                o_ref[block, at + j] = part[block * 16 : (block + 1) * 16, j * IDIM : (j + 1) * IDIM]
     o_ref[:, 8:] = jnp.zeros((NZ, 2, 16, IDIM), jnp.bfloat16)
     for block in range(NZ):
         low = final_ref[:, block * 192 : block * 192 + 96]
@@ -233,7 +233,7 @@
                         jnp.maximum(logits[j * 16 : (j + 1) * 16, n * 128 : (n + 1) * 128], 0.0) * weight
                     )
             for n in range(2):
-                o_ref[block, :, slot + n * 128 : slot + (n + 1) * 128] = halves[n].astype(o_ref.dtype)
+                o_ref[blocks - 1 - block, :, slot + n * 128 : slot + (n + 1) * 128] = halves[n].astype(o_ref.dtype)
 
 
 def make_scores(queries, head_weights, keys):
@@ -246,7 +246,7 @@
             pl.BlockSpec((16, 128), lambda i: (0, 0)),
             pl.BlockSpec((per_step * SLOTS, IDIM), lambda i: (i, 0)),
         ],
-        out_specs=pl.BlockSpec((per_step, 16, SLOTS), lambda i: (i, 0, 0)),
+        out_specs=pl.BlockSpec((per_step, 16, SLOTS), lambda i: (N_SEQ // per_step - 1 - i, 0, 0)),
         out_shape=jax.ShapeDtypeStruct((N_SEQ, 16, SLOTS), jnp.bfloat16),
         scratch_shapes=[
             pltpu.VMEM((IHEADS * 16, 128), jnp.float32),
@@ -265,7 +265,7 @@
     for group in range(N_SEQ):
         here = slice(group * 16, (group + 1) * 16)
         reach = jnp.minimum(filled, pos_ref[here, :] - base + 1)
-        o_ref[here, :] = jnp.where(local < reach, s_ref[group].astype(jnp.float32), 0.0)
+        o_ref[here, :] = jnp.where(local < reach, s_ref[N_SEQ - 1 - group].astype(jnp.float32), 0.0)
 
 
 def finish(numbers, scores, own_positions):
@@ -351,14 +351,14 @@
         jnp.stack([yh]).astype(jnp.int32), parts, latent_gain.reshape(1, QL)
     )
     turned, beside = lax.optimization_barrier((turn(packed), swap(give, "yh")))
-    everyone = lax.all_to_all(jnp.broadcast_to(turned[None, :, :QL], (NZ, own, QL)), "z", 0, 0)
+    everyone = from_last(jnp.broadcast_to(turned[None, :, :QL], (NZ, own, QL)))
     everyone = everyone.reshape(HALF, QL)
     place = jnp.stack([c, yh]).astype(jnp.int32)
     queries = make_queries(place, everyone, index_weight, weight_mine, weight_theirs, packed, beside)
     queries = from_last(queries)
     latent_out = queries[::-1, 8:, :, :local].reshape(rows, local)
     scores = make_scores(queries, turned[:, QL:], all_keys)
-    scores = lax.all_to_all(scores, SEQ, 0, 0)
+    scores = lax.all_to_all(scores, SEQ, 0, 0, axis_index_groups=[list(range(N_SEQ))[::-1]])
 
     own_positions = lax.dynamic_slice_in_dim(positions, head * rows, rows).reshape(rows, 1)
     numbers = jnp.stack([cache_len[0], seq * SLOTS]).astype(jnp.int32)

time: 198 us -> 198 us (level)
  starting transfers between devices: 47 us -> 55.1 us
  waiting for transfers between devices: 52.3 us -> 44.3 us
    all_to_all x2 -> x1, waiting for transfers between devices: 21.5 us -> 3.87 us  [shards(): lax.all_to_all(scores, SEQ, 0, 0, axis_index_groups=[list(range(N_SEQ))[:...]
    all_to_all x2 -> x3, starting transfers between devices: 10.3 us -> 25.3 us  [from_last(): lax.all_to_all(values, 'z', 0, 0, axis_index_groups=[list(range(NZ))[::-1]])]
    all_to_all x2 -> x3, waiting for transfers between devices: 17.8 us -> 27.4 us  [from_last(): lax.all_to_all(values, 'z', 0, 0, axis_index_groups=[list(range(NZ))[::-1]])]
    all_to_all x2 -> x1, starting transfers between devices: 16.4 us -> 9.56 us  [shards(): lax.all_to_all(scores, SEQ, 0, 0, axis_index_groups=[list(range(N_SEQ))[:...]
where the time goes in v15:
time: 198 us; the launch traced here: 197 us
  starting transfers between devices  55.1 us (28%)
  blocking collectives  45 us (23%)
  waiting for transfers between devices  44.3 us (22%)
  Pallas kernels  26.3 us (13%)
  between operations  14.9 us (8%)
  local copies, waits for them, and re-layouts  10.9 us (6%)
    all_to_all x3, waiting for transfers between devices, from_last(): lax.all_to_all(values, 'z', 0, 0, axis_index_groups=[list(range(NZ))[::-1]])  27.4 us
    all_to_all x3, starting transfers between devices, from_last(): lax.all_to_all(values, 'z', 0, 0, axis_index_groups=[list(range(NZ))[::-1]])  25.3 us
    all_to_all x1, blocking collectives, down_weight_rows(): lax.all_to_all(jnp.repeat(own, 2, axis=0), HEAD, 0, 0).transpose(1, 0, 2)  22.9 us
    all_to_all x1, blocking collectives, down_weight_rows(): lax.all_to_all(jnp.broadcast_to(wide[None], (8,) + wide.shape), ('x', 'yl...  22 us
    ppermute x5, waiting for transfers between devices, swap(): return lax.ppermute(values, axis, [(0, 1), (1, 0)])  13 us
    pallas_call x1, Pallas kernels, make_scores(): pl.pallas_call(score_kernel, grid=(N_SEQ // per_step,), in_specs=[pl.Bloc...  11.7 us
    ppermute x5, starting transfers between devices, swap(): return lax.ppermute(values, axis, [(0, 1), (1, 0)])  10.3 us
    ppermute x1, starting transfers between devices, turn(): return lax.ppermute(values, SEQ + HEAD, moves)  9.91 us
  transfers between devices with their start and end apart: 12, of which 7 were waited for; matrix products, arithmetic and copies ran while one was open for 5% of the time, Pallas kernels for 3%

profile of v15, /device:TPU:1, one launch (start us, length us, event | category | flops | bytes accessed | tf_op | source)
XLA Modules:
  0.0 196.7 jit_solution(7670462105096359442)
XLA Ops:
  7.2 7.6 %shard_map.130 = (bf16[8,2,128,896]{3,2,1,0:T(8,128)(2,1)}, bf16[768,512]{1,0:T(8,128)(2,1)}) custom-call(s32[1]{0:T(128)} %bitcast.2.place_ref, bf16[256,512]{1,0:T(8,128)(2,1)} %a_ref.1, bf16[512,7168]{1,0:T(8,128)(2,1)} %b_ref.1, bf16[16,7168]{1,0:T(8,128)(2,1)} %res_ref.1, bf16[1536,512]{1,0:T(8,128)(2,1)} %own_ref.1), custom_call_target="tpu_custom_call" | custom-call | tf_op jit(solution)/shard_map/pallas_call | solution.py:87
  14.9 3.8 %collective-permute-start = (bf16[768,512]{1,0:T(8,128)(2,1)}, bf16[768,512]{1,0:T(8,128)(2,1)S(1)}, u32[]{:S(2)}, u32[]{:S(2)}) collective-permute-start(bf16[768,512]{1,0:T(8,128)(2,1)} %get-tuple-element.19), channel_id=1, source_target_pairs={{0,1},{1,0},{2,3},{3,2},{4,5},{5,4},{6,7},{7,6},{8,9},{9,8},{10,11... | collective-permute-start | bytes 2359304 | tf_op jit(solution)/shard_map/ppermute | solution.py:27
  20.9 22.9 %all_to_all.30 = bf16[16,56,100]{2,1,0:T(8,128)(2,1)S(1)} all-to-all(bf16[16,56,100]{2,1,0:T(8,128)(2,1)S(1)} %bitcast.35), channel_id=1, replica_groups=mesh['x'=4,'yl'=2,'c'=2,'z'=8,'yh'=2] {'z','yh'}, dimensions={0} | all-to-all | bytes 358400 | tf_op jit(solution)/shard_map/all_to_all | solution.py:289
  45.6 22.0 %all_to_all.31 = bf16[8,56,1664]{2,1,0:T(8,128)(2,1)S(1)} all-to-all(bf16[8,56,1664]{2,1,0:T(8,128)(2,1)S(1)} %broadcast_in_dim.20), channel_id=1, replica_groups=mesh['x'=4,'yl'=2,'c'=2,'z'=8,'yh'=2] {'x','yl'}, dimensions={0} | all-to-all | bytes 2981888 | tf_op jit(solution)/shard_map/all_to_all | solution.py:300
  67.6 3.7 %collective-permute-start.1 = (bf16[448,1664]{1,0:T(8,128)(2,1)S(1)}, bf16[448,1664]{1,0:T(8,128)(2,1)S(1)}, u32[]{:S(2)}, u32[]{:S(2)}) collective-permute-start(bf16[448,1664]{1,0:T(8,128)(2,1)S(1)} %bitcast.28), channel_id=1, source_target_pairs={{0,16},{16,0},{1,17},{17,1},{2,18},{18,2},{3,19},{19,3},{4,20},{20... | collective-permute-start | bytes 4472840 | tf_op jit(solution)/shard_map/ppermute | solution.py:27
  71.4 2.9 %collective-permute-done.1.other_ref = bf16[448,1664]{1,0:T(8,128)(2,1)S(1)} collective-permute-done((bf16[448,1664]{1,0:T(8,128)(2,1)S(1)}, bf16[448,1664]{1,0:T(8,128)(2,1)S(1)}, u32[]{:S(2)}, u32[]{:S(2)}) %collective-permute-start.1) | collective-permute-done | bytes 1490976 | tf_op jit(solution)/shard_map/ppermute | solution.py:27
  74.8 1.8 slice_bitcast_fusion
  76.6 2.1 %collective-permute-start.2 = (bf16[128,896]{1,0:T(8,128)(2,1)}, bf16[128,896]{1,0:T(8,128)(2,1)S(1)}, u32[]{:S(2)}, u32[]{:S(2)}) collective-permute-start(bf16[128,896]{1,0:T(8,128)(2,1)} %get-tuple-element.45), channel_id=1, source_target_pairs={{0,1},{1,0},{2,3},{3,2},{4,5},{5,4},{6,7},{7,6},{8,9},{9,8},{10,11... | collective-permute-start | bytes 688136 | tf_op jit(solution)/shard_map/ppermute | solution.py:27
  79.5 5.9 %collective-permute-done.2.got_ref = bf16[128,896]{1,0:T(8,128)(2,1)S(1)} collective-permute-done((bf16[128,896]{1,0:T(8,128)(2,1)}, bf16[128,896]{1,0:T(8,128)(2,1)S(1)}, u32[]{:S(2)}, u32[]{:S(2)}) %collective-permute-start.2) | collective-permute-done | bytes 229408 | tf_op jit(solution)/shard_map/ppermute | solution.py:27
  85.3 1.7 shard_map.131
  87.0 6.3 %all-to-all-start.2 = ((bf16[8,16,2560]{2,1,0:T(8,128)(2,1)}), bf16[8,16,2560]{2,1,0:T(8,128)(2,1)S(1)}, u32[]{:S(2)}, u32[]{:S(2)}) async-start(bf16[8,16,2560]{2,1,0:T(8,128)(2,1)} %bitcast.10), calls=%async_computation.3 | async-start | bytes 1310720 | tf_op jit(solution)/shard_map/all_to_all | solution.py:31
  93.4 11.9 %all-to-all-done.2.parts_ref = bf16[8,16,2560]{2,1,0:T(8,128)(2,1)S(1)} async-done(((bf16[8,16,2560]{2,1,0:T(8,128)(2,1)}), bf16[8,16,2560]{2,1,0:T(8,128)(2,1)S(1)}, u32[]{:S(2)}, u32[]{:S(2)}) %all-to-all-start.2) | async-done | bytes 655392 | tf_op jit(solution)/shard_map/all_to_all | solution.py:31
  105.3 1.0 shard_map.132
  106.3 9.9 %collective-permute-start.4 = (bf16[16,1664]{1,0:T(8,128)(2,1)S(1)}, bf16[16,1664]{1,0:T(8,128)(2,1)S(1)}, u32[]{:S(2)}, u32[]{:S(2)}) collective-permute-start(bf16[16,1664]{1,0:T(8,128)(2,1)S(1)} %get-tuple-element.27.final_ref), channel_id=1, source_target_pairs={{0,0},{1,16},{2,32},{3,48},{4,64},{5,80},{6,96},{7,112},{8,128},{9... | collective-permute-start | bytes 159752 | tf_op jit(solution)/shard_map/ppermute | solution.py:307
  116.4 4.2 %collective-permute-done.5.beside_ref = bf16[16,768]{1,0:T(8,128)(2,1)S(1)} collective-permute-done((bf16[16,768]{1,0:T(8,128)(2,1)S(1)}, bf16[16,768]{1,0:T(8,128)(2,1)S(1)}, u32[]{:S(2)}, u32[]{:S(2)}) %collective-permute-start.5) | collective-permute-done | bytes 24608 | tf_op jit(solution)/shard_map/ppermute | solution.py:27
  121.3 9.8 %all-to-all-start.3 = ((bf16[8,16,1536]{2,1,0:T(8,128)(2,1)}), bf16[8,16,1536]{2,1,0:T(8,128)(2,1)S(1)}, u32[]{:S(2)}, u32[]{:S(2)}) async-start(bf16[8,16,1536]{2,1,0:T(8,128)(2,1)} %broadcast_in_dim.21), calls=%async_computation.4 | async-start | bytes 786432 | tf_op jit(solution)/shard_map/all_to_all | solution.py:31
  131.2 9.3 %all-to-all-done.3 = bf16[8,16,1536]{2,1,0:T(8,128)(2,1)S(1)} async-done(((bf16[8,16,1536]{2,1,0:T(8,128)(2,1)}), bf16[8,16,1536]{2,1,0:T(8,128)(2,1)S(1)}, u32[]{:S(2)}, u32[]{:S(2)}) %all-to-all-start.3) | async-done | bytes 393248 | tf_op jit(solution)/shard_map/all_to_all | solution.py:31
  140.5 2.5 %shard_map.133 = bf16[8,10,16,128]{3,2,1,0:T(8,128)(2,1)} custom-call(s32[2]{0:T(128)S(1)} %pad_add_fusion.place_ref, bf16[128,1536]{1,0:T(8,128)(2,1)S(1)} %bitcast.30, bf16[1536,512]{1,0:T(8,128)(2,1)S(1)} %copy-done, bf16[768,512]{1,0:T(8,128)(2,1)S(1)} %copy-done.2, bf16[768,512]{1,0:T(8,128)(2,1)} %collective-permute-done.3.theirs_ref, ...), custom_call_target="tpu_custom_call" | custom-call | tf_op jit(solution)/shard_map/pallas_call | solution.py:198
  143.0 9.2 %all-to-all-start.4 = ((bf16[8,10,16,128]{3,2,1,0:T(8,128)(2,1)}), bf16[8,10,16,128]{3,2,1,0:T(8,128)(2,1)S(1)}, u32[]{:S(2)}, u32[]{:S(2)}) async-start(bf16[8,10,16,128]{3,2,1,0:T(8,128)(2,1)} %shard_map.133), calls=%async_computation.5 | async-start | bytes 655360 | tf_op jit(solution)/shard_map/all_to_all | solution.py:31
  152.8 6.2 %all-to-all-done.4.q_ref = bf16[8,10,16,128]{3,2,1,0:T(8,128)(2,1)S(1)} async-done(((bf16[8,10,16,128]{3,2,1,0:T(8,128)(2,1)}), bf16[8,10,16,128]{3,2,1,0:T(8,128)(2,1)S(1)}, u32[]{:S(2)}, u32[]{:S(2)}) %all-to-all-start.4) | async-done | bytes 327712 | tf_op jit(solution)/shard_map/all_to_all | solution.py:31
  159.8 11.7 %shard_map.134 = bf16[16,16,1024]{2,1,0:T(8,128)(2,1)} custom-call(bf16[8,10,16,128]{3,2,1,0:T(8,128)(2,1)} %copy-done.4, bf16[16,128]{1,0:T(8,128)(2,1)} %slice.27.w_ref, bf16[16384,128]{1,0:T(8,128)(2,1)} %all-gather.2.cloned.1.call-done.k_ref), custom_call_target="tpu_custom_call" | custom-call | flops 8589934592 | bytes 8388608 | tf_op jit(solution)/shard_map/pallas_call | solution.py:241
  171.5 9.6 %all-to-all-start.5 = ((bf16[16,16,1024]{2,1,0:T(8,128)(2,1)}), bf16[16,16,1024]{2,1,0:T(8,128)(2,1)S(1)}, u32[]{:S(2)}, u32[]{:S(2)}) async-start(bf16[16,16,1024]{2,1,0:T(8,128)(2,1)} %shard_map.134), calls=%async_computation.6 | async-start | bytes 1048576 | tf_op jit(solution)/shard_map/all_to_all | solution.py:361
  184.3 3.9 %all-to-all-done.5.s_ref = bf16[16,16,1024]{2,1,0:T(8,128)(2,1)S(1)} async-done(((bf16[16,16,1024]{2,1,0:T(8,128)(2,1)}), bf16[16,16,1024]{2,1,0:T(8,128)(2,1)S(1)}, u32[]{:S(2)}, u32[]{:S(2)}) %all-to-all-start.5) | async-done | bytes 524320 | tf_op jit(solution)/shard_map/all_to_all | solution.py:361
  188.1 1.7 shard_map.135
  (53 shorter events, 10.0 us)
Async XLA Ops:
  7.2 67.1 %reduce-scatter.2.cloned.1.call-start = ((), (), s32[]{:S(2)}) async-start(), calls=%async_computation.7 | async-start | bytes 4128768 | tf_op jit(solution)/shard_map/reduce_scatter | solution.py:334
  14.8 3.9 %copy-start.5 = (bf16[7168,4]{0,1:T(4,128)(2,1)S(1)}, bf16[7168,4]{0,1:T(4,128)(2,1)}, u32[]{:S(2)}) copy-start(bf16[7168,4]{0,1:T(4,128)(2,1)} %param.16) | copy-start | bytes 172036
  14.8 4.6 %copy-start.3 = (bf16[7168,96]{0,1:T(8,128)(2,1)S(1)}, bf16[7168,96]{0,1:T(8,128)(2,1)}, u32[]{:S(2)}) copy-start(bf16[7168,96]{0,1:T(8,128)(2,1)} %param.15) | copy-start | bytes 4128772
  14.9 144.1 %all-gather.2.cloned.1.call-start = ((), (), s32[]{:S(2)}) async-start(), calls=%async_computation.8 | async-start | bytes 4456448 | tf_op jit(solution)/shard_map/all_gather | solution.py:344
  14.9 29.7 %collective-permute-start = (bf16[768,512]{1,0:T(8,128)(2,1)}, bf16[768,512]{1,0:T(8,128)(2,1)S(1)}, u32[]{:S(2)}, u32[]{:S(2)}) collective-permute-start(bf16[768,512]{1,0:T(8,128)(2,1)} %get-tuple-element.19), channel_id=1, source_target_pairs={{0,1},{1,0},{2,3},{3,2},{4,5},{5,4},{6,7},{7,6},{8,9},{9,8},{10,11... | collective-permute-start | bytes 2359304 | tf_op jit(solution)/shard_map/ppermute | solution.py:27
  44.6 0.9 copy-start.1
  67.6 6.6 %collective-permute-start.1 = (bf16[448,1664]{1,0:T(8,128)(2,1)S(1)}, bf16[448,1664]{1,0:T(8,128)(2,1)S(1)}, u32[]{:S(2)}, u32[]{:S(2)}) collective-permute-start(bf16[448,1664]{1,0:T(8,128)(2,1)S(1)} %bitcast.28), channel_id=1, source_target_pairs={{0,16},{16,0},{1,17},{17,1},{2,18},{18,2},{3,19},{19,3},{4,20},{20... | collective-permute-start | bytes 4472840 | tf_op jit(solution)/shard_map/ppermute | solution.py:27
  74.3 12.7 %collective-permute-start.3 = (bf16[768,512]{1,0:T(8,128)(2,1)}, bf16[768,512]{1,0:T(8,128)(2,1)}, u32[]{:S(2)}, u32[]{:S(2)}) collective-permute-start(bf16[768,512]{1,0:T(8,128)(2,1)} %copy-done.1), channel_id=1, source_target_pairs={{0,16},{16,0},{1,17},{17,1},{2,18},{18,2},{3,19},{19,3},{4,20},{20... | collective-permute-start | bytes 2359304 | tf_op jit(solution)/shard_map/ppermute | solution.py:27
  76.6 8.8 %collective-permute-start.2 = (bf16[128,896]{1,0:T(8,128)(2,1)}, bf16[128,896]{1,0:T(8,128)(2,1)S(1)}, u32[]{:S(2)}, u32[]{:S(2)}) collective-permute-start(bf16[128,896]{1,0:T(8,128)(2,1)} %get-tuple-element.45), channel_id=1, source_target_pairs={{0,1},{1,0},{2,3},{3,2},{4,5},{5,4},{6,7},{7,6},{8,9},{9,8},{10,11... | collective-permute-start | bytes 688136 | tf_op jit(solution)/shard_map/ppermute | solution.py:27
  85.3 8.0 %copy-start.6 = (bf16[1536]{0:T(1024)(128)(2,1)S(1)}, bf16[1536]{0:T(1024)(128)(2,1)}, u32[]{:S(2)}) copy-start(bf16[1536]{0:T(1024)(128)(2,1)} %param.17) | copy-start | bytes 9220
  87.0 53.4 %copy-start = (bf16[1536,512]{1,0:T(8,128)(2,1)S(1)}, bf16[1536,512]{1,0:T(8,128)(2,1)}, u32[]{:S(2)}) copy-start(bf16[1536,512]{1,0:T(8,128)(2,1)} %own_ref.1) | copy-start | bytes 4718596
  87.0 53.4 %copy-start.2 = (bf16[768,512]{1,0:T(8,128)(2,1)S(1)}, bf16[768,512]{1,0:T(8,128)(2,1)}, u32[]{:S(2)}) copy-start(bf16[768,512]{1,0:T(8,128)(2,1)} %copy-done.1) | copy-start | bytes 2359300
  87.0 18.3 %all-to-all-start.2 = ((bf16[8,16,2560]{2,1,0:T(8,128)(2,1)}), bf16[8,16,2560]{2,1,0:T(8,128)(2,1)S(1)}, u32[]{:S(2)}, u32[]{:S(2)}) async-start(bf16[8,16,2560]{2,1,0:T(8,128)(2,1)} %bitcast.10), calls=%async_computation.3 | async-start | bytes 1310720 | tf_op jit(solution)/shard_map/all_to_all | solution.py:31
  106.3 14.2 %collective-permute-start.4 = (bf16[16,1664]{1,0:T(8,128)(2,1)S(1)}, bf16[16,1664]{1,0:T(8,128)(2,1)S(1)}, u32[]{:S(2)}, u32[]{:S(2)}) collective-permute-start(bf16[16,1664]{1,0:T(8,128)(2,1)S(1)} %get-tuple-element.27.final_ref), channel_id=1, source_target_pairs={{0,0},{1,16},{2,32},{3,48},{4,64},{5,80},{6,96},{7,112},{8,128},{9... | collective-permute-start | bytes 159752 | tf_op jit(solution)/shard_map/ppermute | solution.py:307
  116.3 4.3 %collective-permute-start.5 = (bf16[16,768]{1,0:T(8,128)(2,1)S(1)}, bf16[16,768]{1,0:T(8,128)(2,1)S(1)}, u32[]{:S(2)}, u32[]{:S(2)}) collective-permute-start(bf16[16,768]{1,0:T(8,128)(2,1)S(1)} %get-tuple-element.28), channel_id=1, source_target_pairs={{0,1},{1,0},{2,3},{3,2},{4,5},{5,4},{6,7},{7,6},{8,9},{9,8},{10,11... | collective-permute-start | bytes 73736 | tf_op jit(solution)/shard_map/ppermute | solution.py:27
  121.3 19.1 %all-to-all-start.3 = ((bf16[8,16,1536]{2,1,0:T(8,128)(2,1)}), bf16[8,16,1536]{2,1,0:T(8,128)(2,1)S(1)}, u32[]{:S(2)}, u32[]{:S(2)}) async-start(bf16[8,16,1536]{2,1,0:T(8,128)(2,1)} %broadcast_in_dim.21), calls=%async_computation.4 | async-start | bytes 786432 | tf_op jit(solution)/shard_map/all_to_all | solution.py:31
  143.0 16.0 %all-to-all-start.4 = ((bf16[8,10,16,128]{3,2,1,0:T(8,128)(2,1)}), bf16[8,10,16,128]{3,2,1,0:T(8,128)(2,1)S(1)}, u32[]{:S(2)}, u32[]{:S(2)}) async-start(bf16[8,10,16,128]{3,2,1,0:T(8,128)(2,1)} %shard_map.133), calls=%async_computation.5 | async-start | bytes 655360 | tf_op jit(solution)/shard_map/all_to_all | solution.py:31
  159.0 0.7 copy-start.4
  171.5 16.7 %all-to-all-start.5 = ((bf16[16,16,1024]{2,1,0:T(8,128)(2,1)}), bf16[16,16,1024]{2,1,0:T(8,128)(2,1)S(1)}, u32[]{:S(2)}, u32[]{:S(2)}) async-start(bf16[16,16,1024]{2,1,0:T(8,128)(2,1)} %shard_map.134), calls=%async_computation.6 | async-start | bytes 1048576 | tf_op jit(solution)/shard_map/all_to_all | solution.py:361
Sparse Core Ops, SparseCore 0:
  15.0 58.6 reduce-scatter.1
  75.6 39.1 all-gather.1

commit v16 on v15

--- a/solution.py
+++ b/solution.py
@@ -103,9 +103,9 @@
     )(place, attn_out, out_weight, residual, index_weight)
 
 
-def lift_kernel(core_ref, kept_ref, got_ref, gain_ref, mine_ref, other_ref, o_ref):
+def lift_kernel(core_ref, kept_ref, got_ref, gain_ref, mine_ref, other_ref, hidden_ref, o_ref):
     hidden = (kept_ref[...].astype(jnp.float32) + got_ref[...].astype(jnp.float32)).astype(jnp.bfloat16)
-    o_ref[:, QL + 128 :] = hidden
+    hidden_ref[...] = hidden
     wide = hidden.astype(jnp.float32)
     squares = jnp.sum(wide * wide, axis=1, keepdims=True)
     high = squares.astype(jnp.bfloat16).astype(jnp.float32)
@@ -120,7 +120,7 @@
     lane = lax.broadcasted_iota(jnp.int32, (HALF, 128), 1)
     tail = jnp.where(lane == IHEADS, high, jnp.where(lane == IHEADS + 1, squares - high, 0.0))
     o_ref[:, :QL] = lifted[:, :QL].astype(jnp.bfloat16)
-    o_ref[:, QL : QL + 128] = jnp.where(lane < IHEADS, lifted[:, QL:], tail).astype(jnp.bfloat16)
+    o_ref[:, QL:] = jnp.where(lane < IHEADS, lifted[:, QL:], tail).astype(jnp.bfloat16)
 
 
 def lift(core, kept, got, gain, mine, other):
@@ -128,18 +128,19 @@
     return pl.pallas_call(
         lift_kernel,
         in_specs=[pl.BlockSpec(memory_space=pltpu.SMEM)] + [whole] * 5,
-        out_specs=whole,
-        out_shape=jax.ShapeDtypeStruct((HALF, QL + 128 + DZ), jnp.bfloat16),
+        out_specs=[whole, whole],
+        out_shape=[
+            jax.ShapeDtypeStruct((HALF, DZ), jnp.bfloat16),
+            jax.ShapeDtypeStruct((HALF, QL + 128), jnp.bfloat16),
+        ],
         compiler_params=kernel_params(),
     )(core, kept, got, gain, mine, other)
 
 
-def norm_kernel(high_ref, parts_ref, gain_ref, o_ref, give_ref, hidden_ref):
-    total = parts_ref[0, :, : QL + 128].astype(jnp.float32)
+def norm_kernel(high_ref, parts_ref, gain_ref, o_ref, give_ref):
+    total = parts_ref[0].astype(jnp.float32)
     for n in range(1, NZ):
-        total = total + parts_ref[n, :, : QL + 128].astype(jnp.float32)
-    for n in range(NZ):
-        hidden_ref[:, n * DZ : (n + 1) * DZ] = parts_ref[NZ - 1 - n, :, QL + 128 :]
+        total = total + parts_ref[n].astype(jnp.float32)
     mean = (total[:, 1600:1601] + total[:, 1601:1602]) / D
     inverse = lax.rsqrt(mean + EPSILON)
     raw = (total[:, :QL] * inverse).astype(jnp.bfloat16).astype(jnp.float32)
@@ -160,11 +161,10 @@
     return pl.pallas_call(
         norm_kernel,
         in_specs=[pl.BlockSpec(memory_space=pltpu.SMEM), whole, whole],
-        out_specs=[whole] * 3,
+        out_specs=[whole, whole],
         out_shape=[
             jax.ShapeDtypeStruct((16, QL + 128), jnp.bfloat16),
             jax.ShapeDtypeStruct((16, QL // 2), jnp.bfloat16),
-            jax.ShapeDtypeStruct((16, D), jnp.bfloat16),
         ],
         compiler_params=kernel_params(),
     )(high, parts, gain)
@@ -260,20 +260,27 @@
 
 
 def finish_kernel(numbers_ref, s_ref, pos_ref, o_ref):
+    groups = s_ref.shape[0]
     local = lax.broadcasted_iota(jnp.int32, (16, SLOTS), 1)
     filled, base = numbers_ref[0], numbers_ref[1]
-    for group in range(N_SEQ):
+    for group in range(groups):
         here = slice(group * 16, (group + 1) * 16)
         reach = jnp.minimum(filled, pos_ref[here, :] - base + 1)
-        o_ref[here, :] = jnp.where(local < reach, s_ref[N_SEQ - 1 - group].astype(jnp.float32), 0.0)
+        o_ref[here, :] = jnp.where(local < reach, s_ref[groups - 1 - group].astype(jnp.float32), 0.0)
 
 
 def finish(numbers, scores, own_positions):
-    whole = pl.BlockSpec(memory_space=pltpu.VMEM)
+    steps = 4
+    groups = N_SEQ // steps
     return pl.pallas_call(
         finish_kernel,
-        in_specs=[pl.BlockSpec(memory_space=pltpu.SMEM), whole, whole],
-        out_specs=whole,
+        grid=(steps,),
+        in_specs=[
+            pl.BlockSpec(memory_space=pltpu.SMEM),
+            pl.BlockSpec((groups, 16, SLOTS), lambda i: (steps - 1 - i, 0, 0)),
+            pl.BlockSpec((groups * 16, 1), lambda i: (i, 0)),
+        ],
+        out_specs=pl.BlockSpec((groups * 16, SLOTS), lambda i: (i, 0)),
         out_shape=jax.ShapeDtypeStruct((N_SEQ * 16, SLOTS), jnp.float32),
         compiler_params=kernel_params(),
     )(numbers, scores, own_positions)
@@ -344,15 +351,18 @@
     all_keys = lax.all_gather(index_keys, SEQ, axis=0, tiled=True)
     kept, got = summed[0], swap(summed[1], "yh")
     gain = lax.dynamic_slice_in_dim(norm_gain, z * DZ, DZ).reshape(1, DZ)
-    lifted = lift(jnp.stack([c]).astype(jnp.int32), kept, got, gain, down_mine, down_other)
+    hidden, lifted = lift(jnp.stack([c]).astype(jnp.int32), kept, got, gain, down_mine, down_other)
     lifted, weight_theirs = lax.optimization_barrier((lifted, weight_theirs))
     parts = from_last(lifted.reshape(NZ, own, lifted.shape[1]))
-    packed, give, hidden_rows = normalize(
+    packed, give = normalize(
         jnp.stack([yh]).astype(jnp.int32), parts, latent_gain.reshape(1, QL)
     )
+    packed, hidden = lax.optimization_barrier((packed, hidden))
+    hidden_cols = from_last(hidden.reshape(NZ, own, DZ))
     turned, beside = lax.optimization_barrier((turn(packed), swap(give, "yh")))
     everyone = from_last(jnp.broadcast_to(turned[None, :, :QL], (NZ, own, QL)))
-    everyone = everyone.reshape(HALF, QL)
+    everyone, hidden_cols = lax.optimization_barrier((everyone.reshape(HALF, QL), hidden_cols))
+    hidden_rows = hidden_cols[::-1].transpose(1, 0, 2).reshape(own, D)
     place = jnp.stack([c, yh]).astype(jnp.int32)
     queries = make_queries(place, everyone, index_weight, weight_mine, weight_theirs, packed, beside)
     queries = from_last(queries)

time: 198 us -> 200 us (1.010)
  starting transfers between devices: 55.1 us -> 59.6 us
  waiting for transfers between devices: 44.3 us -> 40.1 us
    all_to_all x3 -> x4, starting transfers between devices: 25.3 us -> 35.8 us  [from_last(): lax.all_to_all(values, 'z', 0, 0, axis_index_groups=[list(range(NZ))[::-1]])]
    all_to_all x3 -> x4, waiting for transfers between devices: 27.4 us -> 23.9 us  [from_last(): lax.all_to_all(values, 'z', 0, 0, axis_index_groups=[list(range(NZ))[::-1]])]
    ppermute x1, starting transfers between devices: 9.91 us -> 6.5 us  [turn(): return lax.ppermute(values, SEQ + HEAD, moves)]
    all_to_all x1, starting transfers between devices: 9.56 us -> 6.98 us  [shards(): lax.all_to_all(scores, SEQ, 0, 0, axis_index_groups=[list(range(N_SEQ))[:...]
    unnamed x17 -> x20, local copies, waits for them, and re-layouts: 3.21 us -> 4.02 us
  transfers between devices with their start and end apart: 12 -> 13, of which waited for: 7 -> 7; matrix products, arithmetic and copies ran while one was open for 5% -> 5% of each run, Pallas kernels for 3% -> 2%
where the time goes in v16:
time: 200 us; the launch traced here: 198 us
  starting transfers between devices  59.6 us (30%)
  blocking collectives  45 us (22%)
  waiting for transfers between devices  40.1 us (20%)
  Pallas kernels  25.4 us (13%)
  between operations  14.9 us (7%)
  local copies, waits for them, and re-layouts  12.5 us (6%)
    all_to_all x4, starting transfers between devices, from_last(): lax.all_to_all(values, 'z', 0, 0, axis_index_groups=[list(range(NZ))[::-1]])  35.8 us
    all_to_all x4, waiting for transfers between devices, from_last(): lax.all_to_all(values, 'z', 0, 0, axis_index_groups=[list(range(NZ))[::-1]])  23.9 us
    all_to_all x1, blocking collectives, down_weight_rows(): lax.all_to_all(jnp.repeat(own, 2, axis=0), HEAD, 0, 0).transpose(1, 0, 2)  22.9 us
    all_to_all x1, blocking collectives, down_weight_rows(): lax.all_to_all(jnp.broadcast_to(wide[None], (8,) + wide.shape), ('x', 'yl...  22 us
    ppermute x5, waiting for transfers between devices, swap(): return lax.ppermute(values, axis, [(0, 1), (1, 0)])  13 us
    pallas_call x1, Pallas kernels, make_scores(): pl.pallas_call(score_kernel, grid=(N_SEQ // per_step,), in_specs=[pl.Bloc...  11.7 us
    ppermute x5, starting transfers between devices, swap(): return lax.ppermute(values, axis, [(0, 1), (1, 0)])  10.3 us
    pallas_call x1, Pallas kernels, project(): pl.pallas_call(project_kernel, in_specs=[pl.BlockSpec(memory_space=pltpu....  7.61 us
  transfers between devices with their start and end apart: 13, of which 7 were waited for; matrix products, arithmetic and copies ran while one was open for 5% of the time, Pallas kernels for 2%

profile of v16, /device:TPU:1, one launch (start us, length us, event | category | flops | bytes accessed | tf_op | source)
XLA Modules:
  0.0 197.6 jit_solution(13086874876285373798)
XLA Ops:
  7.2 7.6 %shard_map.130 = (bf16[8,2,128,896]{3,2,1,0:T(8,128)(2,1)}, bf16[768,512]{1,0:T(8,128)(2,1)}) custom-call(s32[1]{0:T(128)} %bitcast.2.place_ref, bf16[256,512]{1,0:T(8,128)(2,1)} %a_ref.1, bf16[512,7168]{1,0:T(8,128)(2,1)} %b_ref.1, bf16[16,7168]{1,0:T(8,128)(2,1)} %res_ref.1, bf16[1536,512]{1,0:T(8,128)(2,1)} %own_ref.1), custom_call_target="tpu_custom_call" | custom-call | tf_op jit(solution)/shard_map/pallas_call | solution.py:87
  14.9 3.8 %collective-permute-start = (bf16[768,512]{1,0:T(8,128)(2,1)}, bf16[768,512]{1,0:T(8,128)(2,1)S(1)}, u32[]{:S(2)}, u32[]{:S(2)}) collective-permute-start(bf16[768,512]{1,0:T(8,128)(2,1)} %get-tuple-element.24), channel_id=1, source_target_pairs={{0,1},{1,0},{2,3},{3,2},{4,5},{5,4},{6,7},{7,6},{8,9},{9,8},{10,11... | collective-permute-start | bytes 2359304 | tf_op jit(solution)/shard_map/ppermute | solution.py:27
  20.9 22.9 %all_to_all.35 = bf16[16,56,100]{2,1,0:T(8,128)(2,1)S(1)} all-to-all(bf16[16,56,100]{2,1,0:T(8,128)(2,1)S(1)} %bitcast.41), channel_id=1, replica_groups=mesh['x'=4,'yl'=2,'c'=2,'z'=8,'yh'=2] {'z','yh'}, dimensions={0} | all-to-all | bytes 358400 | tf_op jit(solution)/shard_map/all_to_all | solution.py:296
  45.6 22.0 %all_to_all.36 = bf16[8,56,1664]{2,1,0:T(8,128)(2,1)S(1)} all-to-all(bf16[8,56,1664]{2,1,0:T(8,128)(2,1)S(1)} %broadcast_in_dim.20), channel_id=1, replica_groups=mesh['x'=4,'yl'=2,'c'=2,'z'=8,'yh'=2] {'x','yl'}, dimensions={0} | all-to-all | bytes 2981888 | tf_op jit(solution)/shard_map/all_to_all | solution.py:307
  67.7 3.7 %collective-permute-start.1 = (bf16[448,1664]{1,0:T(8,128)(2,1)S(1)}, bf16[448,1664]{1,0:T(8,128)(2,1)S(1)}, u32[]{:S(2)}, u32[]{:S(2)}) collective-permute-start(bf16[448,1664]{1,0:T(8,128)(2,1)S(1)} %bitcast.33), channel_id=1, source_target_pairs={{0,16},{16,0},{1,17},{17,1},{2,18},{18,2},{3,19},{19,3},{4,20},{20... | collective-permute-start | bytes 4472840 | tf_op jit(solution)/shard_map/ppermute | solution.py:27
  71.4 2.9 %collective-permute-done.1.other_ref = bf16[448,1664]{1,0:T(8,128)(2,1)S(1)} collective-permute-done((bf16[448,1664]{1,0:T(8,128)(2,1)S(1)}, bf16[448,1664]{1,0:T(8,128)(2,1)S(1)}, u32[]{:S(2)}, u32[]{:S(2)}) %collective-permute-start.1) | collective-permute-done | bytes 1490976 | tf_op jit(solution)/shard_map/ppermute | solution.py:27
  74.8 1.8 slice_bitcast_fusion
  76.6 2.1 %collective-permute-start.2 = (bf16[128,896]{1,0:T(8,128)(2,1)}, bf16[128,896]{1,0:T(8,128)(2,1)S(1)}, u32[]{:S(2)}, u32[]{:S(2)}) collective-permute-start(bf16[128,896]{1,0:T(8,128)(2,1)} %get-tuple-element.55), channel_id=1, source_target_pairs={{0,1},{1,0},{2,3},{3,2},{4,5},{5,4},{6,7},{7,6},{8,9},{9,8},{10,11... | collective-permute-start | bytes 688136 | tf_op jit(solution)/shard_map/ppermute | solution.py:27
  79.5 5.9 %collective-permute-done.2.got_ref = bf16[128,896]{1,0:T(8,128)(2,1)S(1)} collective-permute-done((bf16[128,896]{1,0:T(8,128)(2,1)}, bf16[128,896]{1,0:T(8,128)(2,1)S(1)}, u32[]{:S(2)}, u32[]{:S(2)}) %collective-permute-start.2) | collective-permute-done | bytes 229408 | tf_op jit(solution)/shard_map/ppermute | solution.py:27
  85.3 0.9 shard_map.131
  87.0 6.3 %all-to-all-start.2 = ((bf16[8,16,1664]{2,1,0:T(8,128)(2,1)}), bf16[8,16,1664]{2,1,0:T(8,128)(2,1)S(1)}, u32[]{:S(2)}, u32[]{:S(2)}) async-start(bf16[8,16,1664]{2,1,0:T(8,128)(2,1)} %bitcast.36), calls=%async_computation.3 | async-start | bytes 851968 | tf_op jit(solution)/shard_map/all_to_all | solution.py:31
  93.4 8.2 %all-to-all-done.2.parts_ref = bf16[8,16,1664]{2,1,0:T(8,128)(2,1)S(1)} async-done(((bf16[8,16,1664]{2,1,0:T(8,128)(2,1)}), bf16[8,16,1664]{2,1,0:T(8,128)(2,1)S(1)}, u32[]{:S(2)}, u32[]{:S(2)}) %all-to-all-start.2) | async-done | bytes 426016 | tf_op jit(solution)/shard_map/all_to_all | solution.py:31
  102.0 9.8 %all-to-all-start.4 = ((bf16[8,16,896]{2,1,0:T(8,128)(2,1)}), bf16[8,16,896]{2,1,0:T(8,128)(2,1)S(1)}, u32[]{:S(2)}, u32[]{:S(2)}) async-start(bf16[8,16,896]{2,1,0:T(8,128)(2,1)} %bitcast.12), calls=%async_computation.5 | async-start | bytes 458752 | tf_op jit(solution)/shard_map/all_to_all | solution.py:31
  111.8 6.5 %collective-permute-start.4 = (bf16[16,1664]{1,0:T(8,128)(2,1)S(1)}, bf16[16,1664]{1,0:T(8,128)(2,1)S(1)}, u32[]{:S(2)}, u32[]{:S(2)}) collective-permute-start(bf16[16,1664]{1,0:T(8,128)(2,1)S(1)} %get-tuple-element.34.final_ref), channel_id=1, source_target_pairs={{0,0},{1,16},{2,32},{3,48},{4,64},{5,80},{6,96},{7,112},{8,128},{9... | collective-permute-start | bytes 159752 | tf_op jit(solution)/shard_map/ppermute | solution.py:314
  118.4 4.2 %collective-permute-done.5.beside_ref = bf16[16,768]{1,0:T(8,128)(2,1)S(1)} collective-permute-done((bf16[16,768]{1,0:T(8,128)(2,1)S(1)}, bf16[16,768]{1,0:T(8,128)(2,1)S(1)}, u32[]{:S(2)}, u32[]{:S(2)}) %collective-permute-start.5) | collective-permute-done | bytes 24608 | tf_op jit(solution)/shard_map/ppermute | solution.py:27
  123.4 10.8 %all-to-all-start.3 = ((bf16[8,16,1536]{2,1,0:T(8,128)(2,1)}), bf16[8,16,1536]{2,1,0:T(8,128)(2,1)S(1)}, u32[]{:S(2)}, u32[]{:S(2)}) async-start(bf16[8,16,1536]{2,1,0:T(8,128)(2,1)} %broadcast_in_dim.21), calls=%async_computation.4 | async-start | bytes 786432 | tf_op jit(solution)/shard_map/all_to_all | solution.py:31
  134.2 9.2 %all-to-all-done.3 = bf16[8,16,1536]{2,1,0:T(8,128)(2,1)S(1)} async-done(((bf16[8,16,1536]{2,1,0:T(8,128)(2,1)}), bf16[8,16,1536]{2,1,0:T(8,128)(2,1)S(1)}, u32[]{:S(2)}, u32[]{:S(2)}) %all-to-all-start.3) | async-done | bytes 393248 | tf_op jit(solution)/shard_map/all_to_all | solution.py:31
  143.4 2.5 %shard_map.133 = bf16[8,10,16,128]{3,2,1,0:T(8,128)(2,1)} custom-call(s32[2]{0:T(128)S(1)} %pad_add_fusion.place_ref, bf16[128,1536]{1,0:T(8,128)(2,1)S(1)} %bitcast.35, bf16[1536,512]{1,0:T(8,128)(2,1)S(1)} %copy-done, bf16[768,512]{1,0:T(8,128)(2,1)S(1)} %copy-done.2, bf16[768,512]{1,0:T(8,128)(2,1)} %collective-permute-done.3.theirs_ref, ...), custom_call_target="tpu_custom_call" | custom-call | tf_op jit(solution)/shard_map/pallas_call | solution.py:198
  145.9 8.9 %all-to-all-start.5 = ((bf16[8,10,16,128]{3,2,1,0:T(8,128)(2,1)}), bf16[8,10,16,128]{3,2,1,0:T(8,128)(2,1)S(1)}, u32[]{:S(2)}, u32[]{:S(2)}) async-start(bf16[8,10,16,128]{3,2,1,0:T(8,128)(2,1)} %shard_map.133), calls=%async_computation.6 | async-start | bytes 655360 | tf_op jit(solution)/shard_map/all_to_all | solution.py:31
  155.5 6.5 %all-to-all-done.5.q_ref = bf16[8,10,16,128]{3,2,1,0:T(8,128)(2,1)S(1)} async-done(((bf16[8,10,16,128]{3,2,1,0:T(8,128)(2,1)}), bf16[8,10,16,128]{3,2,1,0:T(8,128)(2,1)S(1)}, u32[]{:S(2)}, u32[]{:S(2)}) %all-to-all-start.5) | async-done | bytes 327712 | tf_op jit(solution)/shard_map/all_to_all | solution.py:31
  162.7 11.7 %shard_map.134 = bf16[16,16,1024]{2,1,0:T(8,128)(2,1)} custom-call(bf16[8,10,16,128]{3,2,1,0:T(8,128)(2,1)} %copy-done.5, bf16[16,128]{1,0:T(8,128)(2,1)} %slice.27.w_ref, bf16[16384,128]{1,0:T(8,128)(2,1)} %all-gather.2.cloned.1.call-done.k_ref), custom_call_target="tpu_custom_call" | custom-call | flops 8589934592 | bytes 8388608 | tf_op jit(solution)/shard_map/pallas_call | solution.py:241
  174.4 7.0 %all-to-all-start.6 = ((bf16[16,16,1024]{2,1,0:T(8,128)(2,1)}), bf16[16,16,1024]{2,1,0:T(8,128)(2,1)S(1)}, u32[]{:S(2)}, u32[]{:S(2)}) async-start(bf16[16,16,1024]{2,1,0:T(8,128)(2,1)} %shard_map.134), calls=%async_computation.7 | async-start | bytes 1048576 | tf_op jit(solution)/shard_map/all_to_all | solution.py:371
  185.3 3.1 %all-to-all-done.6.s_ref = bf16[16,16,1024]{2,1,0:T(8,128)(2,1)S(1)} async-done(((bf16[16,16,1024]{2,1,0:T(8,128)(2,1)}), bf16[16,16,1024]{2,1,0:T(8,128)(2,1)S(1)}, u32[]{:S(2)}, u32[]{:S(2)}) %all-to-all-start.6) | async-done | bytes 524320 | tf_op jit(solution)/shard_map/all_to_all | solution.py:371
  188.5 2.3 %shard_map.135 = f32[256,1024]{1,0:T(8,128)} custom-call(s32[2]{0:T(128)S(1)} %pad_add_fusion.1.numbers_ref, bf16[16,16,1024]{2,1,0:T(8,128)(2,1)S(1)} %all-to-all-done.6.s_ref, s32[256,1]{1,0:T(8,128)S(1)} %copy.33.pos_ref), custom_call_target="tpu_custom_call" | custom-call | tf_op jit(solution)/shard_map/pallas_call | solution.py:275
  (59 shorter events, 12.0 us)
Async XLA Ops:
  7.2 67.1 %reduce-scatter.2.cloned.1.call-start = ((), (), s32[]{:S(2)}) async-start(), calls=%async_computation.8 | async-start | bytes 4128768 | tf_op jit(solution)/shard_map/reduce_scatter | solution.py:341
  14.8 3.9 %copy-start.6 = (bf16[7168,4]{0,1:T(4,128)(2,1)S(1)}, bf16[7168,4]{0,1:T(4,128)(2,1)}, u32[]{:S(2)}) copy-start(bf16[7168,4]{0,1:T(4,128)(2,1)} %param.16) | copy-start | bytes 172036
  14.9 4.6 %copy-start.4 = (bf16[7168,96]{0,1:T(8,128)(2,1)S(1)}, bf16[7168,96]{0,1:T(8,128)(2,1)}, u32[]{:S(2)}) copy-start(bf16[7168,96]{0,1:T(8,128)(2,1)} %param.15) | copy-start | bytes 4128772
  14.9 147.1 %all-gather.2.cloned.1.call-start = ((), (), s32[]{:S(2)}) async-start(), calls=%async_computation.9 | async-start | bytes 4456448 | tf_op jit(solution)/shard_map/all_gather | solution.py:351
  14.9 29.7 %collective-permute-start = (bf16[768,512]{1,0:T(8,128)(2,1)}, bf16[768,512]{1,0:T(8,128)(2,1)S(1)}, u32[]{:S(2)}, u32[]{:S(2)}) collective-permute-start(bf16[768,512]{1,0:T(8,128)(2,1)} %get-tuple-element.24), channel_id=1, source_target_pairs={{0,1},{1,0},{2,3},{3,2},{4,5},{5,4},{6,7},{7,6},{8,9},{9,8},{10,11... | collective-permute-start | bytes 2359304 | tf_op jit(solution)/shard_map/ppermute | solution.py:27
  44.6 0.9 copy-start.1
  67.7 6.6 %collective-permute-start.1 = (bf16[448,1664]{1,0:T(8,128)(2,1)S(1)}, bf16[448,1664]{1,0:T(8,128)(2,1)S(1)}, u32[]{:S(2)}, u32[]{:S(2)}) collective-permute-start(bf16[448,1664]{1,0:T(8,128)(2,1)S(1)} %bitcast.33), channel_id=1, source_target_pairs={{0,16},{16,0},{1,17},{17,1},{2,18},{18,2},{3,19},{19,3},{4,20},{20... | collective-permute-start | bytes 4472840 | tf_op jit(solution)/shard_map/ppermute | solution.py:27
  74.3 12.7 %collective-permute-start.3 = (bf16[768,512]{1,0:T(8,128)(2,1)}, bf16[768,512]{1,0:T(8,128)(2,1)}, u32[]{:S(2)}, u32[]{:S(2)}) collective-permute-start(bf16[768,512]{1,0:T(8,128)(2,1)} %copy-done.1), channel_id=1, source_target_pairs={{0,16},{16,0},{1,17},{17,1},{2,18},{18,2},{3,19},{19,3},{4,20},{20... | collective-permute-start | bytes 2359304 | tf_op jit(solution)/shard_map/ppermute | solution.py:27
  76.6 8.8 %collective-permute-start.2 = (bf16[128,896]{1,0:T(8,128)(2,1)}, bf16[128,896]{1,0:T(8,128)(2,1)S(1)}, u32[]{:S(2)}, u32[]{:S(2)}) collective-permute-start(bf16[128,896]{1,0:T(8,128)(2,1)} %get-tuple-element.55), channel_id=1, source_target_pairs={{0,1},{1,0},{2,3},{3,2},{4,5},{5,4},{6,7},{7,6},{8,9},{9,8},{10,11... | collective-permute-start | bytes 688136 | tf_op jit(solution)/shard_map/ppermute | solution.py:27
  85.3 8.0 %copy-start.7 = (bf16[1536]{0:T(1024)(128)(2,1)S(1)}, bf16[1536]{0:T(1024)(128)(2,1)}, u32[]{:S(2)}) copy-start(bf16[1536]{0:T(1024)(128)(2,1)} %param.17) | copy-start | bytes 9220
  86.2 0.8 copy-start.3
  87.0 56.4 %copy-start = (bf16[1536,512]{1,0:T(8,128)(2,1)S(1)}, bf16[1536,512]{1,0:T(8,128)(2,1)}, u32[]{:S(2)}) copy-start(bf16[1536,512]{1,0:T(8,128)(2,1)} %own_ref.1) | copy-start | bytes 4718596
  87.0 56.4 %copy-start.2 = (bf16[768,512]{1,0:T(8,128)(2,1)S(1)}, bf16[768,512]{1,0:T(8,128)(2,1)}, u32[]{:S(2)}) copy-start(bf16[768,512]{1,0:T(8,128)(2,1)} %copy-done.1) | copy-start | bytes 2359300
  87.0 14.5 %all-to-all-start.2 = ((bf16[8,16,1664]{2,1,0:T(8,128)(2,1)}), bf16[8,16,1664]{2,1,0:T(8,128)(2,1)S(1)}, u32[]{:S(2)}, u32[]{:S(2)}) async-start(bf16[8,16,1664]{2,1,0:T(8,128)(2,1)} %bitcast.36), calls=%async_computation.3 | async-start | bytes 851968 | tf_op jit(solution)/shard_map/all_to_all | solution.py:31
  102.0 20.6 %all-to-all-start.4 = ((bf16[8,16,896]{2,1,0:T(8,128)(2,1)}), bf16[8,16,896]{2,1,0:T(8,128)(2,1)S(1)}, u32[]{:S(2)}, u32[]{:S(2)}) async-start(bf16[8,16,896]{2,1,0:T(8,128)(2,1)} %bitcast.12), calls=%async_computation.5 | async-start | bytes 458752 | tf_op jit(solution)/shard_map/all_to_all | solution.py:31
  111.8 10.8 %collective-permute-start.4 = (bf16[16,1664]{1,0:T(8,128)(2,1)S(1)}, bf16[16,1664]{1,0:T(8,128)(2,1)S(1)}, u32[]{:S(2)}, u32[]{:S(2)}) collective-permute-start(bf16[16,1664]{1,0:T(8,128)(2,1)S(1)} %get-tuple-element.34.final_ref), channel_id=1, source_target_pairs={{0,0},{1,16},{2,32},{3,48},{4,64},{5,80},{6,96},{7,112},{8,128},{9... | collective-permute-start | bytes 159752 | tf_op jit(solution)/shard_map/ppermute | solution.py:314
  118.3 4.3 %collective-permute-start.5 = (bf16[16,768]{1,0:T(8,128)(2,1)S(1)}, bf16[16,768]{1,0:T(8,128)(2,1)S(1)}, u32[]{:S(2)}, u32[]{:S(2)}) collective-permute-start(bf16[16,768]{1,0:T(8,128)(2,1)S(1)} %get-tuple-element.35), channel_id=1, source_target_pairs={{0,1},{1,0},{2,3},{3,2},{4,5},{5,4},{6,7},{7,6},{8,9},{9,8},{10,11... | collective-permute-start | bytes 73736 | tf_op jit(solution)/shard_map/ppermute | solution.py:27
  123.4 20.1 %all-to-all-start.3 = ((bf16[8,16,1536]{2,1,0:T(8,128)(2,1)}), bf16[8,16,1536]{2,1,0:T(8,128)(2,1)S(1)}, u32[]{:S(2)}, u32[]{:S(2)}) async-start(bf16[8,16,1536]{2,1,0:T(8,128)(2,1)} %broadcast_in_dim.21), calls=%async_computation.4 | async-start | bytes 786432 | tf_op jit(solution)/shard_map/all_to_all | solution.py:31
  145.9 16.0 %all-to-all-start.5 = ((bf16[8,10,16,128]{3,2,1,0:T(8,128)(2,1)}), bf16[8,10,16,128]{3,2,1,0:T(8,128)(2,1)S(1)}, u32[]{:S(2)}, u32[]{:S(2)}) async-start(bf16[8,10,16,128]{3,2,1,0:T(8,128)(2,1)} %shard_map.133), calls=%async_computation.6 | async-start | bytes 655360 | tf_op jit(solution)/shard_map/all_to_all | solution.py:31
  162.0 0.7 copy-start.5
  174.4 14.1 %all-to-all-start.6 = ((bf16[16,16,1024]{2,1,0:T(8,128)(2,1)}), bf16[16,16,1024]{2,1,0:T(8,128)(2,1)S(1)}, u32[]{:S(2)}, u32[]{:S(2)}) async-start(bf16[16,16,1024]{2,1,0:T(8,128)(2,1)} %shard_map.134), calls=%async_computation.7 | async-start | bytes 1048576 | tf_op jit(solution)/shard_map/all_to_all | solution.py:371
Sparse Core Ops, SparseCore 0:
  15.0 58.6 reduce-scatter.1
  75.6 39.1 all-gather.1

commit v17 on v16

--- a/solution.py
+++ b/solution.py
@@ -260,27 +260,20 @@
 
 
 def finish_kernel(numbers_ref, s_ref, pos_ref, o_ref):
-    groups = s_ref.shape[0]
     local = lax.broadcasted_iota(jnp.int32, (16, SLOTS), 1)
     filled, base = numbers_ref[0], numbers_ref[1]
-    for group in range(groups):
+    for group in range(N_SEQ):
         here = slice(group * 16, (group + 1) * 16)
         reach = jnp.minimum(filled, pos_ref[here, :] - base + 1)
-        o_ref[here, :] = jnp.where(local < reach, s_ref[groups - 1 - group].astype(jnp.float32), 0.0)
+        o_ref[here, :] = jnp.where(local < reach, s_ref[N_SEQ - 1 - group].astype(jnp.float32), 0.0)
 
 
 def finish(numbers, scores, own_positions):
-    steps = 4
-    groups = N_SEQ // steps
+    whole = pl.BlockSpec(memory_space=pltpu.VMEM)
     return pl.pallas_call(
         finish_kernel,
-        grid=(steps,),
-        in_specs=[
-            pl.BlockSpec(memory_space=pltpu.SMEM),
-            pl.BlockSpec((groups, 16, SLOTS), lambda i: (steps - 1 - i, 0, 0)),
-            pl.BlockSpec((groups * 16, 1), lambda i: (i, 0)),
-        ],
-        out_specs=pl.BlockSpec((groups * 16, SLOTS), lambda i: (i, 0)),
+        in_specs=[pl.BlockSpec(memory_space=pltpu.SMEM), whole, whole],
+        out_specs=whole,
         out_shape=jax.ShapeDtypeStruct((N_SEQ * 16, SLOTS), jnp.float32),
         compiler_params=kernel_params(),
     )(numbers, scores, own_positions)
@@ -344,7 +337,6 @@
     down_mine, down_other, weight_mine = down_weight_rows(
         latent_weight, index_proj, c * 8 + x * 2 + yl, weight_mine
     )
-    weight_theirs = swap(weight_mine, "c")
     summed, index_keys, down_mine, down_other = lax.optimization_barrier(
         (summed, index_keys, down_mine, down_other)
     )
@@ -352,12 +344,13 @@
     kept, got = summed[0], swap(summed[1], "yh")
     gain = lax.dynamic_slice_in_dim(norm_gain, z * DZ, DZ).reshape(1, DZ)
     hidden, lifted = lift(jnp.stack([c]).astype(jnp.int32), kept, got, gain, down_mine, down_other)
-    lifted, weight_theirs = lax.optimization_barrier((lifted, weight_theirs))
     parts = from_last(lifted.reshape(NZ, own, lifted.shape[1]))
     packed, give = normalize(
         jnp.stack([yh]).astype(jnp.int32), parts, latent_gain.reshape(1, QL)
     )
-    packed, hidden = lax.optimization_barrier((packed, hidden))
+    packed, weight_mine = lax.optimization_barrier((packed, weight_mine))
+    weight_theirs = swap(weight_mine, "c")
+    weight_theirs, hidden = lax.optimization_barrier((weight_theirs, hidden))
     hidden_cols = from_last(hidden.reshape(NZ, own, DZ))
     turned, beside = lax.optimization_barrier((turn(packed), swap(give, "yh")))
     everyone = from_last(jnp.broadcast_to(turned[None, :, :QL], (NZ, own, QL)))

time: 200 us -> 208 us (1.040)
  starting transfers between devices: 59.6 us -> 64.6 us
  waiting for transfers between devices: 40.1 us -> 44.5 us
    all_to_all x4, waiting for transfers between devices: 23.9 us -> 28.4 us  [from_last(): lax.all_to_all(values, 'z', 0, 0, axis_index_groups=[list(range(NZ))[::-1]])]
    all_to_all x1, starting transfers between devices: 6.98 us -> 10.9 us  [shards(): lax.all_to_all(scores, SEQ, 0, 0, axis_index_groups=[list(range(N_SEQ))[:...]
    ppermute x5, starting transfers between devices: 10.3 us -> 13.8 us  [swap(): return lax.ppermute(values, axis, [(0, 1), (1, 0)])]
  transfers between devices with their start and end apart: 13 -> 13, of which waited for: 7 -> 8; matrix products, arithmetic and copies ran while one was open for 5% -> 5% of each run, Pallas kernels for 2% -> 2%
where the time goes in v17:
time: 208 us; the launch traced here: 206 us
  starting transfers between devices  64.6 us (31%)
  blocking collectives  45 us (22%)
  waiting for transfers between devices  44.5 us (21%)
  Pallas kernels  24.8 us (12%)
  between operations  14.9 us (7%)
  local copies, waits for them, and re-layouts  12.4 us (6%)
    all_to_all x4, starting transfers between devices, from_last(): lax.all_to_all(values, 'z', 0, 0, axis_index_groups=[list(range(NZ))[::-1]])  35.4 us
    all_to_all x4, waiting for transfers between devices, from_last(): lax.all_to_all(values, 'z', 0, 0, axis_index_groups=[list(range(NZ))[::-1]])  28.4 us
    all_to_all x1, blocking collectives, down_weight_rows(): lax.all_to_all(jnp.repeat(own, 2, axis=0), HEAD, 0, 0).transpose(1, 0, 2)  22.9 us
    all_to_all x1, blocking collectives, down_weight_rows(): lax.all_to_all(jnp.broadcast_to(wide[None], (8,) + wide.shape), ('x', 'yl...  22 us
    ppermute x5, starting transfers between devices, swap(): return lax.ppermute(values, axis, [(0, 1), (1, 0)])  13.8 us
    ppermute x5, waiting for transfers between devices, swap(): return lax.ppermute(values, axis, [(0, 1), (1, 0)])  12.9 us
    pallas_call x1, Pallas kernels, make_scores(): pl.pallas_call(score_kernel, grid=(N_SEQ // per_step,), in_specs=[pl.Bloc...  11.7 us
    all_to_all x1, starting transfers between devices, shards(): lax.all_to_all(scores, SEQ, 0, 0, axis_index_groups=[list(range(N_SEQ))[:...  10.9 us
  transfers between devices with their start and end apart: 13, of which 8 were waited for; matrix products, arithmetic and copies ran while one was open for 5% of the time, Pallas kernels for 2%

profile of v17, /device:TPU:1, one launch (start us, length us, event | category | flops | bytes accessed | tf_op | source)
XLA Modules:
  0.0 206.4 jit_solution(17466394781004728904)
XLA Ops:
  7.2 7.6 %shard_map.130 = (bf16[8,2,128,896]{3,2,1,0:T(8,128)(2,1)}, bf16[768,512]{1,0:T(8,128)(2,1)}) custom-call(s32[1]{0:T(128)} %bitcast.2.place_ref, bf16[256,512]{1,0:T(8,128)(2,1)} %a_ref.1, bf16[512,7168]{1,0:T(8,128)(2,1)} %b_ref.1, bf16[16,7168]{1,0:T(8,128)(2,1)} %res_ref.1, bf16[1536,512]{1,0:T(8,128)(2,1)} %own_ref.1), custom_call_target="tpu_custom_call" | custom-call | tf_op jit(solution)/shard_map/pallas_call | solution.py:87
  14.9 3.8 %collective-permute-start = (bf16[768,512]{1,0:T(8,128)(2,1)}, bf16[768,512]{1,0:T(8,128)(2,1)S(1)}, u32[]{:S(2)}, u32[]{:S(2)}) collective-permute-start(bf16[768,512]{1,0:T(8,128)(2,1)} %get-tuple-element.24), channel_id=1, source_target_pairs={{0,1},{1,0},{2,3},{3,2},{4,5},{5,4},{6,7},{7,6},{8,9},{9,8},{10,11... | collective-permute-start | bytes 2359304 | tf_op jit(solution)/shard_map/ppermute | solution.py:27
  20.9 22.9 %all_to_all.35 = bf16[16,56,100]{2,1,0:T(8,128)(2,1)S(1)} all-to-all(bf16[16,56,100]{2,1,0:T(8,128)(2,1)S(1)} %bitcast.41), channel_id=1, replica_groups=mesh['x'=4,'yl'=2,'c'=2,'z'=8,'yh'=2] {'z','yh'}, dimensions={0} | all-to-all | bytes 358400 | tf_op jit(solution)/shard_map/all_to_all | solution.py:289
  45.6 22.0 %all_to_all.36 = bf16[8,56,1664]{2,1,0:T(8,128)(2,1)S(1)} all-to-all(bf16[8,56,1664]{2,1,0:T(8,128)(2,1)S(1)} %broadcast_in_dim.20), channel_id=1, replica_groups=mesh['x'=4,'yl'=2,'c'=2,'z'=8,'yh'=2] {'x','yl'}, dimensions={0} | all-to-all | bytes 2981888 | tf_op jit(solution)/shard_map/all_to_all | solution.py:300
  67.7 3.7 %collective-permute-start.1 = (bf16[448,1664]{1,0:T(8,128)(2,1)S(1)}, bf16[448,1664]{1,0:T(8,128)(2,1)S(1)}, u32[]{:S(2)}, u32[]{:S(2)}) collective-permute-start(bf16[448,1664]{1,0:T(8,128)(2,1)S(1)} %bitcast.33), channel_id=1, source_target_pairs={{0,16},{16,0},{1,17},{17,1},{2,18},{18,2},{3,19},{19,3},{4,20},{20... | collective-permute-start | bytes 4472840 | tf_op jit(solution)/shard_map/ppermute | solution.py:27
  71.4 2.9 %collective-permute-done.1.other_ref = bf16[448,1664]{1,0:T(8,128)(2,1)S(1)} collective-permute-done((bf16[448,1664]{1,0:T(8,128)(2,1)S(1)}, bf16[448,1664]{1,0:T(8,128)(2,1)S(1)}, u32[]{:S(2)}, u32[]{:S(2)}) %collective-permute-start.1) | collective-permute-done | bytes 1490976 | tf_op jit(solution)/shard_map/ppermute | solution.py:27
  74.3 1.8 slice_bitcast_fusion
  76.1 2.1 %collective-permute-start.2 = (bf16[128,896]{1,0:T(8,128)(2,1)}, bf16[128,896]{1,0:T(8,128)(2,1)S(1)}, u32[]{:S(2)}, u32[]{:S(2)}) collective-permute-start(bf16[128,896]{1,0:T(8,128)(2,1)} %get-tuple-element.55), channel_id=1, source_target_pairs={{0,1},{1,0},{2,3},{3,2},{4,5},{5,4},{6,7},{7,6},{8,9},{9,8},{10,11... | collective-permute-start | bytes 688136 | tf_op jit(solution)/shard_map/ppermute | solution.py:27
  79.0 5.6 %collective-permute-done.2.got_ref = bf16[128,896]{1,0:T(8,128)(2,1)S(1)} collective-permute-done((bf16[128,896]{1,0:T(8,128)(2,1)}, bf16[128,896]{1,0:T(8,128)(2,1)S(1)}, u32[]{:S(2)}, u32[]{:S(2)}) %collective-permute-start.2) | collective-permute-done | bytes 229408 | tf_op jit(solution)/shard_map/ppermute | solution.py:27
  86.3 6.3 %all-to-all-start.2 = ((bf16[8,16,1664]{2,1,0:T(8,128)(2,1)}), bf16[8,16,1664]{2,1,0:T(8,128)(2,1)S(1)}, u32[]{:S(2)}, u32[]{:S(2)}) async-start(bf16[8,16,1664]{2,1,0:T(8,128)(2,1)} %bitcast.36), calls=%async_computation.3 | async-start | bytes 851968 | tf_op jit(solution)/shard_map/all_to_all | solution.py:31
  92.6 7.9 %all-to-all-done.2.parts_ref = bf16[8,16,1664]{2,1,0:T(8,128)(2,1)S(1)} async-done(((bf16[8,16,1664]{2,1,0:T(8,128)(2,1)}), bf16[8,16,1664]{2,1,0:T(8,128)(2,1)S(1)}, u32[]{:S(2)}, u32[]{:S(2)}) %all-to-all-start.2) | async-done | bytes 426016 | tf_op jit(solution)/shard_map/all_to_all | solution.py:31
  100.9 4.1 %collective-permute-start.5 = (bf16[768,512]{1,0:T(8,128)(2,1)}, bf16[768,512]{1,0:T(8,128)(2,1)}, u32[]{:S(2)}, u32[]{:S(2)}) collective-permute-start(bf16[768,512]{1,0:T(8,128)(2,1)} %copy-done.1), channel_id=1, source_target_pairs={{0,16},{16,0},{1,17},{17,1},{2,18},{18,2},{3,19},{19,3},{4,20},{20... | collective-permute-start | bytes 2359304 | tf_op jit(solution)/shard_map/ppermute | solution.py:27
  105.0 4.5 %collective-permute-start.3 = (bf16[16,1664]{1,0:T(8,128)(2,1)S(1)}, bf16[16,1664]{1,0:T(8,128)(2,1)S(1)}, u32[]{:S(2)}, u32[]{:S(2)}) collective-permute-start(bf16[16,1664]{1,0:T(8,128)(2,1)S(1)} %get-tuple-element.32.final_ref), channel_id=1, source_target_pairs={{0,0},{1,16},{2,32},{3,48},{4,64},{5,80},{6,96},{7,112},{8,128},{9... | collective-permute-start | bytes 159752 | tf_op jit(solution)/shard_map/ppermute | solution.py:307
  109.6 4.3 %collective-permute-done.4.beside_ref = bf16[16,768]{1,0:T(8,128)(2,1)S(1)} collective-permute-done((bf16[16,768]{1,0:T(8,128)(2,1)S(1)}, bf16[16,768]{1,0:T(8,128)(2,1)S(1)}, u32[]{:S(2)}, u32[]{:S(2)}) %collective-permute-start.4) | collective-permute-done | bytes 24608 | tf_op jit(solution)/shard_map/ppermute | solution.py:27
  114.7 11.4 %all-to-all-start.3 = ((bf16[8,16,1536]{2,1,0:T(8,128)(2,1)}), bf16[8,16,1536]{2,1,0:T(8,128)(2,1)S(1)}, u32[]{:S(2)}, u32[]{:S(2)}) async-start(bf16[8,16,1536]{2,1,0:T(8,128)(2,1)} %broadcast_in_dim.21), calls=%async_computation.4 | async-start | bytes 786432 | tf_op jit(solution)/shard_map/all_to_all | solution.py:31
  126.1 8.9 %all-to-all-done.3 = bf16[8,16,1536]{2,1,0:T(8,128)(2,1)S(1)} async-done(((bf16[8,16,1536]{2,1,0:T(8,128)(2,1)}), bf16[8,16,1536]{2,1,0:T(8,128)(2,1)S(1)}, u32[]{:S(2)}, u32[]{:S(2)}) %all-to-all-start.3) | async-done | bytes 393248 | tf_op jit(solution)/shard_map/all_to_all | solution.py:31
  135.0 8.5 %all-to-all-start.4 = ((bf16[8,16,896]{2,1,0:T(8,128)(2,1)}), bf16[8,16,896]{2,1,0:T(8,128)(2,1)S(1)}, u32[]{:S(2)}, u32[]{:S(2)}) async-start(bf16[8,16,896]{2,1,0:T(8,128)(2,1)} %bitcast.12), calls=%async_computation.5 | async-start | bytes 458752 | tf_op jit(solution)/shard_map/all_to_all | solution.py:31
  143.5 5.7 %all-to-all-done.4 = bf16[8,16,896]{2,1,0:T(8,128)(2,1)S(1)} async-done(((bf16[8,16,896]{2,1,0:T(8,128)(2,1)}), bf16[8,16,896]{2,1,0:T(8,128)(2,1)S(1)}, u32[]{:S(2)}, u32[]{:S(2)}) %all-to-all-start.4) | async-done | bytes 229408 | tf_op jit(solution)/shard_map/all_to_all | solution.py:31
  149.2 2.5 %shard_map.133 = bf16[8,10,16,128]{3,2,1,0:T(8,128)(2,1)} custom-call(s32[2]{0:T(128)S(1)} %pad_add_fusion.place_ref, bf16[128,1536]{1,0:T(8,128)(2,1)S(1)} %bitcast.35, bf16[1536,512]{1,0:T(8,128)(2,1)S(1)} %copy-done, bf16[768,512]{1,0:T(8,128)(2,1)S(1)} %copy-done.2, bf16[768,512]{1,0:T(8,128)(2,1)} %collective-permute-done.5.theirs_ref, ...), custom_call_target="tpu_custom_call" | custom-call | tf_op jit(solution)/shard_map/pallas_call | solution.py:198
  151.7 9.2 %all-to-all-start.5 = ((bf16[8,10,16,128]{3,2,1,0:T(8,128)(2,1)}), bf16[8,10,16,128]{3,2,1,0:T(8,128)(2,1)S(1)}, u32[]{:S(2)}, u32[]{:S(2)}) async-start(bf16[8,10,16,128]{3,2,1,0:T(8,128)(2,1)} %shard_map.133), calls=%async_computation.6 | async-start | bytes 655360 | tf_op jit(solution)/shard_map/all_to_all | solution.py:31
  161.5 6.0 %all-to-all-done.5.q_ref = bf16[8,10,16,128]{3,2,1,0:T(8,128)(2,1)S(1)} async-done(((bf16[8,10,16,128]{3,2,1,0:T(8,128)(2,1)}), bf16[8,10,16,128]{3,2,1,0:T(8,128)(2,1)S(1)}, u32[]{:S(2)}, u32[]{:S(2)}) %all-to-all-start.5) | async-done | bytes 327712 | tf_op jit(solution)/shard_map/all_to_all | solution.py:31
  168.2 11.7 %shard_map.134 = bf16[16,16,1024]{2,1,0:T(8,128)(2,1)} custom-call(bf16[8,10,16,128]{3,2,1,0:T(8,128)(2,1)} %copy-done.5, bf16[16,128]{1,0:T(8,128)(2,1)} %slice.27.w_ref, bf16[16384,128]{1,0:T(8,128)(2,1)} %all-gather.2.cloned.1.call-done.k_ref), custom_call_target="tpu_custom_call" | custom-call | flops 8589934592 | bytes 8388608 | tf_op jit(solution)/shard_map/pallas_call | solution.py:241
  179.9 10.9 %all-to-all-start.6 = ((bf16[16,16,1024]{2,1,0:T(8,128)(2,1)}), bf16[16,16,1024]{2,1,0:T(8,128)(2,1)S(1)}, u32[]{:S(2)}, u32[]{:S(2)}) async-start(bf16[16,16,1024]{2,1,0:T(8,128)(2,1)} %shard_map.134), calls=%async_computation.7 | async-start | bytes 1048576 | tf_op jit(solution)/shard_map/all_to_all | solution.py:364
  194.8 3.1 %all-to-all-done.6.s_ref = bf16[16,16,1024]{2,1,0:T(8,128)(2,1)S(1)} async-done(((bf16[16,16,1024]{2,1,0:T(8,128)(2,1)}), bf16[16,16,1024]{2,1,0:T(8,128)(2,1)S(1)}, u32[]{:S(2)}, u32[]{:S(2)}) %all-to-all-start.6) | async-done | bytes 524320 | tf_op jit(solution)/shard_map/all_to_all | solution.py:364
  (59 shorter events, 14.1 us)
Async XLA Ops:
  7.2 67.1 %reduce-scatter.2.cloned.1.call-start = ((), (), s32[]{:S(2)}) async-start(), calls=%async_computation.8 | async-start | bytes 4128768 | tf_op jit(solution)/shard_map/reduce_scatter | solution.py:334
  14.8 3.9 %copy-start.6 = (bf16[7168,4]{0,1:T(4,128)(2,1)S(1)}, bf16[7168,4]{0,1:T(4,128)(2,1)}, u32[]{:S(2)}) copy-start(bf16[7168,4]{0,1:T(4,128)(2,1)} %param.16) | copy-start | bytes 172036
  14.9 4.6 %copy-start.4 = (bf16[7168,96]{0,1:T(8,128)(2,1)S(1)}, bf16[7168,96]{0,1:T(8,128)(2,1)}, u32[]{:S(2)}) copy-start(bf16[7168,96]{0,1:T(8,128)(2,1)} %param.15) | copy-start | bytes 4128772
  14.9 152.6 %all-gather.2.cloned.1.call-start = ((), (), s32[]{:S(2)}) async-start(), calls=%async_computation.9 | async-start | bytes 4456448 | tf_op jit(solution)/shard_map/all_gather | solution.py:343
  14.9 29.7 %collective-permute-start = (bf16[768,512]{1,0:T(8,128)(2,1)}, bf16[768,512]{1,0:T(8,128)(2,1)S(1)}, u32[]{:S(2)}, u32[]{:S(2)}) collective-permute-start(bf16[768,512]{1,0:T(8,128)(2,1)} %get-tuple-element.24), channel_id=1, source_target_pairs={{0,1},{1,0},{2,3},{3,2},{4,5},{5,4},{6,7},{7,6},{8,9},{9,8},{10,11... | collective-permute-start | bytes 2359304 | tf_op jit(solution)/shard_map/ppermute | solution.py:27
  44.6 0.9 copy-start.1
  67.7 6.6 %collective-permute-start.1 = (bf16[448,1664]{1,0:T(8,128)(2,1)S(1)}, bf16[448,1664]{1,0:T(8,128)(2,1)S(1)}, u32[]{:S(2)}, u32[]{:S(2)}) collective-permute-start(bf16[448,1664]{1,0:T(8,128)(2,1)S(1)} %bitcast.33), channel_id=1, source_target_pairs={{0,16},{16,0},{1,17},{17,1},{2,18},{18,2},{3,19},{19,3},{4,20},{20... | collective-permute-start | bytes 4472840 | tf_op jit(solution)/shard_map/ppermute | solution.py:27
  76.1 8.5 %collective-permute-start.2 = (bf16[128,896]{1,0:T(8,128)(2,1)}, bf16[128,896]{1,0:T(8,128)(2,1)S(1)}, u32[]{:S(2)}, u32[]{:S(2)}) collective-permute-start(bf16[128,896]{1,0:T(8,128)(2,1)} %get-tuple-element.55), channel_id=1, source_target_pairs={{0,1},{1,0},{2,3},{3,2},{4,5},{5,4},{6,7},{7,6},{8,9},{9,8},{10,11... | collective-permute-start | bytes 688136 | tf_op jit(solution)/shard_map/ppermute | solution.py:27
  84.6 8.0 %copy-start.7 = (bf16[1536]{0:T(1024)(128)(2,1)S(1)}, bf16[1536]{0:T(1024)(128)(2,1)}, u32[]{:S(2)}) copy-start(bf16[1536]{0:T(1024)(128)(2,1)} %param.17) | copy-start | bytes 9220
  85.5 0.8 copy-start.3
  86.3 62.9 %copy-start = (bf16[1536,512]{1,0:T(8,128)(2,1)S(1)}, bf16[1536,512]{1,0:T(8,128)(2,1)}, u32[]{:S(2)}) copy-start(bf16[1536,512]{1,0:T(8,128)(2,1)} %own_ref.1) | copy-start | bytes 4718596
  86.3 62.9 %copy-start.2 = (bf16[768,512]{1,0:T(8,128)(2,1)S(1)}, bf16[768,512]{1,0:T(8,128)(2,1)}, u32[]{:S(2)}) copy-start(bf16[768,512]{1,0:T(8,128)(2,1)} %copy-done.1) | copy-start | bytes 2359300
  86.3 14.2 %all-to-all-start.2 = ((bf16[8,16,1664]{2,1,0:T(8,128)(2,1)}), bf16[8,16,1664]{2,1,0:T(8,128)(2,1)S(1)}, u32[]{:S(2)}, u32[]{:S(2)}) async-start(bf16[8,16,1664]{2,1,0:T(8,128)(2,1)} %bitcast.36), calls=%async_computation.3 | async-start | bytes 851968 | tf_op jit(solution)/shard_map/all_to_all | solution.py:31
  100.9 25.2 %collective-permute-start.5 = (bf16[768,512]{1,0:T(8,128)(2,1)}, bf16[768,512]{1,0:T(8,128)(2,1)}, u32[]{:S(2)}, u32[]{:S(2)}) collective-permute-start(bf16[768,512]{1,0:T(8,128)(2,1)} %copy-done.1), channel_id=1, source_target_pairs={{0,16},{16,0},{1,17},{17,1},{2,18},{18,2},{3,19},{19,3},{4,20},{20... | collective-permute-start | bytes 2359304 | tf_op jit(solution)/shard_map/ppermute | solution.py:27
  105.0 8.9 %collective-permute-start.3 = (bf16[16,1664]{1,0:T(8,128)(2,1)S(1)}, bf16[16,1664]{1,0:T(8,128)(2,1)S(1)}, u32[]{:S(2)}, u32[]{:S(2)}) collective-permute-start(bf16[16,1664]{1,0:T(8,128)(2,1)S(1)} %get-tuple-element.32.final_ref), channel_id=1, source_target_pairs={{0,0},{1,16},{2,32},{3,48},{4,64},{5,80},{6,96},{7,112},{8,128},{9... | collective-permute-start | bytes 159752 | tf_op jit(solution)/shard_map/ppermute | solution.py:307
  109.5 4.4 %collective-permute-start.4 = (bf16[16,768]{1,0:T(8,128)(2,1)S(1)}, bf16[16,768]{1,0:T(8,128)(2,1)S(1)}, u32[]{:S(2)}, u32[]{:S(2)}) collective-permute-start(bf16[16,768]{1,0:T(8,128)(2,1)S(1)} %get-tuple-element.33), channel_id=1, source_target_pairs={{0,1},{1,0},{2,3},{3,2},{4,5},{5,4},{6,7},{7,6},{8,9},{9,8},{10,11... | collective-permute-start | bytes 73736 | tf_op jit(solution)/shard_map/ppermute | solution.py:27
  114.7 20.3 %all-to-all-start.3 = ((bf16[8,16,1536]{2,1,0:T(8,128)(2,1)}), bf16[8,16,1536]{2,1,0:T(8,128)(2,1)S(1)}, u32[]{:S(2)}, u32[]{:S(2)}) async-start(bf16[8,16,1536]{2,1,0:T(8,128)(2,1)} %broadcast_in_dim.21), calls=%async_computation.4 | async-start | bytes 786432 | tf_op jit(solution)/shard_map/all_to_all | solution.py:31
  135.0 14.2 %all-to-all-start.4 = ((bf16[8,16,896]{2,1,0:T(8,128)(2,1)}), bf16[8,16,896]{2,1,0:T(8,128)(2,1)S(1)}, u32[]{:S(2)}, u32[]{:S(2)}) async-start(bf16[8,16,896]{2,1,0:T(8,128)(2,1)} %bitcast.12), calls=%async_computation.5 | async-start | bytes 458752 | tf_op jit(solution)/shard_map/all_to_all | solution.py:31
  151.7 15.8 %all-to-all-start.5 = ((bf16[8,10,16,128]{3,2,1,0:T(8,128)(2,1)}), bf16[8,10,16,128]{3,2,1,0:T(8,128)(2,1)S(1)}, u32[]{:S(2)}, u32[]{:S(2)}) async-start(bf16[8,10,16,128]{3,2,1,0:T(8,128)(2,1)} %shard_map.133), calls=%async_computation.6 | async-start | bytes 655360 | tf_op jit(solution)/shard_map/all_to_all | solution.py:31
  167.5 0.7 copy-start.5
  179.9 18.0 %all-to-all-start.6 = ((bf16[16,16,1024]{2,1,0:T(8,128)(2,1)}), bf16[16,16,1024]{2,1,0:T(8,128)(2,1)S(1)}, u32[]{:S(2)}, u32[]{:S(2)}) async-start(bf16[16,16,1024]{2,1,0:T(8,128)(2,1)} %shard_map.134), calls=%async_computation.7 | async-start | bytes 1048576 | tf_op jit(solution)/shard_map/all_to_all | solution.py:364
Sparse Core Ops, SparseCore 0:
  15.0 58.6 reduce-scatter.1
  75.6 39.2 all-gather.1

commit v18 on v15

--- a/solution.py
+++ b/solution.py
@@ -4,6 +4,7 @@
 import jax.numpy as jnp
 from jax import lax
 from jax.experimental import pallas as pl
+from jax.experimental.layout import Layout, with_layout_constraint
 from jax.experimental.pallas import tpu as pltpu
 from jax.sharding import Mesh
 from jax.sharding import PartitionSpec as P
@@ -279,14 +280,19 @@
     )(numbers, scores, own_positions)
 
 
-def down_weight_rows(latent_weight, index_proj, piece, early):
+def down_weight_rows(latent_weight, index_proj, piece, high, early):
     share = DZ // N_SEQ
 
     def own_rows(weight):
-        return lax.dynamic_slice_in_dim(weight.reshape(NZ, DZ, weight.shape[1]), piece * share, share, 1)
-
-    own = jnp.concatenate([own_rows(latent_weight), own_rows(index_proj)], axis=2)
-    by_head = lax.all_to_all(jnp.repeat(own, 2, axis=0), HEAD, 0, 0).transpose(1, 0, 2)
+        columns = weight.T.reshape(weight.shape[1], NZ, DZ)
+        return lax.dynamic_slice_in_dim(columns, piece * share, share, 2)
+
+    own = jnp.concatenate([own_rows(latent_weight), own_rows(index_proj)], axis=0)
+    own = with_layout_constraint(own, Layout(major_to_minor=(0, 1, 2)))
+    mine = lax.all_to_all(own.transpose(1, 2, 0), "z", 0, 0)
+    theirs = swap(mine, "yh")
+    pair = [jnp.where(high == 0, mine, theirs), jnp.where(high == 0, theirs, mine)]
+    by_head = jnp.stack(pair, axis=1).reshape(N_HEAD, share, own.shape[0]).transpose(1, 0, 2)
     local = latent_weight.shape[1]
     wide = jnp.concatenate(
         [
@@ -335,7 +341,7 @@
 
     weight_mine = swap(half_weight, "yh")
     down_mine, down_other, weight_mine = down_weight_rows(
-        latent_weight, index_proj, c * 8 + x * 2 + yl, weight_mine
+        latent_weight, index_proj, c * 8 + x * 2 + yl, yh, weight_mine
     )
     weight_theirs = swap(weight_mine, "c")
     summed, index_keys, down_mine, down_other = lax.optimization_barrier(

time: 198 us -> 195 us (0.985)
  blocking collectives: 45 us -> 35.4 us
  waiting for transfers between devices: 44.3 us -> 50.2 us
    all_to_all x1, blocking collectives: 22.9 us -> 16.1 us  [down_weight_rows(): mine = lax.all_to_all(own.transpose(1, 2, 0), 'z', 0, 0)]
    ppermute x5 -> x6, waiting for transfers between devices: 13 us -> 18.9 us  [swap(): return lax.ppermute(values, axis, [(0, 1), (1, 0)])]
    all_to_all x1, blocking collectives: 22 us -> 19.3 us  [down_weight_rows(): lax.all_to_all(jnp.broadcast_to(wide[None], (8,) + wide.shape), ('x', 'yl...]
    ppermute x5 -> x6, starting transfers between devices: 10.3 us -> 11.7 us  [swap(): return lax.ppermute(values, axis, [(0, 1), (1, 0)])]
  transfers between devices with their start and end apart: 12 -> 13, of which waited for: 7 -> 8; matrix products, arithmetic and copies ran while one was open for 5% -> 5% of each run, Pallas kernels for 3% -> 3%
where the time goes in v18:
time: 195 us; the launch traced here: 194 us
  starting transfers between devices  56 us (29%)
  waiting for transfers between devices  50.2 us (26%)
  blocking collectives  35.4 us (18%)
  Pallas kernels  26.3 us (13%)
  between operations  14.9 us (8%)
  local copies, waits for them, and re-layouts  10.9 us (6%)
    all_to_all x3, waiting for transfers between devices, from_last(): lax.all_to_all(values, 'z', 0, 0, axis_index_groups=[list(range(NZ))[::-1]])  27.3 us
    all_to_all x3, starting transfers between devices, from_last(): lax.all_to_all(values, 'z', 0, 0, axis_index_groups=[list(range(NZ))[::-1]])  26.1 us
    all_to_all x1, blocking collectives, down_weight_rows(): lax.all_to_all(jnp.broadcast_to(wide[None], (8,) + wide.shape), ('x', 'yl...  19.3 us
    ppermute x6, waiting for transfers between devices, swap(): return lax.ppermute(values, axis, [(0, 1), (1, 0)])  18.9 us
    all_to_all x1, blocking collectives, down_weight_rows(): mine = lax.all_to_all(own.transpose(1, 2, 0), 'z', 0, 0)  16.1 us
    pallas_call x1, Pallas kernels, make_scores(): pl.pallas_call(score_kernel, grid=(N_SEQ // per_step,), in_specs=[pl.Bloc...  11.7 us
    ppermute x6, starting transfers between devices, swap(): return lax.ppermute(values, axis, [(0, 1), (1, 0)])  11.7 us
    ppermute x1, starting transfers between devices, turn(): return lax.ppermute(values, SEQ + HEAD, moves)  9.88 us
  transfers between devices with their start and end apart: 13, of which 8 were waited for; matrix products, arithmetic and copies ran while one was open for 5% of the time, Pallas kernels for 3%

profile of v18, /device:TPU:1, one launch (start us, length us, event | category | flops | bytes accessed | tf_op | source)
XLA Modules:
  0.0 193.8 jit_solution(18068786589870990930)
XLA Ops:
  7.2 7.6 %shard_map.130 = (bf16[8,2,128,896]{3,2,1,0:T(8,128)(2,1)}, bf16[768,512]{1,0:T(8,128)(2,1)}) custom-call(s32[1]{0:T(128)} %bitcast.2.place_ref, bf16[256,512]{1,0:T(8,128)(2,1)} %a_ref.1, bf16[512,7168]{1,0:T(8,128)(2,1)} %b_ref.1, bf16[16,7168]{1,0:T(8,128)(2,1)} %res_ref.1, bf16[1536,512]{1,0:T(8,128)(2,1)} %own_ref.1), custom_call_target="tpu_custom_call" | custom-call | tf_op jit(solution)/shard_map/pallas_call | solution.py:88
  14.9 3.8 %collective-permute-start.1 = (bf16[768,512]{1,0:T(8,128)(2,1)}, bf16[768,512]{1,0:T(8,128)(2,1)S(1)}, u32[]{:S(2)}, u32[]{:S(2)}) collective-permute-start(bf16[768,512]{1,0:T(8,128)(2,1)} %get-tuple-element.19), channel_id=1, source_target_pairs={{0,1},{1,0},{2,3},{3,2},{4,5},{5,4},{6,7},{7,6},{8,9},{9,8},{10,11... | collective-permute-start | bytes 2359304 | tf_op jit(solution)/shard_map/ppermute | solution.py:28
  20.8 16.1 %all_to_all.30 = bf16[8,56,100]{2,1,0:T(8,128)(2,1)S(1)} all-to-all(bf16[8,56,100]{2,1,0:T(8,128)(2,1)S(1)} %copy.26), channel_id=1, replica_groups=mesh['x'=4,'yl'=2,'c'=2,'z'=8,'yh'=2] {'z'}, dimensions={0} | all-to-all | bytes 179200 | tf_op jit(solution)/shard_map/all_to_all | solution.py:292
  37.1 5.0 %collective-permute-done = bf16[8,56,100]{2,1,0:T(8,128)(2,1)S(1)} collective-permute-done((bf16[8,56,100]{2,1,0:T(8,128)(2,1)S(1)}, bf16[8,56,100]{2,1,0:T(8,128)(2,1)S(1)}, u32[]{:S(2)}, u32[]{:S(2)}) %collective-permute-start) | collective-permute-done | bytes 89632 | tf_op jit(solution)/shard_map/ppermute | solution.py:28
  44.0 19.3 %all_to_all.31 = bf16[8,56,1664]{2,1,0:T(8,128)(2,1)S(1)} all-to-all(bf16[8,56,1664]{2,1,0:T(8,128)(2,1)S(1)} %broadcast_in_dim.7), channel_id=1, replica_groups=mesh['x'=4,'yl'=2,'c'=2,'z'=8,'yh'=2] {'x','yl'}, dimensions={0} | all-to-all | bytes 2981888 | tf_op jit(solution)/shard_map/all_to_all | solution.py:306
  63.3 5.9 %collective-permute-start.2 = (bf16[448,1664]{1,0:T(8,128)(2,1)S(1)}, bf16[448,1664]{1,0:T(8,128)(2,1)S(1)}, u32[]{:S(2)}, u32[]{:S(2)}) collective-permute-start(bf16[448,1664]{1,0:T(8,128)(2,1)S(1)} %bitcast.35), channel_id=1, source_target_pairs={{0,16},{16,0},{1,17},{17,1},{2,18},{18,2},{3,19},{19,3},{4,20},{20... | collective-permute-start | bytes 4472840 | tf_op jit(solution)/shard_map/ppermute | solution.py:28
  69.2 2.9 %collective-permute-done.2.other_ref = bf16[448,1664]{1,0:T(8,128)(2,1)S(1)} collective-permute-done((bf16[448,1664]{1,0:T(8,128)(2,1)S(1)}, bf16[448,1664]{1,0:T(8,128)(2,1)S(1)}, u32[]{:S(2)}, u32[]{:S(2)}) %collective-permute-start.2) | collective-permute-done | bytes 1490976 | tf_op jit(solution)/shard_map/ppermute | solution.py:28
  72.6 1.8 slice_bitcast_fusion
  74.4 1.2 collective-permute-start.3
  76.3 6.9 %collective-permute-done.3.got_ref = bf16[128,896]{1,0:T(8,128)(2,1)S(1)} collective-permute-done((bf16[128,896]{1,0:T(8,128)(2,1)}, bf16[128,896]{1,0:T(8,128)(2,1)S(1)}, u32[]{:S(2)}, u32[]{:S(2)}) %collective-permute-start.3) | collective-permute-done | bytes 229408 | tf_op jit(solution)/shard_map/ppermute | solution.py:28
  83.2 1.7 shard_map.131
  84.9 6.3 %all-to-all-start.2 = ((bf16[8,16,2560]{2,1,0:T(8,128)(2,1)}), bf16[8,16,2560]{2,1,0:T(8,128)(2,1)S(1)}, u32[]{:S(2)}, u32[]{:S(2)}) async-start(bf16[8,16,2560]{2,1,0:T(8,128)(2,1)} %bitcast.17), calls=%async_computation.3 | async-start | bytes 1310720 | tf_op jit(solution)/shard_map/all_to_all | solution.py:32
  91.2 11.7 %all-to-all-done.2.parts_ref = bf16[8,16,2560]{2,1,0:T(8,128)(2,1)S(1)} async-done(((bf16[8,16,2560]{2,1,0:T(8,128)(2,1)}), bf16[8,16,2560]{2,1,0:T(8,128)(2,1)S(1)}, u32[]{:S(2)}, u32[]{:S(2)}) %all-to-all-start.2) | async-done | bytes 655392 | tf_op jit(solution)/shard_map/all_to_all | solution.py:32
  104.0 9.9 %collective-permute-start.5 = (bf16[16,1664]{1,0:T(8,128)(2,1)S(1)}, bf16[16,1664]{1,0:T(8,128)(2,1)S(1)}, u32[]{:S(2)}, u32[]{:S(2)}) collective-permute-start(bf16[16,1664]{1,0:T(8,128)(2,1)S(1)} %get-tuple-element.27.final_ref), channel_id=1, source_target_pairs={{0,0},{1,16},{2,32},{3,48},{4,64},{5,80},{6,96},{7,112},{8,128},{9... | collective-permute-start | bytes 159752 | tf_op jit(solution)/shard_map/ppermute | solution.py:313
  114.0 4.2 %collective-permute-done.6.beside_ref = bf16[16,768]{1,0:T(8,128)(2,1)S(1)} collective-permute-done((bf16[16,768]{1,0:T(8,128)(2,1)S(1)}, bf16[16,768]{1,0:T(8,128)(2,1)S(1)}, u32[]{:S(2)}, u32[]{:S(2)}) %collective-permute-start.6) | collective-permute-done | bytes 24608 | tf_op jit(solution)/shard_map/ppermute | solution.py:28
  118.9 12.7 %all-to-all-start.3 = ((bf16[8,16,1536]{2,1,0:T(8,128)(2,1)}), bf16[8,16,1536]{2,1,0:T(8,128)(2,1)S(1)}, u32[]{:S(2)}, u32[]{:S(2)}) async-start(bf16[8,16,1536]{2,1,0:T(8,128)(2,1)} %broadcast_in_dim.8), calls=%async_computation.4 | async-start | bytes 786432 | tf_op jit(solution)/shard_map/all_to_all | solution.py:32
  131.8 8.8 %all-to-all-done.3 = bf16[8,16,1536]{2,1,0:T(8,128)(2,1)S(1)} async-done(((bf16[8,16,1536]{2,1,0:T(8,128)(2,1)}), bf16[8,16,1536]{2,1,0:T(8,128)(2,1)S(1)}, u32[]{:S(2)}, u32[]{:S(2)}) %all-to-all-start.3) | async-done | bytes 393248 | tf_op jit(solution)/shard_map/all_to_all | solution.py:32
  140.5 2.5 %shard_map.133 = bf16[8,10,16,128]{3,2,1,0:T(8,128)(2,1)} custom-call(s32[2]{0:T(128)S(1)} %pad_add_fusion.place_ref, bf16[128,1536]{1,0:T(8,128)(2,1)S(1)} %bitcast.37, bf16[1536,512]{1,0:T(8,128)(2,1)S(1)} %copy-done, bf16[768,512]{1,0:T(8,128)(2,1)S(1)} %copy-done.2, bf16[768,512]{1,0:T(8,128)(2,1)} %collective-permute-done.4.theirs_ref, ...), custom_call_target="tpu_custom_call" | custom-call | tf_op jit(solution)/shard_map/pallas_call | solution.py:199
  143.0 7.0 %all-to-all-start.4 = ((bf16[8,10,16,128]{3,2,1,0:T(8,128)(2,1)}), bf16[8,10,16,128]{3,2,1,0:T(8,128)(2,1)S(1)}, u32[]{:S(2)}, u32[]{:S(2)}) async-start(bf16[8,10,16,128]{3,2,1,0:T(8,128)(2,1)} %shard_map.133), calls=%async_computation.5 | async-start | bytes 655360 | tf_op jit(solution)/shard_map/all_to_all | solution.py:32
  150.6 6.8 %all-to-all-done.4.q_ref = bf16[8,10,16,128]{3,2,1,0:T(8,128)(2,1)S(1)} async-done(((bf16[8,10,16,128]{3,2,1,0:T(8,128)(2,1)}), bf16[8,10,16,128]{3,2,1,0:T(8,128)(2,1)S(1)}, u32[]{:S(2)}, u32[]{:S(2)}) %all-to-all-start.4) | async-done | bytes 327712 | tf_op jit(solution)/shard_map/all_to_all | solution.py:32
  158.2 11.7 %shard_map.134 = bf16[16,16,1024]{2,1,0:T(8,128)(2,1)} custom-call(bf16[8,10,16,128]{3,2,1,0:T(8,128)(2,1)} %copy-done.4, bf16[16,128]{1,0:T(8,128)(2,1)} %slice.27.w_ref, bf16[16384,128]{1,0:T(8,128)(2,1)} %all-gather.2.cloned.1.call-done.k_ref), custom_call_target="tpu_custom_call" | custom-call | flops 8589934592 | bytes 8388608 | tf_op jit(solution)/shard_map/pallas_call | solution.py:242
  169.9 8.3 %all-to-all-start.5 = ((bf16[16,16,1024]{2,1,0:T(8,128)(2,1)}), bf16[16,16,1024]{2,1,0:T(8,128)(2,1)S(1)}, u32[]{:S(2)}, u32[]{:S(2)}) async-start(bf16[16,16,1024]{2,1,0:T(8,128)(2,1)} %shard_map.134), calls=%async_computation.6 | async-start | bytes 1048576 | tf_op jit(solution)/shard_map/all_to_all | solution.py:367
  181.4 3.9 %all-to-all-done.5.s_ref = bf16[16,16,1024]{2,1,0:T(8,128)(2,1)S(1)} async-done(((bf16[16,16,1024]{2,1,0:T(8,128)(2,1)}), bf16[16,16,1024]{2,1,0:T(8,128)(2,1)S(1)}, u32[]{:S(2)}, u32[]{:S(2)}) %all-to-all-start.5) | async-done | bytes 524320 | tf_op jit(solution)/shard_map/all_to_all | solution.py:367
  185.3 1.7 shard_map.135
  (56 shorter events, 11.3 us)
Async XLA Ops:
  7.2 65.0 %reduce-scatter.2.cloned.1.call-start = ((), (), s32[]{:S(2)}) async-start(), calls=%async_computation.7 | async-start | bytes 4128768 | tf_op jit(solution)/shard_map/reduce_scatter | solution.py:340
  14.8 3.9 %copy-start.5 = (bf16[7168,4]{0,1:T(4,128)(2,1)S(1)}, bf16[7168,4]{0,1:T(4,128)(2,1)}, u32[]{:S(2)}) copy-start(bf16[7168,4]{0,1:T(4,128)(2,1)} %param.16) | copy-start | bytes 172036
  14.9 4.6 %copy-start.3 = (bf16[7168,96]{0,1:T(8,128)(2,1)S(1)}, bf16[7168,96]{0,1:T(8,128)(2,1)}, u32[]{:S(2)}) copy-start(bf16[7168,96]{0,1:T(8,128)(2,1)} %param.15) | copy-start | bytes 4128772
  14.9 142.6 %all-gather.2.cloned.1.call-start = ((), (), s32[]{:S(2)}) async-start(), calls=%async_computation.8 | async-start | bytes 4456448 | tf_op jit(solution)/shard_map/all_gather | solution.py:350
  14.9 28.0 %collective-permute-start.1 = (bf16[768,512]{1,0:T(8,128)(2,1)}, bf16[768,512]{1,0:T(8,128)(2,1)S(1)}, u32[]{:S(2)}, u32[]{:S(2)}) collective-permute-start(bf16[768,512]{1,0:T(8,128)(2,1)} %get-tuple-element.19), channel_id=1, source_target_pairs={{0,1},{1,0},{2,3},{3,2},{4,5},{5,4},{6,7},{7,6},{8,9},{9,8},{10,11... | collective-permute-start | bytes 2359304 | tf_op jit(solution)/shard_map/ppermute | solution.py:28
  36.9 5.1 %collective-permute-start = (bf16[8,56,100]{2,1,0:T(8,128)(2,1)S(1)}, bf16[8,56,100]{2,1,0:T(8,128)(2,1)S(1)}, u32[]{:S(2)}, u32[]{:S(2)}) collective-permute-start(bf16[8,56,100]{2,1,0:T(8,128)(2,1)S(1)} %all_to_all.30), channel_id=1, source_target_pairs={{0,1},{1,0},{2,3},{3,2},{4,5},{5,4},{6,7},{7,6},{8,9},{9,8},{10,11... | collective-permute-start | bytes 268808 | tf_op jit(solution)/shard_map/ppermute | solution.py:28
  43.0 0.9 copy-start.1
  63.3 8.9 %collective-permute-start.2 = (bf16[448,1664]{1,0:T(8,128)(2,1)S(1)}, bf16[448,1664]{1,0:T(8,128)(2,1)S(1)}, u32[]{:S(2)}, u32[]{:S(2)}) collective-permute-start(bf16[448,1664]{1,0:T(8,128)(2,1)S(1)} %bitcast.35), channel_id=1, source_target_pairs={{0,16},{16,0},{1,17},{17,1},{2,18},{18,2},{3,19},{19,3},{4,20},{20... | collective-permute-start | bytes 4472840 | tf_op jit(solution)/shard_map/ppermute | solution.py:28
  72.2 12.7 %collective-permute-start.4 = (bf16[768,512]{1,0:T(8,128)(2,1)}, bf16[768,512]{1,0:T(8,128)(2,1)}, u32[]{:S(2)}, u32[]{:S(2)}) collective-permute-start(bf16[768,512]{1,0:T(8,128)(2,1)} %copy-done.1), channel_id=1, source_target_pairs={{0,16},{16,0},{1,17},{17,1},{2,18},{18,2},{3,19},{19,3},{4,20},{20... | collective-permute-start | bytes 2359304 | tf_op jit(solution)/shard_map/ppermute | solution.py:28
  74.4 8.8 %collective-permute-start.3 = (bf16[128,896]{1,0:T(8,128)(2,1)}, bf16[128,896]{1,0:T(8,128)(2,1)S(1)}, u32[]{:S(2)}, u32[]{:S(2)}) collective-permute-start(bf16[128,896]{1,0:T(8,128)(2,1)} %get-tuple-element.45), channel_id=1, source_target_pairs={{0,1},{1,0},{2,3},{3,2},{4,5},{5,4},{6,7},{7,6},{8,9},{9,8},{10,11... | collective-permute-start | bytes 688136 | tf_op jit(solution)/shard_map/ppermute | solution.py:28
  83.2 8.0 %copy-start.6 = (bf16[1536]{0:T(1024)(128)(2,1)S(1)}, bf16[1536]{0:T(1024)(128)(2,1)}, u32[]{:S(2)}) copy-start(bf16[1536]{0:T(1024)(128)(2,1)} %param.17) | copy-start | bytes 9220
  84.9 55.7 %copy-start = (bf16[1536,512]{1,0:T(8,128)(2,1)S(1)}, bf16[1536,512]{1,0:T(8,128)(2,1)}, u32[]{:S(2)}) copy-start(bf16[1536,512]{1,0:T(8,128)(2,1)} %own_ref.1) | copy-start | bytes 4718596
  84.9 55.7 %copy-start.2 = (bf16[768,512]{1,0:T(8,128)(2,1)S(1)}, bf16[768,512]{1,0:T(8,128)(2,1)}, u32[]{:S(2)}) copy-start(bf16[768,512]{1,0:T(8,128)(2,1)} %copy-done.1) | copy-start | bytes 2359300
  84.9 18.1 %all-to-all-start.2 = ((bf16[8,16,2560]{2,1,0:T(8,128)(2,1)}), bf16[8,16,2560]{2,1,0:T(8,128)(2,1)S(1)}, u32[]{:S(2)}, u32[]{:S(2)}) async-start(bf16[8,16,2560]{2,1,0:T(8,128)(2,1)} %bitcast.17), calls=%async_computation.3 | async-start | bytes 1310720 | tf_op jit(solution)/shard_map/all_to_all | solution.py:32
  104.0 14.2 %collective-permute-start.5 = (bf16[16,1664]{1,0:T(8,128)(2,1)S(1)}, bf16[16,1664]{1,0:T(8,128)(2,1)S(1)}, u32[]{:S(2)}, u32[]{:S(2)}) collective-permute-start(bf16[16,1664]{1,0:T(8,128)(2,1)S(1)} %get-tuple-element.27.final_ref), channel_id=1, source_target_pairs={{0,0},{1,16},{2,32},{3,48},{4,64},{5,80},{6,96},{7,112},{8,128},{9... | collective-permute-start | bytes 159752 | tf_op jit(solution)/shard_map/ppermute | solution.py:313
  113.9 4.3 %collective-permute-start.6 = (bf16[16,768]{1,0:T(8,128)(2,1)S(1)}, bf16[16,768]{1,0:T(8,128)(2,1)S(1)}, u32[]{:S(2)}, u32[]{:S(2)}) collective-permute-start(bf16[16,768]{1,0:T(8,128)(2,1)S(1)} %get-tuple-element.28), channel_id=1, source_target_pairs={{0,1},{1,0},{2,3},{3,2},{4,5},{5,4},{6,7},{7,6},{8,9},{9,8},{10,11... | collective-permute-start | bytes 73736 | tf_op jit(solution)/shard_map/ppermute | solution.py:28
  118.9 21.6 %all-to-all-start.3 = ((bf16[8,16,1536]{2,1,0:T(8,128)(2,1)}), bf16[8,16,1536]{2,1,0:T(8,128)(2,1)S(1)}, u32[]{:S(2)}, u32[]{:S(2)}) async-start(bf16[8,16,1536]{2,1,0:T(8,128)(2,1)} %broadcast_in_dim.8), calls=%async_computation.4 | async-start | bytes 786432 | tf_op jit(solution)/shard_map/all_to_all | solution.py:32
  143.0 14.4 %all-to-all-start.4 = ((bf16[8,10,16,128]{3,2,1,0:T(8,128)(2,1)}), bf16[8,10,16,128]{3,2,1,0:T(8,128)(2,1)S(1)}, u32[]{:S(2)}, u32[]{:S(2)}) async-start(bf16[8,10,16,128]{3,2,1,0:T(8,128)(2,1)} %shard_map.133), calls=%async_computation.5 | async-start | bytes 655360 | tf_op jit(solution)/shard_map/all_to_all | solution.py:32
  157.4 0.7 copy-start.4
  169.9 15.4 %all-to-all-start.5 = ((bf16[16,16,1024]{2,1,0:T(8,128)(2,1)}), bf16[16,16,1024]{2,1,0:T(8,128)(2,1)S(1)}, u32[]{:S(2)}, u32[]{:S(2)}) async-start(bf16[16,16,1024]{2,1,0:T(8,128)(2,1)} %shard_map.134), calls=%async_computation.6 | async-start | bytes 1048576 | tf_op jit(solution)/shard_map/all_to_all | solution.py:367
Sparse Core Ops, SparseCore 0:
  15.0 56.2 reduce-scatter.1
  73.2 37.3 all-gather.1

commit v19 on v17

--- a/solution.py
+++ b/solution.py
@@ -4,6 +4,7 @@
 import jax.numpy as jnp
 from jax import lax
 from jax.experimental import pallas as pl
+from jax.experimental.layout import Layout, with_layout_constraint
 from jax.experimental.pallas import tpu as pltpu
 from jax.sharding import Mesh
 from jax.sharding import PartitionSpec as P
@@ -279,14 +280,19 @@
     )(numbers, scores, own_positions)
 
 
-def down_weight_rows(latent_weight, index_proj, piece, early):
+def down_weight_rows(latent_weight, index_proj, piece, high, early):
     share = DZ // N_SEQ
 
     def own_rows(weight):
-        return lax.dynamic_slice_in_dim(weight.reshape(NZ, DZ, weight.shape[1]), piece * share, share, 1)
-
-    own = jnp.concatenate([own_rows(latent_weight), own_rows(index_proj)], axis=2)
-    by_head = lax.all_to_all(jnp.repeat(own, 2, axis=0), HEAD, 0, 0).transpose(1, 0, 2)
+        columns = weight.T.reshape(weight.shape[1], NZ, DZ)
+        return lax.dynamic_slice_in_dim(columns, piece * share, share, 2)
+
+    own = jnp.concatenate([own_rows(latent_weight), own_rows(index_proj)], axis=0)
+    own = with_layout_constraint(own, Layout(major_to_minor=(0, 1, 2)))
+    mine = lax.all_to_all(own.transpose(1, 2, 0), "z", 0, 0)
+    theirs = swap(mine, "yh")
+    pair = [jnp.where(high == 0, mine, theirs), jnp.where(high == 0, theirs, mine)]
+    by_head = jnp.stack(pair, axis=1).reshape(N_HEAD, share, own.shape[0]).transpose(1, 0, 2)
     local = latent_weight.shape[1]
     wide = jnp.concatenate(
         [
@@ -335,8 +341,9 @@
 
     weight_mine = swap(half_weight, "yh")
     down_mine, down_other, weight_mine = down_weight_rows(
-        latent_weight, index_proj, c * 8 + x * 2 + yl, weight_mine
-    )
+        latent_weight, index_proj, c * 8 + x * 2 + yl, yh, weight_mine
+    )
+    weight_theirs = swap(weight_mine, "c")
     summed, index_keys, down_mine, down_other = lax.optimization_barrier(
         (summed, index_keys, down_mine, down_other)
     )
@@ -344,18 +351,17 @@
     kept, got = summed[0], swap(summed[1], "yh")
     gain = lax.dynamic_slice_in_dim(norm_gain, z * DZ, DZ).reshape(1, DZ)
     hidden, lifted = lift(jnp.stack([c]).astype(jnp.int32), kept, got, gain, down_mine, down_other)
+    lifted, weight_theirs = lax.optimization_barrier((lifted, weight_theirs))
     parts = from_last(lifted.reshape(NZ, own, lifted.shape[1]))
     packed, give = normalize(
         jnp.stack([yh]).astype(jnp.int32), parts, latent_gain.reshape(1, QL)
     )
-    packed, weight_mine = lax.optimization_barrier((packed, weight_mine))
-    weight_theirs = swap(weight_mine, "c")
-    weight_theirs, hidden = lax.optimization_barrier((weight_theirs, hidden))
-    hidden_cols = from_last(hidden.reshape(NZ, own, DZ))
     turned, beside = lax.optimization_barrier((turn(packed), swap(give, "yh")))
     everyone = from_last(jnp.broadcast_to(turned[None, :, :QL], (NZ, own, QL)))
-    everyone, hidden_cols = lax.optimization_barrier((everyone.reshape(HALF, QL), hidden_cols))
-    hidden_rows = hidden_cols[::-1].transpose(1, 0, 2).reshape(own, D)
+    everyone, hidden = lax.optimization_barrier((everyone.reshape(HALF, QL), hidden))
+    all_hidden = lax.all_gather(hidden, "z", axis=0, tiled=False)
+    hidden_rows = lax.dynamic_slice_in_dim(all_hidden, (NZ - 1 - z) * own, own, 1)
+    hidden_rows = hidden_rows.transpose(1, 0, 2).reshape(own, D)
     place = jnp.stack([c, yh]).astype(jnp.int32)
     queries = make_queries(place, everyone, index_weight, weight_mine, weight_theirs, packed, beside)
     queries = from_last(queries)

time: 208 us -> 191 us (0.918)
  starting transfers between devices: 64.6 us -> 45.3 us
  blocking collectives: 45 us -> 54.6 us
  waiting for transfers between devices: 44.5 us -> 37.7 us
    all_to_all x4 -> x2, starting transfers between devices: 35.4 us -> 13.9 us  [from_last(): lax.all_to_all(values, 'z', 0, 0, axis_index_groups=[list(range(NZ))[::-1]])]
    all_to_all x1 -> x2, blocking collectives: 22.9 us -> 35.3 us  [the longest x1 19.2 us: from_last(): lax.all_to_all(values, 'z', 0, 0, axis_index_groups=[list(range(NZ))[::-1]])]
    all_to_all x4 -> x2, waiting for transfers between devices: 28.4 us -> 16.5 us  [from_last(): lax.all_to_all(values, 'z', 0, 0, axis_index_groups=[list(range(NZ))[::-1]])]
    ppermute x5 -> x6, waiting for transfers between devices: 12.9 us -> 18.9 us  [swap(): return lax.ppermute(values, axis, [(0, 1), (1, 0)])]
    ppermute x1, starting transfers between devices: 4.49 us -> 7.81 us  [turn(): return lax.ppermute(values, SEQ + HEAD, moves)]
    all_to_all x1, blocking collectives: 22 us -> 19.3 us  [down_weight_rows(): lax.all_to_all(jnp.broadcast_to(wide[None], (8,) + wide.shape), ('x', 'yl...]
    ppermute x5 -> x6, starting transfers between devices: 13.8 us -> 11.7 us  [swap(): return lax.ppermute(values, axis, [(0, 1), (1, 0)])]
  transfers between devices with their start and end apart: 13 -> 13, of which waited for: 8 -> 7; matrix products, arithmetic and copies ran while one was open for 5% -> 6% of each run, Pallas kernels for 2% -> 8%
where the time goes in v19:
time: 191 us; the launch traced here: 190 us
  blocking collectives  54.6 us (29%)
  starting transfers between devices  45.3 us (24%)
  waiting for transfers between devices  37.7 us (20%)
  Pallas kernels  24.8 us (13%)
  between operations  14.6 us (8%)
  local copies, waits for them, and re-layouts  12.6 us (7%)
    all_to_all x1, blocking collectives, down_weight_rows(): lax.all_to_all(jnp.broadcast_to(wide[None], (8,) + wide.shape), ('x', 'yl...  19.3 us
    all_to_all x1, blocking collectives, from_last(): lax.all_to_all(values, 'z', 0, 0, axis_index_groups=[list(range(NZ))[::-1]])  19.2 us
    ppermute x6, waiting for transfers between devices, swap(): return lax.ppermute(values, axis, [(0, 1), (1, 0)])  18.9 us
    all_to_all x2, waiting for transfers between devices, from_last(): lax.all_to_all(values, 'z', 0, 0, axis_index_groups=[list(range(NZ))[::-1]])  16.5 us
    all_to_all x1, blocking collectives, down_weight_rows(): mine = lax.all_to_all(own.transpose(1, 2, 0), 'z', 0, 0)  16.1 us
    all_to_all x2, starting transfers between devices, from_last(): lax.all_to_all(values, 'z', 0, 0, axis_index_groups=[list(range(NZ))[::-1]])  13.9 us
    all_to_all x1, starting transfers between devices, shards(): lax.all_to_all(scores, SEQ, 0, 0, axis_index_groups=[list(range(N_SEQ))[:...  11.9 us
    pallas_call x1, Pallas kernels, make_scores(): pl.pallas_call(score_kernel, grid=(N_SEQ // per_step,), in_specs=[pl.Bloc...  11.7 us
  transfers between devices with their start and end apart: 13, of which 7 were waited for; matrix products, arithmetic and copies ran while one was open for 6% of the time, Pallas kernels for 8%

profile of v19, /device:TPU:1, one launch (start us, length us, event | category | flops | bytes accessed | tf_op | source)
XLA Modules:
  0.0 189.9 jit_solution(12251223764266571735)
XLA Ops:
  7.2 7.6 %shard_map.130 = (bf16[8,2,128,896]{3,2,1,0:T(8,128)(2,1)}, bf16[768,512]{1,0:T(8,128)(2,1)}) custom-call(s32[1]{0:T(128)} %bitcast.2.place_ref, bf16[256,512]{1,0:T(8,128)(2,1)} %a_ref.1, bf16[512,7168]{1,0:T(8,128)(2,1)} %b_ref.1, bf16[16,7168]{1,0:T(8,128)(2,1)} %res_ref.1, bf16[1536,512]{1,0:T(8,128)(2,1)} %own_ref.1), custom_call_target="tpu_custom_call" | custom-call | tf_op jit(solution)/shard_map/pallas_call | solution.py:88
  14.9 3.8 %collective-permute-start.1 = (bf16[768,512]{1,0:T(8,128)(2,1)}, bf16[768,512]{1,0:T(8,128)(2,1)S(1)}, u32[]{:S(2)}, u32[]{:S(2)}) collective-permute-start(bf16[768,512]{1,0:T(8,128)(2,1)} %get-tuple-element.22), channel_id=1, source_target_pairs={{0,1},{1,0},{2,3},{3,2},{4,5},{5,4},{6,7},{7,6},{8,9},{9,8},{10,11... | collective-permute-start | bytes 2359304 | tf_op jit(solution)/shard_map/ppermute | solution.py:28
  20.8 16.1 %all_to_all.30 = bf16[8,56,100]{2,1,0:T(8,128)(2,1)S(1)} all-to-all(bf16[8,56,100]{2,1,0:T(8,128)(2,1)S(1)} %copy.29), channel_id=1, replica_groups=mesh['x'=4,'yl'=2,'c'=2,'z'=8,'yh'=2] {'z'}, dimensions={0} | all-to-all | bytes 179200 | tf_op jit(solution)/shard_map/all_to_all | solution.py:292
  37.1 5.0 %collective-permute-done = bf16[8,56,100]{2,1,0:T(8,128)(2,1)S(1)} collective-permute-done((bf16[8,56,100]{2,1,0:T(8,128)(2,1)S(1)}, bf16[8,56,100]{2,1,0:T(8,128)(2,1)S(1)}, u32[]{:S(2)}, u32[]{:S(2)}) %collective-permute-start) | collective-permute-done | bytes 89632 | tf_op jit(solution)/shard_map/ppermute | solution.py:28
  44.0 19.3 %all_to_all.31 = bf16[8,56,1664]{2,1,0:T(8,128)(2,1)S(1)} all-to-all(bf16[8,56,1664]{2,1,0:T(8,128)(2,1)S(1)} %broadcast_in_dim.7), channel_id=1, replica_groups=mesh['x'=4,'yl'=2,'c'=2,'z'=8,'yh'=2] {'x','yl'}, dimensions={0} | all-to-all | bytes 2981888 | tf_op jit(solution)/shard_map/all_to_all | solution.py:306
  63.3 5.9 %collective-permute-start.2 = (bf16[448,1664]{1,0:T(8,128)(2,1)S(1)}, bf16[448,1664]{1,0:T(8,128)(2,1)S(1)}, u32[]{:S(2)}, u32[]{:S(2)}) collective-permute-start(bf16[448,1664]{1,0:T(8,128)(2,1)S(1)} %bitcast.40), channel_id=1, source_target_pairs={{0,16},{16,0},{1,17},{17,1},{2,18},{18,2},{3,19},{19,3},{4,20},{20... | collective-permute-start | bytes 4472840 | tf_op jit(solution)/shard_map/ppermute | solution.py:28
  69.2 2.9 %collective-permute-done.2.other_ref = bf16[448,1664]{1,0:T(8,128)(2,1)S(1)} collective-permute-done((bf16[448,1664]{1,0:T(8,128)(2,1)S(1)}, bf16[448,1664]{1,0:T(8,128)(2,1)S(1)}, u32[]{:S(2)}, u32[]{:S(2)}) %collective-permute-start.2) | collective-permute-done | bytes 1490976 | tf_op jit(solution)/shard_map/ppermute | solution.py:28
  72.6 1.8 slice_bitcast_fusion
  74.4 1.2 collective-permute-start.3
  76.3 6.9 %collective-permute-done.3.got_ref = bf16[128,896]{1,0:T(8,128)(2,1)S(1)} collective-permute-done((bf16[128,896]{1,0:T(8,128)(2,1)}, bf16[128,896]{1,0:T(8,128)(2,1)S(1)}, u32[]{:S(2)}, u32[]{:S(2)}) %collective-permute-start.3) | collective-permute-done | bytes 229408 | tf_op jit(solution)/shard_map/ppermute | solution.py:28
  83.2 0.9 shard_map.131
  84.9 6.2 %all-to-all-start.2 = ((bf16[8,16,1664]{2,1,0:T(8,128)(2,1)}), bf16[8,16,1664]{2,1,0:T(8,128)(2,1)S(1)}, u32[]{:S(2)}, u32[]{:S(2)}) async-start(bf16[8,16,1664]{2,1,0:T(8,128)(2,1)} %bitcast.43), calls=%async_computation.3 | async-start | bytes 851968 | tf_op jit(solution)/shard_map/all_to_all | solution.py:32
  91.1 8.0 %all-to-all-done.2.parts_ref = bf16[8,16,1664]{2,1,0:T(8,128)(2,1)S(1)} async-done(((bf16[8,16,1664]{2,1,0:T(8,128)(2,1)}), bf16[8,16,1664]{2,1,0:T(8,128)(2,1)S(1)}, u32[]{:S(2)}, u32[]{:S(2)}) %all-to-all-start.2) | async-done | bytes 426016 | tf_op jit(solution)/shard_map/all_to_all | solution.py:32
  99.5 7.8 %collective-permute-start.5 = (bf16[16,1664]{1,0:T(8,128)(2,1)S(1)}, bf16[16,1664]{1,0:T(8,128)(2,1)S(1)}, u32[]{:S(2)}, u32[]{:S(2)}) collective-permute-start(bf16[16,1664]{1,0:T(8,128)(2,1)S(1)} %get-tuple-element.30.final_ref), channel_id=1, source_target_pairs={{0,0},{1,16},{2,32},{3,48},{4,64},{5,80},{6,96},{7,112},{8,128},{9... | collective-permute-start | bytes 159752 | tf_op jit(solution)/shard_map/ppermute | solution.py:313
  107.5 4.2 %collective-permute-done.6.beside_ref = bf16[16,768]{1,0:T(8,128)(2,1)S(1)} collective-permute-done((bf16[16,768]{1,0:T(8,128)(2,1)S(1)}, bf16[16,768]{1,0:T(8,128)(2,1)S(1)}, u32[]{:S(2)}, u32[]{:S(2)}) %collective-permute-start.6) | collective-permute-done | bytes 24608 | tf_op jit(solution)/shard_map/ppermute | solution.py:28
  111.7 19.2 %all_to_all.32 = bf16[8,16,1536]{2,1,0:T(8,128)(2,1)S(1)} all-to-all(bf16[8,16,1536]{2,1,0:T(8,128)(2,1)S(1)} %broadcast_in_dim.8), channel_id=1, replica_groups={{14,12,10,8,6,4,2,0},{15,13,11,9,7,5,3,1},{30,28,26,24,22,20,18,16},{31..., dimensions={0} | all-to-all | bytes 786432 | tf_op jit(solution)/shard_map/all_to_all | solution.py:32
  131.0 2.5 %shard_map.133 = bf16[8,10,16,128]{3,2,1,0:T(8,128)(2,1)} custom-call(s32[2]{0:T(128)S(1)} %pad_add_fusion.place_ref, bf16[128,1536]{1,0:T(8,128)(2,1)S(1)} %bitcast.42, bf16[1536,512]{1,0:T(8,128)(2,1)S(1)} %copy-done, bf16[768,512]{1,0:T(8,128)(2,1)S(1)} %copy-done.2, bf16[768,512]{1,0:T(8,128)(2,1)} %collective-permute-done.4.theirs_ref, ...), custom_call_target="tpu_custom_call" | custom-call | tf_op jit(solution)/shard_map/pallas_call | solution.py:199
  133.5 7.6 %all-to-all-start.4 = ((bf16[8,10,16,128]{3,2,1,0:T(8,128)(2,1)}), bf16[8,10,16,128]{3,2,1,0:T(8,128)(2,1)S(1)}, u32[]{:S(2)}, u32[]{:S(2)}) async-start(bf16[8,10,16,128]{3,2,1,0:T(8,128)(2,1)} %shard_map.133), calls=%async_computation.5 | async-start | bytes 655360 | tf_op jit(solution)/shard_map/all_to_all | solution.py:32
  141.7 8.5 %all-to-all-done.4.q_ref = bf16[8,10,16,128]{3,2,1,0:T(8,128)(2,1)S(1)} async-done(((bf16[8,10,16,128]{3,2,1,0:T(8,128)(2,1)}), bf16[8,10,16,128]{3,2,1,0:T(8,128)(2,1)S(1)}, u32[]{:S(2)}, u32[]{:S(2)}) %all-to-all-start.4) | async-done | bytes 327712 | tf_op jit(solution)/shard_map/all_to_all | solution.py:32
  151.0 11.7 %shard_map.134 = bf16[16,16,1024]{2,1,0:T(8,128)(2,1)} custom-call(bf16[8,10,16,128]{3,2,1,0:T(8,128)(2,1)} %copy-done.5, bf16[16,128]{1,0:T(8,128)(2,1)} %slice.27.w_ref, bf16[16384,128]{1,0:T(8,128)(2,1)} %all-gather.4.cloned.1.call-done.k_ref), custom_call_target="tpu_custom_call" | custom-call | flops 8589934592 | bytes 8388608 | tf_op jit(solution)/shard_map/pallas_call | solution.py:242
  162.7 11.9 %all-to-all-start.5 = ((bf16[16,16,1024]{2,1,0:T(8,128)(2,1)}), bf16[16,16,1024]{2,1,0:T(8,128)(2,1)S(1)}, u32[]{:S(2)}, u32[]{:S(2)}) async-start(bf16[16,16,1024]{2,1,0:T(8,128)(2,1)} %shard_map.134), calls=%async_computation.6 | async-start | bytes 1048576 | tf_op jit(solution)/shard_map/all_to_all | solution.py:370
  177.8 1.0 dynamic-slice_bitcast_fusion
  179.5 2.2 %all-to-all-done.5.s_ref = bf16[16,16,1024]{2,1,0:T(8,128)(2,1)S(1)} async-done(((bf16[16,16,1024]{2,1,0:T(8,128)(2,1)}), bf16[16,16,1024]{2,1,0:T(8,128)(2,1)S(1)}, u32[]{:S(2)}, u32[]{:S(2)}) %all-to-all-start.5) | async-done | bytes 524320 | tf_op jit(solution)/shard_map/all_to_all | solution.py:370
  181.7 1.7 shard_map.135
  (62 shorter events, 11.4 us)
Async XLA Ops:
  7.2 65.0 %reduce-scatter.2.cloned.1.call-start = ((), (), s32[]{:S(2)}) async-start(), calls=%async_computation.7 | async-start | bytes 4128768 | tf_op jit(solution)/shard_map/reduce_scatter | solution.py:340
  14.8 3.9 %copy-start.6 = (bf16[7168,4]{0,1:T(4,128)(2,1)S(1)}, bf16[7168,4]{0,1:T(4,128)(2,1)}, u32[]{:S(2)}) copy-start(bf16[7168,4]{0,1:T(4,128)(2,1)} %param.16) | copy-start | bytes 172036
  14.9 4.6 %copy-start.4 = (bf16[7168,96]{0,1:T(8,128)(2,1)S(1)}, bf16[7168,96]{0,1:T(8,128)(2,1)}, u32[]{:S(2)}) copy-start(bf16[7168,96]{0,1:T(8,128)(2,1)} %param.15) | copy-start | bytes 4128772
  14.9 135.4 %all-gather.4.cloned.1.call-start = ((), (), s32[]{:S(2)}) async-start(), calls=%async_computation.8 | async-start | bytes 4456448 | tf_op jit(solution)/shard_map/all_gather | solution.py:350
  14.9 28.0 %collective-permute-start.1 = (bf16[768,512]{1,0:T(8,128)(2,1)}, bf16[768,512]{1,0:T(8,128)(2,1)S(1)}, u32[]{:S(2)}, u32[]{:S(2)}) collective-permute-start(bf16[768,512]{1,0:T(8,128)(2,1)} %get-tuple-element.22), channel_id=1, source_target_pairs={{0,1},{1,0},{2,3},{3,2},{4,5},{5,4},{6,7},{7,6},{8,9},{9,8},{10,11... | collective-permute-start | bytes 2359304 | tf_op jit(solution)/shard_map/ppermute | solution.py:28
  36.9 5.1 %collective-permute-start = (bf16[8,56,100]{2,1,0:T(8,128)(2,1)S(1)}, bf16[8,56,100]{2,1,0:T(8,128)(2,1)S(1)}, u32[]{:S(2)}, u32[]{:S(2)}) collective-permute-start(bf16[8,56,100]{2,1,0:T(8,128)(2,1)S(1)} %all_to_all.30), channel_id=1, source_target_pairs={{0,1},{1,0},{2,3},{3,2},{4,5},{5,4},{6,7},{7,6},{8,9},{9,8},{10,11... | collective-permute-start | bytes 268808 | tf_op jit(solution)/shard_map/ppermute | solution.py:28
  43.0 0.9 copy-start.1
  63.3 8.9 %collective-permute-start.2 = (bf16[448,1664]{1,0:T(8,128)(2,1)S(1)}, bf16[448,1664]{1,0:T(8,128)(2,1)S(1)}, u32[]{:S(2)}, u32[]{:S(2)}) collective-permute-start(bf16[448,1664]{1,0:T(8,128)(2,1)S(1)} %bitcast.40), channel_id=1, source_target_pairs={{0,16},{16,0},{1,17},{17,1},{2,18},{18,2},{3,19},{19,3},{4,20},{20... | collective-permute-start | bytes 4472840 | tf_op jit(solution)/shard_map/ppermute | solution.py:28
  72.2 12.7 %collective-permute-start.4 = (bf16[768,512]{1,0:T(8,128)(2,1)}, bf16[768,512]{1,0:T(8,128)(2,1)}, u32[]{:S(2)}, u32[]{:S(2)}) collective-permute-start(bf16[768,512]{1,0:T(8,128)(2,1)} %copy-done.1), channel_id=1, source_target_pairs={{0,16},{16,0},{1,17},{17,1},{2,18},{18,2},{3,19},{19,3},{4,20},{20... | collective-permute-start | bytes 2359304 | tf_op jit(solution)/shard_map/ppermute | solution.py:28
  74.4 8.8 %collective-permute-start.3 = (bf16[128,896]{1,0:T(8,128)(2,1)}, bf16[128,896]{1,0:T(8,128)(2,1)S(1)}, u32[]{:S(2)}, u32[]{:S(2)}) collective-permute-start(bf16[128,896]{1,0:T(8,128)(2,1)} %get-tuple-element.51), channel_id=1, source_target_pairs={{0,1},{1,0},{2,3},{3,2},{4,5},{5,4},{6,7},{7,6},{8,9},{9,8},{10,11... | collective-permute-start | bytes 688136 | tf_op jit(solution)/shard_map/ppermute | solution.py:28
  83.2 7.9 %copy-start.7 = (bf16[1536]{0:T(1024)(128)(2,1)S(1)}, bf16[1536]{0:T(1024)(128)(2,1)}, u32[]{:S(2)}) copy-start(bf16[1536]{0:T(1024)(128)(2,1)} %param.17) | copy-start | bytes 9220
  84.1 0.8 copy-start.3
  84.8 46.2 %copy-start = (bf16[1536,512]{1,0:T(8,128)(2,1)S(1)}, bf16[1536,512]{1,0:T(8,128)(2,1)}, u32[]{:S(2)}) copy-start(bf16[1536,512]{1,0:T(8,128)(2,1)} %own_ref.1) | copy-start | bytes 4718596
  84.8 46.2 %copy-start.2 = (bf16[768,512]{1,0:T(8,128)(2,1)S(1)}, bf16[768,512]{1,0:T(8,128)(2,1)}, u32[]{:S(2)}) copy-start(bf16[768,512]{1,0:T(8,128)(2,1)} %copy-done.1) | copy-start | bytes 2359300
  84.9 14.3 %all-to-all-start.2 = ((bf16[8,16,1664]{2,1,0:T(8,128)(2,1)}), bf16[8,16,1664]{2,1,0:T(8,128)(2,1)S(1)}, u32[]{:S(2)}, u32[]{:S(2)}) async-start(bf16[8,16,1664]{2,1,0:T(8,128)(2,1)} %bitcast.43), calls=%async_computation.3 | async-start | bytes 851968 | tf_op jit(solution)/shard_map/all_to_all | solution.py:32
  91.1 86.7 %all-gather.6.cloned.1.call-start = ((), (), s32[]{:S(2)}) async-start(), calls=%async_computation.9 | async-start | bytes 2064384 | tf_op jit(solution)/shard_map/all_gather | solution.py:362
  99.5 12.1 %collective-permute-start.5 = (bf16[16,1664]{1,0:T(8,128)(2,1)S(1)}, bf16[16,1664]{1,0:T(8,128)(2,1)S(1)}, u32[]{:S(2)}, u32[]{:S(2)}) collective-permute-start(bf16[16,1664]{1,0:T(8,128)(2,1)S(1)} %get-tuple-element.30.final_ref), channel_id=1, source_target_pairs={{0,0},{1,16},{2,32},{3,48},{4,64},{5,80},{6,96},{7,112},{8,128},{9... | collective-permute-start | bytes 159752 | tf_op jit(solution)/shard_map/ppermute | solution.py:313
  107.4 4.3 %collective-permute-start.6 = (bf16[16,768]{1,0:T(8,128)(2,1)S(1)}, bf16[16,768]{1,0:T(8,128)(2,1)S(1)}, u32[]{:S(2)}, u32[]{:S(2)}) collective-permute-start(bf16[16,768]{1,0:T(8,128)(2,1)S(1)} %get-tuple-element.31), channel_id=1, source_target_pairs={{0,1},{1,0},{2,3},{3,2},{4,5},{5,4},{6,7},{7,6},{8,9},{9,8},{10,11... | collective-permute-start | bytes 73736 | tf_op jit(solution)/shard_map/ppermute | solution.py:28
  133.5 16.8 %all-to-all-start.4 = ((bf16[8,10,16,128]{3,2,1,0:T(8,128)(2,1)}), bf16[8,10,16,128]{3,2,1,0:T(8,128)(2,1)S(1)}, u32[]{:S(2)}, u32[]{:S(2)}) async-start(bf16[8,10,16,128]{3,2,1,0:T(8,128)(2,1)} %shard_map.133), calls=%async_computation.5 | async-start | bytes 655360 | tf_op jit(solution)/shard_map/all_to_all | solution.py:32
  150.3 0.7 copy-start.5
  162.7 19.0 %all-to-all-start.5 = ((bf16[16,16,1024]{2,1,0:T(8,128)(2,1)}), bf16[16,16,1024]{2,1,0:T(8,128)(2,1)S(1)}, u32[]{:S(2)}, u32[]{:S(2)}) async-start(bf16[16,16,1024]{2,1,0:T(8,128)(2,1)} %shard_map.134), calls=%async_computation.6 | async-start | bytes 1048576 | tf_op jit(solution)/shard_map/all_to_all | solution.py:370
Sparse Core Ops, SparseCore 0:
  15.0 56.2 reduce-scatter.1
  73.2 37.3 all-gather.3
  131.0 41.3 all-gather.5

commit v20 on v19

--- a/solution.py
+++ b/solution.py
@@ -253,7 +253,7 @@
             pltpu.VMEM((IHEADS * 16, 128), jnp.float32),
             pltpu.VMEM((IHEADS * 16, IDIM), jnp.bfloat16),
         ],
-        compiler_params=big_params(),
+        compiler_params=pltpu.CompilerParams(vmem_limit_bytes=59 * 1024 * 1024),
         cost_estimate=pl.CostEstimate(
             flops=4 * IHEADS * 16 * keys.shape[0] * IDIM, bytes_accessed=2 * keys.size * 2, transcendentals=0
         ),

time: 191 us -> 191 us (level)
  no operation moved by 1% of the time
where the time goes in v20:
time: 191 us; the launch traced here: 190 us
  blocking collectives  54.6 us (29%)
  starting transfers between devices  45.3 us (24%)
  waiting for transfers between devices  37.7 us (20%)
  Pallas kernels  24.8 us (13%)
  between operations  14.6 us (8%)
  local copies, waits for them, and re-layouts  12.6 us (7%)
    all_to_all x1, blocking collectives, down_weight_rows(): lax.all_to_all(jnp.broadcast_to(wide[None], (8,) + wide.shape), ('x', 'yl...  19.3 us
    all_to_all x1, blocking collectives, from_last(): lax.all_to_all(values, 'z', 0, 0, axis_index_groups=[list(range(NZ))[::-1]])  19.2 us
    ppermute x6, waiting for transfers between devices, swap(): return lax.ppermute(values, axis, [(0, 1), (1, 0)])  18.9 us
    all_to_all x2, waiting for transfers between devices, from_last(): lax.all_to_all(values, 'z', 0, 0, axis_index_groups=[list(range(NZ))[::-1]])  16.5 us
    all_to_all x1, blocking collectives, down_weight_rows(): mine = lax.all_to_all(own.transpose(1, 2, 0), 'z', 0, 0)  16.1 us
    all_to_all x2, starting transfers between devices, from_last(): lax.all_to_all(values, 'z', 0, 0, axis_index_groups=[list(range(NZ))[::-1]])  13.9 us
    all_to_all x1, starting transfers between devices, shards(): lax.all_to_all(scores, SEQ, 0, 0, axis_index_groups=[list(range(N_SEQ))[:...  11.9 us
    pallas_call x1, Pallas kernels, make_scores(): pl.pallas_call(score_kernel, grid=(N_SEQ // per_step,), in_specs=[pl.Bloc...  11.7 us
  transfers between devices with their start and end apart: 13, of which 7 were waited for; matrix products, arithmetic and copies ran while one was open for 6% of the time, Pallas kernels for 8%

profile of v20, /device:TPU:1, one launch (start us, length us, event | category | flops | bytes accessed | tf_op | source)
XLA Modules:
  0.0 189.9 jit_solution(12251223764266571735)
XLA Ops:
  7.2 7.6 %shard_map.130 = (bf16[8,2,128,896]{3,2,1,0:T(8,128)(2,1)}, bf16[768,512]{1,0:T(8,128)(2,1)}) custom-call(s32[1]{0:T(128)} %bitcast.2.place_ref, bf16[256,512]{1,0:T(8,128)(2,1)} %a_ref.1, bf16[512,7168]{1,0:T(8,128)(2,1)} %b_ref.1, bf16[16,7168]{1,0:T(8,128)(2,1)} %res_ref.1, bf16[1536,512]{1,0:T(8,128)(2,1)} %own_ref.1), custom_call_target="tpu_custom_call" | custom-call | tf_op jit(solution)/shard_map/pallas_call | solution.py:88
  14.9 3.8 %collective-permute-start.1 = (bf16[768,512]{1,0:T(8,128)(2,1)}, bf16[768,512]{1,0:T(8,128)(2,1)S(1)}, u32[]{:S(2)}, u32[]{:S(2)}) collective-permute-start(bf16[768,512]{1,0:T(8,128)(2,1)} %get-tuple-element.22), channel_id=1, source_target_pairs={{0,1},{1,0},{2,3},{3,2},{4,5},{5,4},{6,7},{7,6},{8,9},{9,8},{10,11... | collective-permute-start | bytes 2359304 | tf_op jit(solution)/shard_map/ppermute | solution.py:28
  20.8 16.1 %all_to_all.30 = bf16[8,56,100]{2,1,0:T(8,128)(2,1)S(1)} all-to-all(bf16[8,56,100]{2,1,0:T(8,128)(2,1)S(1)} %copy.29), channel_id=1, replica_groups=mesh['x'=4,'yl'=2,'c'=2,'z'=8,'yh'=2] {'z'}, dimensions={0} | all-to-all | bytes 179200 | tf_op jit(solution)/shard_map/all_to_all | solution.py:292
  37.1 5.0 %collective-permute-done = bf16[8,56,100]{2,1,0:T(8,128)(2,1)S(1)} collective-permute-done((bf16[8,56,100]{2,1,0:T(8,128)(2,1)S(1)}, bf16[8,56,100]{2,1,0:T(8,128)(2,1)S(1)}, u32[]{:S(2)}, u32[]{:S(2)}) %collective-permute-start) | collective-permute-done | bytes 89632 | tf_op jit(solution)/shard_map/ppermute | solution.py:28
  44.0 19.3 %all_to_all.31 = bf16[8,56,1664]{2,1,0:T(8,128)(2,1)S(1)} all-to-all(bf16[8,56,1664]{2,1,0:T(8,128)(2,1)S(1)} %broadcast_in_dim.7), channel_id=1, replica_groups=mesh['x'=4,'yl'=2,'c'=2,'z'=8,'yh'=2] {'x','yl'}, dimensions={0} | all-to-all | bytes 2981888 | tf_op jit(solution)/shard_map/all_to_all | solution.py:306
  63.3 5.9 %collective-permute-start.2 = (bf16[448,1664]{1,0:T(8,128)(2,1)S(1)}, bf16[448,1664]{1,0:T(8,128)(2,1)S(1)}, u32[]{:S(2)}, u32[]{:S(2)}) collective-permute-start(bf16[448,1664]{1,0:T(8,128)(2,1)S(1)} %bitcast.40), channel_id=1, source_target_pairs={{0,16},{16,0},{1,17},{17,1},{2,18},{18,2},{3,19},{19,3},{4,20},{20... | collective-permute-start | bytes 4472840 | tf_op jit(solution)/shard_map/ppermute | solution.py:28
  69.2 2.9 %collective-permute-done.2.other_ref = bf16[448,1664]{1,0:T(8,128)(2,1)S(1)} collective-permute-done((bf16[448,1664]{1,0:T(8,128)(2,1)S(1)}, bf16[448,1664]{1,0:T(8,128)(2,1)S(1)}, u32[]{:S(2)}, u32[]{:S(2)}) %collective-permute-start.2) | collective-permute-done | bytes 1490976 | tf_op jit(solution)/shard_map/ppermute | solution.py:28
  72.6 1.8 slice_bitcast_fusion
  74.4 1.2 collective-permute-start.3
  76.3 6.9 %collective-permute-done.3.got_ref = bf16[128,896]{1,0:T(8,128)(2,1)S(1)} collective-permute-done((bf16[128,896]{1,0:T(8,128)(2,1)}, bf16[128,896]{1,0:T(8,128)(2,1)S(1)}, u32[]{:S(2)}, u32[]{:S(2)}) %collective-permute-start.3) | collective-permute-done | bytes 229408 | tf_op jit(solution)/shard_map/ppermute | solution.py:28
  83.2 0.9 shard_map.131
  84.9 6.2 %all-to-all-start.2 = ((bf16[8,16,1664]{2,1,0:T(8,128)(2,1)}), bf16[8,16,1664]{2,1,0:T(8,128)(2,1)S(1)}, u32[]{:S(2)}, u32[]{:S(2)}) async-start(bf16[8,16,1664]{2,1,0:T(8,128)(2,1)} %bitcast.43), calls=%async_computation.3 | async-start | bytes 851968 | tf_op jit(solution)/shard_map/all_to_all | solution.py:32
  91.1 8.0 %all-to-all-done.2.parts_ref = bf16[8,16,1664]{2,1,0:T(8,128)(2,1)S(1)} async-done(((bf16[8,16,1664]{2,1,0:T(8,128)(2,1)}), bf16[8,16,1664]{2,1,0:T(8,128)(2,1)S(1)}, u32[]{:S(2)}, u32[]{:S(2)}) %all-to-all-start.2) | async-done | bytes 426016 | tf_op jit(solution)/shard_map/all_to_all | solution.py:32
  99.5 7.8 %collective-permute-start.5 = (bf16[16,1664]{1,0:T(8,128)(2,1)S(1)}, bf16[16,1664]{1,0:T(8,128)(2,1)S(1)}, u32[]{:S(2)}, u32[]{:S(2)}) collective-permute-start(bf16[16,1664]{1,0:T(8,128)(2,1)S(1)} %get-tuple-element.30.final_ref), channel_id=1, source_target_pairs={{0,0},{1,16},{2,32},{3,48},{4,64},{5,80},{6,96},{7,112},{8,128},{9... | collective-permute-start | bytes 159752 | tf_op jit(solution)/shard_map/ppermute | solution.py:313
  107.5 4.2 %collective-permute-done.6.beside_ref = bf16[16,768]{1,0:T(8,128)(2,1)S(1)} collective-permute-done((bf16[16,768]{1,0:T(8,128)(2,1)S(1)}, bf16[16,768]{1,0:T(8,128)(2,1)S(1)}, u32[]{:S(2)}, u32[]{:S(2)}) %collective-permute-start.6) | collective-permute-done | bytes 24608 | tf_op jit(solution)/shard_map/ppermute | solution.py:28
  111.7 19.2 %all_to_all.32 = bf16[8,16,1536]{2,1,0:T(8,128)(2,1)S(1)} all-to-all(bf16[8,16,1536]{2,1,0:T(8,128)(2,1)S(1)} %broadcast_in_dim.8), channel_id=1, replica_groups={{14,12,10,8,6,4,2,0},{15,13,11,9,7,5,3,1},{30,28,26,24,22,20,18,16},{31..., dimensions={0} | all-to-all | bytes 786432 | tf_op jit(solution)/shard_map/all_to_all | solution.py:32
  131.0 2.5 %shard_map.133 = bf16[8,10,16,128]{3,2,1,0:T(8,128)(2,1)} custom-call(s32[2]{0:T(128)S(1)} %pad_add_fusion.place_ref, bf16[128,1536]{1,0:T(8,128)(2,1)S(1)} %bitcast.42, bf16[1536,512]{1,0:T(8,128)(2,1)S(1)} %copy-done, bf16[768,512]{1,0:T(8,128)(2,1)S(1)} %copy-done.2, bf16[768,512]{1,0:T(8,128)(2,1)} %collective-permute-done.4.theirs_ref, ...), custom_call_target="tpu_custom_call" | custom-call | tf_op jit(solution)/shard_map/pallas_call | solution.py:199
  133.5 7.6 %all-to-all-start.4 = ((bf16[8,10,16,128]{3,2,1,0:T(8,128)(2,1)}), bf16[8,10,16,128]{3,2,1,0:T(8,128)(2,1)S(1)}, u32[]{:S(2)}, u32[]{:S(2)}) async-start(bf16[8,10,16,128]{3,2,1,0:T(8,128)(2,1)} %shard_map.133), calls=%async_computation.5 | async-start | bytes 655360 | tf_op jit(solution)/shard_map/all_to_all | solution.py:32
  141.7 8.5 %all-to-all-done.4.q_ref = bf16[8,10,16,128]{3,2,1,0:T(8,128)(2,1)S(1)} async-done(((bf16[8,10,16,128]{3,2,1,0:T(8,128)(2,1)}), bf16[8,10,16,128]{3,2,1,0:T(8,128)(2,1)S(1)}, u32[]{:S(2)}, u32[]{:S(2)}) %all-to-all-start.4) | async-done | bytes 327712 | tf_op jit(solution)/shard_map/all_to_all | solution.py:32
  151.0 11.7 %shard_map.134 = bf16[16,16,1024]{2,1,0:T(8,128)(2,1)} custom-call(bf16[8,10,16,128]{3,2,1,0:T(8,128)(2,1)} %copy-done.5, bf16[16,128]{1,0:T(8,128)(2,1)} %slice.27.w_ref, bf16[16384,128]{1,0:T(8,128)(2,1)} %all-gather.4.cloned.1.call-done.k_ref), custom_call_target="tpu_custom_call" | custom-call | flops 8589934592 | bytes 8388608 | tf_op jit(solution)/shard_map/pallas_call | solution.py:242
  162.7 11.9 %all-to-all-start.5 = ((bf16[16,16,1024]{2,1,0:T(8,128)(2,1)}), bf16[16,16,1024]{2,1,0:T(8,128)(2,1)S(1)}, u32[]{:S(2)}, u32[]{:S(2)}) async-start(bf16[16,16,1024]{2,1,0:T(8,128)(2,1)} %shard_map.134), calls=%async_computation.6 | async-start | bytes 1048576 | tf_op jit(solution)/shard_map/all_to_all | solution.py:370
  177.8 1.0 dynamic-slice_bitcast_fusion
  179.5 2.2 %all-to-all-done.5.s_ref = bf16[16,16,1024]{2,1,0:T(8,128)(2,1)S(1)} async-done(((bf16[16,16,1024]{2,1,0:T(8,128)(2,1)}), bf16[16,16,1024]{2,1,0:T(8,128)(2,1)S(1)}, u32[]{:S(2)}, u32[]{:S(2)}) %all-to-all-start.5) | async-done | bytes 524320 | tf_op jit(solution)/shard_map/all_to_all | solution.py:370
  181.7 1.7 shard_map.135
  (62 shorter events, 11.4 us)
Async XLA Ops:
  7.2 65.0 %reduce-scatter.2.cloned.1.call-start = ((), (), s32[]{:S(2)}) async-start(), calls=%async_computation.7 | async-start | bytes 4128768 | tf_op jit(solution)/shard_map/reduce_scatter | solution.py:340
  14.8 3.9 %copy-start.6 = (bf16[7168,4]{0,1:T(4,128)(2,1)S(1)}, bf16[7168,4]{0,1:T(4,128)(2,1)}, u32[]{:S(2)}) copy-start(bf16[7168,4]{0,1:T(4,128)(2,1)} %param.16) | copy-start | bytes 172036
  14.9 4.6 %copy-start.4 = (bf16[7168,96]{0,1:T(8,128)(2,1)S(1)}, bf16[7168,96]{0,1:T(8,128)(2,1)}, u32[]{:S(2)}) copy-start(bf16[7168,96]{0,1:T(8,128)(2,1)} %param.15) | copy-start | bytes 4128772
  14.9 135.4 %all-gather.4.cloned.1.call-start = ((), (), s32[]{:S(2)}) async-start(), calls=%async_computation.8 | async-start | bytes 4456448 | tf_op jit(solution)/shard_map/all_gather | solution.py:350
  14.9 28.0 %collective-permute-start.1 = (bf16[768,512]{1,0:T(8,128)(2,1)}, bf16[768,512]{1,0:T(8,128)(2,1)S(1)}, u32[]{:S(2)}, u32[]{:S(2)}) collective-permute-start(bf16[768,512]{1,0:T(8,128)(2,1)} %get-tuple-element.22), channel_id=1, source_target_pairs={{0,1},{1,0},{2,3},{3,2},{4,5},{5,4},{6,7},{7,6},{8,9},{9,8},{10,11... | collective-permute-start | bytes 2359304 | tf_op jit(solution)/shard_map/ppermute | solution.py:28
  36.9 5.1 %collective-permute-start = (bf16[8,56,100]{2,1,0:T(8,128)(2,1)S(1)}, bf16[8,56,100]{2,1,0:T(8,128)(2,1)S(1)}, u32[]{:S(2)}, u32[]{:S(2)}) collective-permute-start(bf16[8,56,100]{2,1,0:T(8,128)(2,1)S(1)} %all_to_all.30), channel_id=1, source_target_pairs={{0,1},{1,0},{2,3},{3,2},{4,5},{5,4},{6,7},{7,6},{8,9},{9,8},{10,11... | collective-permute-start | bytes 268808 | tf_op jit(solution)/shard_map/ppermute | solution.py:28
  43.0 0.9 copy-start.1
  63.3 8.9 %collective-permute-start.2 = (bf16[448,1664]{1,0:T(8,128)(2,1)S(1)}, bf16[448,1664]{1,0:T(8,128)(2,1)S(1)}, u32[]{:S(2)}, u32[]{:S(2)}) collective-permute-start(bf16[448,1664]{1,0:T(8,128)(2,1)S(1)} %bitcast.40), channel_id=1, source_target_pairs={{0,16},{16,0},{1,17},{17,1},{2,18},{18,2},{3,19},{19,3},{4,20},{20... | collective-permute-start | bytes 4472840 | tf_op jit(solution)/shard_map/ppermute | solution.py:28
  72.2 12.7 %collective-permute-start.4 = (bf16[768,512]{1,0:T(8,128)(2,1)}, bf16[768,512]{1,0:T(8,128)(2,1)}, u32[]{:S(2)}, u32[]{:S(2)}) collective-permute-start(bf16[768,512]{1,0:T(8,128)(2,1)} %copy-done.1), channel_id=1, source_target_pairs={{0,16},{16,0},{1,17},{17,1},{2,18},{18,2},{3,19},{19,3},{4,20},{20... | collective-permute-start | bytes 2359304 | tf_op jit(solution)/shard_map/ppermute | solution.py:28
  74.4 8.8 %collective-permute-start.3 = (bf16[128,896]{1,0:T(8,128)(2,1)}, bf16[128,896]{1,0:T(8,128)(2,1)S(1)}, u32[]{:S(2)}, u32[]{:S(2)}) collective-permute-start(bf16[128,896]{1,0:T(8,128)(2,1)} %get-tuple-element.51), channel_id=1, source_target_pairs={{0,1},{1,0},{2,3},{3,2},{4,5},{5,4},{6,7},{7,6},{8,9},{9,8},{10,11... | collective-permute-start | bytes 688136 | tf_op jit(solution)/shard_map/ppermute | solution.py:28
  83.2 7.9 %copy-start.7 = (bf16[1536]{0:T(1024)(128)(2,1)S(1)}, bf16[1536]{0:T(1024)(128)(2,1)}, u32[]{:S(2)}) copy-start(bf16[1536]{0:T(1024)(128)(2,1)} %param.17) | copy-start | bytes 9220
  84.1 0.8 copy-start.3
  84.8 46.2 %copy-start = (bf16[1536,512]{1,0:T(8,128)(2,1)S(1)}, bf16[1536,512]{1,0:T(8,128)(2,1)}, u32[]{:S(2)}) copy-start(bf16[1536,512]{1,0:T(8,128)(2,1)} %own_ref.1) | copy-start | bytes 4718596
  84.8 46.2 %copy-start.2 = (bf16[768,512]{1,0:T(8,128)(2,1)S(1)}, bf16[768,512]{1,0:T(8,128)(2,1)}, u32[]{:S(2)}) copy-start(bf16[768,512]{1,0:T(8,128)(2,1)} %copy-done.1) | copy-start | bytes 2359300
  84.9 14.3 %all-to-all-start.2 = ((bf16[8,16,1664]{2,1,0:T(8,128)(2,1)}), bf16[8,16,1664]{2,1,0:T(8,128)(2,1)S(1)}, u32[]{:S(2)}, u32[]{:S(2)}) async-start(bf16[8,16,1664]{2,1,0:T(8,128)(2,1)} %bitcast.43), calls=%async_computation.3 | async-start | bytes 851968 | tf_op jit(solution)/shard_map/all_to_all | solution.py:32
  91.1 86.7 %all-gather.6.cloned.1.call-start = ((), (), s32[]{:S(2)}) async-start(), calls=%async_computation.9 | async-start | bytes 2064384 | tf_op jit(solution)/shard_map/all_gather | solution.py:362
  99.5 12.1 %collective-permute-start.5 = (bf16[16,1664]{1,0:T(8,128)(2,1)S(1)}, bf16[16,1664]{1,0:T(8,128)(2,1)S(1)}, u32[]{:S(2)}, u32[]{:S(2)}) collective-permute-start(bf16[16,1664]{1,0:T(8,128)(2,1)S(1)} %get-tuple-element.30.final_ref), channel_id=1, source_target_pairs={{0,0},{1,16},{2,32},{3,48},{4,64},{5,80},{6,96},{7,112},{8,128},{9... | collective-permute-start | bytes 159752 | tf_op jit(solution)/shard_map/ppermute | solution.py:313
  107.4 4.3 %collective-permute-start.6 = (bf16[16,768]{1,0:T(8,128)(2,1)S(1)}, bf16[16,768]{1,0:T(8,128)(2,1)S(1)}, u32[]{:S(2)}, u32[]{:S(2)}) collective-permute-start(bf16[16,768]{1,0:T(8,128)(2,1)S(1)} %get-tuple-element.31), channel_id=1, source_target_pairs={{0,1},{1,0},{2,3},{3,2},{4,5},{5,4},{6,7},{7,6},{8,9},{9,8},{10,11... | collective-permute-start | bytes 73736 | tf_op jit(solution)/shard_map/ppermute | solution.py:28
  133.5 16.8 %all-to-all-start.4 = ((bf16[8,10,16,128]{3,2,1,0:T(8,128)(2,1)}), bf16[8,10,16,128]{3,2,1,0:T(8,128)(2,1)S(1)}, u32[]{:S(2)}, u32[]{:S(2)}) async-start(bf16[8,10,16,128]{3,2,1,0:T(8,128)(2,1)} %shard_map.133), calls=%async_computation.5 | async-start | bytes 655360 | tf_op jit(solution)/shard_map/all_to_all | solution.py:32
  150.3 0.7 copy-start.5
  162.7 19.0 %all-to-all-start.5 = ((bf16[16,16,1024]{2,1,0:T(8,128)(2,1)}), bf16[16,16,1024]{2,1,0:T(8,128)(2,1)S(1)}, u32[]{:S(2)}, u32[]{:S(2)}) async-start(bf16[16,16,1024]{2,1,0:T(8,128)(2,1)} %shard_map.134), calls=%async_computation.6 | async-start | bytes 1048576 | tf_op jit(solution)/shard_map/all_to_all | solution.py:370
Sparse Core Ops, SparseCore 0:
  15.0 56.2 reduce-scatter.1
  73.2 37.3 all-gather.3
  131.0 41.3 all-gather.5
